TPU v7x, 512 devices: a whole 4x4x16 slice. The times are simulated.
512 devices in a mesh: row: 64 (over z_hi, x, y, core), col: 8 (over z_lo).
Axes of the slice: x: 4, y: 4, z: 16 (z_hi: 2, z_lo: 8; z = z_hi * 8 + z_lo), core: 2. Of those that a mesh axis runs over, the one named last changes fastest.
Arguments:
- density: bfloat16 [1024, 64, 1024], P('row', None, 'col'), may hold values from -0.9 to 1.9
- columns: int32 [1024, 16], replicated, may hold values from 0 to 1023, as said below
Outputs:
- purified: float32 [1024, 64, 1024], P('row', None, 'col')
Inputs may be any that keep to these rules, and one draw needn't show every extreme that they name: Stored block a of row i lies in group a // 2: columns[i, a] is congruent to a // 2 modulo 8. The columns of a row are distinct and lie within cyclic distance 48 of i; row 0 always stores a block at distance exactly 48, and other rows may as well. The diagonal column i stands in slot (i mod 8) * 2.
All inputs are finite; a program needn't handle non-finite values.
Results may differ from a plain program's by a relative error of at most 0.0034.
Values may be sent and summed in bfloat16 or wider, within the bound.
No kernel may reach another device: no remote copies, remote signals or barrier semaphores. Data moves between devices by JAX's collectives and lax.ppermute only.
A program may use at most 64 MiB of HBM per device.

v0:
```python
import jax
import jax.numpy as jnp
from jax import lax
from jax.sharding import PartitionSpec as P

SPAN = 3


def passed_along(block, axis, distance):
    devices = range(lax.axis_size(axis))
    route = [((i - distance) % len(devices), i) for i in devices]
    return lax.ppermute(block, axis, route)


def fetch_panels(density):
    panels = []
    for offset in range(-SPAN, SPAN + 1):
        if offset == 0:
            panels.append(density)
        else:
            panels.append(passed_along(density, "row", -offset))
    return panels


def make_accumulate(table, flat_index, live):

    def accumulate(total, piece, start):
        width = table.shape[1]
        count = piece.shape[2] // width
        chosen = jnp.take(table, flat_index, axis=0)
        chosen = jnp.where(live[..., None, None], chosen, jnp.zeros((), table.dtype))
        left = piece.reshape(piece.shape[0], width, count, width)
        part = jnp.einsum("ixby,iabyz->ixaz", left, chosen, preferred_element_type=jnp.float32)
        return part.reshape(total.shape)

    return accumulate


def shards(density, columns):
    row_index = lax.axis_index("row")
    col_index = lax.axis_index("col")
    local_rows = density.shape[0]
    width = density.shape[1]
    group_size = density.shape[2] // width
    total = columns.shape[0]
    panel_count = 2 * SPAN + 1
    base = row_index * local_rows
    own_columns = lax.dynamic_slice_in_dim(columns, base, local_rows, 0)
    group_columns = lax.dynamic_slice_in_dim(own_columns, col_index * group_size, group_size, 1)
    distance = jnp.mod(own_columns - base + total // 2, total) - total // 2
    owner = jnp.floor_divide(distance, local_rows)
    inner = distance - owner * local_rows
    panel_row = (owner + SPAN) * local_rows + inner
    shifts = jnp.arange(panel_count, dtype=jnp.int32)[:, None] - SPAN
    within = jnp.arange(local_rows, dtype=jnp.int32)[None, :]
    global_rows = jnp.mod(base + shifts * local_rows + within, total).reshape(-1)
    panel_columns = jnp.take(columns, global_rows, axis=0)
    panel_columns = lax.dynamic_slice_in_dim(panel_columns, col_index * group_size, group_size, 1)
    candidates = jnp.take(panel_columns, panel_row, axis=0)
    equal = candidates[:, None, :, :] == group_columns[:, :, None, None]
    live = jnp.any(equal, axis=-1)
    slots = jnp.arange(group_size, dtype=jnp.int32)
    chosen_slot = jnp.sum(jnp.where(equal, slots, 0), axis=-1)
    flat_index = panel_row[:, None, :] * group_size + chosen_slot
    panels = fetch_panels(density)
    stacked = jnp.stack(panels)
    table = stacked.reshape(panel_count, local_rows, width, group_size, width)
    table = table.transpose(0, 1, 3, 2, 4).reshape(
        panel_count * local_rows * group_size, width, width
    )
    accumulate = make_accumulate(table, flat_index, live)
    empty = jnp.zeros(density.shape, jnp.float32)
    square = accumulate(
        empty, lax.all_gather(density, "col", axis=2, tiled=True), jnp.int32(0)
    ).astype(jnp.bfloat16)
    cube = accumulate(empty, lax.all_gather(square, "col", axis=2, tiled=True), jnp.int32(0))
    return 3.0 * square.astype(jnp.float32) - 2.0 * cube


def solution(mesh):
    placed = (P("row", None, "col"), P())
    return jax.shard_map(
        shards, mesh=mesh, in_specs=placed, out_specs=P("row", None, "col"), check_vma=False
    )
```

profile of v0, /device:TPU:4, one launch (start us, length us, event | category | flops | bytes accessed | tf_op | source)
XLA Modules:
  0.0 257.1 jit_solution(7515931952301542747)
XLA Ops:
  6.5 2.9 %collective-permute-start = (bf16[16,64,128]{2,1,0:T(8,128)(2,1)}, bf16[16,64,128]{2,1,0:T(8,128)(2,1)S(1)}, u32[]{:S(2)}, u32[]{:S(2)}) collective-permute-start(bf16[16,64,128]{2,1,0:T(8,128)(2,1)} %param.4), channel_id=1, source_target_pairs={{488,0},{496,8},{504,16},{0,24},{8,32},{16,40},{24,48},{32,56},{40... | collective-permute-start | bytes 786440 | tf_op jit(solution)/shard_map/ppermute | solution.py:12
  9.5 3.5 %collective-permute-start.1 = (bf16[16,64,128]{2,1,0:T(8,128)(2,1)}, bf16[16,64,128]{2,1,0:T(8,128)(2,1)S(1)}, u32[]{:S(2)}, u32[]{:S(2)}) collective-permute-start(bf16[16,64,128]{2,1,0:T(8,128)(2,1)} %param.4), channel_id=1, source_target_pairs={{496,0},{504,8},{0,16},{8,24},{16,32},{24,40},{32,48},{40,56},{48,... | collective-permute-start | bytes 786440 | tf_op jit(solution)/shard_map/ppermute | solution.py:12
  13.0 3.0 %collective-permute-start.2 = (bf16[16,64,128]{2,1,0:T(8,128)(2,1)}, bf16[16,64,128]{2,1,0:T(8,128)(2,1)S(1)}, u32[]{:S(2)}, u32[]{:S(2)}) collective-permute-start(bf16[16,64,128]{2,1,0:T(8,128)(2,1)} %param.4), channel_id=1, source_target_pairs={{504,0},{0,8},{8,16},{16,24},{24,32},{32,40},{40,48},{48,56},{56,6... | collective-permute-start | bytes 786440 | tf_op jit(solution)/shard_map/ppermute | solution.py:12
  16.0 5.0 %collective-permute-start.3 = (bf16[16,64,128]{2,1,0:T(8,128)(2,1)}, bf16[16,64,128]{2,1,0:T(8,128)(2,1)S(1)}, u32[]{:S(2)}, u32[]{:S(2)}) collective-permute-start(bf16[16,64,128]{2,1,0:T(8,128)(2,1)} %param.4), channel_id=1, source_target_pairs={{8,0},{16,8},{24,16},{32,24},{40,32},{48,40},{56,48},{64,56},{72,6... | collective-permute-start | bytes 786440 | tf_op jit(solution)/shard_map/ppermute | solution.py:12
  21.0 2.3 collective-permute-start.4
  23.4 0.8 broadcast_multiply_fusion
  24.3 1.0 copy.48
  25.8 0.6 gather_fusion
  26.5 0.7 gather_fusion.1
  27.6 0.8 dynamic_slice.11
  28.5 1.9 collective-permute-start.5
  30.4 1.2 stack.27
  33.2 3.8 %collective-permute-done.5 = bf16[16,64,128]{2,1,0:T(8,128)(2,1)} collective-permute-done((bf16[16,64,128]{2,1,0:T(8,128)(2,1)}, bf16[16,64,128]{2,1,0:T(8,128)(2,1)}, u32[]{:S(2)}, u32[]{:S(2)}) %collective-permute-start.5) | collective-permute-done | bytes 262176 | tf_op jit(solution)/shard_map/ppermute | solution.py:12
  37.0 2.0 stack.30
  38.9 0.9 copy_dynamic-update-slice_fusion.6
  39.9 1.0 copy_dynamic-update-slice_fusion.5
  40.9 0.9 copy_dynamic-update-slice_fusion.4
  41.8 0.9 copy_dynamic-update-slice_fusion.3
  42.7 0.9 copy_dynamic-update-slice_fusion.2
  43.7 0.9 copy_dynamic-update-slice_fusion.1
  44.6 0.9 copy_dynamic-update-slice_fusion
  45.5 21.8 %gather_fusion.2 = bf16[512,64,64]{2,1,0:T(8,128)(2,1)} fusion(bf16[224,64,64]{2,1,0:T(8,128)(2,1)} %bitcast.3, s32[1024]{0:T(1024)S(1)} %pad_clamp_fusion), kind=kCustom, calls=%fused_computation.clone | custom fusion | bytes 8390656 | tf_op jit(solution)/shard_map/jit(_take)/gather | solution.py:30
  67.3 41.2 %all-gather.3.cloned.1.call-done = bf16[16,64,1024]{2,1,0:T(8,128)(2,1)} async-done(((bf16[16,64,128]{2,1,0:T(8,128)(2,1)}), bf16[16,64,1024]{2,1,0:T(8,128)(2,1)}) %all-gather.3.cloned.1.call-update) | async-done | bytes 2097168 | tf_op jit(solution)/shard_map/all_gather | solution.py:74
  108.6 6.4 %reshape.128 = bf16[16,64,16,64]{3,2,1,0:T(8,128)(2,1)} reshape(bf16[16,64,1024]{2,1,0:T(8,128)(2,1)} %all-gather.3.cloned.1.call-done) | data formatting | bytes 4194304 | tf_op jit(solution)/shard_map/reshape | solution.py:32
  115.0 7.2 %fusion.17 = bf16[16,2,64,64]{3,2,1,0:T(8,128)(2,1)S(1)} fusion(bf16[16,64,16,64,1]{3,2,1,0,4:T(8,128)(2,1)} %bitcast.25, bf16[16,2,16,64,64]{4,3,2,1,0:T(8,128)(2,1)} %bitcast.22, pred[16,2,16]{2,1,0:T(4,128)(4,1)S(1)} %copy.53, pred[16,2,16]{2,1,0:T(4,128)(4,1)S(1)} %copy.51), kind=kOutput, calls=%fused_computation.15 | convolution fusion | flops 272760832 | bytes 6554624 | tf_op jit(solution)/shard_map/ixby,iabyz->ixaz/dot_general | solution.py:33
  122.2 0.9 copy.64
  123.1 112.1 %all-gather.5.cloned.1.call-done = bf16[16,64,1024]{2,1,0:T(8,128)(2,1)} async-done(((bf16[16,64,128]{2,1,0:T(8,128)(2,1)}), bf16[16,64,1024]{2,1,0:T(8,128)(2,1)}) %all-gather.5.cloned.1.call-update) | async-done | bytes 2097168 | tf_op jit(solution)/shard_map/all_gather | solution.py:76
  235.2 6.4 %reshape.129 = bf16[16,64,16,64]{3,2,1,0:T(8,128)(2,1)} reshape(bf16[16,64,1024]{2,1,0:T(8,128)(2,1)} %all-gather.5.cloned.1.call-done) | data formatting | bytes 4194304 | tf_op jit(solution)/shard_map/reshape | solution.py:32
  241.6 6.3 %fusion.14 = f32[16,64,2,64]{3,1,2,0:T(8,128)S(1)} fusion(bf16[16,2,16,64,64]{4,3,2,1,0:T(8,128)(2,1)} %bitcast.23, pred[16,2,16]{2,1,0:T(4,128)(4,1)S(1)} %copy.53, pred[16,2,16]{2,1,0:T(4,128)(4,1)S(1)} %copy.51, bf16[16,64,16,64,1]{3,2,1,0,4:T(8,128)(2,1)} %bitcast.24), kind=kOutput, calls=%fused_computation.14 | convolution fusion | flops 272760832 | bytes 6816768 | tf_op jit(solution)/shard_map/ixby,iabyz->ixaz/dot_general | solution.py:33
  248.0 0.8 copy.67
  248.8 0.6 mul.54
  249.4 0.9 multiply_subtract_fusion
  (42 shorter events, 2.5 us)
Async XLA Ops:
  6.5 102.0 %all-gather.3.cloned.1.call-start = ((), (), s32[]{:S(2)}) async-start(), calls=%async_computation | async-start | bytes 2359296 | tf_op jit(solution)/shard_map/all_gather | solution.py:74
  6.5 21.9 %collective-permute-start = (bf16[16,64,128]{2,1,0:T(8,128)(2,1)}, bf16[16,64,128]{2,1,0:T(8,128)(2,1)S(1)}, u32[]{:S(2)}, u32[]{:S(2)}) collective-permute-start(bf16[16,64,128]{2,1,0:T(8,128)(2,1)} %param.4), channel_id=1, source_target_pairs={{488,0},{496,8},{504,16},{0,24},{8,32},{16,40},{24,48},{32,56},{40... | collective-permute-start | bytes 786440 | tf_op jit(solution)/shard_map/ppermute | solution.py:12
  9.5 22.7 %collective-permute-start.1 = (bf16[16,64,128]{2,1,0:T(8,128)(2,1)}, bf16[16,64,128]{2,1,0:T(8,128)(2,1)S(1)}, u32[]{:S(2)}, u32[]{:S(2)}) collective-permute-start(bf16[16,64,128]{2,1,0:T(8,128)(2,1)} %param.4), channel_id=1, source_target_pairs={{496,0},{504,8},{0,16},{8,24},{16,32},{24,40},{32,48},{40,56},{48,... | collective-permute-start | bytes 786440 | tf_op jit(solution)/shard_map/ppermute | solution.py:12
  13.0 19.4 %collective-permute-start.2 = (bf16[16,64,128]{2,1,0:T(8,128)(2,1)}, bf16[16,64,128]{2,1,0:T(8,128)(2,1)S(1)}, u32[]{:S(2)}, u32[]{:S(2)}) collective-permute-start(bf16[16,64,128]{2,1,0:T(8,128)(2,1)} %param.4), channel_id=1, source_target_pairs={{504,0},{0,8},{8,16},{16,24},{24,32},{32,40},{40,48},{48,56},{56,6... | collective-permute-start | bytes 786440 | tf_op jit(solution)/shard_map/ppermute | solution.py:12
  16.0 16.6 %collective-permute-start.3 = (bf16[16,64,128]{2,1,0:T(8,128)(2,1)}, bf16[16,64,128]{2,1,0:T(8,128)(2,1)S(1)}, u32[]{:S(2)}, u32[]{:S(2)}) collective-permute-start(bf16[16,64,128]{2,1,0:T(8,128)(2,1)} %param.4), channel_id=1, source_target_pairs={{8,0},{16,8},{24,16},{32,24},{40,32},{48,40},{56,48},{64,56},{72,6... | collective-permute-start | bytes 786440 | tf_op jit(solution)/shard_map/ppermute | solution.py:12
  21.0 11.9 %collective-permute-start.4 = (bf16[16,64,128]{2,1,0:T(8,128)(2,1)}, bf16[16,64,128]{2,1,0:T(8,128)(2,1)S(1)}, u32[]{:S(2)}, u32[]{:S(2)}) collective-permute-start(bf16[16,64,128]{2,1,0:T(8,128)(2,1)} %param.4), channel_id=1, source_target_pairs={{16,0},{24,8},{32,16},{40,24},{48,32},{56,40},{64,48},{72,56},{80,... | collective-permute-start | bytes 786440 | tf_op jit(solution)/shard_map/ppermute | solution.py:12
  23.3 211.9 %all-gather.5.cloned.1.call-start = ((), (), s32[]{:S(2)}) async-start(), calls=%async_computation.1 | async-start | bytes 2359296 | tf_op jit(solution)/shard_map/all_gather | solution.py:76
  28.5 8.5 %collective-permute-start.5 = (bf16[16,64,128]{2,1,0:T(8,128)(2,1)}, bf16[16,64,128]{2,1,0:T(8,128)(2,1)}, u32[]{:S(2)}, u32[]{:S(2)}) collective-permute-start(bf16[16,64,128]{2,1,0:T(8,128)(2,1)} %param.4), channel_id=1, source_target_pairs={{24,0},{32,8},{40,16},{48,24},{56,32},{64,40},{72,48},{80,56},{88,... | collective-permute-start | bytes 786440 | tf_op jit(solution)/shard_map/ppermute | solution.py:12
  38.9 5.6 %copy-start.1 = (bf16[1,16,64,2,64]{4,3,2,1,0:T(2,128)(2,1)S(1)}, bf16[1,16,64,2,64]{4,3,2,1,0:T(2,128)(2,1)}, u32[]{:S(2)}) copy-start(bf16[1,16,64,2,64]{4,3,2,1,0:T(2,128)(2,1)} %stack.30) | copy-start | bytes 786436
  241.6 7.8 %copy-start = (bf16[16,64,128]{2,1,0:T(8,128)(2,1)S(1)}, bf16[16,64,128]{2,1,0:T(8,128)(2,1)}, u32[]{:S(2)}) copy-start(bf16[16,64,128]{2,1,0:T(8,128)(2,1)} %copy.64) | copy-start | bytes 786436
Sparse Core Ops, SparseCore 0:
  23.4 85.0 all-gather.2
  123.2 111.8 all-gather.4
where the time goes:
time: 258 us; the launch traced here: 257 us
  waiting for transfers between devices  157 us (61%)
  local copies, waits for them, and re-layouts  51.9 us (20%)
  starting transfers between devices  18.7 us (7%)
  between operations  13.7 us (5%)
  matrix products  13.5 us (5%)
    all_gather x1, waiting for transfers between devices, shards(): lax.all_gather(square, 'col', axis=2, tiled=True)  112 us
    all_gather x1, waiting for transfers between devices, shards(): lax.all_gather(density, 'col', axis=2, tiled=True)  41.2 us
    gather x1, local copies, waits for them, and re-layouts, accumulate(): chosen = jnp.take(table, flat_index, axis=0)  21.8 us
    ppermute x6, starting transfers between devices, passed_along(): return lax.ppermute(block, axis, route)  18.6 us
    dot_general x2, matrix products, accumulate(): jnp.einsum('ixby,iabyz->ixaz', left, chosen, preferred_element_type=jnp.f...  13.5 us
    reshape x2, local copies, waits for them, and re-layouts, accumulate(): left = piece.reshape(piece.shape[0], width, count, width)  12.8 us
    unnamed x11, local copies, waits for them, and re-layouts  6.65 us
    another operation x8, local copies, waits for them, and re-layouts, shards(): stacked = jnp.stack(panels)  5.35 us
  transfers between devices with their start and end apart: 8, of which 3 were waited for; matrix products, arithmetic and copies ran while one was open for 15% of the time, Pallas kernels for 0%

commit v1 on v0

v1 whole, which is shorter than its diff:
```python
import jax
import jax.numpy as jnp
from jax import lax
from jax.experimental import pallas as pl
from jax.experimental.pallas import tpu as pltpu
from jax.sharding import PartitionSpec as P

PARTS = 2


def ring_order(count):
    return list(range(0, count, 2)) + list(range(count - 1, 0, -2))


def product_kernel(count, group, keep, index_ref, mask_ref, table_ref, *refs):
    chunks = refs[:count]
    out_ref = refs[-1]
    rows, width, lanes = chunks[0].shape
    blocks = count * group
    for i in range(rows):
        total = None
        for step in range(0, count, 2):
            left = jnp.concatenate([chunks[step][i], chunks[step + 1][i]], axis=1)
            pieces = []
            for b in range(step * group, (step + 2) * group):
                piece = table_ref[index_ref[i * blocks + b]]
                piece = jnp.concatenate([piece, piece], axis=1)
                mask = mask_ref[pl.ds(i * blocks + b, 1), :].astype(piece.dtype)
                pieces.append(piece * mask)
            right = jnp.concatenate(pieces, axis=0)
            part = jnp.dot(left, right, preferred_element_type=jnp.float32)
            total = part if total is None else total + part
        value = total[:, :lanes] + pltpu.roll(total[:, lanes:], width, 1)
        if keep:
            value = 3.0 * refs[count][i].astype(jnp.float32) - 2.0 * value
        out_ref[i] = value.astype(out_ref.dtype)


def product(index, mask, table, chunks, square=None):
    count = len(chunks)
    rows, width, lanes = chunks[0].shape
    group = lanes // width
    keep = square is not None
    vmem = pl.BlockSpec(memory_space=pltpu.VMEM)
    operands = list(chunks) + ([square] if keep else [])
    return pl.pallas_call(
        lambda *refs: product_kernel(count, group, keep, *refs),
        out_shape=jax.ShapeDtypeStruct(
            chunks[0].shape, jnp.float32 if keep else jnp.bfloat16
        ),
        in_specs=[pl.BlockSpec(memory_space=pltpu.SMEM)] + [vmem] * (2 + len(operands)),
        out_specs=vmem,
        compiler_params=pltpu.CompilerParams(vmem_limit_bytes=24 * 1024 * 1024),
        cost_estimate=pl.CostEstimate(
            flops=4 * rows * width * lanes * lanes * count,
            bytes_accessed=8 * 1024 * 1024,
            transcendentals=0,
        ),
    )(index, mask, table, *operands)


def gather_parts(parts, axis):
    count = lax.axis_size(axis)
    order = ring_order(count)
    route = [(order[t], order[(t + 1) % count]) for t in range(count)]
    gathered = [[part] for part in parts]
    for _ in range(count - 1):
        for chain in gathered:
            chain.append(lax.ppermute(chain[-1], axis, route))
    return gathered


def gather_table(density, axis):
    rows = lax.axis_size(axis)
    up = [(r, (r + 2) % rows) for r in range(rows)]
    down = [(r, (r - 2) % rows) for r in range(rows)]
    far = [(r, (r + 3) % rows if r % 2 else (r - 3) % rows) for r in range(rows)]
    other = [(r, r ^ 1) for r in range(rows)]
    before = lax.ppermute(density, axis, up)
    after = lax.ppermute(density, axis, down)
    extra = lax.ppermute(density, axis, far)
    near = jnp.concatenate([before, density, after], axis=0)
    return jnp.concatenate([near, lax.ppermute(near, axis, other), extra], axis=0)


def table_slot(distance, row_index, local_rows):
    owner = jnp.floor_divide(distance, local_rows)
    inner = distance - owner * local_rows
    core = jnp.mod(row_index, 2)
    place = owner + core
    pair = jnp.floor_divide(place, 2)
    same = jnp.mod(place, 2) == core
    panel = jnp.where(jnp.abs(pair) == 2, 6, jnp.where(same, pair + 1, pair + 4))
    return panel * local_rows + inner


def shards(density, columns):
    row_index = lax.axis_index("row")
    col_index = lax.axis_index("col")
    local_rows, width, lanes = density.shape
    group = lanes // width
    total, stored = columns.shape
    count = stored // group
    base = row_index * local_rows

    order = ring_order(count)
    arrival = [[0] * count for _ in range(count)]
    for t in range(count):
        arrival[order[t]] = [order[(t - s) % count] for s in range(count)]
    arrival = lax.dynamic_index_in_dim(
        jnp.array(arrival, jnp.int32), col_index, 0, keepdims=False
    )

    own = lax.dynamic_slice_in_dim(columns, base, local_rows, 0)
    goal = lax.dynamic_slice_in_dim(own, col_index * group, group, 1)
    own = jnp.take(own.reshape(local_rows, count, group), arrival, axis=1)
    own = own.reshape(local_rows, stored)
    distance = jnp.mod(own - base + total // 2, total) - total // 2
    index = table_slot(distance, row_index, local_rows).reshape(-1)
    held = lax.dynamic_slice_in_dim(columns, col_index * group, group, 1)
    held = jnp.take(held, own.reshape(-1), axis=0).reshape(local_rows, stored, group)
    lane_slot = jnp.arange(lanes, dtype=jnp.int32) // width
    mine = jnp.where(lane_slot == 0, held[..., :1], held[..., 1:])
    direct = jnp.where(lane_slot == 0, goal[:, None, :1], goal[:, None, 1:])
    swapped = jnp.where(lane_slot == 0, goal[:, None, 1:], goal[:, None, :1])
    mask = jnp.concatenate([mine == direct, mine == swapped], axis=-1)
    mask = mask.astype(jnp.float32).reshape(local_rows * stored, 2 * lanes)

    half = local_rows // PARTS
    cuts = [slice(p * half, (p + 1) * half) for p in range(PARTS)]
    metas = [slice(p * half * stored, (p + 1) * half * stored) for p in range(PARTS)]
    left = gather_parts([density[cut] for cut in cuts], "col")
    table = gather_table(density, "row")
    table = table.reshape(-1, width, lanes)
    squares = [
        product(index[meta], mask[meta], table, chain)
        for meta, chain in zip(metas, left)
    ]
    left = gather_parts(squares, "col")
    outs = [
        product(index[meta], mask[meta], table, chain, square)
        for meta, chain, square in zip(metas, left, squares)
    ]
    return jnp.concatenate(outs, axis=0)


def solution(mesh):
    placed = (P("row", None, "col"), P())
    return jax.shard_map(
        shards, mesh=mesh, in_specs=placed, out_specs=P("row", None, "col"), check_vma=False
    )
```

time: 258 us -> 193 us (0.75)
  the two profiles are of different devices: /device:TPU:4 before, /device:TPU:96 now
where the time goes in v1:
time: 193 us; the launch traced here: 192 us
  waiting for transfers between devices  89.8 us (47%)
  starting transfers between devices  85 us (44%)
  local copies, waits for them, and re-layouts  7.13 us (4%)
  Pallas kernels  5.86 us (3%)
  other arithmetic  3.73 us (2%)
    ppermute x28, waiting for transfers between devices, gather_parts(): chain.append(lax.ppermute(chain[-1], axis, route))  89.8 us
    ppermute x28, starting transfers between devices, gather_parts(): chain.append(lax.ppermute(chain[-1], axis, route))  60.4 us
    ppermute x1, starting transfers between devices, gather_table(): after = lax.ppermute(density, axis, down)  16.1 us
    pallas_call x4, Pallas kernels, product(): pl.pallas_call(lambda *refs: product_kernel(count, group, keep, *refs), o...  5.86 us
  transfers between devices with their start and end apart: 32, of which 23 were waited for; matrix products, arithmetic and copies ran while one was open for 5% of the time, Pallas kernels for 2%

profile of v1, /device:TPU:96, one launch (start us, length us, event | category | flops | bytes accessed | tf_op | source)
XLA Modules:
  0.0 192.1 jit_solution(8979450759223671665)
XLA Ops:
  0.0 3.6 %collective-permute-start = (bf16[16,64,128]{2,1,0:T(8,128)(2,1)}, bf16[16,64,128]{2,1,0:T(8,128)(2,1)S(1)}, u32[]{:S(2)}, u32[]{:S(2)}) collective-permute-start(bf16[16,64,128]{2,1,0:T(8,128)(2,1)} %param.3), channel_id=1, source_target_pairs={{0,16},{8,24},{16,32},{24,40},{32,48},{40,56},{48,64},{56,72},{64,... | collective-permute-start | bytes 786440 | tf_op jit(solution)/shard_map/ppermute | solution.py:79
  3.6 16.1 %collective-permute-start.1 = (bf16[16,64,128]{2,1,0:T(8,128)(2,1)}, bf16[16,64,128]{2,1,0:T(8,128)(2,1)S(1)}, u32[]{:S(2)}, u32[]{:S(2)}) collective-permute-start(bf16[16,64,128]{2,1,0:T(8,128)(2,1)} %param.3), channel_id=1, source_target_pairs={{0,496},{8,504},{16,0},{24,8},{32,16},{40,24},{48,32},{56,40},{64,... | collective-permute-start | bytes 786440 | tf_op jit(solution)/shard_map/ppermute | solution.py:80
  19.7 3.0 %collective-permute-start.3 = (bf16[16,64,128]{2,1,0:T(8,128)(2,1)}, bf16[16,64,128]{2,1,0:T(8,128)(2,1)}, u32[]{:S(2)}, u32[]{:S(2)}) collective-permute-start(bf16[16,64,128]{2,1,0:T(8,128)(2,1)} %param.3), channel_id=1, source_target_pairs={{0,488},{8,32},{16,504},{24,48},{32,8},{40,64},{48,24},{56,80},{64... | collective-permute-start | bytes 786440 | tf_op jit(solution)/shard_map/ppermute | solution.py:81
  23.7 3.4 %collective-permute-start.18 = (bf16[8,64,128]{2,1,0:T(8,128)(2,1)S(1)}, bf16[8,64,128]{2,1,0:T(8,128)(2,1)S(1)}, u32[]{:S(2)}, u32[]{:S(2)}) collective-permute-start(bf16[8,64,128]{2,1,0:T(8,128)(2,1)S(1)} %get-tuple-element.6.refs_3_), channel_id=1, source_target_pairs={{0,2},{2,4},{4,6},{6,7},{7,5},{5,3},{3,1},{1,0},{8,10},{10,12},{12... | collective-permute-start | bytes 393224 | tf_op jit(solution)/shard_map/ppermute | solution.py:69
  27.1 3.7 %collective-permute-start.4 = (bf16[8,64,128]{2,1,0:T(8,128)(2,1)S(1)}, bf16[8,64,128]{2,1,0:T(8,128)(2,1)S(1)}, u32[]{:S(2)}, u32[]{:S(2)}) collective-permute-start(bf16[8,64,128]{2,1,0:T(8,128)(2,1)S(1)} %get-tuple-element.5.refs_3_), channel_id=1, source_target_pairs={{0,2},{2,4},{4,6},{6,7},{7,5},{5,3},{3,1},{1,0},{8,10},{10,12},{12... | collective-permute-start | bytes 393224 | tf_op jit(solution)/shard_map/ppermute | solution.py:69
  37.3 23.6 %collective-permute-done.18.refs_4_ = bf16[8,64,128]{2,1,0:T(8,128)(2,1)S(1)} collective-permute-done((bf16[8,64,128]{2,1,0:T(8,128)(2,1)S(1)}, bf16[8,64,128]{2,1,0:T(8,128)(2,1)S(1)}, u32[]{:S(2)}, u32[]{:S(2)}) %collective-permute-start.18) | collective-permute-done | bytes 131104 | tf_op jit(solution)/shard_map/ppermute | solution.py:69
  60.9 2.0 %collective-permute-start.19 = (bf16[8,64,128]{2,1,0:T(8,128)(2,1)S(1)}, bf16[8,64,128]{2,1,0:T(8,128)(2,1)S(1)}, u32[]{:S(2)}, u32[]{:S(2)}) collective-permute-start(bf16[8,64,128]{2,1,0:T(8,128)(2,1)S(1)} %collective-permute-done.18.refs_4_), channel_id=1, source_target_pairs={{0,2},{2,4},{4,6},{6,7},{7,5},{5,3},{3,1},{1,0},{8,10},{10,12},{12... | collective-permute-start | bytes 393224 | tf_op jit(solution)/shard_map/ppermute | solution.py:69
  64.6 2.7 %collective-permute-start.5 = (bf16[8,64,128]{2,1,0:T(8,128)(2,1)S(1)}, bf16[8,64,128]{2,1,0:T(8,128)(2,1)S(1)}, u32[]{:S(2)}, u32[]{:S(2)}) collective-permute-start(bf16[8,64,128]{2,1,0:T(8,128)(2,1)S(1)} %collective-permute-done.4.refs_4_), channel_id=1, source_target_pairs={{0,2},{2,4},{4,6},{6,7},{7,5},{5,3},{3,1},{1,0},{8,10},{10,12},{12... | collective-permute-start | bytes 393224 | tf_op jit(solution)/shard_map/ppermute | solution.py:69
  67.3 2.5 %collective-permute-done.19.refs_5_ = bf16[8,64,128]{2,1,0:T(8,128)(2,1)S(1)} collective-permute-done((bf16[8,64,128]{2,1,0:T(8,128)(2,1)S(1)}, bf16[8,64,128]{2,1,0:T(8,128)(2,1)S(1)}, u32[]{:S(2)}, u32[]{:S(2)}) %collective-permute-start.19) | collective-permute-done | bytes 131104 | tf_op jit(solution)/shard_map/ppermute | solution.py:69
  69.9 1.9 collective-permute-start.20
  71.8 3.0 %collective-permute-done.5.refs_5_ = bf16[8,64,128]{2,1,0:T(8,128)(2,1)S(1)} collective-permute-done((bf16[8,64,128]{2,1,0:T(8,128)(2,1)S(1)}, bf16[8,64,128]{2,1,0:T(8,128)(2,1)S(1)}, u32[]{:S(2)}, u32[]{:S(2)}) %collective-permute-start.5) | collective-permute-done | bytes 131104 | tf_op jit(solution)/shard_map/ppermute | solution.py:69
  79.7 1.9 collective-permute-start.21
  81.6 2.2 %collective-permute-done.6.refs_6_ = bf16[8,64,128]{2,1,0:T(8,128)(2,1)S(1)} collective-permute-done((bf16[8,64,128]{2,1,0:T(8,128)(2,1)S(1)}, bf16[8,64,128]{2,1,0:T(8,128)(2,1)S(1)}, u32[]{:S(2)}, u32[]{:S(2)}) %collective-permute-start.6) | collective-permute-done | bytes 131104 | tf_op jit(solution)/shard_map/ppermute | solution.py:69
  85.8 4.2 %collective-permute-done.21.refs_7_ = bf16[8,64,128]{2,1,0:T(8,128)(2,1)S(1)} collective-permute-done((bf16[8,64,128]{2,1,0:T(8,128)(2,1)S(1)}, bf16[8,64,128]{2,1,0:T(8,128)(2,1)S(1)}, u32[]{:S(2)}, u32[]{:S(2)}) %collective-permute-start.21) | collective-permute-done | bytes 131104 | tf_op jit(solution)/shard_map/ppermute | solution.py:69
  95.1 5.0 %collective-permute-done.22.refs_8_ = bf16[8,64,128]{2,1,0:T(8,128)(2,1)S(1)} collective-permute-done((bf16[8,64,128]{2,1,0:T(8,128)(2,1)S(1)}, bf16[8,64,128]{2,1,0:T(8,128)(2,1)S(1)}, u32[]{:S(2)}, u32[]{:S(2)}) %collective-permute-start.22) | collective-permute-done | bytes 131104 | tf_op jit(solution)/shard_map/ppermute | solution.py:69
  102.0 2.5 %collective-permute-start.9 = (bf16[8,64,128]{2,1,0:T(8,128)(2,1)S(1)}, bf16[8,64,128]{2,1,0:T(8,128)(2,1)S(1)}, u32[]{:S(2)}, u32[]{:S(2)}) collective-permute-start(bf16[8,64,128]{2,1,0:T(8,128)(2,1)S(1)} %collective-permute-done.8.refs_8_), channel_id=1, source_target_pairs={{0,2},{2,4},{4,6},{6,7},{7,5},{5,3},{3,1},{1,0},{8,10},{10,12},{12... | collective-permute-start | bytes 393224 | tf_op jit(solution)/shard_map/ppermute | solution.py:69
  104.6 5.7 %collective-permute-done.23.refs_9_ = bf16[8,64,128]{2,1,0:T(8,128)(2,1)S(1)} collective-permute-done((bf16[8,64,128]{2,1,0:T(8,128)(2,1)S(1)}, bf16[8,64,128]{2,1,0:T(8,128)(2,1)S(1)}, u32[]{:S(2)}, u32[]{:S(2)}) %collective-permute-start.23) | collective-permute-done | bytes 131104 | tf_op jit(solution)/shard_map/ppermute | solution.py:69
  112.2 1.9 collective-permute-start.10
  115.3 4.4 %collective-permute-done.24.refs_10_ = bf16[8,64,128]{2,1,0:T(8,128)(2,1)S(1)} collective-permute-done((bf16[8,64,128]{2,1,0:T(8,128)(2,1)S(1)}, bf16[8,64,128]{2,1,0:T(8,128)(2,1)S(1)}, u32[]{:S(2)}, u32[]{:S(2)}) %collective-permute-start.24) | collective-permute-done | bytes 131104 | tf_op jit(solution)/shard_map/ppermute | solution.py:69
  121.1 1.9 collective-permute-start.25
  124.5 2.5 %collective-permute-start.11 = (bf16[8,64,128]{2,1,0:T(8,128)(2,1)S(1)}, bf16[8,64,128]{2,1,0:T(8,128)(2,1)S(1)}, u32[]{:S(2)}, u32[]{:S(2)}) collective-permute-start(bf16[8,64,128]{2,1,0:T(8,128)(2,1)S(1)} %shard_map.37.refs_3_.refs_11_), channel_id=1, source_target_pairs={{0,2},{2,4},{4,6},{6,7},{7,5},{5,3},{3,1},{1,0},{8,10},{10,12},{12... | collective-permute-start | bytes 393224 | tf_op jit(solution)/shard_map/ppermute | solution.py:69
  127.0 3.6 %collective-permute-done.25.refs_4_ = bf16[8,64,128]{2,1,0:T(8,128)(2,1)S(1)} collective-permute-done((bf16[8,64,128]{2,1,0:T(8,128)(2,1)S(1)}, bf16[8,64,128]{2,1,0:T(8,128)(2,1)S(1)}, u32[]{:S(2)}, u32[]{:S(2)}) %collective-permute-start.25) | collective-permute-done | bytes 131104 | tf_op jit(solution)/shard_map/ppermute | solution.py:69
  133.5 2.7 %collective-permute-start.12 = (bf16[8,64,128]{2,1,0:T(8,128)(2,1)S(1)}, bf16[8,64,128]{2,1,0:T(8,128)(2,1)S(1)}, u32[]{:S(2)}, u32[]{:S(2)}) collective-permute-start(bf16[8,64,128]{2,1,0:T(8,128)(2,1)S(1)} %collective-permute-done.11.refs_4_), channel_id=1, source_target_pairs={{0,2},{2,4},{4,6},{6,7},{7,5},{5,3},{3,1},{1,0},{8,10},{10,12},{12... | collective-permute-start | bytes 393224 | tf_op jit(solution)/shard_map/ppermute | solution.py:69
  136.2 4.4 %collective-permute-done.26.refs_5_ = bf16[8,64,128]{2,1,0:T(8,128)(2,1)S(1)} collective-permute-done((bf16[8,64,128]{2,1,0:T(8,128)(2,1)S(1)}, bf16[8,64,128]{2,1,0:T(8,128)(2,1)S(1)}, u32[]{:S(2)}, u32[]{:S(2)}) %collective-permute-start.26) | collective-permute-done | bytes 131104 | tf_op jit(solution)/shard_map/ppermute | solution.py:69
  142.6 2.7 %collective-permute-start.13 = (bf16[8,64,128]{2,1,0:T(8,128)(2,1)S(1)}, bf16[8,64,128]{2,1,0:T(8,128)(2,1)S(1)}, u32[]{:S(2)}, u32[]{:S(2)}) collective-permute-start(bf16[8,64,128]{2,1,0:T(8,128)(2,1)S(1)} %collective-permute-done.12.refs_5_), channel_id=1, source_target_pairs={{0,2},{2,4},{4,6},{6,7},{7,5},{5,3},{3,1},{1,0},{8,10},{10,12},{12... | collective-permute-start | bytes 393224 | tf_op jit(solution)/shard_map/ppermute | solution.py:69
  145.3 4.5 %collective-permute-done.27.refs_6_ = bf16[8,64,128]{2,1,0:T(8,128)(2,1)S(1)} collective-permute-done((bf16[8,64,128]{2,1,0:T(8,128)(2,1)S(1)}, bf16[8,64,128]{2,1,0:T(8,128)(2,1)S(1)}, u32[]{:S(2)}, u32[]{:S(2)}) %collective-permute-start.27) | collective-permute-done | bytes 131104 | tf_op jit(solution)/shard_map/ppermute | solution.py:69
  154.8 4.0 %collective-permute-done.28.refs_7_ = bf16[8,64,128]{2,1,0:T(8,128)(2,1)S(1)} collective-permute-done((bf16[8,64,128]{2,1,0:T(8,128)(2,1)S(1)}, bf16[8,64,128]{2,1,0:T(8,128)(2,1)S(1)}, u32[]{:S(2)}, u32[]{:S(2)}) %collective-permute-start.28) | collective-permute-done | bytes 131104 | tf_op jit(solution)/shard_map/ppermute | solution.py:69
  164.3 3.4 %collective-permute-done.29.refs_8_ = bf16[8,64,128]{2,1,0:T(8,128)(2,1)S(1)} collective-permute-done((bf16[8,64,128]{2,1,0:T(8,128)(2,1)S(1)}, bf16[8,64,128]{2,1,0:T(8,128)(2,1)S(1)}, u32[]{:S(2)}, u32[]{:S(2)}) %collective-permute-start.29) | collective-permute-done | bytes 131104 | tf_op jit(solution)/shard_map/ppermute | solution.py:69
  169.7 2.1 %collective-permute-done.15.refs_8_ = bf16[8,64,128]{2,1,0:T(8,128)(2,1)S(1)} collective-permute-done((bf16[8,64,128]{2,1,0:T(8,128)(2,1)S(1)}, bf16[8,64,128]{2,1,0:T(8,128)(2,1)S(1)}, u32[]{:S(2)}, u32[]{:S(2)}) %collective-permute-start.15) | collective-permute-done | bytes 131104 | tf_op jit(solution)/shard_map/ppermute | solution.py:69
  173.8 3.6 %collective-permute-done.30.refs_9_ = bf16[8,64,128]{2,1,0:T(8,128)(2,1)S(1)} collective-permute-done((bf16[8,64,128]{2,1,0:T(8,128)(2,1)S(1)}, bf16[8,64,128]{2,1,0:T(8,128)(2,1)S(1)}, u32[]{:S(2)}, u32[]{:S(2)}) %collective-permute-start.30) | collective-permute-done | bytes 131104 | tf_op jit(solution)/shard_map/ppermute | solution.py:69
  182.7 3.6 %collective-permute-done.31.refs_10_ = bf16[8,64,128]{2,1,0:T(8,128)(2,1)S(1)} collective-permute-done((bf16[8,64,128]{2,1,0:T(8,128)(2,1)S(1)}, bf16[8,64,128]{2,1,0:T(8,128)(2,1)S(1)}, u32[]{:S(2)}, u32[]{:S(2)}) %collective-permute-start.31) | collective-permute-done | bytes 131104 | tf_op jit(solution)/shard_map/ppermute | solution.py:69
  187.8 1.9 %collective-permute-done.17.refs_10_ = bf16[8,64,128]{2,1,0:T(8,128)(2,1)S(1)} collective-permute-done((bf16[8,64,128]{2,1,0:T(8,128)(2,1)S(1)}, bf16[8,64,128]{2,1,0:T(8,128)(2,1)S(1)}, u32[]{:S(2)}, u32[]{:S(2)}) %collective-permute-start.17) | collective-permute-done | bytes 131104 | tf_op jit(solution)/shard_map/ppermute | solution.py:69
  (79 shorter events, 56.9 us)
Async XLA Ops:
  0.0 76.7 %collective-permute-start = (bf16[16,64,128]{2,1,0:T(8,128)(2,1)}, bf16[16,64,128]{2,1,0:T(8,128)(2,1)S(1)}, u32[]{:S(2)}, u32[]{:S(2)}) collective-permute-start(bf16[16,64,128]{2,1,0:T(8,128)(2,1)} %param.3), channel_id=1, source_target_pairs={{0,16},{8,24},{16,32},{24,40},{32,48},{40,56},{48,64},{56,72},{64,... | collective-permute-start | bytes 786440 | tf_op jit(solution)/shard_map/ppermute | solution.py:79
  3.6 73.1 %collective-permute-start.1 = (bf16[16,64,128]{2,1,0:T(8,128)(2,1)}, bf16[16,64,128]{2,1,0:T(8,128)(2,1)S(1)}, u32[]{:S(2)}, u32[]{:S(2)}) collective-permute-start(bf16[16,64,128]{2,1,0:T(8,128)(2,1)} %param.3), channel_id=1, source_target_pairs={{0,496},{8,504},{16,0},{24,8},{32,16},{40,24},{48,32},{56,40},{64,... | collective-permute-start | bytes 786440 | tf_op jit(solution)/shard_map/ppermute | solution.py:80
  19.7 94.5 %collective-permute-start.3 = (bf16[16,64,128]{2,1,0:T(8,128)(2,1)}, bf16[16,64,128]{2,1,0:T(8,128)(2,1)}, u32[]{:S(2)}, u32[]{:S(2)}) collective-permute-start(bf16[16,64,128]{2,1,0:T(8,128)(2,1)} %param.3), channel_id=1, source_target_pairs={{0,488},{8,32},{16,504},{24,48},{32,8},{40,64},{48,24},{56,80},{64... | collective-permute-start | bytes 786440 | tf_op jit(solution)/shard_map/ppermute | solution.py:81
  23.7 37.2 %collective-permute-start.18 = (bf16[8,64,128]{2,1,0:T(8,128)(2,1)S(1)}, bf16[8,64,128]{2,1,0:T(8,128)(2,1)S(1)}, u32[]{:S(2)}, u32[]{:S(2)}) collective-permute-start(bf16[8,64,128]{2,1,0:T(8,128)(2,1)S(1)} %get-tuple-element.6.refs_3_), channel_id=1, source_target_pairs={{0,2},{2,4},{4,6},{6,7},{7,5},{5,3},{3,1},{1,0},{8,10},{10,12},{12... | collective-permute-start | bytes 393224 | tf_op jit(solution)/shard_map/ppermute | solution.py:69
  27.1 37.5 %collective-permute-start.4 = (bf16[8,64,128]{2,1,0:T(8,128)(2,1)S(1)}, bf16[8,64,128]{2,1,0:T(8,128)(2,1)S(1)}, u32[]{:S(2)}, u32[]{:S(2)}) collective-permute-start(bf16[8,64,128]{2,1,0:T(8,128)(2,1)S(1)} %get-tuple-element.5.refs_3_), channel_id=1, source_target_pairs={{0,2},{2,4},{4,6},{6,7},{7,5},{5,3},{3,1},{1,0},{8,10},{10,12},{12... | collective-permute-start | bytes 393224 | tf_op jit(solution)/shard_map/ppermute | solution.py:69
  60.9 9.0 %collective-permute-start.19 = (bf16[8,64,128]{2,1,0:T(8,128)(2,1)S(1)}, bf16[8,64,128]{2,1,0:T(8,128)(2,1)S(1)}, u32[]{:S(2)}, u32[]{:S(2)}) collective-permute-start(bf16[8,64,128]{2,1,0:T(8,128)(2,1)S(1)} %collective-permute-done.18.refs_4_), channel_id=1, source_target_pairs={{0,2},{2,4},{4,6},{6,7},{7,5},{5,3},{3,1},{1,0},{8,10},{10,12},{12... | collective-permute-start | bytes 393224 | tf_op jit(solution)/shard_map/ppermute | solution.py:69
  64.6 10.2 %collective-permute-start.5 = (bf16[8,64,128]{2,1,0:T(8,128)(2,1)S(1)}, bf16[8,64,128]{2,1,0:T(8,128)(2,1)S(1)}, u32[]{:S(2)}, u32[]{:S(2)}) collective-permute-start(bf16[8,64,128]{2,1,0:T(8,128)(2,1)S(1)} %collective-permute-done.4.refs_4_), channel_id=1, source_target_pairs={{0,2},{2,4},{4,6},{6,7},{7,5},{5,3},{3,1},{1,0},{8,10},{10,12},{12... | collective-permute-start | bytes 393224 | tf_op jit(solution)/shard_map/ppermute | solution.py:69
  69.9 9.8 %collective-permute-start.20 = (bf16[8,64,128]{2,1,0:T(8,128)(2,1)S(1)}, bf16[8,64,128]{2,1,0:T(8,128)(2,1)S(1)}, u32[]{:S(2)}, u32[]{:S(2)}) collective-permute-start(bf16[8,64,128]{2,1,0:T(8,128)(2,1)S(1)} %collective-permute-done.19.refs_5_), channel_id=1, source_target_pairs={{0,2},{2,4},{4,6},{6,7},{7,5},{5,3},{3,1},{1,0},{8,10},{10,12},{12... | collective-permute-start | bytes 393224 | tf_op jit(solution)/shard_map/ppermute | solution.py:69
  74.8 9.0 %collective-permute-start.6 = (bf16[8,64,128]{2,1,0:T(8,128)(2,1)S(1)}, bf16[8,64,128]{2,1,0:T(8,128)(2,1)S(1)}, u32[]{:S(2)}, u32[]{:S(2)}) collective-permute-start(bf16[8,64,128]{2,1,0:T(8,128)(2,1)S(1)} %collective-permute-done.5.refs_5_), channel_id=1, source_target_pairs={{0,2},{2,4},{4,6},{6,7},{7,5},{5,3},{3,1},{1,0},{8,10},{10,12},{12... | collective-permute-start | bytes 393224 | tf_op jit(solution)/shard_map/ppermute | solution.py:69
  77.7 36.4 %collective-permute-start.2 = (bf16[48,64,128]{2,1,0:T(8,128)(2,1)}, bf16[48,64,128]{2,1,0:T(8,128)(2,1)S(1)}, u32[]{:S(2)}, u32[]{:S(2)}) collective-permute-start(bf16[48,64,128]{2,1,0:T(8,128)(2,1)} %pad_maximum_fusion), channel_id=1, source_target_pairs={{0,8},{8,0},{16,24},{24,16},{32,40},{40,32},{48,56},{56,48},{64,72... | collective-permute-start | bytes 2359304 | tf_op jit(solution)/shard_map/ppermute | solution.py:83
  79.7 10.4 %collective-permute-start.21 = (bf16[8,64,128]{2,1,0:T(8,128)(2,1)S(1)}, bf16[8,64,128]{2,1,0:T(8,128)(2,1)S(1)}, u32[]{:S(2)}, u32[]{:S(2)}) collective-permute-start(bf16[8,64,128]{2,1,0:T(8,128)(2,1)S(1)} %collective-permute-done.20.refs_6_), channel_id=1, source_target_pairs={{0,2},{2,4},{4,6},{6,7},{7,5},{5,3},{3,1},{1,0},{8,10},{10,12},{12... | collective-permute-start | bytes 393224 | tf_op jit(solution)/shard_map/ppermute | solution.py:69
  83.8 9.0 %collective-permute-start.7 = (bf16[8,64,128]{2,1,0:T(8,128)(2,1)S(1)}, bf16[8,64,128]{2,1,0:T(8,128)(2,1)S(1)}, u32[]{:S(2)}, u32[]{:S(2)}) collective-permute-start(bf16[8,64,128]{2,1,0:T(8,128)(2,1)S(1)} %collective-permute-done.6.refs_6_), channel_id=1, source_target_pairs={{0,2},{2,4},{4,6},{6,7},{7,5},{5,3},{3,1},{1,0},{8,10},{10,12},{12... | collective-permute-start | bytes 393224 | tf_op jit(solution)/shard_map/ppermute | solution.py:69
  90.0 10.0 %collective-permute-start.22 = (bf16[8,64,128]{2,1,0:T(8,128)(2,1)S(1)}, bf16[8,64,128]{2,1,0:T(8,128)(2,1)S(1)}, u32[]{:S(2)}, u32[]{:S(2)}) collective-permute-start(bf16[8,64,128]{2,1,0:T(8,128)(2,1)S(1)} %collective-permute-done.21.refs_7_), channel_id=1, source_target_pairs={{0,2},{2,4},{4,6},{6,7},{7,5},{5,3},{3,1},{1,0},{8,10},{10,12},{12... | collective-permute-start | bytes 393224 | tf_op jit(solution)/shard_map/ppermute | solution.py:69
  92.7 9.3 %collective-permute-start.8 = (bf16[8,64,128]{2,1,0:T(8,128)(2,1)S(1)}, bf16[8,64,128]{2,1,0:T(8,128)(2,1)S(1)}, u32[]{:S(2)}, u32[]{:S(2)}) collective-permute-start(bf16[8,64,128]{2,1,0:T(8,128)(2,1)S(1)} %collective-permute-done.7.refs_7_), channel_id=1, source_target_pairs={{0,2},{2,4},{4,6},{6,7},{7,5},{5,3},{3,1},{1,0},{8,10},{10,12},{12... | collective-permute-start | bytes 393224 | tf_op jit(solution)/shard_map/ppermute | solution.py:69
  100.1 10.2 %collective-permute-start.23 = (bf16[8,64,128]{2,1,0:T(8,128)(2,1)S(1)}, bf16[8,64,128]{2,1,0:T(8,128)(2,1)S(1)}, u32[]{:S(2)}, u32[]{:S(2)}) collective-permute-start(bf16[8,64,128]{2,1,0:T(8,128)(2,1)S(1)} %collective-permute-done.22.refs_8_), channel_id=1, source_target_pairs={{0,2},{2,4},{4,6},{6,7},{7,5},{5,3},{3,1},{1,0},{8,10},{10,12},{12... | collective-permute-start | bytes 393224 | tf_op jit(solution)/shard_map/ppermute | solution.py:69
  102.0 10.2 %collective-permute-start.9 = (bf16[8,64,128]{2,1,0:T(8,128)(2,1)S(1)}, bf16[8,64,128]{2,1,0:T(8,128)(2,1)S(1)}, u32[]{:S(2)}, u32[]{:S(2)}) collective-permute-start(bf16[8,64,128]{2,1,0:T(8,128)(2,1)S(1)} %collective-permute-done.8.refs_8_), channel_id=1, source_target_pairs={{0,2},{2,4},{4,6},{6,7},{7,5},{5,3},{3,1},{1,0},{8,10},{10,12},{12... | collective-permute-start | bytes 393224 | tf_op jit(solution)/shard_map/ppermute | solution.py:69
  110.3 9.3 %collective-permute-start.24 = (bf16[8,64,128]{2,1,0:T(8,128)(2,1)S(1)}, bf16[8,64,128]{2,1,0:T(8,128)(2,1)S(1)}, u32[]{:S(2)}, u32[]{:S(2)}) collective-permute-start(bf16[8,64,128]{2,1,0:T(8,128)(2,1)S(1)} %collective-permute-done.23.refs_9_), channel_id=1, source_target_pairs={{0,2},{2,4},{4,6},{6,7},{7,5},{5,3},{3,1},{1,0},{8,10},{10,12},{12... | collective-permute-start | bytes 393224 | tf_op jit(solution)/shard_map/ppermute | solution.py:69
  112.2 10.8 %collective-permute-start.10 = (bf16[8,64,128]{2,1,0:T(8,128)(2,1)S(1)}, bf16[8,64,128]{2,1,0:T(8,128)(2,1)S(1)}, u32[]{:S(2)}, u32[]{:S(2)}) collective-permute-start(bf16[8,64,128]{2,1,0:T(8,128)(2,1)S(1)} %collective-permute-done.9.refs_9_), channel_id=1, source_target_pairs={{0,2},{2,4},{4,6},{6,7},{7,5},{5,3},{3,1},{1,0},{8,10},{10,12},{12... | collective-permute-start | bytes 393224 | tf_op jit(solution)/shard_map/ppermute | solution.py:69
  121.1 9.6 %collective-permute-start.25 = (bf16[8,64,128]{2,1,0:T(8,128)(2,1)S(1)}, bf16[8,64,128]{2,1,0:T(8,128)(2,1)S(1)}, u32[]{:S(2)}, u32[]{:S(2)}) collective-permute-start(bf16[8,64,128]{2,1,0:T(8,128)(2,1)S(1)} %shard_map.39.refs_3_.refs_11_), channel_id=1, source_target_pairs={{0,2},{2,4},{4,6},{6,7},{7,5},{5,3},{3,1},{1,0},{8,10},{10,12},{12... | collective-permute-start | bytes 393224 | tf_op jit(solution)/shard_map/ppermute | solution.py:69
  124.5 9.0 %collective-permute-start.11 = (bf16[8,64,128]{2,1,0:T(8,128)(2,1)S(1)}, bf16[8,64,128]{2,1,0:T(8,128)(2,1)S(1)}, u32[]{:S(2)}, u32[]{:S(2)}) collective-permute-start(bf16[8,64,128]{2,1,0:T(8,128)(2,1)S(1)} %shard_map.37.refs_3_.refs_11_), channel_id=1, source_target_pairs={{0,2},{2,4},{4,6},{6,7},{7,5},{5,3},{3,1},{1,0},{8,10},{10,12},{12... | collective-permute-start | bytes 393224 | tf_op jit(solution)/shard_map/ppermute | solution.py:69
  130.7 10.0 %collective-permute-start.26 = (bf16[8,64,128]{2,1,0:T(8,128)(2,1)S(1)}, bf16[8,64,128]{2,1,0:T(8,128)(2,1)S(1)}, u32[]{:S(2)}, u32[]{:S(2)}) collective-permute-start(bf16[8,64,128]{2,1,0:T(8,128)(2,1)S(1)} %collective-permute-done.25.refs_4_), channel_id=1, source_target_pairs={{0,2},{2,4},{4,6},{6,7},{7,5},{5,3},{3,1},{1,0},{8,10},{10,12},{12... | collective-permute-start | bytes 393224 | tf_op jit(solution)/shard_map/ppermute | solution.py:69
  133.5 9.1 %collective-permute-start.12 = (bf16[8,64,128]{2,1,0:T(8,128)(2,1)S(1)}, bf16[8,64,128]{2,1,0:T(8,128)(2,1)S(1)}, u32[]{:S(2)}, u32[]{:S(2)}) collective-permute-start(bf16[8,64,128]{2,1,0:T(8,128)(2,1)S(1)} %collective-permute-done.11.refs_4_), channel_id=1, source_target_pairs={{0,2},{2,4},{4,6},{6,7},{7,5},{5,3},{3,1},{1,0},{8,10},{10,12},{12... | collective-permute-start | bytes 393224 | tf_op jit(solution)/shard_map/ppermute | solution.py:69
  140.7 9.2 %collective-permute-start.27 = (bf16[8,64,128]{2,1,0:T(8,128)(2,1)S(1)}, bf16[8,64,128]{2,1,0:T(8,128)(2,1)S(1)}, u32[]{:S(2)}, u32[]{:S(2)}) collective-permute-start(bf16[8,64,128]{2,1,0:T(8,128)(2,1)S(1)} %collective-permute-done.26.refs_5_), channel_id=1, source_target_pairs={{0,2},{2,4},{4,6},{6,7},{7,5},{5,3},{3,1},{1,0},{8,10},{10,12},{12... | collective-permute-start | bytes 393224 | tf_op jit(solution)/shard_map/ppermute | solution.py:69
  142.6 10.3 %collective-permute-start.13 = (bf16[8,64,128]{2,1,0:T(8,128)(2,1)S(1)}, bf16[8,64,128]{2,1,0:T(8,128)(2,1)S(1)}, u32[]{:S(2)}, u32[]{:S(2)}) collective-permute-start(bf16[8,64,128]{2,1,0:T(8,128)(2,1)S(1)} %collective-permute-done.12.refs_5_), channel_id=1, source_target_pairs={{0,2},{2,4},{4,6},{6,7},{7,5},{5,3},{3,1},{1,0},{8,10},{10,12},{12... | collective-permute-start | bytes 393224 | tf_op jit(solution)/shard_map/ppermute | solution.py:69
  149.9 9.0 %collective-permute-start.28 = (bf16[8,64,128]{2,1,0:T(8,128)(2,1)S(1)}, bf16[8,64,128]{2,1,0:T(8,128)(2,1)S(1)}, u32[]{:S(2)}, u32[]{:S(2)}) collective-permute-start(bf16[8,64,128]{2,1,0:T(8,128)(2,1)S(1)} %collective-permute-done.27.refs_6_), channel_id=1, source_target_pairs={{0,2},{2,4},{4,6},{6,7},{7,5},{5,3},{3,1},{1,0},{8,10},{10,12},{12... | collective-permute-start | bytes 393224 | tf_op jit(solution)/shard_map/ppermute | solution.py:69
  152.9 9.5 %collective-permute-start.14 = (bf16[8,64,128]{2,1,0:T(8,128)(2,1)S(1)}, bf16[8,64,128]{2,1,0:T(8,128)(2,1)S(1)}, u32[]{:S(2)}, u32[]{:S(2)}) collective-permute-start(bf16[8,64,128]{2,1,0:T(8,128)(2,1)S(1)} %collective-permute-done.13.refs_6_), channel_id=1, source_target_pairs={{0,2},{2,4},{4,6},{6,7},{7,5},{5,3},{3,1},{1,0},{8,10},{10,12},{12... | collective-permute-start | bytes 393224 | tf_op jit(solution)/shard_map/ppermute | solution.py:69
  158.8 9.0 %collective-permute-start.29 = (bf16[8,64,128]{2,1,0:T(8,128)(2,1)S(1)}, bf16[8,64,128]{2,1,0:T(8,128)(2,1)S(1)}, u32[]{:S(2)}, u32[]{:S(2)}) collective-permute-start(bf16[8,64,128]{2,1,0:T(8,128)(2,1)S(1)} %collective-permute-done.28.refs_7_), channel_id=1, source_target_pairs={{0,2},{2,4},{4,6},{6,7},{7,5},{5,3},{3,1},{1,0},{8,10},{10,12},{12... | collective-permute-start | bytes 393224 | tf_op jit(solution)/shard_map/ppermute | solution.py:69
  162.4 9.4 %collective-permute-start.15 = (bf16[8,64,128]{2,1,0:T(8,128)(2,1)S(1)}, bf16[8,64,128]{2,1,0:T(8,128)(2,1)S(1)}, u32[]{:S(2)}, u32[]{:S(2)}) collective-permute-start(bf16[8,64,128]{2,1,0:T(8,128)(2,1)S(1)} %collective-permute-done.14.refs_7_), channel_id=1, source_target_pairs={{0,2},{2,4},{4,6},{6,7},{7,5},{5,3},{3,1},{1,0},{8,10},{10,12},{12... | collective-permute-start | bytes 393224 | tf_op jit(solution)/shard_map/ppermute | solution.py:69
  167.8 9.6 %collective-permute-start.30 = (bf16[8,64,128]{2,1,0:T(8,128)(2,1)S(1)}, bf16[8,64,128]{2,1,0:T(8,128)(2,1)S(1)}, u32[]{:S(2)}, u32[]{:S(2)}) collective-permute-start(bf16[8,64,128]{2,1,0:T(8,128)(2,1)S(1)} %collective-permute-done.29.refs_8_), channel_id=1, source_target_pairs={{0,2},{2,4},{4,6},{6,7},{7,5},{5,3},{3,1},{1,0},{8,10},{10,12},{12... | collective-permute-start | bytes 393224 | tf_op jit(solution)/shard_map/ppermute | solution.py:69
  171.8 9.0 %collective-permute-start.16 = (bf16[8,64,128]{2,1,0:T(8,128)(2,1)S(1)}, bf16[8,64,128]{2,1,0:T(8,128)(2,1)S(1)}, u32[]{:S(2)}, u32[]{:S(2)}) collective-permute-start(bf16[8,64,128]{2,1,0:T(8,128)(2,1)S(1)} %collective-permute-done.15.refs_8_), channel_id=1, source_target_pairs={{0,2},{2,4},{4,6},{6,7},{7,5},{5,3},{3,1},{1,0},{8,10},{10,12},{12... | collective-permute-start | bytes 393224 | tf_op jit(solution)/shard_map/ppermute | solution.py:69
  177.4 9.0 %collective-permute-start.31 = (bf16[8,64,128]{2,1,0:T(8,128)(2,1)S(1)}, bf16[8,64,128]{2,1,0:T(8,128)(2,1)S(1)}, u32[]{:S(2)}, u32[]{:S(2)}) collective-permute-start(bf16[8,64,128]{2,1,0:T(8,128)(2,1)S(1)} %collective-permute-done.30.refs_9_), channel_id=1, source_target_pairs={{0,2},{2,4},{4,6},{6,7},{7,5},{5,3},{3,1},{1,0},{8,10},{10,12},{12... | collective-permute-start | bytes 393224 | tf_op jit(solution)/shard_map/ppermute | solution.py:69
  180.8 9.0 %collective-permute-start.17 = (bf16[8,64,128]{2,1,0:T(8,128)(2,1)S(1)}, bf16[8,64,128]{2,1,0:T(8,128)(2,1)S(1)}, u32[]{:S(2)}, u32[]{:S(2)}) collective-permute-start(bf16[8,64,128]{2,1,0:T(8,128)(2,1)S(1)} %collective-permute-done.16.refs_9_), channel_id=1, source_target_pairs={{0,2},{2,4},{4,6},{6,7},{7,5},{5,3},{3,1},{1,0},{8,10},{10,12},{12... | collective-permute-start | bytes 393224 | tf_op jit(solution)/shard_map/ppermute | solution.py:69
  (1 other events, 76.8 us)

commit v2 on v1

v2 whole, which is shorter than its diff:
```python
import jax
import jax.numpy as jnp
import numpy as np
from jax import lax
from jax.experimental import pallas as pl
from jax.experimental.pallas import tpu as pltpu
from jax.sharding import PartitionSpec as P

AXES = ("row", "col")
PANELS = 64
GROUPS = 8
SPAN = 3
TURN = ((0, 3, 1, 2), (1, 2, 0, 3), (2, 0, 3, 1), (3, 1, 2, 0))


def device(half, x, y, core, z):
    return (((half * 4 + x) * 4 + y) * 2 + core) * GROUPS + z


def start(panel, group):
    return panel * GROUPS + group


def between(panel, group):
    half, x, y, core = panel // 32, panel // 8 % 4, panel // 2 % 4, panel % 2
    return device(half, TURN[x][group // 2], panel % 4, y // 2, group)


def place(panel, group):
    half, x = panel // 32, panel // 8 % 4
    return device(half, TURN[x][group // 2], panel % 4, group % 2, panel // 4 % 8)


JOBS = [(panel, group) for panel in range(PANELS) for group in range(GROUPS)]


def route(source, target):
    return sorted((source(*job), target(*job)) for job in JOBS)


def sideways(distance):
    moves = []
    for panel, group in JOBS:
        x = (TURN[panel // 8 % 4][group // 2] - distance) % 4
        other = TURN[panel // 8 % 4].index(x) * 2 + group % 2
        moves.append((place(panel, other), place(panel, group)))
    return sorted(moves)


def arrival(panel, group):
    order = []
    for core in (group % 2, 1 - group % 2):
        for distance in (0, 1, -1, 2):
            x = (TURN[panel // 8 % 4][group // 2] - distance) % 4
            order.append(TURN[panel // 8 % 4].index(x) * 2 + core)
    return order


def send(value, moves):
    return lax.ppermute(value, AXES, moves)


def gather_row(part):
    other = route(place, lambda panel, group: place(panel, group ^ 1))
    near = [part] + [send(part, sideways(distance)) for distance in (1, -1, 2)]
    return near + [send(piece, other) for piece in near]


def gather_table(part):
    panels = []
    for offset in range(-SPAN, SPAN + 1):
        if offset == 0:
            panels.append(part)
        else:
            moves = route(lambda p, g: place((p + offset) % PANELS, g), place)
            panels.append(send(part, moves))
    return jnp.concatenate(panels, axis=0)


def product_kernel(count, group, keep, index_ref, mask_ref, table_ref, *refs):
    chunks = refs[:count]
    out_ref = refs[-1]
    rows, width, lanes = chunks[0].shape
    blocks = count * group
    for i in range(rows):
        total = None
        for step in range(0, count, 2):
            left = jnp.concatenate([chunks[step][i], chunks[step + 1][i]], axis=1)
            pieces = []
            for b in range(step * group, (step + 2) * group):
                piece = table_ref[index_ref[i * blocks + b]]
                piece = jnp.concatenate([piece, piece], axis=1)
                mask = mask_ref[pl.ds(i * blocks + b, 1), :].astype(piece.dtype)
                pieces.append(piece * mask)
            right = jnp.concatenate(pieces, axis=0)
            part = jnp.dot(left, right, preferred_element_type=jnp.float32)
            total = part if total is None else total + part
        value = total[:, :lanes] + pltpu.roll(total[:, lanes:], width, 1)
        if keep:
            value = 3.0 * chunks[0][i].astype(jnp.float32) - 2.0 * value
        out_ref[i] = value.astype(out_ref.dtype)


def product(index, mask, table, chunks, keep):
    count = len(chunks)
    rows, width, lanes = chunks[0].shape
    vmem = pl.BlockSpec(memory_space=pltpu.VMEM)
    return pl.pallas_call(
        lambda *refs: product_kernel(count, lanes // width, keep, *refs),
        out_shape=jax.ShapeDtypeStruct(chunks[0].shape, jnp.bfloat16),
        in_specs=[pl.BlockSpec(memory_space=pltpu.SMEM)] + [vmem] * (2 + count),
        out_specs=vmem,
        compiler_params=pltpu.CompilerParams(vmem_limit_bytes=24 * 1024 * 1024),
        cost_estimate=pl.CostEstimate(
            flops=4 * rows * width * lanes * lanes * count,
            bytes_accessed=8 * 1024 * 1024,
            transcendentals=0,
        ),
    )(index, mask, table, *chunks)


def shards(density, columns):
    local_rows, width, lanes = density.shape
    group = lanes // width
    total, stored = columns.shape

    jobs = np.zeros((PANELS * GROUPS, 2 + GROUPS), np.int32)
    for job in JOBS:
        jobs[place(*job)] = [*job, *arrival(*job)]
    here = lax.axis_index("row") * GROUPS + lax.axis_index("col")
    job = lax.dynamic_index_in_dim(jnp.array(jobs), here, 0, keepdims=False)
    panel, mine, order = job[0], job[1], job[2:]

    part = send(density, route(start, between))
    part = send(part, route(between, place))

    base = panel * local_rows
    own = lax.dynamic_slice_in_dim(columns, base, local_rows, 0)
    goal = lax.dynamic_slice_in_dim(own, mine * group, group, 1)
    own = jnp.take(own.reshape(local_rows, GROUPS, group), order, axis=1)
    own = own.reshape(local_rows, stored)
    distance = jnp.mod(own - base + total // 2, total) - total // 2
    index = (distance + SPAN * local_rows).reshape(-1)
    held = lax.dynamic_slice_in_dim(columns, mine * group, group, 1)
    held = jnp.take(held, own.reshape(-1), axis=0).reshape(local_rows, stored, group)
    lane_slot = jnp.arange(lanes, dtype=jnp.int32) // width
    found = jnp.where(lane_slot == 0, held[..., :1], held[..., 1:])
    direct = jnp.where(lane_slot == 0, goal[:, None, :1], goal[:, None, 1:])
    swapped = jnp.where(lane_slot == 0, goal[:, None, 1:], goal[:, None, :1])
    mask = jnp.concatenate([found == direct, found == swapped], axis=-1)
    mask = mask.astype(jnp.float32).reshape(local_rows * stored, 2 * lanes)

    left = gather_row(part)
    table = gather_table(part).reshape(-1, width, lanes)
    square = product(index, mask, table, left, False)
    result = product(index, mask, table, gather_row(square), True)
    return send(result, route(place, start)).astype(jnp.float32)


def solution(mesh):
    placed = (P("row", None, "col"), P())
    return jax.shard_map(
        shards, mesh=mesh, in_specs=placed, out_specs=P("row", None, "col"), check_vma=False
    )
```

time: 193 us -> 143 us (0.74)
  the two profiles are of different devices: /device:TPU:96 before, /device:TPU:22 now
where the time goes in v2:
time: 143 us; the launch traced here: 142 us
  starting transfers between devices  96.8 us (68%)
  waiting for transfers between devices  30.9 us (22%)
  local copies, waits for them, and re-layouts  6.6 us (5%)
  Pallas kernels  4.37 us (3%)
  between operations  1.81 us (1%)
  other arithmetic  1.44 us (1%)
    ppermute x23, starting transfers between devices, send(): return lax.ppermute(value, AXES, moves)  96.8 us
    ppermute x23, waiting for transfers between devices, send(): return lax.ppermute(value, AXES, moves)  30.9 us
    pallas_call x2, Pallas kernels, product(): pl.pallas_call(lambda *refs: product_kernel(count, lanes // width, keep,...  4.37 us
  transfers between devices with their start and end apart: 23, of which 6 were waited for; matrix products, arithmetic and copies ran while one was open for 5% of the time, Pallas kernels for 0%

profile of v2, /device:TPU:22, one launch (start us, length us, event | category | flops | bytes accessed | tf_op | source)
XLA Modules:
  0.0 141.9 jit_solution(16381240967803634005)
XLA Ops:
  0.0 1.9 %collective-permute-start = (bf16[16,64,128]{2,1,0:T(8,128)(2,1)}, bf16[16,64,128]{2,1,0:T(8,128)(2,1)S(1)}, u32[]{:S(2)}, u32[]{:S(2)}) collective-permute-start(bf16[16,64,128]{2,1,0:T(8,128)(2,1)} %param.3), channel_id=1, source_target_pairs={{0,0},{1,1},{2,194},{3,195},{4,68},{5,69},{6,134},{7,135},{8,16},{... | collective-permute-start | bytes 786440 | tf_op jit(solution)/shard_map/ppermute | solution.py:60
  7.4 0.8 dynamic_slice.16
  9.5 15.8 %collective-permute-start.1 = (bf16[16,64,128]{2,1,0:T(8,128)(2,1)S(1)}, bf16[16,64,128]{2,1,0:T(8,128)(2,1)S(1)}, u32[]{:S(2)}, u32[]{:S(2)}) collective-permute-start(bf16[16,64,128]{2,1,0:T(8,128)(2,1)S(1)} %collective-permute-done), channel_id=1, source_target_pairs={{0,0},{1,8},{2,4},{3,12},{4,2},{5,10},{6,6},{7,14},{8,1},{9,9},{10... | collective-permute-start | bytes 786440 | tf_op jit(solution)/shard_map/ppermute | solution.py:60
  25.8 5.5 %collective-permute-done.1.refs_3_ = bf16[16,64,128]{2,1,0:T(8,128)(2,1)S(1)} collective-permute-done((bf16[16,64,128]{2,1,0:T(8,128)(2,1)S(1)}, bf16[16,64,128]{2,1,0:T(8,128)(2,1)S(1)}, u32[]{:S(2)}, u32[]{:S(2)}) %collective-permute-start.1) | collective-permute-done | bytes 262176 | tf_op jit(solution)/shard_map/ppermute | solution.py:60
  31.3 6.3 %collective-permute-start.2 = (bf16[16,64,128]{2,1,0:T(8,128)(2,1)S(1)}, bf16[16,64,128]{2,1,0:T(8,128)(2,1)S(1)}, u32[]{:S(2)}, u32[]{:S(2)}) collective-permute-start(bf16[16,64,128]{2,1,0:T(8,128)(2,1)S(1)} %collective-permute-done.1.refs_3_), channel_id=1, source_target_pairs={{0,48},{1,49},{2,50},{3,51},{4,52},{5,53},{6,54},{7,55},{8,56},{9,... | collective-permute-start | bytes 786440 | tf_op jit(solution)/shard_map/ppermute | solution.py:60
  37.6 3.9 %collective-permute-start.3 = (bf16[16,64,128]{2,1,0:T(8,128)(2,1)S(1)}, bf16[16,64,128]{2,1,0:T(8,128)(2,1)S(1)}, u32[]{:S(2)}, u32[]{:S(2)}) collective-permute-start(bf16[16,64,128]{2,1,0:T(8,128)(2,1)S(1)} %collective-permute-done.1.refs_3_), channel_id=1, source_target_pairs={{0,32},{1,33},{2,34},{3,35},{4,36},{5,37},{6,38},{7,39},{8,40},{9,... | collective-permute-start | bytes 786440 | tf_op jit(solution)/shard_map/ppermute | solution.py:60
  41.5 2.0 %collective-permute-start.4 = (bf16[16,64,128]{2,1,0:T(8,128)(2,1)S(1)}, bf16[16,64,128]{2,1,0:T(8,128)(2,1)S(1)}, u32[]{:S(2)}, u32[]{:S(2)}) collective-permute-start(bf16[16,64,128]{2,1,0:T(8,128)(2,1)S(1)} %collective-permute-done.1.refs_3_), channel_id=1, source_target_pairs={{0,16},{1,17},{2,18},{3,19},{4,20},{5,21},{6,22},{7,23},{8,24},{9,... | collective-permute-start | bytes 786440 | tf_op jit(solution)/shard_map/ppermute | solution.py:60
  43.9 3.9 %collective-permute-start.5 = (bf16[16,64,128]{2,1,0:T(8,128)(2,1)S(1)}, bf16[16,64,128]{2,1,0:T(8,128)(2,1)S(1)}, u32[]{:S(2)}, u32[]{:S(2)}) collective-permute-start(bf16[16,64,128]{2,1,0:T(8,128)(2,1)S(1)} %collective-permute-done.1.refs_3_), channel_id=1, source_target_pairs={{0,503},{1,48},{2,113},{3,50},{4,179},{5,52},{6,117},{7,54},{8,511... | collective-permute-start | bytes 786440 | tf_op jit(solution)/shard_map/ppermute | solution.py:60
  47.7 9.1 %collective-permute-start.6 = (bf16[16,64,128]{2,1,0:T(8,128)(2,1)S(1)}, bf16[16,64,128]{2,1,0:T(8,128)(2,1)S(1)}, u32[]{:S(2)}, u32[]{:S(2)}) collective-permute-start(bf16[16,64,128]{2,1,0:T(8,128)(2,1)S(1)} %collective-permute-done.1.refs_3_), channel_id=1, source_target_pairs={{0,487},{1,32},{2,97},{3,34},{4,163},{5,36},{6,101},{7,38},{8,495}... | collective-permute-start | bytes 786440 | tf_op jit(solution)/shard_map/ppermute | solution.py:60
  56.9 1.9 %collective-permute-start.8 = (bf16[16,64,128]{2,1,0:T(8,128)(2,1)S(1)}, bf16[16,64,128]{2,1,0:T(8,128)(2,1)S(1)}, u32[]{:S(2)}, u32[]{:S(2)}) collective-permute-start(bf16[16,64,128]{2,1,0:T(8,128)(2,1)S(1)} %collective-permute-done.1.refs_3_), channel_id=1, source_target_pairs={{0,64},{1,65},{2,66},{3,67},{4,68},{5,69},{6,70},{7,71},{8,72},{9,... | collective-permute-start | bytes 786440 | tf_op jit(solution)/shard_map/ppermute | solution.py:60
  58.9 3.9 %collective-permute-start.9 = (bf16[16,64,128]{2,1,0:T(8,128)(2,1)S(1)}, bf16[16,64,128]{2,1,0:T(8,128)(2,1)S(1)}, u32[]{:S(2)}, u32[]{:S(2)}) collective-permute-start(bf16[16,64,128]{2,1,0:T(8,128)(2,1)S(1)} %collective-permute-done.1.refs_3_), channel_id=1, source_target_pairs={{0,192},{1,193},{2,194},{3,195},{4,196},{5,197},{6,198},{7,199},{8... | collective-permute-start | bytes 786440 | tf_op jit(solution)/shard_map/ppermute | solution.py:60
  62.8 3.5 %collective-permute-start.10 = (bf16[16,64,128]{2,1,0:T(8,128)(2,1)S(1)}, bf16[16,64,128]{2,1,0:T(8,128)(2,1)S(1)}, u32[]{:S(2)}, u32[]{:S(2)}) collective-permute-start(bf16[16,64,128]{2,1,0:T(8,128)(2,1)S(1)} %collective-permute-done.1.refs_3_), channel_id=1, source_target_pairs={{0,128},{1,129},{2,130},{3,131},{4,132},{5,133},{6,134},{7,135},{8... | collective-permute-start | bytes 786440 | tf_op jit(solution)/shard_map/ppermute | solution.py:60
  66.4 17.1 %collective-permute-start.7 = (bf16[16,64,128]{2,1,0:T(8,128)(2,1)S(1)}, bf16[16,64,128]{2,1,0:T(8,128)(2,1)S(1)}, u32[]{:S(2)}, u32[]{:S(2)}) collective-permute-start(bf16[16,64,128]{2,1,0:T(8,128)(2,1)S(1)} %collective-permute-done.1.refs_3_), channel_id=1, source_target_pairs={{0,471},{1,16},{2,81},{3,18},{4,147},{5,20},{6,85},{7,22},{8,479},... | collective-permute-start | bytes 786440 | tf_op jit(solution)/shard_map/ppermute | solution.py:60
  83.5 1.9 %collective-permute-start.11 = (bf16[16,64,128]{2,1,0:T(8,128)(2,1)S(1)}, bf16[16,64,128]{2,1,0:T(8,128)(2,1)S(1)}, u32[]{:S(2)}, u32[]{:S(2)}) collective-permute-start(bf16[16,64,128]{2,1,0:T(8,128)(2,1)S(1)} %collective-permute-done.1.refs_3_), channel_id=1, source_target_pairs={{0,8},{1,9},{2,10},{3,11},{4,12},{5,13},{6,14},{7,15},{8,0},{9,1},... | collective-permute-start | bytes 786440 | tf_op jit(solution)/shard_map/ppermute | solution.py:60
  85.5 2.4 %collective-permute-start.12 = (bf16[16,64,128]{2,1,0:T(8,128)(2,1)S(1)}, bf16[16,64,128]{2,1,0:T(8,128)(2,1)S(1)}, u32[]{:S(2)}, u32[]{:S(2)}) collective-permute-start(bf16[16,64,128]{2,1,0:T(8,128)(2,1)S(1)} %collective-permute-done.8.refs_4_), channel_id=1, source_target_pairs={{0,8},{1,9},{2,10},{3,11},{4,12},{5,13},{6,14},{7,15},{8,0},{9,1},... | collective-permute-start | bytes 786440 | tf_op jit(solution)/shard_map/ppermute | solution.py:60
  87.9 1.9 %collective-permute-start.13 = (bf16[16,64,128]{2,1,0:T(8,128)(2,1)S(1)}, bf16[16,64,128]{2,1,0:T(8,128)(2,1)S(1)}, u32[]{:S(2)}, u32[]{:S(2)}) collective-permute-start(bf16[16,64,128]{2,1,0:T(8,128)(2,1)S(1)} %collective-permute-done.9.refs_5_), channel_id=1, source_target_pairs={{0,8},{1,9},{2,10},{3,11},{4,12},{5,13},{6,14},{7,15},{8,0},{9,1},... | collective-permute-start | bytes 786440 | tf_op jit(solution)/shard_map/ppermute | solution.py:60
  89.8 2.4 %collective-permute-start.14 = (bf16[16,64,128]{2,1,0:T(8,128)(2,1)S(1)}, bf16[16,64,128]{2,1,0:T(8,128)(2,1)S(1)}, u32[]{:S(2)}, u32[]{:S(2)}) collective-permute-start(bf16[16,64,128]{2,1,0:T(8,128)(2,1)S(1)} %collective-permute-done.10.refs_6_), channel_id=1, source_target_pairs={{0,8},{1,9},{2,10},{3,11},{4,12},{5,13},{6,14},{7,15},{8,0},{9,1},... | collective-permute-start | bytes 786440 | tf_op jit(solution)/shard_map/ppermute | solution.py:60
  92.4 1.0 collective-permute-done.14.refs_10_
  93.4 2.2 %shard_map.37.refs_3_ = bf16[16,64,128]{2,1,0:T(8,128)(2,1)S(1)} custom-call(s32[256]{0:T(256)S(1)} %fusion.refs_0_, f32[256,256]{1,0:T(8,128)S(1)} %add_convert_fusion.refs_1_, bf16[112,64,128]{2,1,0:T(8,128)(2,1)S(1)} %constant_dynamic-update-slice_fusion.refs_2_, bf16[16,64,128]{2,1,0:T(8,128)(2,1)S(1)} %collective-permute-done.1.refs_3_, ...), custom_call_target="tpu_custom_call" | custom-call | flops 536870912 | bytes 8388608 | tf_op jit(solution)/shard_map/pallas_call | solution.py:108
  95.6 1.9 %collective-permute-start.15 = (bf16[16,64,128]{2,1,0:T(8,128)(2,1)S(1)}, bf16[16,64,128]{2,1,0:T(8,128)(2,1)S(1)}, u32[]{:S(2)}, u32[]{:S(2)}) collective-permute-start(bf16[16,64,128]{2,1,0:T(8,128)(2,1)S(1)} %shard_map.37.refs_3_), channel_id=1, source_target_pairs={{0,64},{1,65},{2,66},{3,67},{4,68},{5,69},{6,70},{7,71},{8,72},{9,... | collective-permute-start | bytes 786440 | tf_op jit(solution)/shard_map/ppermute | solution.py:60
  97.5 3.9 %collective-permute-start.16 = (bf16[16,64,128]{2,1,0:T(8,128)(2,1)S(1)}, bf16[16,64,128]{2,1,0:T(8,128)(2,1)S(1)}, u32[]{:S(2)}, u32[]{:S(2)}) collective-permute-start(bf16[16,64,128]{2,1,0:T(8,128)(2,1)S(1)} %shard_map.37.refs_3_), channel_id=1, source_target_pairs={{0,192},{1,193},{2,194},{3,195},{4,196},{5,197},{6,198},{7,199},{8... | collective-permute-start | bytes 786440 | tf_op jit(solution)/shard_map/ppermute | solution.py:60
  101.4 2.5 %collective-permute-start.17 = (bf16[16,64,128]{2,1,0:T(8,128)(2,1)S(1)}, bf16[16,64,128]{2,1,0:T(8,128)(2,1)S(1)}, u32[]{:S(2)}, u32[]{:S(2)}) collective-permute-start(bf16[16,64,128]{2,1,0:T(8,128)(2,1)S(1)} %shard_map.37.refs_3_), channel_id=1, source_target_pairs={{0,128},{1,129},{2,130},{3,131},{4,132},{5,133},{6,134},{7,135},{8... | collective-permute-start | bytes 786440 | tf_op jit(solution)/shard_map/ppermute | solution.py:60
  104.0 1.9 %collective-permute-start.18 = (bf16[16,64,128]{2,1,0:T(8,128)(2,1)S(1)}, bf16[16,64,128]{2,1,0:T(8,128)(2,1)S(1)}, u32[]{:S(2)}, u32[]{:S(2)}) collective-permute-start(bf16[16,64,128]{2,1,0:T(8,128)(2,1)S(1)} %shard_map.37.refs_3_), channel_id=1, source_target_pairs={{0,8},{1,9},{2,10},{3,11},{4,12},{5,13},{6,14},{7,15},{8,0},{9,1},... | collective-permute-start | bytes 786440 | tf_op jit(solution)/shard_map/ppermute | solution.py:60
  106.0 2.3 %collective-permute-start.19 = (bf16[16,64,128]{2,1,0:T(8,128)(2,1)S(1)}, bf16[16,64,128]{2,1,0:T(8,128)(2,1)S(1)}, u32[]{:S(2)}, u32[]{:S(2)}) collective-permute-start(bf16[16,64,128]{2,1,0:T(8,128)(2,1)S(1)} %collective-permute-done.15.refs_4_), channel_id=1, source_target_pairs={{0,8},{1,9},{2,10},{3,11},{4,12},{5,13},{6,14},{7,15},{8,0},{9,1},... | collective-permute-start | bytes 786440 | tf_op jit(solution)/shard_map/ppermute | solution.py:60
  108.3 6.5 %collective-permute-done.16.refs_5_ = bf16[16,64,128]{2,1,0:T(8,128)(2,1)S(1)} collective-permute-done((bf16[16,64,128]{2,1,0:T(8,128)(2,1)S(1)}, bf16[16,64,128]{2,1,0:T(8,128)(2,1)S(1)}, u32[]{:S(2)}, u32[]{:S(2)}) %collective-permute-start.16) | collective-permute-done | bytes 262176 | tf_op jit(solution)/shard_map/ppermute | solution.py:60
  114.8 1.9 %collective-permute-start.20 = (bf16[16,64,128]{2,1,0:T(8,128)(2,1)S(1)}, bf16[16,64,128]{2,1,0:T(8,128)(2,1)S(1)}, u32[]{:S(2)}, u32[]{:S(2)}) collective-permute-start(bf16[16,64,128]{2,1,0:T(8,128)(2,1)S(1)} %collective-permute-done.16.refs_5_), channel_id=1, source_target_pairs={{0,8},{1,9},{2,10},{3,11},{4,12},{5,13},{6,14},{7,15},{8,0},{9,1},... | collective-permute-start | bytes 786440 | tf_op jit(solution)/shard_map/ppermute | solution.py:60
  116.7 2.4 %collective-permute-start.21 = (bf16[16,64,128]{2,1,0:T(8,128)(2,1)S(1)}, bf16[16,64,128]{2,1,0:T(8,128)(2,1)S(1)}, u32[]{:S(2)}, u32[]{:S(2)}) collective-permute-start(bf16[16,64,128]{2,1,0:T(8,128)(2,1)S(1)} %collective-permute-done.17.refs_6_), channel_id=1, source_target_pairs={{0,8},{1,9},{2,10},{3,11},{4,12},{5,13},{6,14},{7,15},{8,0},{9,1},... | collective-permute-start | bytes 786440 | tf_op jit(solution)/shard_map/ppermute | solution.py:60
  119.2 1.1 collective-permute-done.21.refs_10_
  120.3 2.2 %shard_map.38 = bf16[16,64,128]{2,1,0:T(8,128)(2,1)S(1)} custom-call(s32[256]{0:T(256)S(1)} %fusion.refs_0_, f32[256,256]{1,0:T(8,128)S(1)} %add_convert_fusion.refs_1_, bf16[112,64,128]{2,1,0:T(8,128)(2,1)S(1)} %constant_dynamic-update-slice_fusion.refs_2_, bf16[16,64,128]{2,1,0:T(8,128)(2,1)S(1)} %shard_map.37.refs_3_, ...), custom_call_target="tpu_custom_call" | custom-call | flops 536870912 | bytes 8388608 | tf_op jit(solution)/shard_map/pallas_call | solution.py:108
  122.5 1.9 %collective-permute-start.22 = (bf16[16,64,128]{2,1,0:T(8,128)(2,1)S(1)}, bf16[16,64,128]{2,1,0:T(8,128)(2,1)S(1)}, u32[]{:S(2)}, u32[]{:S(2)}) collective-permute-start(bf16[16,64,128]{2,1,0:T(8,128)(2,1)S(1)} %shard_map.38), channel_id=1, source_target_pairs={{0,0},{1,32},{2,68},{3,100},{4,130},{5,162},{6,198},{7,230},{8,1},... | collective-permute-start | bytes 786440 | tf_op jit(solution)/shard_map/ppermute | solution.py:60
  124.4 16.6 %collective-permute-done.22 = bf16[16,64,128]{2,1,0:T(8,128)(2,1)S(1)} collective-permute-done((bf16[16,64,128]{2,1,0:T(8,128)(2,1)S(1)}, bf16[16,64,128]{2,1,0:T(8,128)(2,1)S(1)}, u32[]{:S(2)}, u32[]{:S(2)}) %collective-permute-start.22) | collective-permute-done | bytes 262176 | tf_op jit(solution)/shard_map/ppermute | solution.py:60
  141.0 0.8 convert_element_type.8
  (59 shorter events, 6.6 us)
Async XLA Ops:
  0.0 9.5 %collective-permute-start = (bf16[16,64,128]{2,1,0:T(8,128)(2,1)}, bf16[16,64,128]{2,1,0:T(8,128)(2,1)S(1)}, u32[]{:S(2)}, u32[]{:S(2)}) collective-permute-start(bf16[16,64,128]{2,1,0:T(8,128)(2,1)} %param.3), channel_id=1, source_target_pairs={{0,0},{1,1},{2,194},{3,195},{4,68},{5,69},{6,134},{7,135},{8,16},{... | collective-permute-start | bytes 786440 | tf_op jit(solution)/shard_map/ppermute | solution.py:60
  9.5 21.8 %collective-permute-start.1 = (bf16[16,64,128]{2,1,0:T(8,128)(2,1)S(1)}, bf16[16,64,128]{2,1,0:T(8,128)(2,1)S(1)}, u32[]{:S(2)}, u32[]{:S(2)}) collective-permute-start(bf16[16,64,128]{2,1,0:T(8,128)(2,1)S(1)} %collective-permute-done), channel_id=1, source_target_pairs={{0,0},{1,8},{2,4},{3,12},{4,2},{5,10},{6,6},{7,14},{8,1},{9,9},{10... | collective-permute-start | bytes 786440 | tf_op jit(solution)/shard_map/ppermute | solution.py:60
  31.3 25.6 %collective-permute-start.2 = (bf16[16,64,128]{2,1,0:T(8,128)(2,1)S(1)}, bf16[16,64,128]{2,1,0:T(8,128)(2,1)S(1)}, u32[]{:S(2)}, u32[]{:S(2)}) collective-permute-start(bf16[16,64,128]{2,1,0:T(8,128)(2,1)S(1)} %collective-permute-done.1.refs_3_), channel_id=1, source_target_pairs={{0,48},{1,49},{2,50},{3,51},{4,52},{5,53},{6,54},{7,55},{8,56},{9,... | collective-permute-start | bytes 786440 | tf_op jit(solution)/shard_map/ppermute | solution.py:60
  37.6 21.3 %collective-permute-start.3 = (bf16[16,64,128]{2,1,0:T(8,128)(2,1)S(1)}, bf16[16,64,128]{2,1,0:T(8,128)(2,1)S(1)}, u32[]{:S(2)}, u32[]{:S(2)}) collective-permute-start(bf16[16,64,128]{2,1,0:T(8,128)(2,1)S(1)} %collective-permute-done.1.refs_3_), channel_id=1, source_target_pairs={{0,32},{1,33},{2,34},{3,35},{4,36},{5,37},{6,38},{7,39},{8,40},{9,... | collective-permute-start | bytes 786440 | tf_op jit(solution)/shard_map/ppermute | solution.py:60
  41.5 21.3 %collective-permute-start.4 = (bf16[16,64,128]{2,1,0:T(8,128)(2,1)S(1)}, bf16[16,64,128]{2,1,0:T(8,128)(2,1)S(1)}, u32[]{:S(2)}, u32[]{:S(2)}) collective-permute-start(bf16[16,64,128]{2,1,0:T(8,128)(2,1)S(1)} %collective-permute-done.1.refs_3_), channel_id=1, source_target_pairs={{0,16},{1,17},{2,18},{3,19},{4,20},{5,21},{6,22},{7,23},{8,24},{9,... | collective-permute-start | bytes 786440 | tf_op jit(solution)/shard_map/ppermute | solution.py:60
  43.9 22.5 %collective-permute-start.5 = (bf16[16,64,128]{2,1,0:T(8,128)(2,1)S(1)}, bf16[16,64,128]{2,1,0:T(8,128)(2,1)S(1)}, u32[]{:S(2)}, u32[]{:S(2)}) collective-permute-start(bf16[16,64,128]{2,1,0:T(8,128)(2,1)S(1)} %collective-permute-done.1.refs_3_), channel_id=1, source_target_pairs={{0,503},{1,48},{2,113},{3,50},{4,179},{5,52},{6,117},{7,54},{8,511... | collective-permute-start | bytes 786440 | tf_op jit(solution)/shard_map/ppermute | solution.py:60
  47.7 35.8 %collective-permute-start.6 = (bf16[16,64,128]{2,1,0:T(8,128)(2,1)S(1)}, bf16[16,64,128]{2,1,0:T(8,128)(2,1)S(1)}, u32[]{:S(2)}, u32[]{:S(2)}) collective-permute-start(bf16[16,64,128]{2,1,0:T(8,128)(2,1)S(1)} %collective-permute-done.1.refs_3_), channel_id=1, source_target_pairs={{0,487},{1,32},{2,97},{3,34},{4,163},{5,36},{6,101},{7,38},{8,495}... | collective-permute-start | bytes 786440 | tf_op jit(solution)/shard_map/ppermute | solution.py:60
  56.9 28.6 %collective-permute-start.8 = (bf16[16,64,128]{2,1,0:T(8,128)(2,1)S(1)}, bf16[16,64,128]{2,1,0:T(8,128)(2,1)S(1)}, u32[]{:S(2)}, u32[]{:S(2)}) collective-permute-start(bf16[16,64,128]{2,1,0:T(8,128)(2,1)S(1)} %collective-permute-done.1.refs_3_), channel_id=1, source_target_pairs={{0,64},{1,65},{2,66},{3,67},{4,68},{5,69},{6,70},{7,71},{8,72},{9,... | collective-permute-start | bytes 786440 | tf_op jit(solution)/shard_map/ppermute | solution.py:60
  58.9 29.0 %collective-permute-start.9 = (bf16[16,64,128]{2,1,0:T(8,128)(2,1)S(1)}, bf16[16,64,128]{2,1,0:T(8,128)(2,1)S(1)}, u32[]{:S(2)}, u32[]{:S(2)}) collective-permute-start(bf16[16,64,128]{2,1,0:T(8,128)(2,1)S(1)} %collective-permute-done.1.refs_3_), channel_id=1, source_target_pairs={{0,192},{1,193},{2,194},{3,195},{4,196},{5,197},{6,198},{7,199},{8... | collective-permute-start | bytes 786440 | tf_op jit(solution)/shard_map/ppermute | solution.py:60
  62.8 27.0 %collective-permute-start.10 = (bf16[16,64,128]{2,1,0:T(8,128)(2,1)S(1)}, bf16[16,64,128]{2,1,0:T(8,128)(2,1)S(1)}, u32[]{:S(2)}, u32[]{:S(2)}) collective-permute-start(bf16[16,64,128]{2,1,0:T(8,128)(2,1)S(1)} %collective-permute-done.1.refs_3_), channel_id=1, source_target_pairs={{0,128},{1,129},{2,130},{3,131},{4,132},{5,133},{6,134},{7,135},{8... | collective-permute-start | bytes 786440 | tf_op jit(solution)/shard_map/ppermute | solution.py:60
  66.4 25.9 %collective-permute-start.7 = (bf16[16,64,128]{2,1,0:T(8,128)(2,1)S(1)}, bf16[16,64,128]{2,1,0:T(8,128)(2,1)S(1)}, u32[]{:S(2)}, u32[]{:S(2)}) collective-permute-start(bf16[16,64,128]{2,1,0:T(8,128)(2,1)S(1)} %collective-permute-done.1.refs_3_), channel_id=1, source_target_pairs={{0,471},{1,16},{2,81},{3,18},{4,147},{5,20},{6,85},{7,22},{8,479},... | collective-permute-start | bytes 786440 | tf_op jit(solution)/shard_map/ppermute | solution.py:60
  83.5 8.9 %collective-permute-start.11 = (bf16[16,64,128]{2,1,0:T(8,128)(2,1)S(1)}, bf16[16,64,128]{2,1,0:T(8,128)(2,1)S(1)}, u32[]{:S(2)}, u32[]{:S(2)}) collective-permute-start(bf16[16,64,128]{2,1,0:T(8,128)(2,1)S(1)} %collective-permute-done.1.refs_3_), channel_id=1, source_target_pairs={{0,8},{1,9},{2,10},{3,11},{4,12},{5,13},{6,14},{7,15},{8,0},{9,1},... | collective-permute-start | bytes 786440 | tf_op jit(solution)/shard_map/ppermute | solution.py:60
  85.5 6.9 %collective-permute-start.12 = (bf16[16,64,128]{2,1,0:T(8,128)(2,1)S(1)}, bf16[16,64,128]{2,1,0:T(8,128)(2,1)S(1)}, u32[]{:S(2)}, u32[]{:S(2)}) collective-permute-start(bf16[16,64,128]{2,1,0:T(8,128)(2,1)S(1)} %collective-permute-done.8.refs_4_), channel_id=1, source_target_pairs={{0,8},{1,9},{2,10},{3,11},{4,12},{5,13},{6,14},{7,15},{8,0},{9,1},... | collective-permute-start | bytes 786440 | tf_op jit(solution)/shard_map/ppermute | solution.py:60
  87.9 4.5 %collective-permute-start.13 = (bf16[16,64,128]{2,1,0:T(8,128)(2,1)S(1)}, bf16[16,64,128]{2,1,0:T(8,128)(2,1)S(1)}, u32[]{:S(2)}, u32[]{:S(2)}) collective-permute-start(bf16[16,64,128]{2,1,0:T(8,128)(2,1)S(1)} %collective-permute-done.9.refs_5_), channel_id=1, source_target_pairs={{0,8},{1,9},{2,10},{3,11},{4,12},{5,13},{6,14},{7,15},{8,0},{9,1},... | collective-permute-start | bytes 786440 | tf_op jit(solution)/shard_map/ppermute | solution.py:60
  89.8 3.6 %collective-permute-start.14 = (bf16[16,64,128]{2,1,0:T(8,128)(2,1)S(1)}, bf16[16,64,128]{2,1,0:T(8,128)(2,1)S(1)}, u32[]{:S(2)}, u32[]{:S(2)}) collective-permute-start(bf16[16,64,128]{2,1,0:T(8,128)(2,1)S(1)} %collective-permute-done.10.refs_6_), channel_id=1, source_target_pairs={{0,8},{1,9},{2,10},{3,11},{4,12},{5,13},{6,14},{7,15},{8,0},{9,1},... | collective-permute-start | bytes 786440 | tf_op jit(solution)/shard_map/ppermute | solution.py:60
  95.6 10.5 %collective-permute-start.15 = (bf16[16,64,128]{2,1,0:T(8,128)(2,1)S(1)}, bf16[16,64,128]{2,1,0:T(8,128)(2,1)S(1)}, u32[]{:S(2)}, u32[]{:S(2)}) collective-permute-start(bf16[16,64,128]{2,1,0:T(8,128)(2,1)S(1)} %shard_map.37.refs_3_), channel_id=1, source_target_pairs={{0,64},{1,65},{2,66},{3,67},{4,68},{5,69},{6,70},{7,71},{8,72},{9,... | collective-permute-start | bytes 786440 | tf_op jit(solution)/shard_map/ppermute | solution.py:60
  97.5 17.3 %collective-permute-start.16 = (bf16[16,64,128]{2,1,0:T(8,128)(2,1)S(1)}, bf16[16,64,128]{2,1,0:T(8,128)(2,1)S(1)}, u32[]{:S(2)}, u32[]{:S(2)}) collective-permute-start(bf16[16,64,128]{2,1,0:T(8,128)(2,1)S(1)} %shard_map.37.refs_3_), channel_id=1, source_target_pairs={{0,192},{1,193},{2,194},{3,195},{4,196},{5,197},{6,198},{7,199},{8... | collective-permute-start | bytes 786440 | tf_op jit(solution)/shard_map/ppermute | solution.py:60
  101.4 15.3 %collective-permute-start.17 = (bf16[16,64,128]{2,1,0:T(8,128)(2,1)S(1)}, bf16[16,64,128]{2,1,0:T(8,128)(2,1)S(1)}, u32[]{:S(2)}, u32[]{:S(2)}) collective-permute-start(bf16[16,64,128]{2,1,0:T(8,128)(2,1)S(1)} %shard_map.37.refs_3_), channel_id=1, source_target_pairs={{0,128},{1,129},{2,130},{3,131},{4,132},{5,133},{6,134},{7,135},{8... | collective-permute-start | bytes 786440 | tf_op jit(solution)/shard_map/ppermute | solution.py:60
  104.0 15.2 %collective-permute-start.18 = (bf16[16,64,128]{2,1,0:T(8,128)(2,1)S(1)}, bf16[16,64,128]{2,1,0:T(8,128)(2,1)S(1)}, u32[]{:S(2)}, u32[]{:S(2)}) collective-permute-start(bf16[16,64,128]{2,1,0:T(8,128)(2,1)S(1)} %shard_map.37.refs_3_), channel_id=1, source_target_pairs={{0,8},{1,9},{2,10},{3,11},{4,12},{5,13},{6,14},{7,15},{8,0},{9,1},... | collective-permute-start | bytes 786440 | tf_op jit(solution)/shard_map/ppermute | solution.py:60
  106.0 13.1 %collective-permute-start.19 = (bf16[16,64,128]{2,1,0:T(8,128)(2,1)S(1)}, bf16[16,64,128]{2,1,0:T(8,128)(2,1)S(1)}, u32[]{:S(2)}, u32[]{:S(2)}) collective-permute-start(bf16[16,64,128]{2,1,0:T(8,128)(2,1)S(1)} %collective-permute-done.15.refs_4_), channel_id=1, source_target_pairs={{0,8},{1,9},{2,10},{3,11},{4,12},{5,13},{6,14},{7,15},{8,0},{9,1},... | collective-permute-start | bytes 786440 | tf_op jit(solution)/shard_map/ppermute | solution.py:60
  114.8 4.4 %collective-permute-start.20 = (bf16[16,64,128]{2,1,0:T(8,128)(2,1)S(1)}, bf16[16,64,128]{2,1,0:T(8,128)(2,1)S(1)}, u32[]{:S(2)}, u32[]{:S(2)}) collective-permute-start(bf16[16,64,128]{2,1,0:T(8,128)(2,1)S(1)} %collective-permute-done.16.refs_5_), channel_id=1, source_target_pairs={{0,8},{1,9},{2,10},{3,11},{4,12},{5,13},{6,14},{7,15},{8,0},{9,1},... | collective-permute-start | bytes 786440 | tf_op jit(solution)/shard_map/ppermute | solution.py:60
  116.7 3.6 %collective-permute-start.21 = (bf16[16,64,128]{2,1,0:T(8,128)(2,1)S(1)}, bf16[16,64,128]{2,1,0:T(8,128)(2,1)S(1)}, u32[]{:S(2)}, u32[]{:S(2)}) collective-permute-start(bf16[16,64,128]{2,1,0:T(8,128)(2,1)S(1)} %collective-permute-done.17.refs_6_), channel_id=1, source_target_pairs={{0,8},{1,9},{2,10},{3,11},{4,12},{5,13},{6,14},{7,15},{8,0},{9,1},... | collective-permute-start | bytes 786440 | tf_op jit(solution)/shard_map/ppermute | solution.py:60
  122.5 18.6 %collective-permute-start.22 = (bf16[16,64,128]{2,1,0:T(8,128)(2,1)S(1)}, bf16[16,64,128]{2,1,0:T(8,128)(2,1)S(1)}, u32[]{:S(2)}, u32[]{:S(2)}) collective-permute-start(bf16[16,64,128]{2,1,0:T(8,128)(2,1)S(1)} %shard_map.38), channel_id=1, source_target_pairs={{0,0},{1,32},{2,68},{3,100},{4,130},{5,162},{6,198},{7,230},{8,1},... | collective-permute-start | bytes 786440 | tf_op jit(solution)/shard_map/ppermute | solution.py:60

commit v3 on v2

--- a/solution.py
+++ b/solution.py
@@ -9,7 +9,6 @@
 AXES = ("row", "col")
 PANELS = 64
 GROUPS = 8
-SPAN = 3
 TURN = ((0, 3, 1, 2), (1, 2, 0, 3), (2, 0, 3, 1), (3, 1, 2, 0))
 
 
@@ -50,7 +49,7 @@
 def arrival(panel, group):
     order = []
     for core in (group % 2, 1 - group % 2):
-        for distance in (0, 1, -1, 2):
+        for distance in (0, 2, 1, -1):
             x = (TURN[panel // 8 % 4][group // 2] - distance) % 4
             order.append(TURN[panel // 8 % 4].index(x) * 2 + core)
     return order
@@ -60,21 +59,49 @@
     return lax.ppermute(value, AXES, moves)
 
 
-def gather_row(part):
+def gather_row(part, after=()):
     other = route(place, lambda panel, group: place(panel, group ^ 1))
-    near = [part] + [send(part, sideways(distance)) for distance in (1, -1, 2)]
-    return near + [send(piece, other) for piece in near]
+    near = [part] + [send(part, sideways(distance)) for distance in (2, 1, -1)]
+    near = lax.optimization_barrier((near, after))[0]
+    far = send(jnp.concatenate(near, axis=0), other)
+    return near + jnp.split(far, len(near), axis=0)
 
 
-def gather_table(part):
-    panels = []
-    for offset in range(-SPAN, SPAN + 1):
-        if offset == 0:
-            panels.append(part)
-        else:
-            moves = route(lambda p, g: place((p + offset) % PANELS, g), place)
-            panels.append(send(part, moves))
-    return jnp.concatenate(panels, axis=0)
+def column_panel(panel, distance):
+    return panel // 4 * 4 + (panel + distance) % 4
+
+
+def passed(panel, distance):
+    wanted = column_panel(panel, distance)
+    return (wanted - 4 if wanted > panel else wanted + 4) % PANELS
+
+
+def gather_beside(part):
+    beside = []
+    for distance in (2, 1, 3):
+        moves = route(lambda p, g: place(column_panel(p, distance), g), place)
+        beside.append(send(part, moves))
+    return beside
+
+
+def gather_table(part, beside):
+    beyond = []
+    for distance, piece in zip((2, 1, 3), beside):
+        moves = route(
+            lambda p, g: place(passed(p, distance) // 4 * 4 + p % 4, g), place
+        )
+        beyond.append(send(piece, moves))
+    return jnp.concatenate([part] + beside + beyond, axis=0)
+
+
+def table_panel(owner, panel):
+    index = jnp.zeros_like(owner)
+    for slot, distance in enumerate((2, 1, 3)):
+        wanted = column_panel(panel, distance)
+        index = jnp.where(owner == wanted - panel, 1 + slot, index)
+        outer = jnp.where(wanted > panel, wanted - 4, wanted + 4)
+        index = jnp.where(owner == outer - panel, 4 + slot, index)
+    return index
 
 
 def product_kernel(count, group, keep, index_ref, mask_ref, table_ref, *refs):
@@ -140,7 +167,9 @@
     own = jnp.take(own.reshape(local_rows, GROUPS, group), order, axis=1)
     own = own.reshape(local_rows, stored)
     distance = jnp.mod(own - base + total // 2, total) - total // 2
-    index = (distance + SPAN * local_rows).reshape(-1)
+    owner = jnp.floor_divide(distance, local_rows)
+    index = table_panel(owner, panel) * local_rows + distance - owner * local_rows
+    index = index.reshape(-1)
     held = lax.dynamic_slice_in_dim(columns, mine * group, group, 1)
     held = jnp.take(held, own.reshape(-1), axis=0).reshape(local_rows, stored, group)
     lane_slot = jnp.arange(lanes, dtype=jnp.int32) // width
@@ -150,8 +179,9 @@
     mask = jnp.concatenate([found == direct, found == swapped], axis=-1)
     mask = mask.astype(jnp.float32).reshape(local_rows * stored, 2 * lanes)
 
-    left = gather_row(part)
-    table = gather_table(part).reshape(-1, width, lanes)
+    beside = gather_beside(part)
+    left = gather_row(part, beside)
+    table = gather_table(part, beside).reshape(-1, width, lanes)
     square = product(index, mask, table, left, False)
     result = product(index, mask, table, gather_row(square), True)
     return send(result, route(place, start)).astype(jnp.float32)

time: 143 us -> 148 us (1.035)
  the two profiles are of different devices: /device:TPU:22 before, /device:TPU:6 now
where the time goes in v3:
time: 148 us; the launch traced here: 147 us
  starting transfers between devices  63.8 us (43%)
  waiting for transfers between devices  59.1 us (40%)
  between operations  11.7 us (8%)
  local copies, waits for them, and re-layouts  6.74 us (5%)
  Pallas kernels  4.38 us (3%)
  other arithmetic  1.71 us (1%)
    ppermute x17, starting transfers between devices, send(): return lax.ppermute(value, AXES, moves)  63.8 us
    ppermute x17, waiting for transfers between devices, send(): return lax.ppermute(value, AXES, moves)  59.1 us
    pallas_call x2, Pallas kernels, product(): pl.pallas_call(lambda *refs: product_kernel(count, lanes // width, keep,...  4.38 us
  transfers between devices with their start and end apart: 17, of which 11 were waited for; matrix products, arithmetic and copies ran while one was open for 5% of the time, Pallas kernels for 0%

profile of v3, /device:TPU:6, one launch (start us, length us, event | category | flops | bytes accessed | tf_op | source)
XLA Modules:
  0.0 147.4 jit_solution(6998121438248180907)
XLA Ops:
  0.0 1.6 %collective-permute-start = (bf16[16,64,128]{2,1,0:T(8,128)(2,1)}, bf16[16,64,128]{2,1,0:T(8,128)(2,1)S(1)}, u32[]{:S(2)}, u32[]{:S(2)}) collective-permute-start(bf16[16,64,128]{2,1,0:T(8,128)(2,1)} %param.3), channel_id=1, source_target_pairs={{0,0},{1,1},{2,194},{3,195},{4,68},{5,69},{6,134},{7,135},{8,16},{... | collective-permute-start | bytes 786440 | tf_op jit(solution)/shard_map/ppermute | solution.py:59
  8.3 15.9 %collective-permute-start.1 = (bf16[16,64,128]{2,1,0:T(8,128)(2,1)S(1)}, bf16[16,64,128]{2,1,0:T(8,128)(2,1)S(1)}, u32[]{:S(2)}, u32[]{:S(2)}) collective-permute-start(bf16[16,64,128]{2,1,0:T(8,128)(2,1)S(1)} %collective-permute-done), channel_id=1, source_target_pairs={{0,0},{1,8},{2,4},{3,12},{4,2},{5,10},{6,6},{7,14},{8,1},{9,9},{10... | collective-permute-start | bytes 786440 | tf_op jit(solution)/shard_map/ppermute | solution.py:59
  24.2 5.9 %collective-permute-done.1.refs_3_ = bf16[16,64,128]{2,1,0:T(8,128)(2,1)S(1)} collective-permute-done((bf16[16,64,128]{2,1,0:T(8,128)(2,1)S(1)}, bf16[16,64,128]{2,1,0:T(8,128)(2,1)S(1)}, u32[]{:S(2)}, u32[]{:S(2)}) %collective-permute-start.1) | collective-permute-done | bytes 262176 | tf_op jit(solution)/shard_map/ppermute | solution.py:59
  30.2 6.2 %collective-permute-start.2 = (bf16[16,64,128]{2,1,0:T(8,128)(2,1)S(1)}, bf16[16,64,128]{2,1,0:T(8,128)(2,1)S(1)}, u32[]{:S(2)}, u32[]{:S(2)}) collective-permute-start(bf16[16,64,128]{2,1,0:T(8,128)(2,1)S(1)} %collective-permute-done.1.refs_3_), channel_id=1, source_target_pairs={{0,32},{1,33},{2,34},{3,35},{4,36},{5,37},{6,38},{7,39},{8,40},{9,... | collective-permute-start | bytes 786440 | tf_op jit(solution)/shard_map/ppermute | solution.py:59
  47.0 0.8 dynamic_slice.16
  47.8 2.7 %collective-permute-start.3 = (bf16[16,64,128]{2,1,0:T(8,128)(2,1)S(1)}, bf16[16,64,128]{2,1,0:T(8,128)(2,1)S(1)}, u32[]{:S(2)}, u32[]{:S(2)}) collective-permute-start(bf16[16,64,128]{2,1,0:T(8,128)(2,1)S(1)} %collective-permute-done.1.refs_3_), channel_id=1, source_target_pairs={{0,48},{1,49},{2,50},{3,51},{4,52},{5,53},{6,54},{7,55},{8,56},{9,... | collective-permute-start | bytes 786440 | tf_op jit(solution)/shard_map/ppermute | solution.py:59
  50.5 3.2 %collective-permute-start.4 = (bf16[16,64,128]{2,1,0:T(8,128)(2,1)S(1)}, bf16[16,64,128]{2,1,0:T(8,128)(2,1)S(1)}, u32[]{:S(2)}, u32[]{:S(2)}) collective-permute-start(bf16[16,64,128]{2,1,0:T(8,128)(2,1)S(1)} %collective-permute-done.1.refs_3_), channel_id=1, source_target_pairs={{0,16},{1,17},{2,18},{3,19},{4,20},{5,21},{6,22},{7,23},{8,24},{9,... | collective-permute-start | bytes 786440 | tf_op jit(solution)/shard_map/ppermute | solution.py:59
  53.7 4.1 %collective-permute-start.8 = (bf16[16,64,128]{2,1,0:T(8,128)(2,1)S(1)}, bf16[16,64,128]{2,1,0:T(8,128)(2,1)S(1)}, u32[]{:S(2)}, u32[]{:S(2)}) collective-permute-start(bf16[16,64,128]{2,1,0:T(8,128)(2,1)S(1)} %collective-permute-done.1.refs_3_), channel_id=1, source_target_pairs={{0,128},{1,129},{2,130},{3,131},{4,132},{5,133},{6,134},{7,135},{8... | collective-permute-start | bytes 786440 | tf_op jit(solution)/shard_map/ppermute | solution.py:59
  57.8 8.2 %collective-permute-start.9 = (bf16[16,64,128]{2,1,0:T(8,128)(2,1)S(1)}, bf16[16,64,128]{2,1,0:T(8,128)(2,1)S(1)}, u32[]{:S(2)}, u32[]{:S(2)}) collective-permute-start(bf16[16,64,128]{2,1,0:T(8,128)(2,1)S(1)} %collective-permute-done.1.refs_3_), channel_id=1, source_target_pairs={{0,64},{1,65},{2,66},{3,67},{4,68},{5,69},{6,70},{7,71},{8,72},{9,... | collective-permute-start | bytes 786440 | tf_op jit(solution)/shard_map/ppermute | solution.py:59
  66.0 1.9 %collective-permute-start.10 = (bf16[16,64,128]{2,1,0:T(8,128)(2,1)S(1)}, bf16[16,64,128]{2,1,0:T(8,128)(2,1)S(1)}, u32[]{:S(2)}, u32[]{:S(2)}) collective-permute-start(bf16[16,64,128]{2,1,0:T(8,128)(2,1)S(1)} %collective-permute-done.1.refs_3_), channel_id=1, source_target_pairs={{0,192},{1,193},{2,194},{3,195},{4,196},{5,197},{6,198},{7,199},{8... | collective-permute-start | bytes 786440 | tf_op jit(solution)/shard_map/ppermute | solution.py:59
  68.2 1.6 %collective-permute-done.9.refs_5_ = bf16[16,64,128]{2,1,0:T(8,128)(2,1)S(1)} collective-permute-done((bf16[16,64,128]{2,1,0:T(8,128)(2,1)S(1)}, bf16[16,64,128]{2,1,0:T(8,128)(2,1)S(1)}, u32[]{:S(2)}, u32[]{:S(2)}) %collective-permute-start.9) | collective-permute-done | bytes 262176 | tf_op jit(solution)/shard_map/ppermute | solution.py:59
  69.9 5.6 %collective-permute-done.10.refs_6_ = bf16[16,64,128]{2,1,0:T(8,128)(2,1)S(1)} collective-permute-done((bf16[16,64,128]{2,1,0:T(8,128)(2,1)S(1)}, bf16[16,64,128]{2,1,0:T(8,128)(2,1)S(1)}, u32[]{:S(2)}, u32[]{:S(2)}) %collective-permute-start.10) | collective-permute-done | bytes 262176 | tf_op jit(solution)/shard_map/ppermute | solution.py:59
  75.6 1.9 %collective-permute-start.11 = (bf16[64,64,128]{2,1,0:T(8,128)(2,1)S(1)}, bf16[64,64,128]{2,1,0:T(8,128)(2,1)S(1)}, u32[]{:S(2)}, u32[]{:S(2)}) collective-permute-start(bf16[64,64,128]{2,1,0:T(8,128)(2,1)S(1)} %pad_maximum_fusion), channel_id=1, source_target_pairs={{0,8},{1,9},{2,10},{3,11},{4,12},{5,13},{6,14},{7,15},{8,0},{9,1},... | collective-permute-start | bytes 3145736 | tf_op jit(solution)/shard_map/ppermute | solution.py:59
  77.6 2.0 %collective-permute-start.5 = (bf16[16,64,128]{2,1,0:T(8,128)(2,1)S(1)}, bf16[16,64,128]{2,1,0:T(8,128)(2,1)S(1)}, u32[]{:S(2)}, u32[]{:S(2)}) collective-permute-start(bf16[16,64,128]{2,1,0:T(8,128)(2,1)S(1)} %collective-permute-done.2), channel_id=1, source_target_pairs={{0,1},{1,66},{2,3},{3,196},{4,5},{5,70},{6,7},{7,384},{8,9},{9,74}... | collective-permute-start | bytes 786440 | tf_op jit(solution)/shard_map/ppermute | solution.py:59
  79.6 1.9 %collective-permute-start.6 = (bf16[16,64,128]{2,1,0:T(8,128)(2,1)S(1)}, bf16[16,64,128]{2,1,0:T(8,128)(2,1)S(1)}, u32[]{:S(2)}, u32[]{:S(2)}) collective-permute-start(bf16[16,64,128]{2,1,0:T(8,128)(2,1)S(1)} %collective-permute-done.3), channel_id=1, source_target_pairs={{0,1},{1,66},{2,3},{3,196},{4,5},{5,70},{6,7},{7,384},{8,9},{9,74}... | collective-permute-start | bytes 786440 | tf_op jit(solution)/shard_map/ppermute | solution.py:59
  81.6 1.9 %collective-permute-start.7 = (bf16[16,64,128]{2,1,0:T(8,128)(2,1)S(1)}, bf16[16,64,128]{2,1,0:T(8,128)(2,1)S(1)}, u32[]{:S(2)}, u32[]{:S(2)}) collective-permute-start(bf16[16,64,128]{2,1,0:T(8,128)(2,1)S(1)} %collective-permute-done.4), channel_id=1, source_target_pairs={{0,1},{1,66},{2,3},{3,196},{4,5},{5,70},{6,7},{7,384},{8,9},{9,74}... | collective-permute-start | bytes 786440 | tf_op jit(solution)/shard_map/ppermute | solution.py:59
  83.6 9.1 %collective-permute-done.5 = bf16[16,64,128]{2,1,0:T(8,128)(2,1)S(1)} collective-permute-done((bf16[16,64,128]{2,1,0:T(8,128)(2,1)S(1)}, bf16[16,64,128]{2,1,0:T(8,128)(2,1)S(1)}, u32[]{:S(2)}, u32[]{:S(2)}) %collective-permute-start.5) | collective-permute-done | bytes 262176 | tf_op jit(solution)/shard_map/ppermute | solution.py:59
  92.8 5.6 %collective-permute-done.6 = bf16[16,64,128]{2,1,0:T(8,128)(2,1)S(1)} collective-permute-done((bf16[16,64,128]{2,1,0:T(8,128)(2,1)S(1)}, bf16[16,64,128]{2,1,0:T(8,128)(2,1)S(1)}, u32[]{:S(2)}, u32[]{:S(2)}) %collective-permute-start.6) | collective-permute-done | bytes 262176 | tf_op jit(solution)/shard_map/ppermute | solution.py:59
  98.4 5.4 %collective-permute-done.7 = bf16[16,64,128]{2,1,0:T(8,128)(2,1)S(1)} collective-permute-done((bf16[16,64,128]{2,1,0:T(8,128)(2,1)S(1)}, bf16[16,64,128]{2,1,0:T(8,128)(2,1)S(1)}, u32[]{:S(2)}, u32[]{:S(2)}) %collective-permute-start.7) | collective-permute-done | bytes 262176 | tf_op jit(solution)/shard_map/ppermute | solution.py:59
  103.9 2.2 %shard_map.37.refs_3_ = bf16[16,64,128]{2,1,0:T(8,128)(2,1)S(1)} custom-call(s32[256]{0:T(256)S(1)} %fusion.3.refs_0_, f32[256,256]{1,0:T(8,128)S(1)} %add_convert_fusion.refs_1_, bf16[112,64,128]{2,1,0:T(8,128)(2,1)S(1)} %constant_dynamic-update-slice_fusion.refs_2_, bf16[16,64,128]{2,1,0:T(8,128)(2,1)S(1)} %collective-permute-done.1.refs_3_, ...), custom_call_target="tpu_custom_call" | custom-call | flops 536870912 | bytes 8388608 | tf_op jit(solution)/shard_map/pallas_call | solution.py:135
  106.1 2.5 %collective-permute-start.12 = (bf16[16,64,128]{2,1,0:T(8,128)(2,1)S(1)}, bf16[16,64,128]{2,1,0:T(8,128)(2,1)S(1)}, u32[]{:S(2)}, u32[]{:S(2)}) collective-permute-start(bf16[16,64,128]{2,1,0:T(8,128)(2,1)S(1)} %shard_map.37.refs_3_), channel_id=1, source_target_pairs={{0,128},{1,129},{2,130},{3,131},{4,132},{5,133},{6,134},{7,135},{8... | collective-permute-start | bytes 786440 | tf_op jit(solution)/shard_map/ppermute | solution.py:59
  108.6 3.6 %collective-permute-start.13 = (bf16[16,64,128]{2,1,0:T(8,128)(2,1)S(1)}, bf16[16,64,128]{2,1,0:T(8,128)(2,1)S(1)}, u32[]{:S(2)}, u32[]{:S(2)}) collective-permute-start(bf16[16,64,128]{2,1,0:T(8,128)(2,1)S(1)} %shard_map.37.refs_3_), channel_id=1, source_target_pairs={{0,64},{1,65},{2,66},{3,67},{4,68},{5,69},{6,70},{7,71},{8,72},{9,... | collective-permute-start | bytes 786440 | tf_op jit(solution)/shard_map/ppermute | solution.py:59
  112.2 2.2 %collective-permute-start.14 = (bf16[16,64,128]{2,1,0:T(8,128)(2,1)S(1)}, bf16[16,64,128]{2,1,0:T(8,128)(2,1)S(1)}, u32[]{:S(2)}, u32[]{:S(2)}) collective-permute-start(bf16[16,64,128]{2,1,0:T(8,128)(2,1)S(1)} %shard_map.37.refs_3_), channel_id=1, source_target_pairs={{0,192},{1,193},{2,194},{3,195},{4,196},{5,197},{6,198},{7,199},{8... | collective-permute-start | bytes 786440 | tf_op jit(solution)/shard_map/ppermute | solution.py:59
  114.5 3.4 %collective-permute-done.12.refs_4_ = bf16[16,64,128]{2,1,0:T(8,128)(2,1)S(1)} collective-permute-done((bf16[16,64,128]{2,1,0:T(8,128)(2,1)S(1)}, bf16[16,64,128]{2,1,0:T(8,128)(2,1)S(1)}, u32[]{:S(2)}, u32[]{:S(2)}) %collective-permute-start.12) | collective-permute-done | bytes 262176 | tf_op jit(solution)/shard_map/ppermute | solution.py:59
  117.9 4.5 %collective-permute-done.13.refs_5_ = bf16[16,64,128]{2,1,0:T(8,128)(2,1)S(1)} collective-permute-done((bf16[16,64,128]{2,1,0:T(8,128)(2,1)S(1)}, bf16[16,64,128]{2,1,0:T(8,128)(2,1)S(1)}, u32[]{:S(2)}, u32[]{:S(2)}) %collective-permute-start.13) | collective-permute-done | bytes 262176 | tf_op jit(solution)/shard_map/ppermute | solution.py:59
  122.4 0.9 collective-permute-done.14.refs_6_
  123.4 1.9 %collective-permute-start.15 = (bf16[64,64,128]{2,1,0:T(8,128)(2,1)S(1)}, bf16[64,64,128]{2,1,0:T(8,128)(2,1)S(1)}, u32[]{:S(2)}, u32[]{:S(2)}) collective-permute-start(bf16[64,64,128]{2,1,0:T(8,128)(2,1)S(1)} %pad_maximum_fusion.1), channel_id=1, source_target_pairs={{0,8},{1,9},{2,10},{3,11},{4,12},{5,13},{6,14},{7,15},{8,0},{9,1},... | collective-permute-start | bytes 3145736 | tf_op jit(solution)/shard_map/ppermute | solution.py:59
  125.3 2.6 %collective-permute-done.15 = bf16[64,64,128]{2,1,0:T(8,128)(2,1)S(1)} collective-permute-done((bf16[64,64,128]{2,1,0:T(8,128)(2,1)S(1)}, bf16[64,64,128]{2,1,0:T(8,128)(2,1)S(1)}, u32[]{:S(2)}, u32[]{:S(2)}) %collective-permute-start.15) | collective-permute-done | bytes 1048608 | tf_op jit(solution)/shard_map/ppermute | solution.py:59
  128.0 2.2 %shard_map.38 = bf16[16,64,128]{2,1,0:T(8,128)(2,1)S(1)} custom-call(s32[256]{0:T(256)S(1)} %fusion.3.refs_0_, f32[256,256]{1,0:T(8,128)S(1)} %add_convert_fusion.refs_1_, bf16[112,64,128]{2,1,0:T(8,128)(2,1)S(1)} %constant_dynamic-update-slice_fusion.refs_2_, bf16[16,64,128]{2,1,0:T(8,128)(2,1)S(1)} %shard_map.37.refs_3_, ...), custom_call_target="tpu_custom_call" | custom-call | flops 536870912 | bytes 8388608 | tf_op jit(solution)/shard_map/pallas_call | solution.py:135
  130.2 1.9 %collective-permute-start.16 = (bf16[16,64,128]{2,1,0:T(8,128)(2,1)S(1)}, bf16[16,64,128]{2,1,0:T(8,128)(2,1)S(1)}, u32[]{:S(2)}, u32[]{:S(2)}) collective-permute-start(bf16[16,64,128]{2,1,0:T(8,128)(2,1)S(1)} %shard_map.38), channel_id=1, source_target_pairs={{0,0},{1,32},{2,68},{3,100},{4,130},{5,162},{6,198},{7,230},{8,1},... | collective-permute-start | bytes 786440 | tf_op jit(solution)/shard_map/ppermute | solution.py:59
  132.1 14.4 %collective-permute-done.16 = bf16[16,64,128]{2,1,0:T(8,128)(2,1)S(1)} collective-permute-done((bf16[16,64,128]{2,1,0:T(8,128)(2,1)S(1)}, bf16[16,64,128]{2,1,0:T(8,128)(2,1)S(1)}, u32[]{:S(2)}, u32[]{:S(2)}) %collective-permute-start.16) | collective-permute-done | bytes 262176 | tf_op jit(solution)/shard_map/ppermute | solution.py:59
  146.6 0.8 convert_element_type.8
  (51 shorter events, 6.8 us)
Async XLA Ops:
  0.0 8.3 %collective-permute-start = (bf16[16,64,128]{2,1,0:T(8,128)(2,1)}, bf16[16,64,128]{2,1,0:T(8,128)(2,1)S(1)}, u32[]{:S(2)}, u32[]{:S(2)}) collective-permute-start(bf16[16,64,128]{2,1,0:T(8,128)(2,1)} %param.3), channel_id=1, source_target_pairs={{0,0},{1,1},{2,194},{3,195},{4,68},{5,69},{6,134},{7,135},{8,16},{... | collective-permute-start | bytes 786440 | tf_op jit(solution)/shard_map/ppermute | solution.py:59
  8.3 21.9 %collective-permute-start.1 = (bf16[16,64,128]{2,1,0:T(8,128)(2,1)S(1)}, bf16[16,64,128]{2,1,0:T(8,128)(2,1)S(1)}, u32[]{:S(2)}, u32[]{:S(2)}) collective-permute-start(bf16[16,64,128]{2,1,0:T(8,128)(2,1)S(1)} %collective-permute-done), channel_id=1, source_target_pairs={{0,0},{1,8},{2,4},{3,12},{4,2},{5,10},{6,6},{7,14},{8,1},{9,9},{10... | collective-permute-start | bytes 786440 | tf_op jit(solution)/shard_map/ppermute | solution.py:59
  30.2 35.8 %collective-permute-start.2 = (bf16[16,64,128]{2,1,0:T(8,128)(2,1)S(1)}, bf16[16,64,128]{2,1,0:T(8,128)(2,1)S(1)}, u32[]{:S(2)}, u32[]{:S(2)}) collective-permute-start(bf16[16,64,128]{2,1,0:T(8,128)(2,1)S(1)} %collective-permute-done.1.refs_3_), channel_id=1, source_target_pairs={{0,32},{1,33},{2,34},{3,35},{4,36},{5,37},{6,38},{7,39},{8,40},{9,... | collective-permute-start | bytes 786440 | tf_op jit(solution)/shard_map/ppermute | solution.py:59
  47.8 20.4 %collective-permute-start.3 = (bf16[16,64,128]{2,1,0:T(8,128)(2,1)S(1)}, bf16[16,64,128]{2,1,0:T(8,128)(2,1)S(1)}, u32[]{:S(2)}, u32[]{:S(2)}) collective-permute-start(bf16[16,64,128]{2,1,0:T(8,128)(2,1)S(1)} %collective-permute-done.1.refs_3_), channel_id=1, source_target_pairs={{0,48},{1,49},{2,50},{3,51},{4,52},{5,53},{6,54},{7,55},{8,56},{9,... | collective-permute-start | bytes 786440 | tf_op jit(solution)/shard_map/ppermute | solution.py:59
  50.5 17.7 %collective-permute-start.4 = (bf16[16,64,128]{2,1,0:T(8,128)(2,1)S(1)}, bf16[16,64,128]{2,1,0:T(8,128)(2,1)S(1)}, u32[]{:S(2)}, u32[]{:S(2)}) collective-permute-start(bf16[16,64,128]{2,1,0:T(8,128)(2,1)S(1)} %collective-permute-done.1.refs_3_), channel_id=1, source_target_pairs={{0,16},{1,17},{2,18},{3,19},{4,20},{5,21},{6,22},{7,23},{8,24},{9,... | collective-permute-start | bytes 786440 | tf_op jit(solution)/shard_map/ppermute | solution.py:59
  53.7 14.6 %collective-permute-start.8 = (bf16[16,64,128]{2,1,0:T(8,128)(2,1)S(1)}, bf16[16,64,128]{2,1,0:T(8,128)(2,1)S(1)}, u32[]{:S(2)}, u32[]{:S(2)}) collective-permute-start(bf16[16,64,128]{2,1,0:T(8,128)(2,1)S(1)} %collective-permute-done.1.refs_3_), channel_id=1, source_target_pairs={{0,128},{1,129},{2,130},{3,131},{4,132},{5,133},{6,134},{7,135},{8... | collective-permute-start | bytes 786440 | tf_op jit(solution)/shard_map/ppermute | solution.py:59
  57.8 12.1 %collective-permute-start.9 = (bf16[16,64,128]{2,1,0:T(8,128)(2,1)S(1)}, bf16[16,64,128]{2,1,0:T(8,128)(2,1)S(1)}, u32[]{:S(2)}, u32[]{:S(2)}) collective-permute-start(bf16[16,64,128]{2,1,0:T(8,128)(2,1)S(1)} %collective-permute-done.1.refs_3_), channel_id=1, source_target_pairs={{0,64},{1,65},{2,66},{3,67},{4,68},{5,69},{6,70},{7,71},{8,72},{9,... | collective-permute-start | bytes 786440 | tf_op jit(solution)/shard_map/ppermute | solution.py:59
  66.0 9.5 %collective-permute-start.10 = (bf16[16,64,128]{2,1,0:T(8,128)(2,1)S(1)}, bf16[16,64,128]{2,1,0:T(8,128)(2,1)S(1)}, u32[]{:S(2)}, u32[]{:S(2)}) collective-permute-start(bf16[16,64,128]{2,1,0:T(8,128)(2,1)S(1)} %collective-permute-done.1.refs_3_), channel_id=1, source_target_pairs={{0,192},{1,193},{2,194},{3,195},{4,196},{5,197},{6,198},{7,199},{8... | collective-permute-start | bytes 786440 | tf_op jit(solution)/shard_map/ppermute | solution.py:59
  75.6 28.2 %collective-permute-start.11 = (bf16[64,64,128]{2,1,0:T(8,128)(2,1)S(1)}, bf16[64,64,128]{2,1,0:T(8,128)(2,1)S(1)}, u32[]{:S(2)}, u32[]{:S(2)}) collective-permute-start(bf16[64,64,128]{2,1,0:T(8,128)(2,1)S(1)} %pad_maximum_fusion), channel_id=1, source_target_pairs={{0,8},{1,9},{2,10},{3,11},{4,12},{5,13},{6,14},{7,15},{8,0},{9,1},... | collective-permute-start | bytes 3145736 | tf_op jit(solution)/shard_map/ppermute | solution.py:59
  77.6 15.1 %collective-permute-start.5 = (bf16[16,64,128]{2,1,0:T(8,128)(2,1)S(1)}, bf16[16,64,128]{2,1,0:T(8,128)(2,1)S(1)}, u32[]{:S(2)}, u32[]{:S(2)}) collective-permute-start(bf16[16,64,128]{2,1,0:T(8,128)(2,1)S(1)} %collective-permute-done.2), channel_id=1, source_target_pairs={{0,1},{1,66},{2,3},{3,196},{4,5},{5,70},{6,7},{7,384},{8,9},{9,74}... | collective-permute-start | bytes 786440 | tf_op jit(solution)/shard_map/ppermute | solution.py:59
  79.6 18.7 %collective-permute-start.6 = (bf16[16,64,128]{2,1,0:T(8,128)(2,1)S(1)}, bf16[16,64,128]{2,1,0:T(8,128)(2,1)S(1)}, u32[]{:S(2)}, u32[]{:S(2)}) collective-permute-start(bf16[16,64,128]{2,1,0:T(8,128)(2,1)S(1)} %collective-permute-done.3), channel_id=1, source_target_pairs={{0,1},{1,66},{2,3},{3,196},{4,5},{5,70},{6,7},{7,384},{8,9},{9,74}... | collective-permute-start | bytes 786440 | tf_op jit(solution)/shard_map/ppermute | solution.py:59
  81.6 22.2 %collective-permute-start.7 = (bf16[16,64,128]{2,1,0:T(8,128)(2,1)S(1)}, bf16[16,64,128]{2,1,0:T(8,128)(2,1)S(1)}, u32[]{:S(2)}, u32[]{:S(2)}) collective-permute-start(bf16[16,64,128]{2,1,0:T(8,128)(2,1)S(1)} %collective-permute-done.4), channel_id=1, source_target_pairs={{0,1},{1,66},{2,3},{3,196},{4,5},{5,70},{6,7},{7,384},{8,9},{9,74}... | collective-permute-start | bytes 786440 | tf_op jit(solution)/shard_map/ppermute | solution.py:59
  106.1 11.8 %collective-permute-start.12 = (bf16[16,64,128]{2,1,0:T(8,128)(2,1)S(1)}, bf16[16,64,128]{2,1,0:T(8,128)(2,1)S(1)}, u32[]{:S(2)}, u32[]{:S(2)}) collective-permute-start(bf16[16,64,128]{2,1,0:T(8,128)(2,1)S(1)} %shard_map.37.refs_3_), channel_id=1, source_target_pairs={{0,128},{1,129},{2,130},{3,131},{4,132},{5,133},{6,134},{7,135},{8... | collective-permute-start | bytes 786440 | tf_op jit(solution)/shard_map/ppermute | solution.py:59
  108.6 13.8 %collective-permute-start.13 = (bf16[16,64,128]{2,1,0:T(8,128)(2,1)S(1)}, bf16[16,64,128]{2,1,0:T(8,128)(2,1)S(1)}, u32[]{:S(2)}, u32[]{:S(2)}) collective-permute-start(bf16[16,64,128]{2,1,0:T(8,128)(2,1)S(1)} %shard_map.37.refs_3_), channel_id=1, source_target_pairs={{0,64},{1,65},{2,66},{3,67},{4,68},{5,69},{6,70},{7,71},{8,72},{9,... | collective-permute-start | bytes 786440 | tf_op jit(solution)/shard_map/ppermute | solution.py:59
  112.2 11.0 %collective-permute-start.14 = (bf16[16,64,128]{2,1,0:T(8,128)(2,1)S(1)}, bf16[16,64,128]{2,1,0:T(8,128)(2,1)S(1)}, u32[]{:S(2)}, u32[]{:S(2)}) collective-permute-start(bf16[16,64,128]{2,1,0:T(8,128)(2,1)S(1)} %shard_map.37.refs_3_), channel_id=1, source_target_pairs={{0,192},{1,193},{2,194},{3,195},{4,196},{5,197},{6,198},{7,199},{8... | collective-permute-start | bytes 786440 | tf_op jit(solution)/shard_map/ppermute | solution.py:59
  123.4 4.6 %collective-permute-start.15 = (bf16[64,64,128]{2,1,0:T(8,128)(2,1)S(1)}, bf16[64,64,128]{2,1,0:T(8,128)(2,1)S(1)}, u32[]{:S(2)}, u32[]{:S(2)}) collective-permute-start(bf16[64,64,128]{2,1,0:T(8,128)(2,1)S(1)} %pad_maximum_fusion.1), channel_id=1, source_target_pairs={{0,8},{1,9},{2,10},{3,11},{4,12},{5,13},{6,14},{7,15},{8,0},{9,1},... | collective-permute-start | bytes 3145736 | tf_op jit(solution)/shard_map/ppermute | solution.py:59
  130.2 16.4 %collective-permute-start.16 = (bf16[16,64,128]{2,1,0:T(8,128)(2,1)S(1)}, bf16[16,64,128]{2,1,0:T(8,128)(2,1)S(1)}, u32[]{:S(2)}, u32[]{:S(2)}) collective-permute-start(bf16[16,64,128]{2,1,0:T(8,128)(2,1)S(1)} %shard_map.38), channel_id=1, source_target_pairs={{0,0},{1,32},{2,68},{3,100},{4,130},{5,162},{6,198},{7,230},{8,1},... | collective-permute-start | bytes 786440 | tf_op jit(solution)/shard_map/ppermute | solution.py:59

commit v4 on v2

--- a/solution.py
+++ b/solution.py
@@ -9,26 +9,39 @@
 AXES = ("row", "col")
 PANELS = 64
 GROUPS = 8
-SPAN = 3
-TURN = ((0, 3, 1, 2), (1, 2, 0, 3), (2, 0, 3, 1), (3, 1, 2, 0))
+SPOTS = (
+    (2, 3, 0, 1), (1, 0, 3, 2), (3, 0, 1, 2), (1, 2, 3, 0),
+    (2, 1, 0, 3), (3, 1, 2, 0), (0, 2, 1, 3), (0, 3, 2, 1),
+)
 
 
 def device(half, x, y, core, z):
     return (((half * 4 + x) * 4 + y) * 2 + core) * GROUPS + z
 
 
+def spot(panel, group):
+    return SPOTS[group][panel // 8 % 4]
+
+
+def held_at(panel, x):
+    return [group for group in range(GROUPS) if spot(panel, group) == x % 4]
+
+
+def lane(panel, group):
+    return held_at(panel, spot(panel, group)).index(group)
+
+
 def start(panel, group):
     return panel * GROUPS + group
 
 
 def between(panel, group):
-    half, x, y, core = panel // 32, panel // 8 % 4, panel // 2 % 4, panel % 2
-    return device(half, TURN[x][group // 2], panel % 4, y // 2, group)
+    return device(panel // 32, spot(panel, group), panel % 4, panel // 4 % 2, group)
 
 
 def place(panel, group):
-    half, x = panel // 32, panel // 8 % 4
-    return device(half, TURN[x][group // 2], panel % 4, group % 2, panel // 4 % 8)
+    x = spot(panel, group)
+    return device(panel // 32, x, panel % 4, lane(panel, group), panel // 4 % 8)
 
 
 JOBS = [(panel, group) for panel in range(PANELS) for group in range(GROUPS)]
@@ -38,43 +51,63 @@
     return sorted((source(*job), target(*job)) for job in JOBS)
 
 
-def sideways(distance):
-    moves = []
-    for panel, group in JOBS:
-        x = (TURN[panel // 8 % 4][group // 2] - distance) % 4
-        other = TURN[panel // 8 % 4].index(x) * 2 + group % 2
-        moves.append((place(panel, other), place(panel, group)))
-    return sorted(moves)
+def beside(panel, group, distance):
+    return held_at(panel, spot(panel, group) - distance)[lane(panel, group)]
+
+
+def opposite(panel, group):
+    return held_at(panel, spot(panel, group))[1 - lane(panel, group)]
 
 
 def arrival(panel, group):
-    order = []
-    for core in (group % 2, 1 - group % 2):
-        for distance in (0, 1, -1, 2):
-            x = (TURN[panel // 8 % 4][group // 2] - distance) % 4
-            order.append(TURN[panel // 8 % 4].index(x) * 2 + core)
-    return order
-
-
-def send(value, moves):
-    return lax.ppermute(value, AXES, moves)
-
-
-def gather_row(part):
-    other = route(place, lambda panel, group: place(panel, group ^ 1))
-    near = [part] + [send(part, sideways(distance)) for distance in (1, -1, 2)]
-    return near + [send(piece, other) for piece in near]
-
-
-def gather_table(part):
-    panels = []
-    for offset in range(-SPAN, SPAN + 1):
-        if offset == 0:
-            panels.append(part)
-        else:
-            moves = route(lambda p, g: place((p + offset) % PANELS, g), place)
-            panels.append(send(part, moves))
-    return jnp.concatenate(panels, axis=0)
+    near = [beside(panel, group, distance) for distance in (0, 2, 1, -1)]
+    return near + [opposite(panel, other) for other in near]
+
+
+def column_panel(panel, distance):
+    return panel // 4 * 4 + (panel + distance) % 4
+
+
+def send(value, source):
+    return lax.ppermute(value, AXES, route(source, place))
+
+
+def gather_row(part, after=()):
+    near = [part]
+    for distance in (2, 1, -1):
+        near.append(send(part, lambda p, g: place(p, beside(p, g, distance))))
+    near = lax.optimization_barrier((near, after))[0]
+    far = send(jnp.concatenate(near, axis=0), lambda p, g: place(p, opposite(p, g)))
+    return near + jnp.split(far, len(near), axis=0)
+
+
+def gather_column(part):
+    return [
+        send(part, lambda p, g: place(column_panel(p, distance), g))
+        for distance in (2, 1, 3)
+    ]
+
+
+def gather_table(part, column, panel):
+    low = panel % 4 < 2
+    two, one, three = column
+    pair = jnp.concatenate([two, jnp.where(low, one, three)], axis=0)
+    rest = jnp.where(low, three, one)
+    pair = send(pair, lambda p, g: place((p + (-4 if p % 4 < 2 else 4)) % PANELS, g))
+    rest = send(rest, lambda p, g: place((p + (4 if p % 2 else -4)) % PANELS, g))
+    return jnp.concatenate([part, two, one, three, pair, rest], axis=0)
+
+
+def table_panel(owner, panel):
+    y = panel % 4
+    index = jnp.zeros_like(owner)
+    for slot, distance in enumerate((2, 1, 3)):
+        same = (y + distance) % 4 - y
+        index = jnp.where(owner == same, 1 + slot, index)
+        outer = jnp.where(same > 0, same - 4, same + 4)
+        swap = jnp.where(y < 2, 4 + slot, 7 - slot) if slot else 4
+        index = jnp.where(owner == outer, swap, index)
+    return index
 
 
 def product_kernel(count, group, keep, index_ref, mask_ref, table_ref, *refs):
@@ -131,8 +164,7 @@
     job = lax.dynamic_index_in_dim(jnp.array(jobs), here, 0, keepdims=False)
     panel, mine, order = job[0], job[1], job[2:]
 
-    part = send(density, route(start, between))
-    part = send(part, route(between, place))
+    part = lax.ppermute(density, AXES, route(start, between))
 
     base = panel * local_rows
     own = lax.dynamic_slice_in_dim(columns, base, local_rows, 0)
@@ -140,7 +172,9 @@
     own = jnp.take(own.reshape(local_rows, GROUPS, group), order, axis=1)
     own = own.reshape(local_rows, stored)
     distance = jnp.mod(own - base + total // 2, total) - total // 2
-    index = (distance + SPAN * local_rows).reshape(-1)
+    owner = jnp.floor_divide(distance, local_rows)
+    index = table_panel(owner, panel) * local_rows + distance - owner * local_rows
+    index = index.reshape(-1)
     held = lax.dynamic_slice_in_dim(columns, mine * group, group, 1)
     held = jnp.take(held, own.reshape(-1), axis=0).reshape(local_rows, stored, group)
     lane_slot = jnp.arange(lanes, dtype=jnp.int32) // width
@@ -150,11 +184,15 @@
     mask = jnp.concatenate([found == direct, found == swapped], axis=-1)
     mask = mask.astype(jnp.float32).reshape(local_rows * stored, 2 * lanes)
 
-    left = gather_row(part)
-    table = gather_table(part).reshape(-1, width, lanes)
+    part, index, mask = lax.optimization_barrier((part, index, mask))
+    part = send(part, between)
+
+    column = gather_column(part)
+    left = gather_row(part, column)
+    table = gather_table(part, column, panel).reshape(-1, width, lanes)
     square = product(index, mask, table, left, False)
     result = product(index, mask, table, gather_row(square), True)
-    return send(result, route(place, start)).astype(jnp.float32)
+    return lax.ppermute(result, AXES, route(place, start)).astype(jnp.float32)
 
 
 def solution(mesh):

time: 143 us -> 139 us (0.972)
  the two profiles are of different devices: /device:TPU:22 before, /device:TPU:4 now
where the time goes in v4:
time: 139 us; the launch traced here: 138 us
  starting transfers between devices  72.7 us (52%)
  waiting for transfers between devices  49.1 us (35%)
  local copies, waits for them, and re-layouts  6.7 us (5%)
  Pallas kernels  4.43 us (3%)
  between operations  3.59 us (3%)
  other arithmetic  1.93 us (1%)
    ppermute x14, starting transfers between devices, send(): return lax.ppermute(value, AXES, route(source, place))  62.3 us
    ppermute x14, waiting for transfers between devices, send(): return lax.ppermute(value, AXES, route(source, place))  32.1 us
    ppermute x1, waiting for transfers between devices, shards(): return lax.ppermute(result, AXES, route(place, start)).astype(jnp.float32)  16.9 us
    ppermute x1, starting transfers between devices, shards(): part = lax.ppermute(density, AXES, route(start, between))  7.78 us
    pallas_call x2, Pallas kernels, product(): pl.pallas_call(lambda *refs: product_kernel(count, lanes // width, keep,...  4.43 us
  transfers between devices with their start and end apart: 16, of which 8 were waited for; matrix products, arithmetic and copies ran while one was open for 5% of the time, Pallas kernels for 0%

profile of v4, /device:TPU:4, one launch (start us, length us, event | category | flops | bytes accessed | tf_op | source)
XLA Modules:
  0.0 138.4 jit_solution(17704939788214253033)
XLA Ops:
  0.0 7.8 %collective-permute-start = (bf16[16,64,128]{2,1,0:T(8,128)(2,1)}, bf16[16,64,128]{2,1,0:T(8,128)(2,1)S(1)}, u32[]{:S(2)}, u32[]{:S(2)}) collective-permute-start(bf16[16,64,128]{2,1,0:T(8,128)(2,1)} %param.3), channel_id=1, source_target_pairs={{0,128},{1,65},{2,194},{3,67},{4,132},{5,197},{6,6},{7,7},{8,144},... | collective-permute-start | bytes 786440 | tf_op jit(solution)/shard_map/ppermute | solution.py:167
  7.8 0.7 constant_dynamic-slice_fusion.2
  8.6 0.6 fusion.10
  10.7 0.8 constant_dynamic-slice_fusion.1
  11.5 0.8 constant_dynamic-slice_fusion
  12.2 0.8 dynamic_slice.16
  14.2 0.7 gather_fusion.1
  18.1 0.7 collective-permute-start.1
  18.8 1.9 %collective-permute-start.4 = (bf16[16,64,128]{2,1,0:T(8,128)(2,1)S(1)}, bf16[16,64,128]{2,1,0:T(8,128)(2,1)S(1)}, u32[]{:S(2)}, u32[]{:S(2)}) collective-permute-start(bf16[16,64,128]{2,1,0:T(8,128)(2,1)S(1)} %collective-permute-done.1.refs_3_), channel_id=1, source_target_pairs={{0,16},{1,17},{2,18},{3,19},{4,20},{5,21},{6,22},{7,23},{8,24},{9,... | collective-permute-start | bytes 786440 | tf_op jit(solution)/shard_map/ppermute | solution.py:72
  20.7 5.1 %collective-permute-start.3 = (bf16[16,64,128]{2,1,0:T(8,128)(2,1)S(1)}, bf16[16,64,128]{2,1,0:T(8,128)(2,1)S(1)}, u32[]{:S(2)}, u32[]{:S(2)}) collective-permute-start(bf16[16,64,128]{2,1,0:T(8,128)(2,1)S(1)} %collective-permute-done.1.refs_3_), channel_id=1, source_target_pairs={{0,48},{1,49},{2,50},{3,51},{4,52},{5,53},{6,54},{7,55},{8,56},{9,... | collective-permute-start | bytes 786440 | tf_op jit(solution)/shard_map/ppermute | solution.py:72
  25.9 1.9 %collective-permute-start.2 = (bf16[16,64,128]{2,1,0:T(8,128)(2,1)S(1)}, bf16[16,64,128]{2,1,0:T(8,128)(2,1)S(1)}, u32[]{:S(2)}, u32[]{:S(2)}) collective-permute-start(bf16[16,64,128]{2,1,0:T(8,128)(2,1)S(1)} %collective-permute-done.1.refs_3_), channel_id=1, source_target_pairs={{0,32},{1,33},{2,34},{3,35},{4,36},{5,37},{6,38},{7,39},{8,40},{9,... | collective-permute-start | bytes 786440 | tf_op jit(solution)/shard_map/ppermute | solution.py:72
  27.8 22.5 %collective-permute-start.7 = (bf16[16,64,128]{2,1,0:T(8,128)(2,1)S(1)}, bf16[16,64,128]{2,1,0:T(8,128)(2,1)S(1)}, u32[]{:S(2)}, u32[]{:S(2)}) collective-permute-start(bf16[16,64,128]{2,1,0:T(8,128)(2,1)S(1)} %collective-permute-done.1.refs_3_), channel_id=1, source_target_pairs={{0,128},{1,129},{2,130},{3,131},{4,132},{5,133},{6,134},{7,135},{8... | collective-permute-start | bytes 786440 | tf_op jit(solution)/shard_map/ppermute | solution.py:72
  50.3 1.9 %collective-permute-start.8 = (bf16[16,64,128]{2,1,0:T(8,128)(2,1)S(1)}, bf16[16,64,128]{2,1,0:T(8,128)(2,1)S(1)}, u32[]{:S(2)}, u32[]{:S(2)}) collective-permute-start(bf16[16,64,128]{2,1,0:T(8,128)(2,1)S(1)} %collective-permute-done.1.refs_3_), channel_id=1, source_target_pairs={{0,64},{1,65},{2,66},{3,67},{4,68},{5,69},{6,70},{7,71},{8,72},{9,... | collective-permute-start | bytes 786440 | tf_op jit(solution)/shard_map/ppermute | solution.py:72
  52.2 3.9 %collective-permute-start.9 = (bf16[16,64,128]{2,1,0:T(8,128)(2,1)S(1)}, bf16[16,64,128]{2,1,0:T(8,128)(2,1)S(1)}, u32[]{:S(2)}, u32[]{:S(2)}) collective-permute-start(bf16[16,64,128]{2,1,0:T(8,128)(2,1)S(1)} %collective-permute-done.1.refs_3_), channel_id=1, source_target_pairs={{0,192},{1,193},{2,194},{3,195},{4,196},{5,197},{6,198},{7,199},{8... | collective-permute-start | bytes 786440 | tf_op jit(solution)/shard_map/ppermute | solution.py:72
  56.2 4.0 %collective-permute-done.8.refs_5_ = bf16[16,64,128]{2,1,0:T(8,128)(2,1)S(1)} collective-permute-done((bf16[16,64,128]{2,1,0:T(8,128)(2,1)S(1)}, bf16[16,64,128]{2,1,0:T(8,128)(2,1)S(1)}, u32[]{:S(2)}, u32[]{:S(2)}) %collective-permute-start.8) | collective-permute-done | bytes 262176 | tf_op jit(solution)/shard_map/ppermute | solution.py:72
  60.6 1.9 %collective-permute-start.10 = (bf16[64,64,128]{2,1,0:T(8,128)(2,1)S(1)}, bf16[64,64,128]{2,1,0:T(8,128)(2,1)S(1)}, u32[]{:S(2)}, u32[]{:S(2)}) collective-permute-start(bf16[64,64,128]{2,1,0:T(8,128)(2,1)S(1)} %pad_maximum_fusion), channel_id=1, source_target_pairs={{0,8},{1,9},{2,10},{3,11},{4,12},{5,13},{6,14},{7,15},{8,0},{9,1},... | collective-permute-start | bytes 3145736 | tf_op jit(solution)/shard_map/ppermute | solution.py:72
  62.8 2.4 %collective-permute-start.5 = (bf16[32,64,128]{2,1,0:T(8,128)(2,1)S(1)}, bf16[32,64,128]{2,1,0:T(8,128)(2,1)S(1)}, u32[]{:S(2)}, u32[]{:S(2)}) collective-permute-start(bf16[32,64,128]{2,1,0:T(8,128)(2,1)S(1)} %pad_maximum_fusion.2), channel_id=1, source_target_pairs={{0,1},{1,138},{2,3},{3,196},{4,5},{5,70},{6,7},{7,328},{8,9},{9,20... | collective-permute-start | bytes 1572872 | tf_op jit(solution)/shard_map/ppermute | solution.py:72
  65.3 8.0 %collective-permute-start.6 = (bf16[16,64,128]{2,1,0:T(8,128)(2,1)S(1)}, bf16[16,64,128]{2,1,0:T(8,128)(2,1)S(1)}, u32[]{:S(2)}, u32[]{:S(2)}) collective-permute-start(bf16[16,64,128]{2,1,0:T(8,128)(2,1)S(1)} %get-tuple-element.35), channel_id=1, source_target_pairs={{0,1},{1,138},{2,3},{3,196},{4,5},{5,70},{6,7},{7,328},{8,9},{9,20... | collective-permute-start | bytes 786440 | tf_op jit(solution)/shard_map/ppermute | solution.py:72
  73.3 12.0 %collective-permute-done.5 = bf16[32,64,128]{2,1,0:T(8,128)(2,1)S(1)} collective-permute-done((bf16[32,64,128]{2,1,0:T(8,128)(2,1)S(1)}, bf16[32,64,128]{2,1,0:T(8,128)(2,1)S(1)}, u32[]{:S(2)}, u32[]{:S(2)}) %collective-permute-start.5) | collective-permute-done | bytes 524320 | tf_op jit(solution)/shard_map/ppermute | solution.py:72
  85.4 5.4 %collective-permute-done.6 = bf16[16,64,128]{2,1,0:T(8,128)(2,1)S(1)} collective-permute-done((bf16[16,64,128]{2,1,0:T(8,128)(2,1)S(1)}, bf16[16,64,128]{2,1,0:T(8,128)(2,1)S(1)}, u32[]{:S(2)}, u32[]{:S(2)}) %collective-permute-start.6) | collective-permute-done | bytes 262176 | tf_op jit(solution)/shard_map/ppermute | solution.py:72
  90.9 2.2 %shard_map.37.refs_3_ = bf16[16,64,128]{2,1,0:T(8,128)(2,1)S(1)} custom-call(s32[256]{0:T(256)S(1)} %fusion.3.refs_0_, f32[256,256]{1,0:T(8,128)S(1)} %add_convert_fusion.refs_1_, bf16[112,64,128]{2,1,0:T(8,128)(2,1)S(1)} %constant_dynamic-update-slice_fusion.refs_2_, bf16[16,64,128]{2,1,0:T(8,128)(2,1)S(1)} %collective-permute-done.1.refs_3_, ...), custom_call_target="tpu_custom_call" | custom-call | flops 536870912 | bytes 8388608 | tf_op jit(solution)/shard_map/pallas_call | solution.py:141
  93.1 4.2 %collective-permute-start.11 = (bf16[16,64,128]{2,1,0:T(8,128)(2,1)S(1)}, bf16[16,64,128]{2,1,0:T(8,128)(2,1)S(1)}, u32[]{:S(2)}, u32[]{:S(2)}) collective-permute-start(bf16[16,64,128]{2,1,0:T(8,128)(2,1)S(1)} %shard_map.37.refs_3_), channel_id=1, source_target_pairs={{0,128},{1,129},{2,130},{3,131},{4,132},{5,133},{6,134},{7,135},{8... | collective-permute-start | bytes 786440 | tf_op jit(solution)/shard_map/ppermute | solution.py:72
  97.3 2.7 %collective-permute-start.12 = (bf16[16,64,128]{2,1,0:T(8,128)(2,1)S(1)}, bf16[16,64,128]{2,1,0:T(8,128)(2,1)S(1)}, u32[]{:S(2)}, u32[]{:S(2)}) collective-permute-start(bf16[16,64,128]{2,1,0:T(8,128)(2,1)S(1)} %shard_map.37.refs_3_), channel_id=1, source_target_pairs={{0,64},{1,65},{2,66},{3,67},{4,68},{5,69},{6,70},{7,71},{8,72},{9,... | collective-permute-start | bytes 786440 | tf_op jit(solution)/shard_map/ppermute | solution.py:72
  100.0 3.2 %collective-permute-start.13 = (bf16[16,64,128]{2,1,0:T(8,128)(2,1)S(1)}, bf16[16,64,128]{2,1,0:T(8,128)(2,1)S(1)}, u32[]{:S(2)}, u32[]{:S(2)}) collective-permute-start(bf16[16,64,128]{2,1,0:T(8,128)(2,1)S(1)} %shard_map.37.refs_3_), channel_id=1, source_target_pairs={{0,192},{1,193},{2,194},{3,195},{4,196},{5,197},{6,198},{7,199},{8... | collective-permute-start | bytes 786440 | tf_op jit(solution)/shard_map/ppermute | solution.py:72
  103.2 2.6 %collective-permute-done.11.refs_4_ = bf16[16,64,128]{2,1,0:T(8,128)(2,1)S(1)} collective-permute-done((bf16[16,64,128]{2,1,0:T(8,128)(2,1)S(1)}, bf16[16,64,128]{2,1,0:T(8,128)(2,1)S(1)}, u32[]{:S(2)}, u32[]{:S(2)}) %collective-permute-start.11) | collective-permute-done | bytes 262176 | tf_op jit(solution)/shard_map/ppermute | solution.py:72
  105.7 5.3 %collective-permute-done.12.refs_5_ = bf16[16,64,128]{2,1,0:T(8,128)(2,1)S(1)} collective-permute-done((bf16[16,64,128]{2,1,0:T(8,128)(2,1)S(1)}, bf16[16,64,128]{2,1,0:T(8,128)(2,1)S(1)}, u32[]{:S(2)}, u32[]{:S(2)}) %collective-permute-start.12) | collective-permute-done | bytes 262176 | tf_op jit(solution)/shard_map/ppermute | solution.py:72
  111.2 1.9 %collective-permute-start.14 = (bf16[64,64,128]{2,1,0:T(8,128)(2,1)S(1)}, bf16[64,64,128]{2,1,0:T(8,128)(2,1)S(1)}, u32[]{:S(2)}, u32[]{:S(2)}) collective-permute-start(bf16[64,64,128]{2,1,0:T(8,128)(2,1)S(1)} %pad_maximum_fusion.1), channel_id=1, source_target_pairs={{0,8},{1,9},{2,10},{3,11},{4,12},{5,13},{6,14},{7,15},{8,0},{9,1},... | collective-permute-start | bytes 3145736 | tf_op jit(solution)/shard_map/ppermute | solution.py:72
  113.1 2.6 %collective-permute-done.14 = bf16[64,64,128]{2,1,0:T(8,128)(2,1)S(1)} collective-permute-done((bf16[64,64,128]{2,1,0:T(8,128)(2,1)S(1)}, bf16[64,64,128]{2,1,0:T(8,128)(2,1)S(1)}, u32[]{:S(2)}, u32[]{:S(2)}) %collective-permute-start.14) | collective-permute-done | bytes 1048608 | tf_op jit(solution)/shard_map/ppermute | solution.py:72
  115.8 2.2 %shard_map.38 = bf16[16,64,128]{2,1,0:T(8,128)(2,1)S(1)} custom-call(s32[256]{0:T(256)S(1)} %fusion.3.refs_0_, f32[256,256]{1,0:T(8,128)S(1)} %add_convert_fusion.refs_1_, bf16[112,64,128]{2,1,0:T(8,128)(2,1)S(1)} %constant_dynamic-update-slice_fusion.refs_2_, bf16[16,64,128]{2,1,0:T(8,128)(2,1)S(1)} %shard_map.37.refs_3_, ...), custom_call_target="tpu_custom_call" | custom-call | flops 536870912 | bytes 8388608 | tf_op jit(solution)/shard_map/pallas_call | solution.py:141
  118.0 2.6 %collective-permute-start.15 = (bf16[16,64,128]{2,1,0:T(8,128)(2,1)S(1)}, bf16[16,64,128]{2,1,0:T(8,128)(2,1)S(1)}, u32[]{:S(2)}, u32[]{:S(2)}) collective-permute-start(bf16[16,64,128]{2,1,0:T(8,128)(2,1)S(1)} %shard_map.38), channel_id=1, source_target_pairs={{0,6},{1,38},{2,65},{3,97},{4,128},{5,160},{6,195},{7,227},{8,7},{... | collective-permute-start | bytes 786440 | tf_op jit(solution)/shard_map/ppermute | solution.py:195
  120.6 16.9 %collective-permute-done.15 = bf16[16,64,128]{2,1,0:T(8,128)(2,1)S(1)} collective-permute-done((bf16[16,64,128]{2,1,0:T(8,128)(2,1)S(1)}, bf16[16,64,128]{2,1,0:T(8,128)(2,1)S(1)}, u32[]{:S(2)}, u32[]{:S(2)}) %collective-permute-start.15) | collective-permute-done | bytes 262176 | tf_op jit(solution)/shard_map/ppermute | solution.py:195
  137.6 0.8 convert_element_type.8
  (49 shorter events, 3.7 us)
Async XLA Ops:
  0.0 18.1 %collective-permute-start = (bf16[16,64,128]{2,1,0:T(8,128)(2,1)}, bf16[16,64,128]{2,1,0:T(8,128)(2,1)S(1)}, u32[]{:S(2)}, u32[]{:S(2)}) collective-permute-start(bf16[16,64,128]{2,1,0:T(8,128)(2,1)} %param.3), channel_id=1, source_target_pairs={{0,128},{1,65},{2,194},{3,67},{4,132},{5,197},{6,6},{7,7},{8,144},... | collective-permute-start | bytes 786440 | tf_op jit(solution)/shard_map/ppermute | solution.py:167
  18.1 0.7 collective-permute-start.1
  18.8 33.4 %collective-permute-start.4 = (bf16[16,64,128]{2,1,0:T(8,128)(2,1)S(1)}, bf16[16,64,128]{2,1,0:T(8,128)(2,1)S(1)}, u32[]{:S(2)}, u32[]{:S(2)}) collective-permute-start(bf16[16,64,128]{2,1,0:T(8,128)(2,1)S(1)} %collective-permute-done.1.refs_3_), channel_id=1, source_target_pairs={{0,16},{1,17},{2,18},{3,19},{4,20},{5,21},{6,22},{7,23},{8,24},{9,... | collective-permute-start | bytes 786440 | tf_op jit(solution)/shard_map/ppermute | solution.py:72
  20.7 35.5 %collective-permute-start.3 = (bf16[16,64,128]{2,1,0:T(8,128)(2,1)S(1)}, bf16[16,64,128]{2,1,0:T(8,128)(2,1)S(1)}, u32[]{:S(2)}, u32[]{:S(2)}) collective-permute-start(bf16[16,64,128]{2,1,0:T(8,128)(2,1)S(1)} %collective-permute-done.1.refs_3_), channel_id=1, source_target_pairs={{0,48},{1,49},{2,50},{3,51},{4,52},{5,53},{6,54},{7,55},{8,56},{9,... | collective-permute-start | bytes 786440 | tf_op jit(solution)/shard_map/ppermute | solution.py:72
  25.9 30.4 %collective-permute-start.2 = (bf16[16,64,128]{2,1,0:T(8,128)(2,1)S(1)}, bf16[16,64,128]{2,1,0:T(8,128)(2,1)S(1)}, u32[]{:S(2)}, u32[]{:S(2)}) collective-permute-start(bf16[16,64,128]{2,1,0:T(8,128)(2,1)S(1)} %collective-permute-done.1.refs_3_), channel_id=1, source_target_pairs={{0,32},{1,33},{2,34},{3,35},{4,36},{5,37},{6,38},{7,39},{8,40},{9,... | collective-permute-start | bytes 786440 | tf_op jit(solution)/shard_map/ppermute | solution.py:72
  27.8 28.4 %collective-permute-start.7 = (bf16[16,64,128]{2,1,0:T(8,128)(2,1)S(1)}, bf16[16,64,128]{2,1,0:T(8,128)(2,1)S(1)}, u32[]{:S(2)}, u32[]{:S(2)}) collective-permute-start(bf16[16,64,128]{2,1,0:T(8,128)(2,1)S(1)} %collective-permute-done.1.refs_3_), channel_id=1, source_target_pairs={{0,128},{1,129},{2,130},{3,131},{4,132},{5,133},{6,134},{7,135},{8... | collective-permute-start | bytes 786440 | tf_op jit(solution)/shard_map/ppermute | solution.py:72
  50.3 10.0 %collective-permute-start.8 = (bf16[16,64,128]{2,1,0:T(8,128)(2,1)S(1)}, bf16[16,64,128]{2,1,0:T(8,128)(2,1)S(1)}, u32[]{:S(2)}, u32[]{:S(2)}) collective-permute-start(bf16[16,64,128]{2,1,0:T(8,128)(2,1)S(1)} %collective-permute-done.1.refs_3_), channel_id=1, source_target_pairs={{0,64},{1,65},{2,66},{3,67},{4,68},{5,69},{6,70},{7,71},{8,72},{9,... | collective-permute-start | bytes 786440 | tf_op jit(solution)/shard_map/ppermute | solution.py:72
  52.2 8.3 %collective-permute-start.9 = (bf16[16,64,128]{2,1,0:T(8,128)(2,1)S(1)}, bf16[16,64,128]{2,1,0:T(8,128)(2,1)S(1)}, u32[]{:S(2)}, u32[]{:S(2)}) collective-permute-start(bf16[16,64,128]{2,1,0:T(8,128)(2,1)S(1)} %collective-permute-done.1.refs_3_), channel_id=1, source_target_pairs={{0,192},{1,193},{2,194},{3,195},{4,196},{5,197},{6,198},{7,199},{8... | collective-permute-start | bytes 786440 | tf_op jit(solution)/shard_map/ppermute | solution.py:72
  60.6 30.2 %collective-permute-start.10 = (bf16[64,64,128]{2,1,0:T(8,128)(2,1)S(1)}, bf16[64,64,128]{2,1,0:T(8,128)(2,1)S(1)}, u32[]{:S(2)}, u32[]{:S(2)}) collective-permute-start(bf16[64,64,128]{2,1,0:T(8,128)(2,1)S(1)} %pad_maximum_fusion), channel_id=1, source_target_pairs={{0,8},{1,9},{2,10},{3,11},{4,12},{5,13},{6,14},{7,15},{8,0},{9,1},... | collective-permute-start | bytes 3145736 | tf_op jit(solution)/shard_map/ppermute | solution.py:72
  62.8 22.5 %collective-permute-start.5 = (bf16[32,64,128]{2,1,0:T(8,128)(2,1)S(1)}, bf16[32,64,128]{2,1,0:T(8,128)(2,1)S(1)}, u32[]{:S(2)}, u32[]{:S(2)}) collective-permute-start(bf16[32,64,128]{2,1,0:T(8,128)(2,1)S(1)} %pad_maximum_fusion.2), channel_id=1, source_target_pairs={{0,1},{1,138},{2,3},{3,196},{4,5},{5,70},{6,7},{7,328},{8,9},{9,20... | collective-permute-start | bytes 1572872 | tf_op jit(solution)/shard_map/ppermute | solution.py:72
  65.3 25.5 %collective-permute-start.6 = (bf16[16,64,128]{2,1,0:T(8,128)(2,1)S(1)}, bf16[16,64,128]{2,1,0:T(8,128)(2,1)S(1)}, u32[]{:S(2)}, u32[]{:S(2)}) collective-permute-start(bf16[16,64,128]{2,1,0:T(8,128)(2,1)S(1)} %get-tuple-element.35), channel_id=1, source_target_pairs={{0,1},{1,138},{2,3},{3,196},{4,5},{5,70},{6,7},{7,328},{8,9},{9,20... | collective-permute-start | bytes 786440 | tf_op jit(solution)/shard_map/ppermute | solution.py:72
  93.1 12.6 %collective-permute-start.11 = (bf16[16,64,128]{2,1,0:T(8,128)(2,1)S(1)}, bf16[16,64,128]{2,1,0:T(8,128)(2,1)S(1)}, u32[]{:S(2)}, u32[]{:S(2)}) collective-permute-start(bf16[16,64,128]{2,1,0:T(8,128)(2,1)S(1)} %shard_map.37.refs_3_), channel_id=1, source_target_pairs={{0,128},{1,129},{2,130},{3,131},{4,132},{5,133},{6,134},{7,135},{8... | collective-permute-start | bytes 786440 | tf_op jit(solution)/shard_map/ppermute | solution.py:72
  97.3 13.7 %collective-permute-start.12 = (bf16[16,64,128]{2,1,0:T(8,128)(2,1)S(1)}, bf16[16,64,128]{2,1,0:T(8,128)(2,1)S(1)}, u32[]{:S(2)}, u32[]{:S(2)}) collective-permute-start(bf16[16,64,128]{2,1,0:T(8,128)(2,1)S(1)} %shard_map.37.refs_3_), channel_id=1, source_target_pairs={{0,64},{1,65},{2,66},{3,67},{4,68},{5,69},{6,70},{7,71},{8,72},{9,... | collective-permute-start | bytes 786440 | tf_op jit(solution)/shard_map/ppermute | solution.py:72
  100.0 11.0 %collective-permute-start.13 = (bf16[16,64,128]{2,1,0:T(8,128)(2,1)S(1)}, bf16[16,64,128]{2,1,0:T(8,128)(2,1)S(1)}, u32[]{:S(2)}, u32[]{:S(2)}) collective-permute-start(bf16[16,64,128]{2,1,0:T(8,128)(2,1)S(1)} %shard_map.37.refs_3_), channel_id=1, source_target_pairs={{0,192},{1,193},{2,194},{3,195},{4,196},{5,197},{6,198},{7,199},{8... | collective-permute-start | bytes 786440 | tf_op jit(solution)/shard_map/ppermute | solution.py:72
  111.2 4.6 %collective-permute-start.14 = (bf16[64,64,128]{2,1,0:T(8,128)(2,1)S(1)}, bf16[64,64,128]{2,1,0:T(8,128)(2,1)S(1)}, u32[]{:S(2)}, u32[]{:S(2)}) collective-permute-start(bf16[64,64,128]{2,1,0:T(8,128)(2,1)S(1)} %pad_maximum_fusion.1), channel_id=1, source_target_pairs={{0,8},{1,9},{2,10},{3,11},{4,12},{5,13},{6,14},{7,15},{8,0},{9,1},... | collective-permute-start | bytes 3145736 | tf_op jit(solution)/shard_map/ppermute | solution.py:72
  118.0 19.6 %collective-permute-start.15 = (bf16[16,64,128]{2,1,0:T(8,128)(2,1)S(1)}, bf16[16,64,128]{2,1,0:T(8,128)(2,1)S(1)}, u32[]{:S(2)}, u32[]{:S(2)}) collective-permute-start(bf16[16,64,128]{2,1,0:T(8,128)(2,1)S(1)} %shard_map.38), channel_id=1, source_target_pairs={{0,6},{1,38},{2,65},{3,97},{4,128},{5,160},{6,195},{7,227},{8,7},{... | collective-permute-start | bytes 786440 | tf_op jit(solution)/shard_map/ppermute | solution.py:195

commit v5 on v4

--- a/solution.py
+++ b/solution.py
@@ -59,6 +59,10 @@
     return held_at(panel, spot(panel, group))[1 - lane(panel, group)]
 
 
+def plane_order(panel, group):
+    return [group for x in range(4) for group in held_at(panel, x)]
+
+
 def arrival(panel, group):
     near = [beside(panel, group, distance) for distance in (0, 2, 1, -1)]
     return near + [opposite(panel, other) for other in near]
@@ -72,11 +76,19 @@
     return lax.ppermute(value, AXES, route(source, place))
 
 
-def gather_row(part, after=()):
+def gather_plane(part):
+    planes = [
+        [device(half, x, y, core, 0) // GROUPS for x in range(4) for core in range(2)]
+        for half in range(2)
+        for y in range(4)
+    ]
+    return lax.all_gather(part, "row", axis=0, tiled=True, axis_index_groups=planes)
+
+
+def gather_row(part):
     near = [part]
     for distance in (2, 1, -1):
         near.append(send(part, lambda p, g: place(p, beside(p, g, distance))))
-    near = lax.optimization_barrier((near, after))[0]
     far = send(jnp.concatenate(near, axis=0), lambda p, g: place(p, opposite(p, g)))
     return near + jnp.split(far, len(near), axis=0)
 
@@ -111,9 +123,9 @@
 
 
 def product_kernel(count, group, keep, index_ref, mask_ref, table_ref, *refs):
-    chunks = refs[:count]
     out_ref = refs[-1]
-    rows, width, lanes = chunks[0].shape
+    rows, width, lanes = out_ref.shape
+    chunks = [ref.at[pl.ds(j, rows)] for ref in refs[:-1] for j in range(0, ref.shape[0], rows)]
     blocks = count * group
     for i in range(rows):
         total = None
@@ -134,14 +146,14 @@
         out_ref[i] = value.astype(out_ref.dtype)
 
 
-def product(index, mask, table, chunks, keep):
-    count = len(chunks)
-    rows, width, lanes = chunks[0].shape
+def product(index, mask, table, chunks, rows, keep):
+    width, lanes = table.shape[1:]
+    count = sum(chunk.shape[0] for chunk in chunks) // rows
     vmem = pl.BlockSpec(memory_space=pltpu.VMEM)
     return pl.pallas_call(
         lambda *refs: product_kernel(count, lanes // width, keep, *refs),
-        out_shape=jax.ShapeDtypeStruct(chunks[0].shape, jnp.bfloat16),
-        in_specs=[pl.BlockSpec(memory_space=pltpu.SMEM)] + [vmem] * (2 + count),
+        out_shape=jax.ShapeDtypeStruct((rows, width, lanes), jnp.bfloat16),
+        in_specs=[pl.BlockSpec(memory_space=pltpu.SMEM)] + [vmem] * (2 + len(chunks)),
         out_specs=vmem,
         compiler_params=pltpu.CompilerParams(vmem_limit_bytes=24 * 1024 * 1024),
         cost_estimate=pl.CostEstimate(
@@ -157,41 +169,41 @@
     group = lanes // width
     total, stored = columns.shape
 
-    jobs = np.zeros((PANELS * GROUPS, 2 + GROUPS), np.int32)
+    jobs = np.zeros((PANELS * GROUPS, 2 + 2 * GROUPS), np.int32)
     for job in JOBS:
-        jobs[place(*job)] = [*job, *arrival(*job)]
+        jobs[place(*job)] = [*job, *plane_order(*job), *arrival(*job)]
     here = lax.axis_index("row") * GROUPS + lax.axis_index("col")
     job = lax.dynamic_index_in_dim(jnp.array(jobs), here, 0, keepdims=False)
-    panel, mine, order = job[0], job[1], job[2:]
+    panel, mine = job[0], job[1]
 
     part = lax.ppermute(density, AXES, route(start, between))
 
     base = panel * local_rows
     own = lax.dynamic_slice_in_dim(columns, base, local_rows, 0)
     goal = lax.dynamic_slice_in_dim(own, mine * group, group, 1)
-    own = jnp.take(own.reshape(local_rows, GROUPS, group), order, axis=1)
-    own = own.reshape(local_rows, stored)
+    orders = job[2:].reshape(2, GROUPS)
+    own = jnp.take(own.reshape(local_rows, GROUPS, group), orders, axis=1)
+    own = own.swapaxes(0, 1).reshape(2, local_rows, stored)
     distance = jnp.mod(own - base + total // 2, total) - total // 2
     owner = jnp.floor_divide(distance, local_rows)
     index = table_panel(owner, panel) * local_rows + distance - owner * local_rows
-    index = index.reshape(-1)
+    index = index.reshape(2, -1)
     held = lax.dynamic_slice_in_dim(columns, mine * group, group, 1)
-    held = jnp.take(held, own.reshape(-1), axis=0).reshape(local_rows, stored, group)
+    held = jnp.take(held, own.reshape(-1), axis=0).reshape(2, local_rows, stored, group)
     lane_slot = jnp.arange(lanes, dtype=jnp.int32) // width
     found = jnp.where(lane_slot == 0, held[..., :1], held[..., 1:])
     direct = jnp.where(lane_slot == 0, goal[:, None, :1], goal[:, None, 1:])
     swapped = jnp.where(lane_slot == 0, goal[:, None, 1:], goal[:, None, :1])
     mask = jnp.concatenate([found == direct, found == swapped], axis=-1)
-    mask = mask.astype(jnp.float32).reshape(local_rows * stored, 2 * lanes)
-
+    mask = mask.astype(jnp.float32).reshape(2, local_rows * stored, 2 * lanes)
     part, index, mask = lax.optimization_barrier((part, index, mask))
     part = send(part, between)
 
-    column = gather_column(part)
-    left = gather_row(part, column)
-    table = gather_table(part, column, panel).reshape(-1, width, lanes)
-    square = product(index, mask, table, left, False)
-    result = product(index, mask, table, gather_row(square), True)
+    left = gather_plane(part)
+    table = gather_table(part, gather_column(part), panel).reshape(-1, width, lanes)
+    square = product(index[0], mask[0], table, [left], local_rows, False)
+    left = gather_row(square)
+    result = product(index[1], mask[1], table, left, local_rows, True)
     return lax.ppermute(result, AXES, route(place, start)).astype(jnp.float32)
 
 

time: 139 us -> 145 us (1.043)
  starting transfers between devices: 72.7 us -> 54.3 us
  between operations: 3.59 us -> 17.2 us
  waiting for transfers between devices: 49.1 us -> 56.6 us
  local copies, waits for them, and re-layouts: 6.7 us -> 10.5 us
    ppermute x14 -> x10, starting transfers between devices: 62.3 us -> 44.6 us  [send(): return lax.ppermute(value, AXES, route(source, place))]
    unnamed x5 -> x9, local copies, waits for them, and re-layouts: 0.38 us -> 3.63 us
    all_gather x0 -> x1, waiting for transfers between devices: none -> 2.89 us  [gather_plane(): lax.all_gather(part, 'row', axis=0, tiled=True, axis_index_groups=planes)]
    ppermute x1, waiting for transfers between devices: 16.9 us -> 19.6 us  [shards(): return lax.ppermute(result, AXES, route(place, start)).astype(jnp.float32)]
    ppermute x14 -> x10, waiting for transfers between devices: 32.1 us -> 34.1 us  [send(): return lax.ppermute(value, AXES, route(source, place))]
  transfers between devices with their start and end apart: 16 -> 13, of which waited for: 8 -> 11; matrix products, arithmetic and copies ran while one was open for 5% -> 6% of each run, Pallas kernels for 0% -> 0%
where the time goes in v5:
time: 145 us
  waiting for transfers between devices  56.6 us (39%)
  starting transfers between devices  54.3 us (37%)
  between operations  17.2 us (12%)
  local copies, waits for them, and re-layouts  10.5 us (7%)
  Pallas kernels  4.39 us (3%)
  other arithmetic  1.72 us (1%)
    ppermute x10, starting transfers between devices, send(): return lax.ppermute(value, AXES, route(source, place))  44.6 us
    ppermute x10, waiting for transfers between devices, send(): return lax.ppermute(value, AXES, route(source, place))  34.1 us
    ppermute x1, waiting for transfers between devices, shards(): return lax.ppermute(result, AXES, route(place, start)).astype(jnp.float32)  19.6 us
    ppermute x1, starting transfers between devices, shards(): part = lax.ppermute(density, AXES, route(start, between))  7.78 us
    pallas_call x2, Pallas kernels, product(): pl.pallas_call(lambda *refs: product_kernel(count, lanes // width, keep,...  4.39 us
    unnamed x9, local copies, waits for them, and re-layouts  3.63 us
  transfers between devices with their start and end apart: 13, of which 11 were waited for; matrix products, arithmetic and copies ran while one was open for 6% of the time, Pallas kernels for 0%

profile of v5, /device:TPU:4, one launch (start us, length us, event | category | flops | bytes accessed | tf_op | source)
XLA Modules:
  0.0 144.8 jit_solution(1913976455576098506)
XLA Ops:
  6.5 7.8 %collective-permute-start = (bf16[16,64,128]{2,1,0:T(8,128)(2,1)}, bf16[16,64,128]{2,1,0:T(8,128)(2,1)S(1)}, u32[]{:S(2)}, u32[]{:S(2)}) collective-permute-start(bf16[16,64,128]{2,1,0:T(8,128)(2,1)} %param.3), channel_id=1, source_target_pairs={{0,128},{1,65},{2,194},{3,67},{4,132},{5,197},{6,6},{7,7},{8,144},... | collective-permute-start | bytes 786440 | tf_op jit(solution)/shard_map/ppermute | solution.py:179
  14.3 0.7 constant_dynamic-slice_fusion.2
  17.3 0.8 constant_dynamic-slice_fusion.1
  19.1 0.8 constant_dynamic-slice_fusion
  20.1 1.0 gather_fusion.1
  21.8 0.8 dynamic_slice.16
  26.1 0.7 copy-done.1
  26.9 1.9 %collective-permute-start.2 = (bf16[16,64,128]{2,1,0:T(8,128)(2,1)}, bf16[16,64,128]{2,1,0:T(8,128)(2,1)S(1)}, u32[]{:S(2)}, u32[]{:S(2)}) collective-permute-start(bf16[16,64,128]{2,1,0:T(8,128)(2,1)} %copy-done.1), channel_id=1, source_target_pairs={{0,32},{1,33},{2,34},{3,35},{4,36},{5,37},{6,38},{7,39},{8,40},{9,... | collective-permute-start | bytes 786440 | tf_op jit(solution)/shard_map/ppermute | solution.py:76
  28.8 1.9 %collective-permute-start.3 = (bf16[16,64,128]{2,1,0:T(8,128)(2,1)}, bf16[16,64,128]{2,1,0:T(8,128)(2,1)S(1)}, u32[]{:S(2)}, u32[]{:S(2)}) collective-permute-start(bf16[16,64,128]{2,1,0:T(8,128)(2,1)} %copy-done.1), channel_id=1, source_target_pairs={{0,48},{1,49},{2,50},{3,51},{4,52},{5,53},{6,54},{7,55},{8,56},{9,... | collective-permute-start | bytes 786440 | tf_op jit(solution)/shard_map/ppermute | solution.py:76
  30.7 3.9 %collective-permute-start.4 = (bf16[16,64,128]{2,1,0:T(8,128)(2,1)}, bf16[16,64,128]{2,1,0:T(8,128)(2,1)S(1)}, u32[]{:S(2)}, u32[]{:S(2)}) collective-permute-start(bf16[16,64,128]{2,1,0:T(8,128)(2,1)} %copy-done.1), channel_id=1, source_target_pairs={{0,16},{1,17},{2,18},{3,19},{4,20},{5,21},{6,22},{7,23},{8,24},{9,... | collective-permute-start | bytes 786440 | tf_op jit(solution)/shard_map/ppermute | solution.py:76
  34.6 1.0 constant_dynamic-update-slice_fusion.5
  35.6 1.2 collective-permute-done.2
  37.3 4.0 %collective-permute-done.4 = bf16[16,64,128]{2,1,0:T(8,128)(2,1)S(1)} collective-permute-done((bf16[16,64,128]{2,1,0:T(8,128)(2,1)}, bf16[16,64,128]{2,1,0:T(8,128)(2,1)S(1)}, u32[]{:S(2)}, u32[]{:S(2)}) %collective-permute-start.4) | collective-permute-done | bytes 262176 | tf_op jit(solution)/shard_map/ppermute | solution.py:76
  41.5 20.8 %collective-permute-start.5 = (bf16[32,64,128]{2,1,0:T(8,128)(2,1)S(1)}, bf16[32,64,128]{2,1,0:T(8,128)(2,1)S(1)}, u32[]{:S(2)}, u32[]{:S(2)}) collective-permute-start(bf16[32,64,128]{2,1,0:T(8,128)(2,1)S(1)} %pad_maximum_fusion.1), channel_id=1, source_target_pairs={{0,1},{1,138},{2,3},{3,196},{4,5},{5,70},{6,7},{7,328},{8,9},{9,20... | collective-permute-start | bytes 1572872 | tf_op jit(solution)/shard_map/ppermute | solution.py:76
  62.3 1.9 %collective-permute-start.6 = (bf16[16,64,128]{2,1,0:T(8,128)(2,1)S(1)}, bf16[16,64,128]{2,1,0:T(8,128)(2,1)S(1)}, u32[]{:S(2)}, u32[]{:S(2)}) collective-permute-start(bf16[16,64,128]{2,1,0:T(8,128)(2,1)S(1)} %get-tuple-element.19), channel_id=1, source_target_pairs={{0,1},{1,138},{2,3},{3,196},{4,5},{5,70},{6,7},{7,328},{8,9},{9,20... | collective-permute-start | bytes 786440 | tf_op jit(solution)/shard_map/ppermute | solution.py:76
  64.3 15.0 %collective-permute-done.5 = bf16[32,64,128]{2,1,0:T(8,128)(2,1)S(1)} collective-permute-done((bf16[32,64,128]{2,1,0:T(8,128)(2,1)S(1)}, bf16[32,64,128]{2,1,0:T(8,128)(2,1)S(1)}, u32[]{:S(2)}, u32[]{:S(2)}) %collective-permute-start.5) | collective-permute-done | bytes 524320 | tf_op jit(solution)/shard_map/ppermute | solution.py:76
  79.3 2.7 %collective-permute-done.6 = bf16[16,64,128]{2,1,0:T(8,128)(2,1)S(1)} collective-permute-done((bf16[16,64,128]{2,1,0:T(8,128)(2,1)S(1)}, bf16[16,64,128]{2,1,0:T(8,128)(2,1)S(1)}, u32[]{:S(2)}, u32[]{:S(2)}) %collective-permute-start.6) | collective-permute-done | bytes 262176 | tf_op jit(solution)/shard_map/ppermute | solution.py:76
  82.1 2.9 %all-gather.2.cloned.1.call-done.refs_3_ = bf16[128,64,128]{2,1,0:T(8,128)(2,1)} async-done(((bf16[16,64,128]{2,1,0:T(8,128)(2,1)}), bf16[128,64,128]{2,1,0:T(8,128)(2,1)}) %all-gather.2.cloned.1.call-update) | async-done | bytes 2097168 | tf_op jit(solution)/shard_map/all_gather | solution.py:85
  85.0 1.6 %copy-done = bf16[128,64,128]{2,1,0:T(8,128)(2,1)S(1)} copy-done((bf16[128,64,128]{2,1,0:T(8,128)(2,1)S(1)}, bf16[128,64,128]{2,1,0:T(8,128)(2,1)}, u32[]{:S(2)}) %copy-start) | copy-done | bytes 2097176
  86.6 2.2 %shard_map.37.refs_3_ = bf16[16,64,128]{2,1,0:T(8,128)(2,1)S(1)} custom-call(s32[256]{0:T(256)S(1)} %bitcast.43, f32[256,256]{1,0:T(8,128)S(1)} %get-tuple-element.17.refs_1_, bf16[112,64,128]{2,1,0:T(8,128)(2,1)S(1)} %constant_dynamic-update-slice_fusion.refs_2_, bf16[128,64,128]{2,1,0:T(8,128)(2,1)S(1)} %copy-done), custom_call_target="tpu_custom_call" | custom-call | flops 536870912 | bytes 8388608 | tf_op jit(solution)/shard_map/pallas_call | solution.py:153
  88.8 4.6 %collective-permute-start.7 = (bf16[16,64,128]{2,1,0:T(8,128)(2,1)S(1)}, bf16[16,64,128]{2,1,0:T(8,128)(2,1)S(1)}, u32[]{:S(2)}, u32[]{:S(2)}) collective-permute-start(bf16[16,64,128]{2,1,0:T(8,128)(2,1)S(1)} %shard_map.37.refs_3_), channel_id=1, source_target_pairs={{0,128},{1,129},{2,130},{3,131},{4,132},{5,133},{6,134},{7,135},{8... | collective-permute-start | bytes 786440 | tf_op jit(solution)/shard_map/ppermute | solution.py:76
  93.4 5.0 %collective-permute-start.8 = (bf16[16,64,128]{2,1,0:T(8,128)(2,1)S(1)}, bf16[16,64,128]{2,1,0:T(8,128)(2,1)S(1)}, u32[]{:S(2)}, u32[]{:S(2)}) collective-permute-start(bf16[16,64,128]{2,1,0:T(8,128)(2,1)S(1)} %shard_map.37.refs_3_), channel_id=1, source_target_pairs={{0,64},{1,65},{2,66},{3,67},{4,68},{5,69},{6,70},{7,71},{8,72},{9,... | collective-permute-start | bytes 786440 | tf_op jit(solution)/shard_map/ppermute | solution.py:76
  98.4 1.9 %collective-permute-start.9 = (bf16[16,64,128]{2,1,0:T(8,128)(2,1)S(1)}, bf16[16,64,128]{2,1,0:T(8,128)(2,1)S(1)}, u32[]{:S(2)}, u32[]{:S(2)}) collective-permute-start(bf16[16,64,128]{2,1,0:T(8,128)(2,1)S(1)} %shard_map.37.refs_3_), channel_id=1, source_target_pairs={{0,192},{1,193},{2,194},{3,195},{4,196},{5,197},{6,198},{7,199},{8... | collective-permute-start | bytes 786440 | tf_op jit(solution)/shard_map/ppermute | solution.py:76
  100.4 1.0 collective-permute-done.7.refs_4_
  101.4 4.9 %collective-permute-done.8.refs_5_ = bf16[16,64,128]{2,1,0:T(8,128)(2,1)S(1)} collective-permute-done((bf16[16,64,128]{2,1,0:T(8,128)(2,1)S(1)}, bf16[16,64,128]{2,1,0:T(8,128)(2,1)S(1)}, u32[]{:S(2)}, u32[]{:S(2)}) %collective-permute-start.8) | collective-permute-done | bytes 262176 | tf_op jit(solution)/shard_map/ppermute | solution.py:76
  106.3 2.3 %collective-permute-done.9.refs_6_ = bf16[16,64,128]{2,1,0:T(8,128)(2,1)S(1)} collective-permute-done((bf16[16,64,128]{2,1,0:T(8,128)(2,1)S(1)}, bf16[16,64,128]{2,1,0:T(8,128)(2,1)S(1)}, u32[]{:S(2)}, u32[]{:S(2)}) %collective-permute-start.9) | collective-permute-done | bytes 262176 | tf_op jit(solution)/shard_map/ppermute | solution.py:76
  108.7 1.9 %collective-permute-start.10 = (bf16[64,64,128]{2,1,0:T(8,128)(2,1)S(1)}, bf16[64,64,128]{2,1,0:T(8,128)(2,1)S(1)}, u32[]{:S(2)}, u32[]{:S(2)}) collective-permute-start(bf16[64,64,128]{2,1,0:T(8,128)(2,1)S(1)} %pad_maximum_fusion), channel_id=1, source_target_pairs={{0,8},{1,9},{2,10},{3,11},{4,12},{5,13},{6,14},{7,15},{8,0},{9,1},... | collective-permute-start | bytes 3145736 | tf_op jit(solution)/shard_map/ppermute | solution.py:76
  110.6 2.6 %collective-permute-done.10 = bf16[64,64,128]{2,1,0:T(8,128)(2,1)S(1)} collective-permute-done((bf16[64,64,128]{2,1,0:T(8,128)(2,1)S(1)}, bf16[64,64,128]{2,1,0:T(8,128)(2,1)S(1)}, u32[]{:S(2)}, u32[]{:S(2)}) %collective-permute-start.10) | collective-permute-done | bytes 1048608 | tf_op jit(solution)/shard_map/ppermute | solution.py:76
  113.3 2.2 %shard_map.38 = bf16[16,64,128]{2,1,0:T(8,128)(2,1)S(1)} custom-call(s32[256]{0:T(256)S(1)} %bitcast.42, f32[256,256]{1,0:T(8,128)S(1)} %get-tuple-element.18.refs_1_, bf16[112,64,128]{2,1,0:T(8,128)(2,1)S(1)} %constant_dynamic-update-slice_fusion.refs_2_, bf16[16,64,128]{2,1,0:T(8,128)(2,1)S(1)} %shard_map.37.refs_3_, ...), custom_call_target="tpu_custom_call" | custom-call | flops 536870912 | bytes 8388608 | tf_op jit(solution)/shard_map/pallas_call | solution.py:153
  115.5 1.9 %collective-permute-start.11 = (bf16[16,64,128]{2,1,0:T(8,128)(2,1)S(1)}, bf16[16,64,128]{2,1,0:T(8,128)(2,1)S(1)}, u32[]{:S(2)}, u32[]{:S(2)}) collective-permute-start(bf16[16,64,128]{2,1,0:T(8,128)(2,1)S(1)} %shard_map.38), channel_id=1, source_target_pairs={{0,6},{1,38},{2,65},{3,97},{4,128},{5,160},{6,195},{7,227},{8,7},{... | collective-permute-start | bytes 786440 | tf_op jit(solution)/shard_map/ppermute | solution.py:207
  117.5 19.6 %collective-permute-done.11 = bf16[16,64,128]{2,1,0:T(8,128)(2,1)S(1)} collective-permute-done((bf16[16,64,128]{2,1,0:T(8,128)(2,1)S(1)}, bf16[16,64,128]{2,1,0:T(8,128)(2,1)S(1)}, u32[]{:S(2)}, u32[]{:S(2)}) %collective-permute-start.11) | collective-permute-done | bytes 262176 | tf_op jit(solution)/shard_map/ppermute | solution.py:207
  137.1 0.8 convert_element_type.8
  (51 shorter events, 5.2 us)
Async XLA Ops:
  6.5 78.5 %all-gather.2.cloned.1.call-start = ((), (), s32[]{:S(2)}) async-start(), calls=%async_computation | async-start | bytes 2359296 | tf_op jit(solution)/shard_map/all_gather | solution.py:85
  6.5 18.9 %collective-permute-start = (bf16[16,64,128]{2,1,0:T(8,128)(2,1)}, bf16[16,64,128]{2,1,0:T(8,128)(2,1)S(1)}, u32[]{:S(2)}, u32[]{:S(2)}) collective-permute-start(bf16[16,64,128]{2,1,0:T(8,128)(2,1)} %param.3), channel_id=1, source_target_pairs={{0,128},{1,65},{2,194},{3,67},{4,132},{5,197},{6,6},{7,7},{8,144},... | collective-permute-start | bytes 786440 | tf_op jit(solution)/shard_map/ppermute | solution.py:179
  25.4 0.7 collective-permute-start.1
  26.1 0.7 copy-start.1
  26.9 10.0 %collective-permute-start.2 = (bf16[16,64,128]{2,1,0:T(8,128)(2,1)}, bf16[16,64,128]{2,1,0:T(8,128)(2,1)S(1)}, u32[]{:S(2)}, u32[]{:S(2)}) collective-permute-start(bf16[16,64,128]{2,1,0:T(8,128)(2,1)} %copy-done.1), channel_id=1, source_target_pairs={{0,32},{1,33},{2,34},{3,35},{4,36},{5,37},{6,38},{7,39},{8,40},{9,... | collective-permute-start | bytes 786440 | tf_op jit(solution)/shard_map/ppermute | solution.py:76
  28.8 8.5 %collective-permute-start.3 = (bf16[16,64,128]{2,1,0:T(8,128)(2,1)}, bf16[16,64,128]{2,1,0:T(8,128)(2,1)S(1)}, u32[]{:S(2)}, u32[]{:S(2)}) collective-permute-start(bf16[16,64,128]{2,1,0:T(8,128)(2,1)} %copy-done.1), channel_id=1, source_target_pairs={{0,48},{1,49},{2,50},{3,51},{4,52},{5,53},{6,54},{7,55},{8,56},{9,... | collective-permute-start | bytes 786440 | tf_op jit(solution)/shard_map/ppermute | solution.py:76
  30.7 10.5 %collective-permute-start.4 = (bf16[16,64,128]{2,1,0:T(8,128)(2,1)}, bf16[16,64,128]{2,1,0:T(8,128)(2,1)S(1)}, u32[]{:S(2)}, u32[]{:S(2)}) collective-permute-start(bf16[16,64,128]{2,1,0:T(8,128)(2,1)} %copy-done.1), channel_id=1, source_target_pairs={{0,16},{1,17},{2,18},{3,19},{4,20},{5,21},{6,22},{7,23},{8,24},{9,... | collective-permute-start | bytes 786440 | tf_op jit(solution)/shard_map/ppermute | solution.py:76
  41.5 37.8 %collective-permute-start.5 = (bf16[32,64,128]{2,1,0:T(8,128)(2,1)S(1)}, bf16[32,64,128]{2,1,0:T(8,128)(2,1)S(1)}, u32[]{:S(2)}, u32[]{:S(2)}) collective-permute-start(bf16[32,64,128]{2,1,0:T(8,128)(2,1)S(1)} %pad_maximum_fusion.1), channel_id=1, source_target_pairs={{0,1},{1,138},{2,3},{3,196},{4,5},{5,70},{6,7},{7,328},{8,9},{9,20... | collective-permute-start | bytes 1572872 | tf_op jit(solution)/shard_map/ppermute | solution.py:76
  62.3 19.8 %collective-permute-start.6 = (bf16[16,64,128]{2,1,0:T(8,128)(2,1)S(1)}, bf16[16,64,128]{2,1,0:T(8,128)(2,1)S(1)}, u32[]{:S(2)}, u32[]{:S(2)}) collective-permute-start(bf16[16,64,128]{2,1,0:T(8,128)(2,1)S(1)} %get-tuple-element.19), channel_id=1, source_target_pairs={{0,1},{1,138},{2,3},{3,196},{4,5},{5,70},{6,7},{7,328},{8,9},{9,20... | collective-permute-start | bytes 786440 | tf_op jit(solution)/shard_map/ppermute | solution.py:76
  85.0 1.6 %copy-start = (bf16[128,64,128]{2,1,0:T(8,128)(2,1)S(1)}, bf16[128,64,128]{2,1,0:T(8,128)(2,1)}, u32[]{:S(2)}) copy-start(bf16[128,64,128]{2,1,0:T(8,128)(2,1)} %all-gather.2.cloned.1.call-done.refs_3_) | copy-start | bytes 6291460
  88.8 12.6 %collective-permute-start.7 = (bf16[16,64,128]{2,1,0:T(8,128)(2,1)S(1)}, bf16[16,64,128]{2,1,0:T(8,128)(2,1)S(1)}, u32[]{:S(2)}, u32[]{:S(2)}) collective-permute-start(bf16[16,64,128]{2,1,0:T(8,128)(2,1)S(1)} %shard_map.37.refs_3_), channel_id=1, source_target_pairs={{0,128},{1,129},{2,130},{3,131},{4,132},{5,133},{6,134},{7,135},{8... | collective-permute-start | bytes 786440 | tf_op jit(solution)/shard_map/ppermute | solution.py:76
  93.4 12.9 %collective-permute-start.8 = (bf16[16,64,128]{2,1,0:T(8,128)(2,1)S(1)}, bf16[16,64,128]{2,1,0:T(8,128)(2,1)S(1)}, u32[]{:S(2)}, u32[]{:S(2)}) collective-permute-start(bf16[16,64,128]{2,1,0:T(8,128)(2,1)S(1)} %shard_map.37.refs_3_), channel_id=1, source_target_pairs={{0,64},{1,65},{2,66},{3,67},{4,68},{5,69},{6,70},{7,71},{8,72},{9,... | collective-permute-start | bytes 786440 | tf_op jit(solution)/shard_map/ppermute | solution.py:76
  98.4 10.1 %collective-permute-start.9 = (bf16[16,64,128]{2,1,0:T(8,128)(2,1)S(1)}, bf16[16,64,128]{2,1,0:T(8,128)(2,1)S(1)}, u32[]{:S(2)}, u32[]{:S(2)}) collective-permute-start(bf16[16,64,128]{2,1,0:T(8,128)(2,1)S(1)} %shard_map.37.refs_3_), channel_id=1, source_target_pairs={{0,192},{1,193},{2,194},{3,195},{4,196},{5,197},{6,198},{7,199},{8... | collective-permute-start | bytes 786440 | tf_op jit(solution)/shard_map/ppermute | solution.py:76
  108.7 4.6 %collective-permute-start.10 = (bf16[64,64,128]{2,1,0:T(8,128)(2,1)S(1)}, bf16[64,64,128]{2,1,0:T(8,128)(2,1)S(1)}, u32[]{:S(2)}, u32[]{:S(2)}) collective-permute-start(bf16[64,64,128]{2,1,0:T(8,128)(2,1)S(1)} %pad_maximum_fusion), channel_id=1, source_target_pairs={{0,8},{1,9},{2,10},{3,11},{4,12},{5,13},{6,14},{7,15},{8,0},{9,1},... | collective-permute-start | bytes 3145736 | tf_op jit(solution)/shard_map/ppermute | solution.py:76
  115.5 21.6 %collective-permute-start.11 = (bf16[16,64,128]{2,1,0:T(8,128)(2,1)S(1)}, bf16[16,64,128]{2,1,0:T(8,128)(2,1)S(1)}, u32[]{:S(2)}, u32[]{:S(2)}) collective-permute-start(bf16[16,64,128]{2,1,0:T(8,128)(2,1)S(1)} %shard_map.38), channel_id=1, source_target_pairs={{0,6},{1,38},{2,65},{3,97},{4,128},{5,160},{6,195},{7,227},{8,7},{... | collective-permute-start | bytes 786440 | tf_op jit(solution)/shard_map/ppermute | solution.py:207
Sparse Core Ops, SparseCore 0:
  27.0 57.9 all-gather.1

commit v6 on v4

--- a/solution.py
+++ b/solution.py
@@ -72,13 +72,16 @@
     return lax.ppermute(value, AXES, route(source, place))
 
 
-def gather_row(part, after=()):
-    near = [part]
-    for distance in (2, 1, -1):
-        near.append(send(part, lambda p, g: place(p, beside(p, g, distance))))
-    near = lax.optimization_barrier((near, after))[0]
+def gather_row(near):
     far = send(jnp.concatenate(near, axis=0), lambda p, g: place(p, opposite(p, g)))
     return near + jnp.split(far, len(near), axis=0)
+
+
+def gather_beside(part, distances):
+    return [
+        send(part, lambda p, g: place(p, beside(p, g, distance)))
+        for distance in distances
+    ]
 
 
 def gather_column(part):
@@ -88,14 +91,17 @@
     ]
 
 
-def gather_table(part, column, panel):
+def rows_to_pass(column, panel):
     low = panel % 4 < 2
     two, one, three = column
     pair = jnp.concatenate([two, jnp.where(low, one, three)], axis=0)
-    rest = jnp.where(low, three, one)
+    return pair, jnp.where(low, three, one)
+
+
+def pass_rows(pair, rest):
     pair = send(pair, lambda p, g: place((p + (-4 if p % 4 < 2 else 4)) % PANELS, g))
     rest = send(rest, lambda p, g: place((p + (4 if p % 2 else -4)) % PANELS, g))
-    return jnp.concatenate([part, two, one, three, pair, rest], axis=0)
+    return [pair, rest]
 
 
 def table_panel(owner, panel):
@@ -165,6 +171,8 @@
     panel, mine, order = job[0], job[1], job[2:]
 
     part = lax.ppermute(density, AXES, route(start, between))
+    part, columns = lax.optimization_barrier((part, columns))
+    part = send(part, between)
 
     base = panel * local_rows
     own = lax.dynamic_slice_in_dim(columns, base, local_rows, 0)
@@ -185,13 +193,20 @@
     mask = mask.astype(jnp.float32).reshape(local_rows * stored, 2 * lanes)
 
     part, index, mask = lax.optimization_barrier((part, index, mask))
-    part = send(part, between)
 
     column = gather_column(part)
-    left = gather_row(part, column)
-    table = gather_table(part, column, panel).reshape(-1, width, lanes)
+    near = [part] + gather_beside(part, (2,))
+    pair, rest = rows_to_pass(column, panel)
+    part, pair, rest = lax.optimization_barrier((part, pair, rest))
+    outer = pass_rows(pair, rest)
+    near = near + gather_beside(part, (1, -1))
+    near, outer = lax.optimization_barrier((near, outer))
+    left = gather_row(near)
+    table = jnp.concatenate(near[:1] + column + outer, axis=0)
+    table = table.reshape(-1, width, lanes)
     square = product(index, mask, table, left, False)
-    result = product(index, mask, table, gather_row(square), True)
+    left = gather_row([square] + gather_beside(square, (2, 1, -1)))
+    result = product(index, mask, table, left, True)
     return lax.ppermute(result, AXES, route(place, start)).astype(jnp.float32)
 
 

time: 139 us -> 134 us (0.964)
  the two profiles are of different devices: /device:TPU:4 before, /device:TPU:2 now
where the time goes in v6:
time: 134 us; the launch traced here: 133 us
  starting transfers between devices  63.9 us (48%)
  waiting for transfers between devices  52.8 us (39%)
  local copies, waits for them, and re-layouts  7 us (5%)
  Pallas kernels  4.43 us (3%)
  between operations  3.53 us (3%)
  other arithmetic  1.81 us (1%)
    ppermute x14, starting transfers between devices, send(): return lax.ppermute(value, AXES, route(source, place))  57.9 us
    ppermute x14, waiting for transfers between devices, send(): return lax.ppermute(value, AXES, route(source, place))  27.7 us
    ppermute x1, waiting for transfers between devices, shards(): return lax.ppermute(result, AXES, route(place, start)).astype(jnp.float32)  21.7 us
    pallas_call x2, Pallas kernels, product(): pl.pallas_call(lambda *refs: product_kernel(count, lanes // width, keep,...  4.43 us
    ppermute x1, starting transfers between devices, shards(): part = lax.ppermute(density, AXES, route(start, between))  4.02 us
    ppermute x1, waiting for transfers between devices, shards(): part = lax.ppermute(density, AXES, route(start, between))  3.45 us
  transfers between devices with their start and end apart: 16, of which 11 were waited for; matrix products, arithmetic and copies ran while one was open for 4% of the time, Pallas kernels for 0%

profile of v6, /device:TPU:2, one launch (start us, length us, event | category | flops | bytes accessed | tf_op | source)
XLA Modules:
  0.0 133.5 jit_solution(8350207570941999371)
XLA Ops:
  0.0 4.0 %collective-permute-start = (bf16[16,64,128]{2,1,0:T(8,128)(2,1)}, bf16[16,64,128]{2,1,0:T(8,128)(2,1)S(1)}, u32[]{:S(2)}, u32[]{:S(2)}) collective-permute-start(bf16[16,64,128]{2,1,0:T(8,128)(2,1)} %param.3), channel_id=1, source_target_pairs={{0,128},{1,65},{2,194},{3,67},{4,132},{5,197},{6,6},{7,7},{8,144},... | collective-permute-start | bytes 786440 | tf_op jit(solution)/shard_map/ppermute | solution.py:173
  9.0 3.4 %collective-permute-done = bf16[16,64,128]{2,1,0:T(8,128)(2,1)S(1)} collective-permute-done((bf16[16,64,128]{2,1,0:T(8,128)(2,1)}, bf16[16,64,128]{2,1,0:T(8,128)(2,1)S(1)}, u32[]{:S(2)}, u32[]{:S(2)}) %collective-permute-start) | collective-permute-done | bytes 262176 | tf_op jit(solution)/shard_map/ppermute | solution.py:173
  12.4 0.8 constant_dynamic-slice_fusion.1
  13.2 1.0 copy.14
  14.2 10.3 %collective-permute-start.1 = (bf16[16,64,128]{2,1,0:T(8,128)(2,1)S(1)}, bf16[16,64,128]{2,1,0:T(8,128)(2,1)S(1)}, u32[]{:S(2)}, u32[]{:S(2)}) collective-permute-start(bf16[16,64,128]{2,1,0:T(8,128)(2,1)S(1)} %collective-permute-done), channel_id=1, source_target_pairs={{0,4},{1,2},{2,10},{3,6},{4,12},{5,14},{6,0},{7,8},{8,5},{9,3},{10... | collective-permute-start | bytes 786440 | tf_op jit(solution)/shard_map/ppermute | solution.py:72
  24.5 0.8 dynamic_slice.16
  26.5 0.7 gather_fusion.1
  28.9 3.9 %collective-permute-start.5 = (bf16[16,64,128]{2,1,0:T(8,128)(2,1)S(1)}, bf16[16,64,128]{2,1,0:T(8,128)(2,1)S(1)}, u32[]{:S(2)}, u32[]{:S(2)}) collective-permute-start(bf16[16,64,128]{2,1,0:T(8,128)(2,1)S(1)} %collective-permute-done.1.refs_3_), channel_id=1, source_target_pairs={{0,16},{1,17},{2,18},{3,19},{4,20},{5,21},{6,22},{7,23},{8,24},{9,... | collective-permute-start | bytes 786440 | tf_op jit(solution)/shard_map/ppermute | solution.py:72
  32.8 5.0 %collective-permute-start.4 = (bf16[16,64,128]{2,1,0:T(8,128)(2,1)S(1)}, bf16[16,64,128]{2,1,0:T(8,128)(2,1)S(1)}, u32[]{:S(2)}, u32[]{:S(2)}) collective-permute-start(bf16[16,64,128]{2,1,0:T(8,128)(2,1)S(1)} %collective-permute-done.1.refs_3_), channel_id=1, source_target_pairs={{0,48},{1,49},{2,50},{3,51},{4,52},{5,53},{6,54},{7,55},{8,56},{9,... | collective-permute-start | bytes 786440 | tf_op jit(solution)/shard_map/ppermute | solution.py:72
  37.8 3.4 %collective-permute-start.3 = (bf16[16,64,128]{2,1,0:T(8,128)(2,1)S(1)}, bf16[16,64,128]{2,1,0:T(8,128)(2,1)S(1)}, u32[]{:S(2)}, u32[]{:S(2)}) collective-permute-start(bf16[16,64,128]{2,1,0:T(8,128)(2,1)S(1)} %collective-permute-done.1.refs_3_), channel_id=1, source_target_pairs={{0,32},{1,33},{2,34},{3,35},{4,36},{5,37},{6,38},{7,39},{8,40},{9,... | collective-permute-start | bytes 786440 | tf_op jit(solution)/shard_map/ppermute | solution.py:72
  41.1 1.7 %collective-permute-done.4 = bf16[16,64,128]{2,1,0:T(8,128)(2,1)S(1)} collective-permute-done((bf16[16,64,128]{2,1,0:T(8,128)(2,1)S(1)}, bf16[16,64,128]{2,1,0:T(8,128)(2,1)S(1)}, u32[]{:S(2)}, u32[]{:S(2)}) %collective-permute-start.4) | collective-permute-done | bytes 262176 | tf_op jit(solution)/shard_map/ppermute | solution.py:72
  42.9 6.2 %collective-permute-done.3 = bf16[16,64,128]{2,1,0:T(8,128)(2,1)S(1)} collective-permute-done((bf16[16,64,128]{2,1,0:T(8,128)(2,1)S(1)}, bf16[16,64,128]{2,1,0:T(8,128)(2,1)S(1)}, u32[]{:S(2)}, u32[]{:S(2)}) %collective-permute-start.3) | collective-permute-done | bytes 262176 | tf_op jit(solution)/shard_map/ppermute | solution.py:72
  49.1 1.9 %collective-permute-start.8 = (bf16[32,64,128]{2,1,0:T(8,128)(2,1)S(1)}, bf16[32,64,128]{2,1,0:T(8,128)(2,1)S(1)}, u32[]{:S(2)}, u32[]{:S(2)}) collective-permute-start(bf16[32,64,128]{2,1,0:T(8,128)(2,1)S(1)} %pad_maximum_fusion.2), channel_id=1, source_target_pairs={{0,1},{1,138},{2,3},{3,196},{4,5},{5,70},{6,7},{7,328},{8,9},{9,20... | collective-permute-start | bytes 1572872 | tf_op jit(solution)/shard_map/ppermute | solution.py:72
  51.1 3.3 %collective-permute-start.2 = (bf16[16,64,128]{2,1,0:T(8,128)(2,1)S(1)}, bf16[16,64,128]{2,1,0:T(8,128)(2,1)S(1)}, u32[]{:S(2)}, u32[]{:S(2)}) collective-permute-start(bf16[16,64,128]{2,1,0:T(8,128)(2,1)S(1)} %collective-permute-done.1.refs_3_), channel_id=1, source_target_pairs={{0,128},{1,129},{2,130},{3,131},{4,132},{5,133},{6,134},{7,135},{8... | collective-permute-start | bytes 786440 | tf_op jit(solution)/shard_map/ppermute | solution.py:72
  54.4 5.4 %collective-permute-start.6 = (bf16[16,64,128]{2,1,0:T(8,128)(2,1)S(1)}, bf16[16,64,128]{2,1,0:T(8,128)(2,1)S(1)}, u32[]{:S(2)}, u32[]{:S(2)}) collective-permute-start(bf16[16,64,128]{2,1,0:T(8,128)(2,1)S(1)} %collective-permute-done.1.refs_3_), channel_id=1, source_target_pairs={{0,64},{1,65},{2,66},{3,67},{4,68},{5,69},{6,70},{7,71},{8,72},{9,... | collective-permute-start | bytes 786440 | tf_op jit(solution)/shard_map/ppermute | solution.py:72
  59.8 1.9 %collective-permute-start.7 = (bf16[16,64,128]{2,1,0:T(8,128)(2,1)S(1)}, bf16[16,64,128]{2,1,0:T(8,128)(2,1)S(1)}, u32[]{:S(2)}, u32[]{:S(2)}) collective-permute-start(bf16[16,64,128]{2,1,0:T(8,128)(2,1)S(1)} %collective-permute-done.1.refs_3_), channel_id=1, source_target_pairs={{0,192},{1,193},{2,194},{3,195},{4,196},{5,197},{6,198},{7,199},{8... | collective-permute-start | bytes 786440 | tf_op jit(solution)/shard_map/ppermute | solution.py:72
  61.7 6.7 %collective-permute-start.9 = (bf16[16,64,128]{2,1,0:T(8,128)(2,1)S(1)}, bf16[16,64,128]{2,1,0:T(8,128)(2,1)S(1)}, u32[]{:S(2)}, u32[]{:S(2)}) collective-permute-start(bf16[16,64,128]{2,1,0:T(8,128)(2,1)S(1)} %get-tuple-element.26), channel_id=1, source_target_pairs={{0,1},{1,138},{2,3},{3,196},{4,5},{5,70},{6,7},{7,328},{8,9},{9,20... | collective-permute-start | bytes 786440 | tf_op jit(solution)/shard_map/ppermute | solution.py:72
  68.8 7.9 %collective-permute-done.6.refs_5_ = bf16[16,64,128]{2,1,0:T(8,128)(2,1)S(1)} collective-permute-done((bf16[16,64,128]{2,1,0:T(8,128)(2,1)S(1)}, bf16[16,64,128]{2,1,0:T(8,128)(2,1)S(1)}, u32[]{:S(2)}, u32[]{:S(2)}) %collective-permute-start.6) | collective-permute-done | bytes 262176 | tf_op jit(solution)/shard_map/ppermute | solution.py:72
  76.8 2.7 %collective-permute-start.10 = (bf16[64,64,128]{2,1,0:T(8,128)(2,1)S(1)}, bf16[64,64,128]{2,1,0:T(8,128)(2,1)S(1)}, u32[]{:S(2)}, u32[]{:S(2)}) collective-permute-start(bf16[64,64,128]{2,1,0:T(8,128)(2,1)S(1)} %pad_maximum_fusion), channel_id=1, source_target_pairs={{0,8},{1,9},{2,10},{3,11},{4,12},{5,13},{6,14},{7,15},{8,0},{9,1},... | collective-permute-start | bytes 3145736 | tf_op jit(solution)/shard_map/ppermute | solution.py:72
  79.7 2.0 %collective-permute-done.10 = bf16[64,64,128]{2,1,0:T(8,128)(2,1)S(1)} collective-permute-done((bf16[64,64,128]{2,1,0:T(8,128)(2,1)S(1)}, bf16[64,64,128]{2,1,0:T(8,128)(2,1)S(1)}, u32[]{:S(2)}, u32[]{:S(2)}) %collective-permute-start.10) | collective-permute-done | bytes 1048608 | tf_op jit(solution)/shard_map/ppermute | solution.py:72
  81.8 2.2 %shard_map.37.refs_3_ = bf16[16,64,128]{2,1,0:T(8,128)(2,1)S(1)} custom-call(s32[256]{0:T(256)S(1)} %fusion.3.refs_0_, f32[256,256]{1,0:T(8,128)S(1)} %add_convert_fusion.refs_1_, bf16[112,64,128]{2,1,0:T(8,128)(2,1)S(1)} %constant_dynamic-update-slice_fusion.refs_2_, bf16[16,64,128]{2,1,0:T(8,128)(2,1)S(1)} %collective-permute-done.1.refs_3_, ...), custom_call_target="tpu_custom_call" | custom-call | flops 536870912 | bytes 8388608 | tf_op jit(solution)/shard_map/pallas_call | solution.py:147
  84.0 5.7 %collective-permute-start.11 = (bf16[16,64,128]{2,1,0:T(8,128)(2,1)S(1)}, bf16[16,64,128]{2,1,0:T(8,128)(2,1)S(1)}, u32[]{:S(2)}, u32[]{:S(2)}) collective-permute-start(bf16[16,64,128]{2,1,0:T(8,128)(2,1)S(1)} %shard_map.37.refs_3_), channel_id=1, source_target_pairs={{0,128},{1,129},{2,130},{3,131},{4,132},{5,133},{6,134},{7,135},{8... | collective-permute-start | bytes 786440 | tf_op jit(solution)/shard_map/ppermute | solution.py:72
  89.7 1.9 %collective-permute-start.12 = (bf16[16,64,128]{2,1,0:T(8,128)(2,1)S(1)}, bf16[16,64,128]{2,1,0:T(8,128)(2,1)S(1)}, u32[]{:S(2)}, u32[]{:S(2)}) collective-permute-start(bf16[16,64,128]{2,1,0:T(8,128)(2,1)S(1)} %shard_map.37.refs_3_), channel_id=1, source_target_pairs={{0,64},{1,65},{2,66},{3,67},{4,68},{5,69},{6,70},{7,71},{8,72},{9,... | collective-permute-start | bytes 786440 | tf_op jit(solution)/shard_map/ppermute | solution.py:72
  91.6 3.9 %collective-permute-start.13 = (bf16[16,64,128]{2,1,0:T(8,128)(2,1)S(1)}, bf16[16,64,128]{2,1,0:T(8,128)(2,1)S(1)}, u32[]{:S(2)}, u32[]{:S(2)}) collective-permute-start(bf16[16,64,128]{2,1,0:T(8,128)(2,1)S(1)} %shard_map.37.refs_3_), channel_id=1, source_target_pairs={{0,192},{1,193},{2,194},{3,195},{4,196},{5,197},{6,198},{7,199},{8... | collective-permute-start | bytes 786440 | tf_op jit(solution)/shard_map/ppermute | solution.py:72
  95.6 0.8 collective-permute-done.11.refs_4_
  96.3 5.7 %collective-permute-done.12.refs_5_ = bf16[16,64,128]{2,1,0:T(8,128)(2,1)S(1)} collective-permute-done((bf16[16,64,128]{2,1,0:T(8,128)(2,1)S(1)}, bf16[16,64,128]{2,1,0:T(8,128)(2,1)S(1)}, u32[]{:S(2)}, u32[]{:S(2)}) %collective-permute-start.12) | collective-permute-done | bytes 262176 | tf_op jit(solution)/shard_map/ppermute | solution.py:72
  102.1 1.9 %collective-permute-start.14 = (bf16[64,64,128]{2,1,0:T(8,128)(2,1)S(1)}, bf16[64,64,128]{2,1,0:T(8,128)(2,1)S(1)}, u32[]{:S(2)}, u32[]{:S(2)}) collective-permute-start(bf16[64,64,128]{2,1,0:T(8,128)(2,1)S(1)} %pad_maximum_fusion.1), channel_id=1, source_target_pairs={{0,8},{1,9},{2,10},{3,11},{4,12},{5,13},{6,14},{7,15},{8,0},{9,1},... | collective-permute-start | bytes 3145736 | tf_op jit(solution)/shard_map/ppermute | solution.py:72
  104.1 2.6 %collective-permute-done.14 = bf16[64,64,128]{2,1,0:T(8,128)(2,1)S(1)} collective-permute-done((bf16[64,64,128]{2,1,0:T(8,128)(2,1)S(1)}, bf16[64,64,128]{2,1,0:T(8,128)(2,1)S(1)}, u32[]{:S(2)}, u32[]{:S(2)}) %collective-permute-start.14) | collective-permute-done | bytes 1048608 | tf_op jit(solution)/shard_map/ppermute | solution.py:72
  106.8 2.2 %shard_map.38 = bf16[16,64,128]{2,1,0:T(8,128)(2,1)S(1)} custom-call(s32[256]{0:T(256)S(1)} %fusion.3.refs_0_, f32[256,256]{1,0:T(8,128)S(1)} %add_convert_fusion.refs_1_, bf16[112,64,128]{2,1,0:T(8,128)(2,1)S(1)} %constant_dynamic-update-slice_fusion.refs_2_, bf16[16,64,128]{2,1,0:T(8,128)(2,1)S(1)} %shard_map.37.refs_3_, ...), custom_call_target="tpu_custom_call" | custom-call | flops 536870912 | bytes 8388608 | tf_op jit(solution)/shard_map/pallas_call | solution.py:147
  109.0 1.9 %collective-permute-start.15 = (bf16[16,64,128]{2,1,0:T(8,128)(2,1)S(1)}, bf16[16,64,128]{2,1,0:T(8,128)(2,1)S(1)}, u32[]{:S(2)}, u32[]{:S(2)}) collective-permute-start(bf16[16,64,128]{2,1,0:T(8,128)(2,1)S(1)} %shard_map.38), channel_id=1, source_target_pairs={{0,6},{1,38},{2,65},{3,97},{4,128},{5,160},{6,195},{7,227},{8,7},{... | collective-permute-start | bytes 786440 | tf_op jit(solution)/shard_map/ppermute | solution.py:210
  110.9 21.7 %collective-permute-done.15 = bf16[16,64,128]{2,1,0:T(8,128)(2,1)S(1)} collective-permute-done((bf16[16,64,128]{2,1,0:T(8,128)(2,1)S(1)}, bf16[16,64,128]{2,1,0:T(8,128)(2,1)S(1)}, u32[]{:S(2)}, u32[]{:S(2)}) %collective-permute-start.15) | collective-permute-done | bytes 262176 | tf_op jit(solution)/shard_map/ppermute | solution.py:210
  132.6 0.8 convert_element_type.8
  (50 shorter events, 5.5 us)
Async XLA Ops:
  0.0 12.4 %collective-permute-start = (bf16[16,64,128]{2,1,0:T(8,128)(2,1)}, bf16[16,64,128]{2,1,0:T(8,128)(2,1)S(1)}, u32[]{:S(2)}, u32[]{:S(2)}) collective-permute-start(bf16[16,64,128]{2,1,0:T(8,128)(2,1)} %param.3), channel_id=1, source_target_pairs={{0,128},{1,65},{2,194},{3,67},{4,132},{5,197},{6,6},{7,7},{8,144},... | collective-permute-start | bytes 786440 | tf_op jit(solution)/shard_map/ppermute | solution.py:173
  14.2 14.6 %collective-permute-start.1 = (bf16[16,64,128]{2,1,0:T(8,128)(2,1)S(1)}, bf16[16,64,128]{2,1,0:T(8,128)(2,1)S(1)}, u32[]{:S(2)}, u32[]{:S(2)}) collective-permute-start(bf16[16,64,128]{2,1,0:T(8,128)(2,1)S(1)} %collective-permute-done), channel_id=1, source_target_pairs={{0,4},{1,2},{2,10},{3,6},{4,12},{5,14},{6,0},{7,8},{8,5},{9,3},{10... | collective-permute-start | bytes 786440 | tf_op jit(solution)/shard_map/ppermute | solution.py:72
  28.9 12.3 %collective-permute-start.5 = (bf16[16,64,128]{2,1,0:T(8,128)(2,1)S(1)}, bf16[16,64,128]{2,1,0:T(8,128)(2,1)S(1)}, u32[]{:S(2)}, u32[]{:S(2)}) collective-permute-start(bf16[16,64,128]{2,1,0:T(8,128)(2,1)S(1)} %collective-permute-done.1.refs_3_), channel_id=1, source_target_pairs={{0,16},{1,17},{2,18},{3,19},{4,20},{5,21},{6,22},{7,23},{8,24},{9,... | collective-permute-start | bytes 786440 | tf_op jit(solution)/shard_map/ppermute | solution.py:72
  32.8 10.1 %collective-permute-start.4 = (bf16[16,64,128]{2,1,0:T(8,128)(2,1)S(1)}, bf16[16,64,128]{2,1,0:T(8,128)(2,1)S(1)}, u32[]{:S(2)}, u32[]{:S(2)}) collective-permute-start(bf16[16,64,128]{2,1,0:T(8,128)(2,1)S(1)} %collective-permute-done.1.refs_3_), channel_id=1, source_target_pairs={{0,48},{1,49},{2,50},{3,51},{4,52},{5,53},{6,54},{7,55},{8,56},{9,... | collective-permute-start | bytes 786440 | tf_op jit(solution)/shard_map/ppermute | solution.py:72
  37.8 11.3 %collective-permute-start.3 = (bf16[16,64,128]{2,1,0:T(8,128)(2,1)S(1)}, bf16[16,64,128]{2,1,0:T(8,128)(2,1)S(1)}, u32[]{:S(2)}, u32[]{:S(2)}) collective-permute-start(bf16[16,64,128]{2,1,0:T(8,128)(2,1)S(1)} %collective-permute-done.1.refs_3_), channel_id=1, source_target_pairs={{0,32},{1,33},{2,34},{3,35},{4,36},{5,37},{6,38},{7,39},{8,40},{9,... | collective-permute-start | bytes 786440 | tf_op jit(solution)/shard_map/ppermute | solution.py:72
  49.1 27.5 %collective-permute-start.8 = (bf16[32,64,128]{2,1,0:T(8,128)(2,1)S(1)}, bf16[32,64,128]{2,1,0:T(8,128)(2,1)S(1)}, u32[]{:S(2)}, u32[]{:S(2)}) collective-permute-start(bf16[32,64,128]{2,1,0:T(8,128)(2,1)S(1)} %pad_maximum_fusion.2), channel_id=1, source_target_pairs={{0,1},{1,138},{2,3},{3,196},{4,5},{5,70},{6,7},{7,328},{8,9},{9,20... | collective-permute-start | bytes 1572872 | tf_op jit(solution)/shard_map/ppermute | solution.py:72
  51.1 17.7 %collective-permute-start.2 = (bf16[16,64,128]{2,1,0:T(8,128)(2,1)S(1)}, bf16[16,64,128]{2,1,0:T(8,128)(2,1)S(1)}, u32[]{:S(2)}, u32[]{:S(2)}) collective-permute-start(bf16[16,64,128]{2,1,0:T(8,128)(2,1)S(1)} %collective-permute-done.1.refs_3_), channel_id=1, source_target_pairs={{0,128},{1,129},{2,130},{3,131},{4,132},{5,133},{6,134},{7,135},{8... | collective-permute-start | bytes 786440 | tf_op jit(solution)/shard_map/ppermute | solution.py:72
  54.4 22.2 %collective-permute-start.6 = (bf16[16,64,128]{2,1,0:T(8,128)(2,1)S(1)}, bf16[16,64,128]{2,1,0:T(8,128)(2,1)S(1)}, u32[]{:S(2)}, u32[]{:S(2)}) collective-permute-start(bf16[16,64,128]{2,1,0:T(8,128)(2,1)S(1)} %collective-permute-done.1.refs_3_), channel_id=1, source_target_pairs={{0,64},{1,65},{2,66},{3,67},{4,68},{5,69},{6,70},{7,71},{8,72},{9,... | collective-permute-start | bytes 786440 | tf_op jit(solution)/shard_map/ppermute | solution.py:72
  59.8 16.8 %collective-permute-start.7 = (bf16[16,64,128]{2,1,0:T(8,128)(2,1)S(1)}, bf16[16,64,128]{2,1,0:T(8,128)(2,1)S(1)}, u32[]{:S(2)}, u32[]{:S(2)}) collective-permute-start(bf16[16,64,128]{2,1,0:T(8,128)(2,1)S(1)} %collective-permute-done.1.refs_3_), channel_id=1, source_target_pairs={{0,192},{1,193},{2,194},{3,195},{4,196},{5,197},{6,198},{7,199},{8... | collective-permute-start | bytes 786440 | tf_op jit(solution)/shard_map/ppermute | solution.py:72
  61.7 14.9 %collective-permute-start.9 = (bf16[16,64,128]{2,1,0:T(8,128)(2,1)S(1)}, bf16[16,64,128]{2,1,0:T(8,128)(2,1)S(1)}, u32[]{:S(2)}, u32[]{:S(2)}) collective-permute-start(bf16[16,64,128]{2,1,0:T(8,128)(2,1)S(1)} %get-tuple-element.26), channel_id=1, source_target_pairs={{0,1},{1,138},{2,3},{3,196},{4,5},{5,70},{6,7},{7,328},{8,9},{9,20... | collective-permute-start | bytes 786440 | tf_op jit(solution)/shard_map/ppermute | solution.py:72
  76.8 5.0 %collective-permute-start.10 = (bf16[64,64,128]{2,1,0:T(8,128)(2,1)S(1)}, bf16[64,64,128]{2,1,0:T(8,128)(2,1)S(1)}, u32[]{:S(2)}, u32[]{:S(2)}) collective-permute-start(bf16[64,64,128]{2,1,0:T(8,128)(2,1)S(1)} %pad_maximum_fusion), channel_id=1, source_target_pairs={{0,8},{1,9},{2,10},{3,11},{4,12},{5,13},{6,14},{7,15},{8,0},{9,1},... | collective-permute-start | bytes 3145736 | tf_op jit(solution)/shard_map/ppermute | solution.py:72
  84.0 12.3 %collective-permute-start.11 = (bf16[16,64,128]{2,1,0:T(8,128)(2,1)S(1)}, bf16[16,64,128]{2,1,0:T(8,128)(2,1)S(1)}, u32[]{:S(2)}, u32[]{:S(2)}) collective-permute-start(bf16[16,64,128]{2,1,0:T(8,128)(2,1)S(1)} %shard_map.37.refs_3_), channel_id=1, source_target_pairs={{0,128},{1,129},{2,130},{3,131},{4,132},{5,133},{6,134},{7,135},{8... | collective-permute-start | bytes 786440 | tf_op jit(solution)/shard_map/ppermute | solution.py:72
  89.7 12.3 %collective-permute-start.12 = (bf16[16,64,128]{2,1,0:T(8,128)(2,1)S(1)}, bf16[16,64,128]{2,1,0:T(8,128)(2,1)S(1)}, u32[]{:S(2)}, u32[]{:S(2)}) collective-permute-start(bf16[16,64,128]{2,1,0:T(8,128)(2,1)S(1)} %shard_map.37.refs_3_), channel_id=1, source_target_pairs={{0,64},{1,65},{2,66},{3,67},{4,68},{5,69},{6,70},{7,71},{8,72},{9,... | collective-permute-start | bytes 786440 | tf_op jit(solution)/shard_map/ppermute | solution.py:72
  91.6 10.4 %collective-permute-start.13 = (bf16[16,64,128]{2,1,0:T(8,128)(2,1)S(1)}, bf16[16,64,128]{2,1,0:T(8,128)(2,1)S(1)}, u32[]{:S(2)}, u32[]{:S(2)}) collective-permute-start(bf16[16,64,128]{2,1,0:T(8,128)(2,1)S(1)} %shard_map.37.refs_3_), channel_id=1, source_target_pairs={{0,192},{1,193},{2,194},{3,195},{4,196},{5,197},{6,198},{7,199},{8... | collective-permute-start | bytes 786440 | tf_op jit(solution)/shard_map/ppermute | solution.py:72
  102.1 4.6 %collective-permute-start.14 = (bf16[64,64,128]{2,1,0:T(8,128)(2,1)S(1)}, bf16[64,64,128]{2,1,0:T(8,128)(2,1)S(1)}, u32[]{:S(2)}, u32[]{:S(2)}) collective-permute-start(bf16[64,64,128]{2,1,0:T(8,128)(2,1)S(1)} %pad_maximum_fusion.1), channel_id=1, source_target_pairs={{0,8},{1,9},{2,10},{3,11},{4,12},{5,13},{6,14},{7,15},{8,0},{9,1},... | collective-permute-start | bytes 3145736 | tf_op jit(solution)/shard_map/ppermute | solution.py:72
  109.0 23.6 %collective-permute-start.15 = (bf16[16,64,128]{2,1,0:T(8,128)(2,1)S(1)}, bf16[16,64,128]{2,1,0:T(8,128)(2,1)S(1)}, u32[]{:S(2)}, u32[]{:S(2)}) collective-permute-start(bf16[16,64,128]{2,1,0:T(8,128)(2,1)S(1)} %shard_map.38), channel_id=1, source_target_pairs={{0,6},{1,38},{2,65},{3,97},{4,128},{5,160},{6,195},{7,227},{8,7},{... | collective-permute-start | bytes 786440 | tf_op jit(solution)/shard_map/ppermute | solution.py:210

commit v7 on v4

v7 whole, which is shorter than its diff:
```python
import jax
import jax.numpy as jnp
import numpy as np
from jax import lax
from jax.experimental import pallas as pl
from jax.experimental.pallas import tpu as pltpu
from jax.sharding import PartitionSpec as P

AXES = ("row", "col")
PIECES = 5
PANELS = 64
GROUPS = 8
SPOTS = (
    (2, 3, 0, 1), (1, 0, 3, 2), (3, 0, 1, 2), (1, 2, 3, 0),
    (2, 1, 0, 3), (3, 1, 2, 0), (0, 2, 1, 3), (0, 3, 2, 1),
)


def device(half, x, y, core, z):
    return (((half * 4 + x) * 4 + y) * 2 + core) * GROUPS + z


def spot(panel, group):
    return SPOTS[group][panel // 8 % 4]


def held_at(panel, x):
    return [group for group in range(GROUPS) if spot(panel, group) == x % 4]


def lane(panel, group):
    return held_at(panel, spot(panel, group)).index(group)


def start(panel, group):
    return panel * GROUPS + group


def between(panel, group):
    return device(panel // 32, spot(panel, group), panel % 4, panel // 4 % 2, group)


def place(panel, group):
    x = spot(panel, group)
    return device(panel // 32, x, panel % 4, lane(panel, group), panel // 4 % 8)


JOBS = [(panel, group) for panel in range(PANELS) for group in range(GROUPS)]


def route(source, target):
    return sorted((source(*job), target(*job)) for job in JOBS)


def opposite(panel, group):
    return held_at(panel, spot(panel, group))[1 - lane(panel, group)]


def arrival(panel, group):
    mine = lane(panel, group)
    return [held_at(panel, x)[core] for core in (mine, 1 - mine) for x in range(4)]


def send(value, source):
    return lax.ppermute(value, AXES, route(source, place))


def gather_ring(part, ring):
    copies = jnp.concatenate([part] * 4, axis=0)
    return lax.all_to_all(copies, "row", 0, 0, tiled=True, axis_index_groups=ring)


X_RINGS = [
    [device(half, x, y, core, 0) // GROUPS for x in range(4)]
    for half in range(2) for y in range(4) for core in range(2)
]
def gather_row(near):
    return [near, send(near, lambda p, g: place(p, opposite(p, g)))]


def gather_column(part):
    return [
        send(part, lambda p, g: place(p // 4 * 4 + (p % 4 ^ flip), g))
        for flip in (1, 2, 3)
    ]


def pass_rows(pair, rest):
    pair = send(pair, lambda p, g: place((p + (-4 if p % 4 < 2 else 4)) % PANELS, g))
    rest = send(rest, lambda p, g: place((p + (4 if p % 2 else -4)) % PANELS, g))
    return pair, rest


def table_panel(owner, panel):
    y = panel % 4
    place_y = y + owner
    inner = jnp.mod(place_y, 4)
    flip = jnp.bitwise_xor(inner, y)
    return jnp.where(place_y == inner, flip, jnp.where(flip == 1, 6, flip + 2))


def product_kernel(count, group, keep, index_ref, mask_ref, *refs):
    out_ref, table_ref = refs[-2:]
    rows, width, lanes = out_ref.shape
    filled = 0
    for ref in refs[:PIECES]:
        table_ref[pl.ds(filled, ref.shape[0])] = ref[...]
        filled += ref.shape[0]
    refs = refs[PIECES:]
    chunks = [
        ref.at[pl.ds(j * rows, rows)]
        for ref in refs[:2]
        for j in range(ref.shape[0] // rows)
    ]
    blocks = count * group
    for i in range(rows):
        total = None
        for step in range(0, count, 2):
            left = jnp.concatenate([chunks[step][i], chunks[step + 1][i]], axis=1)
            pieces = []
            for b in range(step * group, (step + 2) * group):
                piece = table_ref[index_ref[i * blocks + b]]
                piece = jnp.concatenate([piece, piece], axis=1)
                mask = mask_ref[pl.ds(i * blocks + b, 1), :].astype(piece.dtype)
                pieces.append(piece * mask)
            right = jnp.concatenate(pieces, axis=0)
            part = jnp.dot(left, right, preferred_element_type=jnp.float32)
            total = part if total is None else total + part
        value = total[:, :lanes] + pltpu.roll(total[:, lanes:], width, 1)
        if keep:
            value = 3.0 * refs[2][i].astype(jnp.float32) - 2.0 * value
        out_ref[i] = value.astype(out_ref.dtype)


def product(index, mask, table, chunks, rows, keep):
    width, lanes = chunks[0].shape[1:]
    count = sum(chunk.shape[0] for chunk in chunks[:2]) // rows
    vmem = pl.BlockSpec(memory_space=pltpu.VMEM)
    return pl.pallas_call(
        lambda *refs: product_kernel(count, lanes // width, keep, *refs),
        out_shape=jax.ShapeDtypeStruct((rows, width, lanes), jnp.bfloat16),
        in_specs=[pl.BlockSpec(memory_space=pltpu.SMEM)]
        + [vmem] * (1 + len(table) + len(chunks)),
        out_specs=vmem,
        scratch_shapes=[
            pltpu.VMEM((sum(piece.shape[0] for piece in table), width, lanes), jnp.bfloat16)
        ],
        compiler_params=pltpu.CompilerParams(vmem_limit_bytes=24 * 1024 * 1024),
        cost_estimate=pl.CostEstimate(
            flops=4 * rows * width * lanes * lanes * count,
            bytes_accessed=8 * 1024 * 1024,
            transcendentals=0,
        ),
    )(index, mask, *table, *chunks)


def shards(density, columns):
    local_rows, width, lanes = density.shape
    group = lanes // width
    total, stored = columns.shape

    jobs = np.zeros((PANELS * GROUPS, 2 + GROUPS), np.int32)
    for job in JOBS:
        jobs[place(*job)] = [*job, *arrival(*job)]
    here = lax.axis_index("row") * GROUPS + lax.axis_index("col")
    job = lax.dynamic_index_in_dim(jnp.array(jobs), here, 0, keepdims=False)
    panel, mine, order = job[0], job[1], job[2:]

    base = panel * local_rows
    own = lax.dynamic_slice_in_dim(columns, base, local_rows, 0)
    goal = lax.dynamic_slice_in_dim(own, mine * group, group, 1)
    held = lax.dynamic_slice_in_dim(columns, mine * group, group, 1)
    own = jnp.take(own.reshape(local_rows, GROUPS, group), order, axis=1)
    own = own.reshape(local_rows, stored)
    distance = jnp.mod(own - base + total // 2, total) - total // 2
    owner = jnp.floor_divide(distance, local_rows)
    index = table_panel(owner, panel) * local_rows + distance - owner * local_rows
    index = index.reshape(-1)

    part = lax.ppermute(density, AXES, route(start, between))
    part, own, goal, held, index = lax.optimization_barrier((part, own, goal, held, index))
    part = send(part, between)

    held = jnp.take(held, own.reshape(-1), axis=0).reshape(local_rows, stored, group)
    lane_slot = jnp.arange(lanes, dtype=jnp.int32) // width
    found = jnp.where(lane_slot == 0, held[..., :1], held[..., 1:])
    direct = jnp.where(lane_slot == 0, goal[:, None, :1], goal[:, None, 1:])
    swapped = jnp.where(lane_slot == 0, goal[:, None, 1:], goal[:, None, :1])
    mask = jnp.concatenate([found == direct, found == swapped], axis=-1)
    mask = mask.astype(jnp.float32).reshape(local_rows * stored, 2 * lanes)

    part, index, mask = lax.optimization_barrier((part, index, mask))

    one, two, three = gather_column(part)
    pair = jnp.concatenate([two, three], axis=0)
    outer, rest = pass_rows(pair, one)
    near = gather_ring(part, X_RINGS)
    near, outer, rest = lax.optimization_barrier((near, outer, rest))
    left = gather_row(near)
    table = [part, one, pair, outer, rest]
    square = product(index, mask, table, left, local_rows, False)
    left = gather_row(gather_ring(square, X_RINGS))
    result = product(index, mask, table, left + [square], local_rows, True)
    return lax.ppermute(result, AXES, route(place, start)).astype(jnp.float32)


def solution(mesh):
    placed = (P("row", None, "col"), P())
    return jax.shard_map(
        shards, mesh=mesh, in_specs=placed, out_specs=P("row", None, "col"), check_vma=False
    )
```

time: 139 us -> 131 us (0.942)
  blocking collectives: 0 us -> 18.1 us
  starting transfers between devices: 72.7 us -> 55.4 us
  waiting for transfers between devices: 49.1 us -> 38.7 us
    ppermute x14 -> x8, starting transfers between devices: 62.3 us -> 16.5 us  [send(): return lax.ppermute(value, AXES, route(source, place))]
    all_to_all x0 -> x1, starting transfers between devices: none -> 26.5 us  [gather_ring(): lax.all_to_all(copies, 'row', 0, 0, tiled=True, axis_index_groups=ring)]
    all_to_all x0 -> x1, blocking collectives: none -> 18.1 us  [gather_ring(): lax.all_to_all(copies, 'row', 0, 0, tiled=True, axis_index_groups=ring)]
    ppermute x14 -> x8, waiting for transfers between devices: 32.1 us -> 25.1 us  [send(): return lax.ppermute(value, AXES, route(source, place))]
    ppermute x1, waiting for transfers between devices: 16.9 us -> 13.6 us  [shards(): return lax.ppermute(result, AXES, route(place, start)).astype(jnp.float32)]
    ppermute x1, starting transfers between devices: 2.63 us -> 4.62 us  [shards(): return lax.ppermute(result, AXES, route(place, start)).astype(jnp.float32)]
  transfers between devices with their start and end apart: 16 -> 11, of which waited for: 8 -> 5; matrix products, arithmetic and copies ran while one was open for 5% -> 5% of each run, Pallas kernels for 0% -> 0%
where the time goes in v7:
time: 131 us; the launch traced here: 129 us
  starting transfers between devices  55.4 us (42%)
  waiting for transfers between devices  38.7 us (30%)
  blocking collectives  18.1 us (14%)
  local copies, waits for them, and re-layouts  6.29 us (5%)
  Pallas kernels  4.61 us (4%)
  between operations  3.45 us (3%)
  other arithmetic  2.55 us (2%)
    all_to_all x1, starting transfers between devices, gather_ring(): lax.all_to_all(copies, 'row', 0, 0, tiled=True, axis_index_groups=ring)  26.5 us
    ppermute x8, waiting for transfers between devices, send(): return lax.ppermute(value, AXES, route(source, place))  25.1 us
    all_to_all x1, blocking collectives, gather_ring(): lax.all_to_all(copies, 'row', 0, 0, tiled=True, axis_index_groups=ring)  18.1 us
    ppermute x8, starting transfers between devices, send(): return lax.ppermute(value, AXES, route(source, place))  16.5 us
    ppermute x1, waiting for transfers between devices, shards(): return lax.ppermute(result, AXES, route(place, start)).astype(jnp.float32)  13.6 us
    ppermute x1, starting transfers between devices, shards(): part = lax.ppermute(density, AXES, route(start, between))  7.78 us
    ppermute x1, starting transfers between devices, shards(): return lax.ppermute(result, AXES, route(place, start)).astype(jnp.float32)  4.62 us
    pallas_call x2, Pallas kernels, product(): pl.pallas_call(lambda *refs: product_kernel(count, lanes // width, keep,...  4.61 us
  transfers between devices with their start and end apart: 11, of which 5 were waited for; matrix products, arithmetic and copies ran while one was open for 5% of the time, Pallas kernels for 0%

profile of v7, /device:TPU:4, one launch (start us, length us, event | category | flops | bytes accessed | tf_op | source)
XLA Modules:
  0.0 129.1 jit_solution(3583738261445565572)
XLA Ops:
  0.0 7.8 %collective-permute-start = (bf16[16,64,128]{2,1,0:T(8,128)(2,1)}, bf16[16,64,128]{2,1,0:T(8,128)(2,1)S(1)}, u32[]{:S(2)}, u32[]{:S(2)}) collective-permute-start(bf16[16,64,128]{2,1,0:T(8,128)(2,1)} %param.3), channel_id=1, source_target_pairs={{0,128},{1,65},{2,194},{3,67},{4,132},{5,197},{6,6},{7,7},{8,144},... | collective-permute-start | bytes 786440 | tf_op jit(solution)/shard_map/ppermute | solution.py:180
  7.8 0.7 constant_dynamic-slice_fusion.2
  8.6 0.6 fusion.9
  12.7 0.8 constant_dynamic-slice_fusion
  13.5 0.8 constant_dynamic-slice_fusion.1
  14.3 0.6 gather_fusion
  15.0 0.1 gather.16
  15.2 0.2 copy.15
  15.4 0.8 dynamic_slice.15
  16.6 0.7 gather_fusion.1
  17.3 0.1 copy.14
  17.6 0.7 collective-permute-start.1
  18.4 0.1 select_compare_fusion.1
  18.6 2.3 %collective-permute-start.3 = (bf16[16,64,128]{2,1,0:T(8,128)(2,1)S(1)}, bf16[16,64,128]{2,1,0:T(8,128)(2,1)S(1)}, u32[]{:S(2)}, u32[]{:S(2)}) collective-permute-start(bf16[16,64,128]{2,1,0:T(8,128)(2,1)S(1)} %collective-permute-done.1.refs_2_), channel_id=1, source_target_pairs={{0,32},{1,33},{2,34},{3,35},{4,36},{5,37},{6,38},{7,39},{8,40},{9,... | collective-permute-start | bytes 786440 | tf_op jit(solution)/shard_map/ppermute | solution.py:65
  20.9 2.7 %collective-permute-start.4 = (bf16[16,64,128]{2,1,0:T(8,128)(2,1)S(1)}, bf16[16,64,128]{2,1,0:T(8,128)(2,1)S(1)}, u32[]{:S(2)}, u32[]{:S(2)}) collective-permute-start(bf16[16,64,128]{2,1,0:T(8,128)(2,1)S(1)} %collective-permute-done.1.refs_2_), channel_id=1, source_target_pairs={{0,48},{1,49},{2,50},{3,51},{4,52},{5,53},{6,54},{7,55},{8,56},{9,... | collective-permute-start | bytes 786440 | tf_op jit(solution)/shard_map/ppermute | solution.py:65
  23.6 1.1 pad_maximum_fusion
  24.7 26.5 %all-to-all-start = ((bf16[64,64,128]{2,1,0:T(8,128)(2,1)}), bf16[64,64,128]{2,1,0:T(8,128)(2,1)S(1)}, u32[]{:S(2)}, u32[]{:S(2)}) async-start(bf16[64,64,128]{2,1,0:T(8,128)(2,1)} %pad_maximum_fusion), calls=%async_computation | async-start | bytes 2097152 | tf_op jit(solution)/shard_map/all_to_all | solution.py:70
  51.2 1.9 %collective-permute-start.2 = (bf16[16,64,128]{2,1,0:T(8,128)(2,1)S(1)}, bf16[16,64,128]{2,1,0:T(8,128)(2,1)S(1)}, u32[]{:S(2)}, u32[]{:S(2)}) collective-permute-start(bf16[16,64,128]{2,1,0:T(8,128)(2,1)S(1)} %collective-permute-done.1.refs_2_), channel_id=1, source_target_pairs={{0,16},{1,17},{2,18},{3,19},{4,20},{5,21},{6,22},{7,23},{8,24},{9,... | collective-permute-start | bytes 786440 | tf_op jit(solution)/shard_map/ppermute | solution.py:65
  53.2 2.3 %collective-permute-start.5 = (bf16[32,64,128]{2,1,0:T(8,128)(2,1)S(1)}, bf16[32,64,128]{2,1,0:T(8,128)(2,1)S(1)}, u32[]{:S(2)}, u32[]{:S(2)}) collective-permute-start(bf16[32,64,128]{2,1,0:T(8,128)(2,1)S(1)} %constant_dynamic-update-slice_fusion.refs_4_), channel_id=1, source_target_pairs={{0,1},{1,138},{2,3},{3,196},{4,5},{5,70},{6,7},{7,328},{8,9},{9,20... | collective-permute-start | bytes 1572872 | tf_op jit(solution)/shard_map/ppermute | solution.py:65
  55.5 3.9 %collective-permute-done.2.refs_3_ = bf16[16,64,128]{2,1,0:T(8,128)(2,1)S(1)} collective-permute-done((bf16[16,64,128]{2,1,0:T(8,128)(2,1)S(1)}, bf16[16,64,128]{2,1,0:T(8,128)(2,1)S(1)}, u32[]{:S(2)}, u32[]{:S(2)}) %collective-permute-start.2) | collective-permute-done | bytes 262176 | tf_op jit(solution)/shard_map/ppermute | solution.py:65
  59.4 2.3 %collective-permute-start.6 = (bf16[16,64,128]{2,1,0:T(8,128)(2,1)S(1)}, bf16[16,64,128]{2,1,0:T(8,128)(2,1)S(1)}, u32[]{:S(2)}, u32[]{:S(2)}) collective-permute-start(bf16[16,64,128]{2,1,0:T(8,128)(2,1)S(1)} %collective-permute-done.2.refs_3_), channel_id=1, source_target_pairs={{0,1},{1,138},{2,3},{3,196},{4,5},{5,70},{6,7},{7,328},{8,9},{9,20... | collective-permute-start | bytes 786440 | tf_op jit(solution)/shard_map/ppermute | solution.py:65
  61.7 16.3 %collective-permute-done.6.refs_6_ = bf16[16,64,128]{2,1,0:T(8,128)(2,1)S(1)} collective-permute-done((bf16[16,64,128]{2,1,0:T(8,128)(2,1)S(1)}, bf16[16,64,128]{2,1,0:T(8,128)(2,1)S(1)}, u32[]{:S(2)}, u32[]{:S(2)}) %collective-permute-start.6) | collective-permute-done | bytes 262176 | tf_op jit(solution)/shard_map/ppermute | solution.py:65
  78.0 2.3 %collective-permute-start.7 = (bf16[64,64,128]{2,1,0:T(8,128)(2,1)S(1)}, bf16[64,64,128]{2,1,0:T(8,128)(2,1)S(1)}, u32[]{:S(2)}, u32[]{:S(2)}) collective-permute-start(bf16[64,64,128]{2,1,0:T(8,128)(2,1)S(1)} %all-to-all-done.refs_7_), channel_id=1, source_target_pairs={{0,8},{1,9},{2,10},{3,11},{4,12},{5,13},{6,14},{7,15},{8,0},{9,1},... | collective-permute-start | bytes 3145736 | tf_op jit(solution)/shard_map/ppermute | solution.py:65
  80.4 2.3 %collective-permute-done.7.refs_8_ = bf16[64,64,128]{2,1,0:T(8,128)(2,1)S(1)} collective-permute-done((bf16[64,64,128]{2,1,0:T(8,128)(2,1)S(1)}, bf16[64,64,128]{2,1,0:T(8,128)(2,1)S(1)}, u32[]{:S(2)}, u32[]{:S(2)}) %collective-permute-start.7) | collective-permute-done | bytes 1048608 | tf_op jit(solution)/shard_map/ppermute | solution.py:65
  82.6 2.3 %shard_map.37.refs_9_ = bf16[16,64,128]{2,1,0:T(8,128)(2,1)S(1)} custom-call(s32[256]{0:T(256)S(1)} %fusion.5.refs_0_, f32[256,256]{1,0:T(8,128)S(1)} %add_convert_fusion.refs_1_, bf16[16,64,128]{2,1,0:T(8,128)(2,1)S(1)} %collective-permute-done.1.refs_2_, bf16[16,64,128]{2,1,0:T(8,128)(2,1)S(1)} %collective-permute-done.2.refs_3_, ...), custom_call_target="tpu_custom_call" | custom-call | flops 536870912 | bytes 8388608 | tf_op jit(solution)/shard_map/pallas_call | solution.py:139
  85.1 18.1 %all_to_all.10.refs_7_ = bf16[64,64,128]{2,1,0:T(8,128)(2,1)S(1)} all-to-all(bf16[64,64,128]{2,1,0:T(8,128)(2,1)S(1)} %pad_maximum_fusion.1), channel_id=1, replica_groups={{0,64,128,192},{8,72,136,200},{16,80,144,208},{24,88,152,216},{32,96,16..., dimensions={0} | all-to-all | bytes 2097152 | tf_op jit(solution)/shard_map/all_to_all | solution.py:70
  103.2 1.9 %collective-permute-start.8 = (bf16[64,64,128]{2,1,0:T(8,128)(2,1)S(1)}, bf16[64,64,128]{2,1,0:T(8,128)(2,1)S(1)}, u32[]{:S(2)}, u32[]{:S(2)}) collective-permute-start(bf16[64,64,128]{2,1,0:T(8,128)(2,1)S(1)} %all_to_all.10.refs_7_), channel_id=1, source_target_pairs={{0,8},{1,9},{2,10},{3,11},{4,12},{5,13},{6,14},{7,15},{8,0},{9,1},... | collective-permute-start | bytes 3145736 | tf_op jit(solution)/shard_map/ppermute | solution.py:65
  105.1 2.6 %collective-permute-done.8.refs_8_ = bf16[64,64,128]{2,1,0:T(8,128)(2,1)S(1)} collective-permute-done((bf16[64,64,128]{2,1,0:T(8,128)(2,1)S(1)}, bf16[64,64,128]{2,1,0:T(8,128)(2,1)S(1)}, u32[]{:S(2)}, u32[]{:S(2)}) %collective-permute-start.8) | collective-permute-done | bytes 1048608 | tf_op jit(solution)/shard_map/ppermute | solution.py:65
  107.8 2.3 %shard_map.38 = bf16[16,64,128]{2,1,0:T(8,128)(2,1)S(1)} custom-call(s32[256]{0:T(256)S(1)} %fusion.5.refs_0_, f32[256,256]{1,0:T(8,128)S(1)} %add_convert_fusion.refs_1_, bf16[16,64,128]{2,1,0:T(8,128)(2,1)S(1)} %collective-permute-done.1.refs_2_, bf16[16,64,128]{2,1,0:T(8,128)(2,1)S(1)} %collective-permute-done.2.refs_3_, ...), custom_call_target="tpu_custom_call" | custom-call | flops 536870912 | bytes 8388608 | tf_op jit(solution)/shard_map/pallas_call | solution.py:139
  110.1 4.6 %collective-permute-start.9 = (bf16[16,64,128]{2,1,0:T(8,128)(2,1)S(1)}, bf16[16,64,128]{2,1,0:T(8,128)(2,1)S(1)}, u32[]{:S(2)}, u32[]{:S(2)}) collective-permute-start(bf16[16,64,128]{2,1,0:T(8,128)(2,1)S(1)} %shard_map.38), channel_id=1, source_target_pairs={{0,6},{1,38},{2,65},{3,97},{4,128},{5,160},{6,195},{7,227},{8,7},{... | collective-permute-start | bytes 786440 | tf_op jit(solution)/shard_map/ppermute | solution.py:204
  114.7 13.6 %collective-permute-done.9 = bf16[16,64,128]{2,1,0:T(8,128)(2,1)S(1)} collective-permute-done((bf16[16,64,128]{2,1,0:T(8,128)(2,1)S(1)}, bf16[16,64,128]{2,1,0:T(8,128)(2,1)S(1)}, u32[]{:S(2)}, u32[]{:S(2)}) %collective-permute-start.9) | collective-permute-done | bytes 262176 | tf_op jit(solution)/shard_map/ppermute | solution.py:204
  128.3 0.8 convert_element_type.8
  (33 shorter events, 1.4 us)
Async XLA Ops:
  0.0 16.3 %collective-permute-start = (bf16[16,64,128]{2,1,0:T(8,128)(2,1)}, bf16[16,64,128]{2,1,0:T(8,128)(2,1)S(1)}, u32[]{:S(2)}, u32[]{:S(2)}) collective-permute-start(bf16[16,64,128]{2,1,0:T(8,128)(2,1)} %param.3), channel_id=1, source_target_pairs={{0,128},{1,65},{2,194},{3,67},{4,132},{5,197},{6,6},{7,7},{8,144},... | collective-permute-start | bytes 786440 | tf_op jit(solution)/shard_map/ppermute | solution.py:180
  17.6 0.9 collective-permute-start.1
  18.6 34.5 %collective-permute-start.3 = (bf16[16,64,128]{2,1,0:T(8,128)(2,1)S(1)}, bf16[16,64,128]{2,1,0:T(8,128)(2,1)S(1)}, u32[]{:S(2)}, u32[]{:S(2)}) collective-permute-start(bf16[16,64,128]{2,1,0:T(8,128)(2,1)S(1)} %collective-permute-done.1.refs_2_), channel_id=1, source_target_pairs={{0,32},{1,33},{2,34},{3,35},{4,36},{5,37},{6,38},{7,39},{8,40},{9,... | collective-permute-start | bytes 786440 | tf_op jit(solution)/shard_map/ppermute | solution.py:65
  20.9 32.2 %collective-permute-start.4 = (bf16[16,64,128]{2,1,0:T(8,128)(2,1)S(1)}, bf16[16,64,128]{2,1,0:T(8,128)(2,1)S(1)}, u32[]{:S(2)}, u32[]{:S(2)}) collective-permute-start(bf16[16,64,128]{2,1,0:T(8,128)(2,1)S(1)} %collective-permute-done.1.refs_2_), channel_id=1, source_target_pairs={{0,48},{1,49},{2,50},{3,51},{4,52},{5,53},{6,54},{7,55},{8,56},{9,... | collective-permute-start | bytes 786440 | tf_op jit(solution)/shard_map/ppermute | solution.py:65
  24.7 53.4 %all-to-all-start = ((bf16[64,64,128]{2,1,0:T(8,128)(2,1)}), bf16[64,64,128]{2,1,0:T(8,128)(2,1)S(1)}, u32[]{:S(2)}, u32[]{:S(2)}) async-start(bf16[64,64,128]{2,1,0:T(8,128)(2,1)} %pad_maximum_fusion), calls=%async_computation | async-start | bytes 2097152 | tf_op jit(solution)/shard_map/all_to_all | solution.py:70
  51.2 8.3 %collective-permute-start.2 = (bf16[16,64,128]{2,1,0:T(8,128)(2,1)S(1)}, bf16[16,64,128]{2,1,0:T(8,128)(2,1)S(1)}, u32[]{:S(2)}, u32[]{:S(2)}) collective-permute-start(bf16[16,64,128]{2,1,0:T(8,128)(2,1)S(1)} %collective-permute-done.1.refs_2_), channel_id=1, source_target_pairs={{0,16},{1,17},{2,18},{3,19},{4,20},{5,21},{6,22},{7,23},{8,24},{9,... | collective-permute-start | bytes 786440 | tf_op jit(solution)/shard_map/ppermute | solution.py:65
  53.2 24.9 %collective-permute-start.5 = (bf16[32,64,128]{2,1,0:T(8,128)(2,1)S(1)}, bf16[32,64,128]{2,1,0:T(8,128)(2,1)S(1)}, u32[]{:S(2)}, u32[]{:S(2)}) collective-permute-start(bf16[32,64,128]{2,1,0:T(8,128)(2,1)S(1)} %constant_dynamic-update-slice_fusion.refs_4_), channel_id=1, source_target_pairs={{0,1},{1,138},{2,3},{3,196},{4,5},{5,70},{6,7},{7,328},{8,9},{9,20... | collective-permute-start | bytes 1572872 | tf_op jit(solution)/shard_map/ppermute | solution.py:65
  59.4 18.6 %collective-permute-start.6 = (bf16[16,64,128]{2,1,0:T(8,128)(2,1)S(1)}, bf16[16,64,128]{2,1,0:T(8,128)(2,1)S(1)}, u32[]{:S(2)}, u32[]{:S(2)}) collective-permute-start(bf16[16,64,128]{2,1,0:T(8,128)(2,1)S(1)} %collective-permute-done.2.refs_3_), channel_id=1, source_target_pairs={{0,1},{1,138},{2,3},{3,196},{4,5},{5,70},{6,7},{7,328},{8,9},{9,20... | collective-permute-start | bytes 786440 | tf_op jit(solution)/shard_map/ppermute | solution.py:65
  78.0 4.6 %collective-permute-start.7 = (bf16[64,64,128]{2,1,0:T(8,128)(2,1)S(1)}, bf16[64,64,128]{2,1,0:T(8,128)(2,1)S(1)}, u32[]{:S(2)}, u32[]{:S(2)}) collective-permute-start(bf16[64,64,128]{2,1,0:T(8,128)(2,1)S(1)} %all-to-all-done.refs_7_), channel_id=1, source_target_pairs={{0,8},{1,9},{2,10},{3,11},{4,12},{5,13},{6,14},{7,15},{8,0},{9,1},... | collective-permute-start | bytes 3145736 | tf_op jit(solution)/shard_map/ppermute | solution.py:65
  103.2 4.5 %collective-permute-start.8 = (bf16[64,64,128]{2,1,0:T(8,128)(2,1)S(1)}, bf16[64,64,128]{2,1,0:T(8,128)(2,1)S(1)}, u32[]{:S(2)}, u32[]{:S(2)}) collective-permute-start(bf16[64,64,128]{2,1,0:T(8,128)(2,1)S(1)} %all_to_all.10.refs_7_), channel_id=1, source_target_pairs={{0,8},{1,9},{2,10},{3,11},{4,12},{5,13},{6,14},{7,15},{8,0},{9,1},... | collective-permute-start | bytes 3145736 | tf_op jit(solution)/shard_map/ppermute | solution.py:65
  110.1 18.2 %collective-permute-start.9 = (bf16[16,64,128]{2,1,0:T(8,128)(2,1)S(1)}, bf16[16,64,128]{2,1,0:T(8,128)(2,1)S(1)}, u32[]{:S(2)}, u32[]{:S(2)}) collective-permute-start(bf16[16,64,128]{2,1,0:T(8,128)(2,1)S(1)} %shard_map.38), channel_id=1, source_target_pairs={{0,6},{1,38},{2,65},{3,97},{4,128},{5,160},{6,195},{7,227},{8,7},{... | collective-permute-start | bytes 786440 | tf_op jit(solution)/shard_map/ppermute | solution.py:204

commit v8 on v7

--- a/solution.py
+++ b/solution.py
@@ -164,23 +164,21 @@
         jobs[place(*job)] = [*job, *arrival(*job)]
     here = lax.axis_index("row") * GROUPS + lax.axis_index("col")
     job = lax.dynamic_index_in_dim(jnp.array(jobs), here, 0, keepdims=False)
+    part = lax.ppermute(density, AXES, route(start, between))
+    own = lax.dynamic_slice_in_dim(columns, job[0] * local_rows, local_rows, 0)
+    part, own, job = lax.optimization_barrier((part, own, job))
+    part = send(part, between)
     panel, mine, order = job[0], job[1], job[2:]
 
     base = panel * local_rows
-    own = lax.dynamic_slice_in_dim(columns, base, local_rows, 0)
     goal = lax.dynamic_slice_in_dim(own, mine * group, group, 1)
-    held = lax.dynamic_slice_in_dim(columns, mine * group, group, 1)
     own = jnp.take(own.reshape(local_rows, GROUPS, group), order, axis=1)
     own = own.reshape(local_rows, stored)
     distance = jnp.mod(own - base + total // 2, total) - total // 2
     owner = jnp.floor_divide(distance, local_rows)
     index = table_panel(owner, panel) * local_rows + distance - owner * local_rows
     index = index.reshape(-1)
-
-    part = lax.ppermute(density, AXES, route(start, between))
-    part, own, goal, held, index = lax.optimization_barrier((part, own, goal, held, index))
-    part = send(part, between)
-
+    held = lax.dynamic_slice_in_dim(columns, mine * group, group, 1)
     held = jnp.take(held, own.reshape(-1), axis=0).reshape(local_rows, stored, group)
     lane_slot = jnp.arange(lanes, dtype=jnp.int32) // width
     found = jnp.where(lane_slot == 0, held[..., :1], held[..., 1:])

time: 131 us -> 129 us (0.985)
  starting transfers between devices: 55.4 us -> 50.1 us
  waiting for transfers between devices: 38.7 us -> 43.9 us
  local copies, waits for them, and re-layouts: 6.29 us -> 4.2 us
    all_to_all x1, starting transfers between devices: 26.5 us -> 18.8 us  [gather_ring(): lax.all_to_all(copies, 'row', 0, 0, tiled=True, axis_index_groups=ring)]
    ppermute x1, waiting for transfers between devices: 0.01 us -> 4.57 us  [shards(): part = lax.ppermute(density, AXES, route(start, between))]
    ppermute x8, starting transfers between devices: 16.5 us -> 18.7 us  [send(): return lax.ppermute(value, AXES, route(source, place))]
    dynamic_slice x2 -> x1, local copies, waits for them, and re-layouts: 1.47 us -> 0.08 us  [shards(): own = lax.dynamic_slice_in_dim(columns, job[0] * local_rows, local_rows, 0)]
  transfers between devices with their start and end apart: 11 -> 11, of which waited for: 5 -> 6; matrix products, arithmetic and copies ran while one was open for 5% -> 3% of each run, Pallas kernels for 0% -> 0%
where the time goes in v8:
time: 129 us; the launch traced here: 127 us
  starting transfers between devices  50.1 us (39%)
  waiting for transfers between devices  43.9 us (34%)
  blocking collectives  17.5 us (14%)
  Pallas kernels  4.61 us (4%)
  local copies, waits for them, and re-layouts  4.2 us (3%)
  between operations  3.74 us (3%)
  other arithmetic  2.56 us (2%)
    ppermute x8, waiting for transfers between devices, send(): return lax.ppermute(value, AXES, route(source, place))  24.9 us
    all_to_all x1, starting transfers between devices, gather_ring(): lax.all_to_all(copies, 'row', 0, 0, tiled=True, axis_index_groups=ring)  18.8 us
    ppermute x8, starting transfers between devices, send(): return lax.ppermute(value, AXES, route(source, place))  18.7 us
    all_to_all x1, blocking collectives, gather_ring(): lax.all_to_all(copies, 'row', 0, 0, tiled=True, axis_index_groups=ring)  17.5 us
    ppermute x1, waiting for transfers between devices, shards(): return lax.ppermute(result, AXES, route(place, start)).astype(jnp.float32)  14.4 us
    ppermute x1, starting transfers between devices, shards(): part = lax.ppermute(density, AXES, route(start, between))  7.91 us
    ppermute x1, starting transfers between devices, shards(): return lax.ppermute(result, AXES, route(place, start)).astype(jnp.float32)  4.62 us
    pallas_call x2, Pallas kernels, product(): pl.pallas_call(lambda *refs: product_kernel(count, lanes // width, keep,...  4.61 us
  transfers between devices with their start and end apart: 11, of which 6 were waited for; matrix products, arithmetic and copies ran while one was open for 3% of the time, Pallas kernels for 0%

profile of v8, /device:TPU:4, one launch (start us, length us, event | category | flops | bytes accessed | tf_op | source)
XLA Modules:
  0.0 126.6 jit_solution(13904789013636856549)
XLA Ops:
  0.0 7.9 %collective-permute-start = (bf16[16,64,128]{2,1,0:T(8,128)(2,1)}, bf16[16,64,128]{2,1,0:T(8,128)(2,1)S(1)}, u32[]{:S(2)}, u32[]{:S(2)}) collective-permute-start(bf16[16,64,128]{2,1,0:T(8,128)(2,1)} %param.3), channel_id=1, source_target_pairs={{0,128},{1,65},{2,194},{3,67},{4,132},{5,197},{6,6},{7,7},{8,144},... | collective-permute-start | bytes 786440 | tf_op jit(solution)/shard_map/ppermute | solution.py:167
  7.9 0.7 fusion.7
  8.8 4.6 %collective-permute-done = bf16[16,64,128]{2,1,0:T(8,128)(2,1)S(1)} collective-permute-done((bf16[16,64,128]{2,1,0:T(8,128)(2,1)}, bf16[16,64,128]{2,1,0:T(8,128)(2,1)S(1)}, u32[]{:S(2)}, u32[]{:S(2)}) %collective-permute-start) | collective-permute-done | bytes 262176 | tf_op jit(solution)/shard_map/ppermute | solution.py:167
  13.4 0.6 fusion.9
  14.9 0.6 gather_fusion
  15.7 0.1 copy.17
  15.8 0.1 select_n.143
  16.0 0.7 collective-permute-start.1
  16.7 0.2 copy.19
  16.9 0.7 gather_fusion.1
  17.7 0.1 copy.18
  18.1 0.1 select_compare_fusion.1
  21.3 0.1 gather.15
  21.5 5.4 %collective-permute-start.3 = (bf16[16,64,128]{2,1,0:T(8,128)(2,1)S(1)}, bf16[16,64,128]{2,1,0:T(8,128)(2,1)S(1)}, u32[]{:S(2)}, u32[]{:S(2)}) collective-permute-start(bf16[16,64,128]{2,1,0:T(8,128)(2,1)S(1)} %collective-permute-done.1.refs_2_), channel_id=1, source_target_pairs={{0,32},{1,33},{2,34},{3,35},{4,36},{5,37},{6,38},{7,39},{8,40},{9,... | collective-permute-start | bytes 786440 | tf_op jit(solution)/shard_map/ppermute | solution.py:65
  26.9 2.7 %collective-permute-start.4 = (bf16[16,64,128]{2,1,0:T(8,128)(2,1)S(1)}, bf16[16,64,128]{2,1,0:T(8,128)(2,1)S(1)}, u32[]{:S(2)}, u32[]{:S(2)}) collective-permute-start(bf16[16,64,128]{2,1,0:T(8,128)(2,1)S(1)} %collective-permute-done.1.refs_2_), channel_id=1, source_target_pairs={{0,48},{1,49},{2,50},{3,51},{4,52},{5,53},{6,54},{7,55},{8,56},{9,... | collective-permute-start | bytes 786440 | tf_op jit(solution)/shard_map/ppermute | solution.py:65
  29.6 1.1 pad_maximum_fusion
  30.7 18.8 %all-to-all-start = ((bf16[64,64,128]{2,1,0:T(8,128)(2,1)}), bf16[64,64,128]{2,1,0:T(8,128)(2,1)S(1)}, u32[]{:S(2)}, u32[]{:S(2)}) async-start(bf16[64,64,128]{2,1,0:T(8,128)(2,1)} %pad_maximum_fusion), calls=%async_computation | async-start | bytes 2097152 | tf_op jit(solution)/shard_map/all_to_all | solution.py:70
  49.5 1.9 %collective-permute-start.2 = (bf16[16,64,128]{2,1,0:T(8,128)(2,1)S(1)}, bf16[16,64,128]{2,1,0:T(8,128)(2,1)S(1)}, u32[]{:S(2)}, u32[]{:S(2)}) collective-permute-start(bf16[16,64,128]{2,1,0:T(8,128)(2,1)S(1)} %collective-permute-done.1.refs_2_), channel_id=1, source_target_pairs={{0,16},{1,17},{2,18},{3,19},{4,20},{5,21},{6,22},{7,23},{8,24},{9,... | collective-permute-start | bytes 786440 | tf_op jit(solution)/shard_map/ppermute | solution.py:65
  51.5 1.9 %collective-permute-start.5 = (bf16[32,64,128]{2,1,0:T(8,128)(2,1)S(1)}, bf16[32,64,128]{2,1,0:T(8,128)(2,1)S(1)}, u32[]{:S(2)}, u32[]{:S(2)}) collective-permute-start(bf16[32,64,128]{2,1,0:T(8,128)(2,1)S(1)} %constant_dynamic-update-slice_fusion.refs_4_), channel_id=1, source_target_pairs={{0,1},{1,138},{2,3},{3,196},{4,5},{5,70},{6,7},{7,328},{8,9},{9,20... | collective-permute-start | bytes 1572872 | tf_op jit(solution)/shard_map/ppermute | solution.py:65
  53.4 6.4 %collective-permute-done.2.refs_3_ = bf16[16,64,128]{2,1,0:T(8,128)(2,1)S(1)} collective-permute-done((bf16[16,64,128]{2,1,0:T(8,128)(2,1)S(1)}, bf16[16,64,128]{2,1,0:T(8,128)(2,1)S(1)}, u32[]{:S(2)}, u32[]{:S(2)}) %collective-permute-start.2) | collective-permute-done | bytes 262176 | tf_op jit(solution)/shard_map/ppermute | solution.py:65
  59.8 1.9 %collective-permute-start.6 = (bf16[16,64,128]{2,1,0:T(8,128)(2,1)S(1)}, bf16[16,64,128]{2,1,0:T(8,128)(2,1)S(1)}, u32[]{:S(2)}, u32[]{:S(2)}) collective-permute-start(bf16[16,64,128]{2,1,0:T(8,128)(2,1)S(1)} %collective-permute-done.2.refs_3_), channel_id=1, source_target_pairs={{0,1},{1,138},{2,3},{3,196},{4,5},{5,70},{6,7},{7,328},{8,9},{9,20... | collective-permute-start | bytes 786440 | tf_op jit(solution)/shard_map/ppermute | solution.py:65
  61.7 13.7 %collective-permute-done.6.refs_6_ = bf16[16,64,128]{2,1,0:T(8,128)(2,1)S(1)} collective-permute-done((bf16[16,64,128]{2,1,0:T(8,128)(2,1)S(1)}, bf16[16,64,128]{2,1,0:T(8,128)(2,1)S(1)}, u32[]{:S(2)}, u32[]{:S(2)}) %collective-permute-start.6) | collective-permute-done | bytes 262176 | tf_op jit(solution)/shard_map/ppermute | solution.py:65
  75.4 2.3 %collective-permute-start.7 = (bf16[64,64,128]{2,1,0:T(8,128)(2,1)S(1)}, bf16[64,64,128]{2,1,0:T(8,128)(2,1)S(1)}, u32[]{:S(2)}, u32[]{:S(2)}) collective-permute-start(bf16[64,64,128]{2,1,0:T(8,128)(2,1)S(1)} %all-to-all-done.refs_7_), channel_id=1, source_target_pairs={{0,8},{1,9},{2,10},{3,11},{4,12},{5,13},{6,14},{7,15},{8,0},{9,1},... | collective-permute-start | bytes 3145736 | tf_op jit(solution)/shard_map/ppermute | solution.py:65
  77.7 2.3 %collective-permute-done.7.refs_8_ = bf16[64,64,128]{2,1,0:T(8,128)(2,1)S(1)} collective-permute-done((bf16[64,64,128]{2,1,0:T(8,128)(2,1)S(1)}, bf16[64,64,128]{2,1,0:T(8,128)(2,1)S(1)}, u32[]{:S(2)}, u32[]{:S(2)}) %collective-permute-start.7) | collective-permute-done | bytes 1048608 | tf_op jit(solution)/shard_map/ppermute | solution.py:65
  80.0 2.3 %shard_map.37.refs_9_ = bf16[16,64,128]{2,1,0:T(8,128)(2,1)S(1)} custom-call(s32[256]{0:T(256)S(1)} %fusion.5.refs_0_, f32[256,256]{1,0:T(8,128)S(1)} %add_convert_fusion.refs_1_, bf16[16,64,128]{2,1,0:T(8,128)(2,1)S(1)} %collective-permute-done.1.refs_2_, bf16[16,64,128]{2,1,0:T(8,128)(2,1)S(1)} %collective-permute-done.2.refs_3_, ...), custom_call_target="tpu_custom_call" | custom-call | flops 536870912 | bytes 8388608 | tf_op jit(solution)/shard_map/pallas_call | solution.py:139
  82.4 17.5 %all_to_all.10.refs_7_ = bf16[64,64,128]{2,1,0:T(8,128)(2,1)S(1)} all-to-all(bf16[64,64,128]{2,1,0:T(8,128)(2,1)S(1)} %pad_maximum_fusion.1), channel_id=1, replica_groups={{0,64,128,192},{8,72,136,200},{16,80,144,208},{24,88,152,216},{32,96,16..., dimensions={0} | all-to-all | bytes 2097152 | tf_op jit(solution)/shard_map/all_to_all | solution.py:70
  99.9 1.9 %collective-permute-start.8 = (bf16[64,64,128]{2,1,0:T(8,128)(2,1)S(1)}, bf16[64,64,128]{2,1,0:T(8,128)(2,1)S(1)}, u32[]{:S(2)}, u32[]{:S(2)}) collective-permute-start(bf16[64,64,128]{2,1,0:T(8,128)(2,1)S(1)} %all_to_all.10.refs_7_), channel_id=1, source_target_pairs={{0,8},{1,9},{2,10},{3,11},{4,12},{5,13},{6,14},{7,15},{8,0},{9,1},... | collective-permute-start | bytes 3145736 | tf_op jit(solution)/shard_map/ppermute | solution.py:65
  101.8 2.6 %collective-permute-done.8.refs_8_ = bf16[64,64,128]{2,1,0:T(8,128)(2,1)S(1)} collective-permute-done((bf16[64,64,128]{2,1,0:T(8,128)(2,1)S(1)}, bf16[64,64,128]{2,1,0:T(8,128)(2,1)S(1)}, u32[]{:S(2)}, u32[]{:S(2)}) %collective-permute-start.8) | collective-permute-done | bytes 1048608 | tf_op jit(solution)/shard_map/ppermute | solution.py:65
  104.5 2.3 %shard_map.38 = bf16[16,64,128]{2,1,0:T(8,128)(2,1)S(1)} custom-call(s32[256]{0:T(256)S(1)} %fusion.5.refs_0_, f32[256,256]{1,0:T(8,128)S(1)} %add_convert_fusion.refs_1_, bf16[16,64,128]{2,1,0:T(8,128)(2,1)S(1)} %collective-permute-done.1.refs_2_, bf16[16,64,128]{2,1,0:T(8,128)(2,1)S(1)} %collective-permute-done.2.refs_3_, ...), custom_call_target="tpu_custom_call" | custom-call | flops 536870912 | bytes 8388608 | tf_op jit(solution)/shard_map/pallas_call | solution.py:139
  106.8 4.6 %collective-permute-start.9 = (bf16[16,64,128]{2,1,0:T(8,128)(2,1)S(1)}, bf16[16,64,128]{2,1,0:T(8,128)(2,1)S(1)}, u32[]{:S(2)}, u32[]{:S(2)}) collective-permute-start(bf16[16,64,128]{2,1,0:T(8,128)(2,1)S(1)} %shard_map.38), channel_id=1, source_target_pairs={{0,6},{1,38},{2,65},{3,97},{4,128},{5,160},{6,195},{7,227},{8,7},{... | collective-permute-start | bytes 786440 | tf_op jit(solution)/shard_map/ppermute | solution.py:202
  111.4 14.4 %collective-permute-done.9 = bf16[16,64,128]{2,1,0:T(8,128)(2,1)S(1)} collective-permute-done((bf16[16,64,128]{2,1,0:T(8,128)(2,1)S(1)}, bf16[16,64,128]{2,1,0:T(8,128)(2,1)S(1)}, u32[]{:S(2)}, u32[]{:S(2)}) %collective-permute-start.9) | collective-permute-done | bytes 262176 | tf_op jit(solution)/shard_map/ppermute | solution.py:202
  125.8 0.8 convert_element_type.8
  (34 shorter events, 1.3 us)
Async XLA Ops:
  0.0 8.7 %copy-start = (s32[1024,16]{0,1:T(8,128)S(1)}, s32[1024,16]{0,1:T(8,128)}, u32[]{:S(2)}) copy-start(s32[1024,16]{0,1:T(8,128)} %param.4) | copy-start | bytes 196612
  0.0 13.3 %collective-permute-start = (bf16[16,64,128]{2,1,0:T(8,128)(2,1)}, bf16[16,64,128]{2,1,0:T(8,128)(2,1)S(1)}, u32[]{:S(2)}, u32[]{:S(2)}) collective-permute-start(bf16[16,64,128]{2,1,0:T(8,128)(2,1)} %param.3), channel_id=1, source_target_pairs={{0,128},{1,65},{2,194},{3,67},{4,132},{5,197},{6,6},{7,7},{8,144},... | collective-permute-start | bytes 786440 | tf_op jit(solution)/shard_map/ppermute | solution.py:167
  16.0 5.4 %collective-permute-start.1 = (bf16[16,64,128]{2,1,0:T(8,128)(2,1)S(1)}, bf16[16,64,128]{2,1,0:T(8,128)(2,1)S(1)}, u32[]{:S(2)}, u32[]{:S(2)}) collective-permute-start(bf16[16,64,128]{2,1,0:T(8,128)(2,1)S(1)} %collective-permute-done), channel_id=1, source_target_pairs={{0,4},{1,2},{2,10},{3,6},{4,12},{5,14},{6,0},{7,8},{8,5},{9,3},{10... | collective-permute-start | bytes 786440 | tf_op jit(solution)/shard_map/ppermute | solution.py:65
  21.5 29.9 %collective-permute-start.3 = (bf16[16,64,128]{2,1,0:T(8,128)(2,1)S(1)}, bf16[16,64,128]{2,1,0:T(8,128)(2,1)S(1)}, u32[]{:S(2)}, u32[]{:S(2)}) collective-permute-start(bf16[16,64,128]{2,1,0:T(8,128)(2,1)S(1)} %collective-permute-done.1.refs_2_), channel_id=1, source_target_pairs={{0,32},{1,33},{2,34},{3,35},{4,36},{5,37},{6,38},{7,39},{8,40},{9,... | collective-permute-start | bytes 786440 | tf_op jit(solution)/shard_map/ppermute | solution.py:65
  26.9 24.5 %collective-permute-start.4 = (bf16[16,64,128]{2,1,0:T(8,128)(2,1)S(1)}, bf16[16,64,128]{2,1,0:T(8,128)(2,1)S(1)}, u32[]{:S(2)}, u32[]{:S(2)}) collective-permute-start(bf16[16,64,128]{2,1,0:T(8,128)(2,1)S(1)} %collective-permute-done.1.refs_2_), channel_id=1, source_target_pairs={{0,48},{1,49},{2,50},{3,51},{4,52},{5,53},{6,54},{7,55},{8,56},{9,... | collective-permute-start | bytes 786440 | tf_op jit(solution)/shard_map/ppermute | solution.py:65
  30.7 44.7 %all-to-all-start = ((bf16[64,64,128]{2,1,0:T(8,128)(2,1)}), bf16[64,64,128]{2,1,0:T(8,128)(2,1)S(1)}, u32[]{:S(2)}, u32[]{:S(2)}) async-start(bf16[64,64,128]{2,1,0:T(8,128)(2,1)} %pad_maximum_fusion), calls=%async_computation | async-start | bytes 2097152 | tf_op jit(solution)/shard_map/all_to_all | solution.py:70
  49.5 10.3 %collective-permute-start.2 = (bf16[16,64,128]{2,1,0:T(8,128)(2,1)S(1)}, bf16[16,64,128]{2,1,0:T(8,128)(2,1)S(1)}, u32[]{:S(2)}, u32[]{:S(2)}) collective-permute-start(bf16[16,64,128]{2,1,0:T(8,128)(2,1)S(1)} %collective-permute-done.1.refs_2_), channel_id=1, source_target_pairs={{0,16},{1,17},{2,18},{3,19},{4,20},{5,21},{6,22},{7,23},{8,24},{9,... | collective-permute-start | bytes 786440 | tf_op jit(solution)/shard_map/ppermute | solution.py:65
  51.5 23.9 %collective-permute-start.5 = (bf16[32,64,128]{2,1,0:T(8,128)(2,1)S(1)}, bf16[32,64,128]{2,1,0:T(8,128)(2,1)S(1)}, u32[]{:S(2)}, u32[]{:S(2)}) collective-permute-start(bf16[32,64,128]{2,1,0:T(8,128)(2,1)S(1)} %constant_dynamic-update-slice_fusion.refs_4_), channel_id=1, source_target_pairs={{0,1},{1,138},{2,3},{3,196},{4,5},{5,70},{6,7},{7,328},{8,9},{9,20... | collective-permute-start | bytes 1572872 | tf_op jit(solution)/shard_map/ppermute | solution.py:65
  59.8 15.6 %collective-permute-start.6 = (bf16[16,64,128]{2,1,0:T(8,128)(2,1)S(1)}, bf16[16,64,128]{2,1,0:T(8,128)(2,1)S(1)}, u32[]{:S(2)}, u32[]{:S(2)}) collective-permute-start(bf16[16,64,128]{2,1,0:T(8,128)(2,1)S(1)} %collective-permute-done.2.refs_3_), channel_id=1, source_target_pairs={{0,1},{1,138},{2,3},{3,196},{4,5},{5,70},{6,7},{7,328},{8,9},{9,20... | collective-permute-start | bytes 786440 | tf_op jit(solution)/shard_map/ppermute | solution.py:65
  75.4 4.6 %collective-permute-start.7 = (bf16[64,64,128]{2,1,0:T(8,128)(2,1)S(1)}, bf16[64,64,128]{2,1,0:T(8,128)(2,1)S(1)}, u32[]{:S(2)}, u32[]{:S(2)}) collective-permute-start(bf16[64,64,128]{2,1,0:T(8,128)(2,1)S(1)} %all-to-all-done.refs_7_), channel_id=1, source_target_pairs={{0,8},{1,9},{2,10},{3,11},{4,12},{5,13},{6,14},{7,15},{8,0},{9,1},... | collective-permute-start | bytes 3145736 | tf_op jit(solution)/shard_map/ppermute | solution.py:65
  99.9 4.5 %collective-permute-start.8 = (bf16[64,64,128]{2,1,0:T(8,128)(2,1)S(1)}, bf16[64,64,128]{2,1,0:T(8,128)(2,1)S(1)}, u32[]{:S(2)}, u32[]{:S(2)}) collective-permute-start(bf16[64,64,128]{2,1,0:T(8,128)(2,1)S(1)} %all_to_all.10.refs_7_), channel_id=1, source_target_pairs={{0,8},{1,9},{2,10},{3,11},{4,12},{5,13},{6,14},{7,15},{8,0},{9,1},... | collective-permute-start | bytes 3145736 | tf_op jit(solution)/shard_map/ppermute | solution.py:65
  106.8 19.0 %collective-permute-start.9 = (bf16[16,64,128]{2,1,0:T(8,128)(2,1)S(1)}, bf16[16,64,128]{2,1,0:T(8,128)(2,1)S(1)}, u32[]{:S(2)}, u32[]{:S(2)}) collective-permute-start(bf16[16,64,128]{2,1,0:T(8,128)(2,1)S(1)} %shard_map.38), channel_id=1, source_target_pairs={{0,6},{1,38},{2,65},{3,97},{4,128},{5,160},{6,195},{7,227},{8,7},{... | collective-permute-start | bytes 786440 | tf_op jit(solution)/shard_map/ppermute | solution.py:202

commit v9 on v8

--- a/solution.py
+++ b/solution.py
@@ -159,21 +159,25 @@
     group = lanes // width
     total, stored = columns.shape
 
-    jobs = np.zeros((PANELS * GROUPS, 2 + GROUPS), np.int32)
+    jobs = np.zeros((PANELS * GROUPS, 2, GROUPS), np.int32)
     for job in JOBS:
-        jobs[place(*job)] = [*job, *arrival(*job)]
+        jobs[place(*job), 0, :2] = job
+        jobs[place(*job), 1] = arrival(*job)
     here = lax.axis_index("row") * GROUPS + lax.axis_index("col")
     job = lax.dynamic_index_in_dim(jnp.array(jobs), here, 0, keepdims=False)
     part = lax.ppermute(density, AXES, route(start, between))
-    own = lax.dynamic_slice_in_dim(columns, job[0] * local_rows, local_rows, 0)
+    own = lax.dynamic_slice_in_dim(columns, job[0, 0] * local_rows, local_rows, 0)
     part, own, job = lax.optimization_barrier((part, own, job))
     part = send(part, between)
-    panel, mine, order = job[0], job[1], job[2:]
+    panel, mine, order = job[0, 0], job[0, 1], job[1]
 
     base = panel * local_rows
     goal = lax.dynamic_slice_in_dim(own, mine * group, group, 1)
-    own = jnp.take(own.reshape(local_rows, GROUPS, group), order, axis=1)
-    own = own.reshape(local_rows, stored)
+    chosen = order[:, None] == jnp.arange(GROUPS, dtype=jnp.int32)[None, :]
+    own = jnp.sum(
+        jnp.where(chosen[None, :, :, None], own.reshape(local_rows, 1, GROUPS, group), 0),
+        axis=2,
+    ).reshape(local_rows, stored)
     distance = jnp.mod(own - base + total // 2, total) - total // 2
     owner = jnp.floor_divide(distance, local_rows)
     index = table_panel(owner, panel) * local_rows + distance - owner * local_rows

time: 129 us -> 129 us (level)
  no operation moved by 1% of the time
where the time goes in v9:
time: 129 us; the launch traced here: 126 us
  starting transfers between devices  51.1 us (40%)
  waiting for transfers between devices  42.8 us (33%)
  blocking collectives  17.5 us (14%)
  Pallas kernels  4.61 us (4%)
  between operations  4.06 us (3%)
  local copies, waits for them, and re-layouts  3.86 us (3%)
  other arithmetic  2.51 us (2%)
    ppermute x8, waiting for transfers between devices, send(): return lax.ppermute(value, AXES, route(source, place))  24.9 us
    all_to_all x1, starting transfers between devices, gather_ring(): lax.all_to_all(copies, 'row', 0, 0, tiled=True, axis_index_groups=ring)  19.8 us
    ppermute x8, starting transfers between devices, send(): return lax.ppermute(value, AXES, route(source, place))  18.7 us
    all_to_all x1, blocking collectives, gather_ring(): lax.all_to_all(copies, 'row', 0, 0, tiled=True, axis_index_groups=ring)  17.5 us
    ppermute x1, waiting for transfers between devices, shards(): return lax.ppermute(result, AXES, route(place, start)).astype(jnp.float32)  14.4 us
    ppermute x1, starting transfers between devices, shards(): part = lax.ppermute(density, AXES, route(start, between))  7.91 us
    ppermute x1, starting transfers between devices, shards(): return lax.ppermute(result, AXES, route(place, start)).astype(jnp.float32)  4.63 us
    pallas_call x2, Pallas kernels, product(): pl.pallas_call(lambda *refs: product_kernel(count, lanes // width, keep,...  4.61 us
  transfers between devices with their start and end apart: 11, of which 6 were waited for; matrix products, arithmetic and copies ran while one was open for 3% of the time, Pallas kernels for 0%

profile of v9, /device:TPU:4, one launch (start us, length us, event | category | flops | bytes accessed | tf_op | source)
XLA Modules:
  0.0 126.5 jit_solution(7447352878766011825)
XLA Ops:
  0.0 7.9 %collective-permute-start = (bf16[16,64,128]{2,1,0:T(8,128)(2,1)}, bf16[16,64,128]{2,1,0:T(8,128)(2,1)S(1)}, u32[]{:S(2)}, u32[]{:S(2)}) collective-permute-start(bf16[16,64,128]{2,1,0:T(8,128)(2,1)} %param.3), channel_id=1, source_target_pairs={{0,128},{1,65},{2,194},{3,67},{4,132},{5,197},{6,6},{7,7},{8,144},... | collective-permute-start | bytes 786440 | tf_op jit(solution)/shard_map/ppermute | solution.py:168
  7.9 0.7 dynamic-slice_bitcast_fusion
  8.6 0.5 slice.26
  9.9 3.5 %collective-permute-done = bf16[16,64,128]{2,1,0:T(8,128)(2,1)S(1)} collective-permute-done((bf16[16,64,128]{2,1,0:T(8,128)(2,1)}, bf16[16,64,128]{2,1,0:T(8,128)(2,1)S(1)}, u32[]{:S(2)}, u32[]{:S(2)}) %collective-permute-start) | collective-permute-done | bytes 262176 | tf_op jit(solution)/shard_map/ppermute | solution.py:168
  13.4 0.6 fusion.9
  15.4 0.1 copy.22
  15.7 0.1 reshape_reshape.3
  15.8 0.7 collective-permute-start.1
  16.5 0.2 copy.24
  16.8 0.7 gather_fusion
  17.5 0.1 copy.23
  17.9 0.1 select_compare_fusion.1
  20.1 0.1 add.86
  20.3 5.4 %collective-permute-start.3 = (bf16[16,64,128]{2,1,0:T(8,128)(2,1)S(1)}, bf16[16,64,128]{2,1,0:T(8,128)(2,1)S(1)}, u32[]{:S(2)}, u32[]{:S(2)}) collective-permute-start(bf16[16,64,128]{2,1,0:T(8,128)(2,1)S(1)} %collective-permute-done.1.refs_2_), channel_id=1, source_target_pairs={{0,32},{1,33},{2,34},{3,35},{4,36},{5,37},{6,38},{7,39},{8,40},{9,... | collective-permute-start | bytes 786440 | tf_op jit(solution)/shard_map/ppermute | solution.py:65
  25.7 2.7 %collective-permute-start.4 = (bf16[16,64,128]{2,1,0:T(8,128)(2,1)S(1)}, bf16[16,64,128]{2,1,0:T(8,128)(2,1)S(1)}, u32[]{:S(2)}, u32[]{:S(2)}) collective-permute-start(bf16[16,64,128]{2,1,0:T(8,128)(2,1)S(1)} %collective-permute-done.1.refs_2_), channel_id=1, source_target_pairs={{0,48},{1,49},{2,50},{3,51},{4,52},{5,53},{6,54},{7,55},{8,56},{9,... | collective-permute-start | bytes 786440 | tf_op jit(solution)/shard_map/ppermute | solution.py:65
  28.4 1.1 pad_maximum_fusion
  29.5 19.8 %all-to-all-start = ((bf16[64,64,128]{2,1,0:T(8,128)(2,1)}), bf16[64,64,128]{2,1,0:T(8,128)(2,1)S(1)}, u32[]{:S(2)}, u32[]{:S(2)}) async-start(bf16[64,64,128]{2,1,0:T(8,128)(2,1)} %pad_maximum_fusion), calls=%async_computation | async-start | bytes 2097152 | tf_op jit(solution)/shard_map/all_to_all | solution.py:70
  49.3 1.9 %collective-permute-start.2 = (bf16[16,64,128]{2,1,0:T(8,128)(2,1)S(1)}, bf16[16,64,128]{2,1,0:T(8,128)(2,1)S(1)}, u32[]{:S(2)}, u32[]{:S(2)}) collective-permute-start(bf16[16,64,128]{2,1,0:T(8,128)(2,1)S(1)} %collective-permute-done.1.refs_2_), channel_id=1, source_target_pairs={{0,16},{1,17},{2,18},{3,19},{4,20},{5,21},{6,22},{7,23},{8,24},{9,... | collective-permute-start | bytes 786440 | tf_op jit(solution)/shard_map/ppermute | solution.py:65
  51.3 1.9 %collective-permute-start.5 = (bf16[32,64,128]{2,1,0:T(8,128)(2,1)S(1)}, bf16[32,64,128]{2,1,0:T(8,128)(2,1)S(1)}, u32[]{:S(2)}, u32[]{:S(2)}) collective-permute-start(bf16[32,64,128]{2,1,0:T(8,128)(2,1)S(1)} %constant_dynamic-update-slice_fusion.refs_4_), channel_id=1, source_target_pairs={{0,1},{1,138},{2,3},{3,196},{4,5},{5,70},{6,7},{7,328},{8,9},{9,20... | collective-permute-start | bytes 1572872 | tf_op jit(solution)/shard_map/ppermute | solution.py:65
  53.2 6.4 %collective-permute-done.2.refs_3_ = bf16[16,64,128]{2,1,0:T(8,128)(2,1)S(1)} collective-permute-done((bf16[16,64,128]{2,1,0:T(8,128)(2,1)S(1)}, bf16[16,64,128]{2,1,0:T(8,128)(2,1)S(1)}, u32[]{:S(2)}, u32[]{:S(2)}) %collective-permute-start.2) | collective-permute-done | bytes 262176 | tf_op jit(solution)/shard_map/ppermute | solution.py:65
  59.6 1.9 %collective-permute-start.6 = (bf16[16,64,128]{2,1,0:T(8,128)(2,1)S(1)}, bf16[16,64,128]{2,1,0:T(8,128)(2,1)S(1)}, u32[]{:S(2)}, u32[]{:S(2)}) collective-permute-start(bf16[16,64,128]{2,1,0:T(8,128)(2,1)S(1)} %collective-permute-done.2.refs_3_), channel_id=1, source_target_pairs={{0,1},{1,138},{2,3},{3,196},{4,5},{5,70},{6,7},{7,328},{8,9},{9,20... | collective-permute-start | bytes 786440 | tf_op jit(solution)/shard_map/ppermute | solution.py:65
  61.5 13.7 %collective-permute-done.6.refs_6_ = bf16[16,64,128]{2,1,0:T(8,128)(2,1)S(1)} collective-permute-done((bf16[16,64,128]{2,1,0:T(8,128)(2,1)S(1)}, bf16[16,64,128]{2,1,0:T(8,128)(2,1)S(1)}, u32[]{:S(2)}, u32[]{:S(2)}) %collective-permute-start.6) | collective-permute-done | bytes 262176 | tf_op jit(solution)/shard_map/ppermute | solution.py:65
  75.2 2.3 %collective-permute-start.7 = (bf16[64,64,128]{2,1,0:T(8,128)(2,1)S(1)}, bf16[64,64,128]{2,1,0:T(8,128)(2,1)S(1)}, u32[]{:S(2)}, u32[]{:S(2)}) collective-permute-start(bf16[64,64,128]{2,1,0:T(8,128)(2,1)S(1)} %all-to-all-done.refs_7_), channel_id=1, source_target_pairs={{0,8},{1,9},{2,10},{3,11},{4,12},{5,13},{6,14},{7,15},{8,0},{9,1},... | collective-permute-start | bytes 3145736 | tf_op jit(solution)/shard_map/ppermute | solution.py:65
  77.5 2.3 %collective-permute-done.7.refs_8_ = bf16[64,64,128]{2,1,0:T(8,128)(2,1)S(1)} collective-permute-done((bf16[64,64,128]{2,1,0:T(8,128)(2,1)S(1)}, bf16[64,64,128]{2,1,0:T(8,128)(2,1)S(1)}, u32[]{:S(2)}, u32[]{:S(2)}) %collective-permute-start.7) | collective-permute-done | bytes 1048608 | tf_op jit(solution)/shard_map/ppermute | solution.py:65
  79.8 2.3 %shard_map.37.refs_9_ = bf16[16,64,128]{2,1,0:T(8,128)(2,1)S(1)} custom-call(s32[256]{0:T(256)S(1)} %fusion.6.refs_0_, f32[256,256]{1,0:T(8,128)S(1)} %add_convert_fusion.refs_1_, bf16[16,64,128]{2,1,0:T(8,128)(2,1)S(1)} %collective-permute-done.1.refs_2_, bf16[16,64,128]{2,1,0:T(8,128)(2,1)S(1)} %collective-permute-done.2.refs_3_, ...), custom_call_target="tpu_custom_call" | custom-call | flops 536870912 | bytes 8388608 | tf_op jit(solution)/shard_map/pallas_call | solution.py:139
  82.2 17.5 %all_to_all.10.refs_7_ = bf16[64,64,128]{2,1,0:T(8,128)(2,1)S(1)} all-to-all(bf16[64,64,128]{2,1,0:T(8,128)(2,1)S(1)} %pad_maximum_fusion.1), channel_id=1, replica_groups={{0,64,128,192},{8,72,136,200},{16,80,144,208},{24,88,152,216},{32,96,16..., dimensions={0} | all-to-all | bytes 2097152 | tf_op jit(solution)/shard_map/all_to_all | solution.py:70
  99.7 1.9 %collective-permute-start.8 = (bf16[64,64,128]{2,1,0:T(8,128)(2,1)S(1)}, bf16[64,64,128]{2,1,0:T(8,128)(2,1)S(1)}, u32[]{:S(2)}, u32[]{:S(2)}) collective-permute-start(bf16[64,64,128]{2,1,0:T(8,128)(2,1)S(1)} %all_to_all.10.refs_7_), channel_id=1, source_target_pairs={{0,8},{1,9},{2,10},{3,11},{4,12},{5,13},{6,14},{7,15},{8,0},{9,1},... | collective-permute-start | bytes 3145736 | tf_op jit(solution)/shard_map/ppermute | solution.py:65
  101.7 2.6 %collective-permute-done.8.refs_8_ = bf16[64,64,128]{2,1,0:T(8,128)(2,1)S(1)} collective-permute-done((bf16[64,64,128]{2,1,0:T(8,128)(2,1)S(1)}, bf16[64,64,128]{2,1,0:T(8,128)(2,1)S(1)}, u32[]{:S(2)}, u32[]{:S(2)}) %collective-permute-start.8) | collective-permute-done | bytes 1048608 | tf_op jit(solution)/shard_map/ppermute | solution.py:65
  104.3 2.3 %shard_map.38 = bf16[16,64,128]{2,1,0:T(8,128)(2,1)S(1)} custom-call(s32[256]{0:T(256)S(1)} %fusion.6.refs_0_, f32[256,256]{1,0:T(8,128)S(1)} %add_convert_fusion.refs_1_, bf16[16,64,128]{2,1,0:T(8,128)(2,1)S(1)} %collective-permute-done.1.refs_2_, bf16[16,64,128]{2,1,0:T(8,128)(2,1)S(1)} %collective-permute-done.2.refs_3_, ...), custom_call_target="tpu_custom_call" | custom-call | flops 536870912 | bytes 8388608 | tf_op jit(solution)/shard_map/pallas_call | solution.py:139
  106.6 4.6 %collective-permute-start.9 = (bf16[16,64,128]{2,1,0:T(8,128)(2,1)S(1)}, bf16[16,64,128]{2,1,0:T(8,128)(2,1)S(1)}, u32[]{:S(2)}, u32[]{:S(2)}) collective-permute-start(bf16[16,64,128]{2,1,0:T(8,128)(2,1)S(1)} %shard_map.38), channel_id=1, source_target_pairs={{0,6},{1,38},{2,65},{3,97},{4,128},{5,160},{6,195},{7,227},{8,7},{... | collective-permute-start | bytes 786440 | tf_op jit(solution)/shard_map/ppermute | solution.py:206
  111.2 14.4 %collective-permute-done.9 = bf16[16,64,128]{2,1,0:T(8,128)(2,1)S(1)} collective-permute-done((bf16[16,64,128]{2,1,0:T(8,128)(2,1)S(1)}, bf16[16,64,128]{2,1,0:T(8,128)(2,1)S(1)}, u32[]{:S(2)}, u32[]{:S(2)}) %collective-permute-start.9) | collective-permute-done | bytes 262176 | tf_op jit(solution)/shard_map/ppermute | solution.py:206
  125.6 0.8 convert_element_type.8
  (32 shorter events, 1.0 us)
Async XLA Ops:
  0.0 9.8 %copy-start = (s32[1024,16]{0,1:T(8,128)S(1)}, s32[1024,16]{0,1:T(8,128)}, u32[]{:S(2)}) copy-start(s32[1024,16]{0,1:T(8,128)} %param.4) | copy-start | bytes 196612
  0.0 13.3 %collective-permute-start = (bf16[16,64,128]{2,1,0:T(8,128)(2,1)}, bf16[16,64,128]{2,1,0:T(8,128)(2,1)S(1)}, u32[]{:S(2)}, u32[]{:S(2)}) collective-permute-start(bf16[16,64,128]{2,1,0:T(8,128)(2,1)} %param.3), channel_id=1, source_target_pairs={{0,128},{1,65},{2,194},{3,67},{4,132},{5,197},{6,6},{7,7},{8,144},... | collective-permute-start | bytes 786440 | tf_op jit(solution)/shard_map/ppermute | solution.py:168
  15.8 4.4 %collective-permute-start.1 = (bf16[16,64,128]{2,1,0:T(8,128)(2,1)S(1)}, bf16[16,64,128]{2,1,0:T(8,128)(2,1)S(1)}, u32[]{:S(2)}, u32[]{:S(2)}) collective-permute-start(bf16[16,64,128]{2,1,0:T(8,128)(2,1)S(1)} %collective-permute-done), channel_id=1, source_target_pairs={{0,4},{1,2},{2,10},{3,6},{4,12},{5,14},{6,0},{7,8},{8,5},{9,3},{10... | collective-permute-start | bytes 786440 | tf_op jit(solution)/shard_map/ppermute | solution.py:65
  20.3 30.9 %collective-permute-start.3 = (bf16[16,64,128]{2,1,0:T(8,128)(2,1)S(1)}, bf16[16,64,128]{2,1,0:T(8,128)(2,1)S(1)}, u32[]{:S(2)}, u32[]{:S(2)}) collective-permute-start(bf16[16,64,128]{2,1,0:T(8,128)(2,1)S(1)} %collective-permute-done.1.refs_2_), channel_id=1, source_target_pairs={{0,32},{1,33},{2,34},{3,35},{4,36},{5,37},{6,38},{7,39},{8,40},{9,... | collective-permute-start | bytes 786440 | tf_op jit(solution)/shard_map/ppermute | solution.py:65
  25.7 25.5 %collective-permute-start.4 = (bf16[16,64,128]{2,1,0:T(8,128)(2,1)S(1)}, bf16[16,64,128]{2,1,0:T(8,128)(2,1)S(1)}, u32[]{:S(2)}, u32[]{:S(2)}) collective-permute-start(bf16[16,64,128]{2,1,0:T(8,128)(2,1)S(1)} %collective-permute-done.1.refs_2_), channel_id=1, source_target_pairs={{0,48},{1,49},{2,50},{3,51},{4,52},{5,53},{6,54},{7,55},{8,56},{9,... | collective-permute-start | bytes 786440 | tf_op jit(solution)/shard_map/ppermute | solution.py:65
  29.5 45.7 %all-to-all-start = ((bf16[64,64,128]{2,1,0:T(8,128)(2,1)}), bf16[64,64,128]{2,1,0:T(8,128)(2,1)S(1)}, u32[]{:S(2)}, u32[]{:S(2)}) async-start(bf16[64,64,128]{2,1,0:T(8,128)(2,1)} %pad_maximum_fusion), calls=%async_computation | async-start | bytes 2097152 | tf_op jit(solution)/shard_map/all_to_all | solution.py:70
  49.3 10.3 %collective-permute-start.2 = (bf16[16,64,128]{2,1,0:T(8,128)(2,1)S(1)}, bf16[16,64,128]{2,1,0:T(8,128)(2,1)S(1)}, u32[]{:S(2)}, u32[]{:S(2)}) collective-permute-start(bf16[16,64,128]{2,1,0:T(8,128)(2,1)S(1)} %collective-permute-done.1.refs_2_), channel_id=1, source_target_pairs={{0,16},{1,17},{2,18},{3,19},{4,20},{5,21},{6,22},{7,23},{8,24},{9,... | collective-permute-start | bytes 786440 | tf_op jit(solution)/shard_map/ppermute | solution.py:65
  51.3 23.9 %collective-permute-start.5 = (bf16[32,64,128]{2,1,0:T(8,128)(2,1)S(1)}, bf16[32,64,128]{2,1,0:T(8,128)(2,1)S(1)}, u32[]{:S(2)}, u32[]{:S(2)}) collective-permute-start(bf16[32,64,128]{2,1,0:T(8,128)(2,1)S(1)} %constant_dynamic-update-slice_fusion.refs_4_), channel_id=1, source_target_pairs={{0,1},{1,138},{2,3},{3,196},{4,5},{5,70},{6,7},{7,328},{8,9},{9,20... | collective-permute-start | bytes 1572872 | tf_op jit(solution)/shard_map/ppermute | solution.py:65
  59.6 15.6 %collective-permute-start.6 = (bf16[16,64,128]{2,1,0:T(8,128)(2,1)S(1)}, bf16[16,64,128]{2,1,0:T(8,128)(2,1)S(1)}, u32[]{:S(2)}, u32[]{:S(2)}) collective-permute-start(bf16[16,64,128]{2,1,0:T(8,128)(2,1)S(1)} %collective-permute-done.2.refs_3_), channel_id=1, source_target_pairs={{0,1},{1,138},{2,3},{3,196},{4,5},{5,70},{6,7},{7,328},{8,9},{9,20... | collective-permute-start | bytes 786440 | tf_op jit(solution)/shard_map/ppermute | solution.py:65
  75.2 4.6 %collective-permute-start.7 = (bf16[64,64,128]{2,1,0:T(8,128)(2,1)S(1)}, bf16[64,64,128]{2,1,0:T(8,128)(2,1)S(1)}, u32[]{:S(2)}, u32[]{:S(2)}) collective-permute-start(bf16[64,64,128]{2,1,0:T(8,128)(2,1)S(1)} %all-to-all-done.refs_7_), channel_id=1, source_target_pairs={{0,8},{1,9},{2,10},{3,11},{4,12},{5,13},{6,14},{7,15},{8,0},{9,1},... | collective-permute-start | bytes 3145736 | tf_op jit(solution)/shard_map/ppermute | solution.py:65
  99.7 4.5 %collective-permute-start.8 = (bf16[64,64,128]{2,1,0:T(8,128)(2,1)S(1)}, bf16[64,64,128]{2,1,0:T(8,128)(2,1)S(1)}, u32[]{:S(2)}, u32[]{:S(2)}) collective-permute-start(bf16[64,64,128]{2,1,0:T(8,128)(2,1)S(1)} %all_to_all.10.refs_7_), channel_id=1, source_target_pairs={{0,8},{1,9},{2,10},{3,11},{4,12},{5,13},{6,14},{7,15},{8,0},{9,1},... | collective-permute-start | bytes 3145736 | tf_op jit(solution)/shard_map/ppermute | solution.py:65
  106.6 19.0 %collective-permute-start.9 = (bf16[16,64,128]{2,1,0:T(8,128)(2,1)S(1)}, bf16[16,64,128]{2,1,0:T(8,128)(2,1)S(1)}, u32[]{:S(2)}, u32[]{:S(2)}) collective-permute-start(bf16[16,64,128]{2,1,0:T(8,128)(2,1)S(1)} %shard_map.38), channel_id=1, source_target_pairs={{0,6},{1,38},{2,65},{3,97},{4,128},{5,160},{6,195},{7,227},{8,7},{... | collective-permute-start | bytes 786440 | tf_op jit(solution)/shard_map/ppermute | solution.py:206

commit v10 on v9

--- a/solution.py
+++ b/solution.py
@@ -85,9 +85,9 @@
     ]
 
 
-def pass_rows(pair, rest):
+def pass_rows(part, pair):
     pair = send(pair, lambda p, g: place((p + (-4 if p % 4 < 2 else 4)) % PANELS, g))
-    rest = send(rest, lambda p, g: place((p + (4 if p % 2 else -4)) % PANELS, g))
+    rest = send(part, lambda p, g: place(((p ^ 1) + (4 if p % 2 else -4)) % PANELS, g))
     return pair, rest
 
 
@@ -195,9 +195,9 @@
 
     one, two, three = gather_column(part)
     pair = jnp.concatenate([two, three], axis=0)
-    outer, rest = pass_rows(pair, one)
+    outer, rest = pass_rows(part, pair)
     near = gather_ring(part, X_RINGS)
-    near, outer, rest = lax.optimization_barrier((near, outer, rest))
+    near, outer, rest, one = lax.optimization_barrier((near, outer, rest, one))
     left = gather_row(near)
     table = [part, one, pair, outer, rest]
     square = product(index, mask, table, left, local_rows, False)

time: 129 us -> 131 us (1.016); the launches traced: 126 us -> 130 us
  starting transfers between devices: 51.1 us -> 59.4 us
  waiting for transfers between devices: 42.8 us -> 38 us
    ppermute x8, waiting for transfers between devices: 24.9 us -> 16.4 us  [send(): return lax.ppermute(value, AXES, route(source, place))]
    ppermute x8, starting transfers between devices: 18.7 us -> 27 us  [send(): return lax.ppermute(value, AXES, route(source, place))]
    ppermute x1, waiting for transfers between devices: 14.4 us -> 18.1 us  [shards(): return lax.ppermute(result, AXES, route(place, start)).astype(jnp.float32)]
where the time goes in v10:
time: 131 us; the launch traced here: 130 us
  starting transfers between devices  59.4 us (45%)
  waiting for transfers between devices  38 us (29%)
  blocking collectives  17.5 us (13%)
  Pallas kernels  4.61 us (4%)
  between operations  4.05 us (3%)
  local copies, waits for them, and re-layouts  3.86 us (3%)
  other arithmetic  2.51 us (2%)
    ppermute x8, starting transfers between devices, send(): return lax.ppermute(value, AXES, route(source, place))  27 us
    all_to_all x1, starting transfers between devices, gather_ring(): lax.all_to_all(copies, 'row', 0, 0, tiled=True, axis_index_groups=ring)  19.8 us
    ppermute x1, waiting for transfers between devices, shards(): return lax.ppermute(result, AXES, route(place, start)).astype(jnp.float32)  18.1 us
    all_to_all x1, blocking collectives, gather_ring(): lax.all_to_all(copies, 'row', 0, 0, tiled=True, axis_index_groups=ring)  17.5 us
    ppermute x8, waiting for transfers between devices, send(): return lax.ppermute(value, AXES, route(source, place))  16.4 us
    ppermute x1, starting transfers between devices, shards(): part = lax.ppermute(density, AXES, route(start, between))  7.91 us
    ppermute x1, starting transfers between devices, shards(): return lax.ppermute(result, AXES, route(place, start)).astype(jnp.float32)  4.62 us
    pallas_call x2, Pallas kernels, product(): pl.pallas_call(lambda *refs: product_kernel(count, lanes // width, keep,...  4.61 us
  transfers between devices with their start and end apart: 11, of which 6 were waited for; matrix products, arithmetic and copies ran while one was open for 3% of the time, Pallas kernels for 0%

profile of v10, /device:TPU:4, one launch (start us, length us, event | category | flops | bytes accessed | tf_op | source)
XLA Modules:
  0.0 130.0 jit_solution(12055451661535618761)
XLA Ops:
  0.0 7.9 %collective-permute-start = (bf16[16,64,128]{2,1,0:T(8,128)(2,1)}, bf16[16,64,128]{2,1,0:T(8,128)(2,1)S(1)}, u32[]{:S(2)}, u32[]{:S(2)}) collective-permute-start(bf16[16,64,128]{2,1,0:T(8,128)(2,1)} %param.3), channel_id=1, source_target_pairs={{0,128},{1,65},{2,194},{3,67},{4,132},{5,197},{6,6},{7,7},{8,144},... | collective-permute-start | bytes 786440 | tf_op jit(solution)/shard_map/ppermute | solution.py:168
  7.9 0.7 dynamic-slice_bitcast_fusion
  8.6 0.5 slice.26
  9.9 3.5 %collective-permute-done = bf16[16,64,128]{2,1,0:T(8,128)(2,1)S(1)} collective-permute-done((bf16[16,64,128]{2,1,0:T(8,128)(2,1)}, bf16[16,64,128]{2,1,0:T(8,128)(2,1)S(1)}, u32[]{:S(2)}, u32[]{:S(2)}) %collective-permute-start) | collective-permute-done | bytes 262176 | tf_op jit(solution)/shard_map/ppermute | solution.py:168
  13.4 0.6 fusion.9
  15.4 0.1 copy.22
  15.7 0.1 reshape_reshape.3
  15.8 0.7 collective-permute-start.1
  16.5 0.2 copy.24
  16.8 0.7 gather_fusion
  17.5 0.1 copy.23
  17.9 0.1 select_compare_fusion.1
  20.1 0.1 add.86
  20.3 5.4 %collective-permute-start.2 = (bf16[16,64,128]{2,1,0:T(8,128)(2,1)S(1)}, bf16[16,64,128]{2,1,0:T(8,128)(2,1)S(1)}, u32[]{:S(2)}, u32[]{:S(2)}) collective-permute-start(bf16[16,64,128]{2,1,0:T(8,128)(2,1)S(1)} %collective-permute-done.1.refs_2_), channel_id=1, source_target_pairs={{0,32},{1,33},{2,34},{3,35},{4,36},{5,37},{6,38},{7,39},{8,40},{9,... | collective-permute-start | bytes 786440 | tf_op jit(solution)/shard_map/ppermute | solution.py:65
  25.7 2.7 %collective-permute-start.3 = (bf16[16,64,128]{2,1,0:T(8,128)(2,1)S(1)}, bf16[16,64,128]{2,1,0:T(8,128)(2,1)S(1)}, u32[]{:S(2)}, u32[]{:S(2)}) collective-permute-start(bf16[16,64,128]{2,1,0:T(8,128)(2,1)S(1)} %collective-permute-done.1.refs_2_), channel_id=1, source_target_pairs={{0,48},{1,49},{2,50},{3,51},{4,52},{5,53},{6,54},{7,55},{8,56},{9,... | collective-permute-start | bytes 786440 | tf_op jit(solution)/shard_map/ppermute | solution.py:65
  28.4 1.1 pad_maximum_fusion
  29.5 19.8 %all-to-all-start = ((bf16[64,64,128]{2,1,0:T(8,128)(2,1)}), bf16[64,64,128]{2,1,0:T(8,128)(2,1)S(1)}, u32[]{:S(2)}, u32[]{:S(2)}) async-start(bf16[64,64,128]{2,1,0:T(8,128)(2,1)} %pad_maximum_fusion), calls=%async_computation | async-start | bytes 2097152 | tf_op jit(solution)/shard_map/all_to_all | solution.py:70
  49.4 1.9 %collective-permute-start.4 = (bf16[32,64,128]{2,1,0:T(8,128)(2,1)S(1)}, bf16[32,64,128]{2,1,0:T(8,128)(2,1)S(1)}, u32[]{:S(2)}, u32[]{:S(2)}) collective-permute-start(bf16[32,64,128]{2,1,0:T(8,128)(2,1)S(1)} %constant_dynamic-update-slice_fusion.refs_4_), channel_id=1, source_target_pairs={{0,1},{1,138},{2,3},{3,196},{4,5},{5,70},{6,7},{7,328},{8,9},{9,20... | collective-permute-start | bytes 1572872 | tf_op jit(solution)/shard_map/ppermute | solution.py:65
  51.3 2.2 %collective-permute-start.6 = (bf16[16,64,128]{2,1,0:T(8,128)(2,1)S(1)}, bf16[16,64,128]{2,1,0:T(8,128)(2,1)S(1)}, u32[]{:S(2)}, u32[]{:S(2)}) collective-permute-start(bf16[16,64,128]{2,1,0:T(8,128)(2,1)S(1)} %collective-permute-done.1.refs_2_), channel_id=1, source_target_pairs={{0,16},{1,17},{2,18},{3,19},{4,20},{5,21},{6,22},{7,23},{8,24},{9,... | collective-permute-start | bytes 786440 | tf_op jit(solution)/shard_map/ppermute | solution.py:65
  53.5 9.7 %collective-permute-start.5 = (bf16[16,64,128]{2,1,0:T(8,128)(2,1)S(1)}, bf16[16,64,128]{2,1,0:T(8,128)(2,1)S(1)}, u32[]{:S(2)}, u32[]{:S(2)}) collective-permute-start(bf16[16,64,128]{2,1,0:T(8,128)(2,1)S(1)} %collective-permute-done.1.refs_2_), channel_id=1, source_target_pairs={{0,479},{1,16},{2,81},{3,18},{4,211},{5,20},{6,221},{7,22},{8,351}... | collective-permute-start | bytes 786440 | tf_op jit(solution)/shard_map/ppermute | solution.py:65
  63.2 1.9 %collective-permute-done.6.refs_3_ = bf16[16,64,128]{2,1,0:T(8,128)(2,1)S(1)} collective-permute-done((bf16[16,64,128]{2,1,0:T(8,128)(2,1)S(1)}, bf16[16,64,128]{2,1,0:T(8,128)(2,1)S(1)}, u32[]{:S(2)}, u32[]{:S(2)}) %collective-permute-start.6) | collective-permute-done | bytes 262176 | tf_op jit(solution)/shard_map/ppermute | solution.py:65
  65.1 9.6 %collective-permute-done.5.refs_6_ = bf16[16,64,128]{2,1,0:T(8,128)(2,1)S(1)} collective-permute-done((bf16[16,64,128]{2,1,0:T(8,128)(2,1)S(1)}, bf16[16,64,128]{2,1,0:T(8,128)(2,1)S(1)}, u32[]{:S(2)}, u32[]{:S(2)}) %collective-permute-start.5) | collective-permute-done | bytes 262176 | tf_op jit(solution)/shard_map/ppermute | solution.py:65
  74.7 2.6 %collective-permute-start.7 = (bf16[64,64,128]{2,1,0:T(8,128)(2,1)S(1)}, bf16[64,64,128]{2,1,0:T(8,128)(2,1)S(1)}, u32[]{:S(2)}, u32[]{:S(2)}) collective-permute-start(bf16[64,64,128]{2,1,0:T(8,128)(2,1)S(1)} %all-to-all-done.refs_7_), channel_id=1, source_target_pairs={{0,8},{1,9},{2,10},{3,11},{4,12},{5,13},{6,14},{7,15},{8,0},{9,1},... | collective-permute-start | bytes 3145736 | tf_op jit(solution)/shard_map/ppermute | solution.py:65
  77.3 2.3 %collective-permute-done.7.refs_8_ = bf16[64,64,128]{2,1,0:T(8,128)(2,1)S(1)} collective-permute-done((bf16[64,64,128]{2,1,0:T(8,128)(2,1)S(1)}, bf16[64,64,128]{2,1,0:T(8,128)(2,1)S(1)}, u32[]{:S(2)}, u32[]{:S(2)}) %collective-permute-start.7) | collective-permute-done | bytes 1048608 | tf_op jit(solution)/shard_map/ppermute | solution.py:65
  79.6 2.3 %shard_map.37.refs_9_ = bf16[16,64,128]{2,1,0:T(8,128)(2,1)S(1)} custom-call(s32[256]{0:T(256)S(1)} %fusion.6.refs_0_, f32[256,256]{1,0:T(8,128)S(1)} %add_convert_fusion.refs_1_, bf16[16,64,128]{2,1,0:T(8,128)(2,1)S(1)} %collective-permute-done.1.refs_2_, bf16[16,64,128]{2,1,0:T(8,128)(2,1)S(1)} %collective-permute-done.6.refs_3_, ...), custom_call_target="tpu_custom_call" | custom-call | flops 536870912 | bytes 8388608 | tf_op jit(solution)/shard_map/pallas_call | solution.py:139
  82.0 17.5 %all_to_all.10.refs_7_ = bf16[64,64,128]{2,1,0:T(8,128)(2,1)S(1)} all-to-all(bf16[64,64,128]{2,1,0:T(8,128)(2,1)S(1)} %pad_maximum_fusion.1), channel_id=1, replica_groups={{0,64,128,192},{8,72,136,200},{16,80,144,208},{24,88,152,216},{32,96,16..., dimensions={0} | all-to-all | bytes 2097152 | tf_op jit(solution)/shard_map/all_to_all | solution.py:70
  99.5 1.9 %collective-permute-start.8 = (bf16[64,64,128]{2,1,0:T(8,128)(2,1)S(1)}, bf16[64,64,128]{2,1,0:T(8,128)(2,1)S(1)}, u32[]{:S(2)}, u32[]{:S(2)}) collective-permute-start(bf16[64,64,128]{2,1,0:T(8,128)(2,1)S(1)} %all_to_all.10.refs_7_), channel_id=1, source_target_pairs={{0,8},{1,9},{2,10},{3,11},{4,12},{5,13},{6,14},{7,15},{8,0},{9,1},... | collective-permute-start | bytes 3145736 | tf_op jit(solution)/shard_map/ppermute | solution.py:65
  101.4 2.6 %collective-permute-done.8.refs_8_ = bf16[64,64,128]{2,1,0:T(8,128)(2,1)S(1)} collective-permute-done((bf16[64,64,128]{2,1,0:T(8,128)(2,1)S(1)}, bf16[64,64,128]{2,1,0:T(8,128)(2,1)S(1)}, u32[]{:S(2)}, u32[]{:S(2)}) %collective-permute-start.8) | collective-permute-done | bytes 1048608 | tf_op jit(solution)/shard_map/ppermute | solution.py:65
  104.1 2.3 %shard_map.38 = bf16[16,64,128]{2,1,0:T(8,128)(2,1)S(1)} custom-call(s32[256]{0:T(256)S(1)} %fusion.6.refs_0_, f32[256,256]{1,0:T(8,128)S(1)} %add_convert_fusion.refs_1_, bf16[16,64,128]{2,1,0:T(8,128)(2,1)S(1)} %collective-permute-done.1.refs_2_, bf16[16,64,128]{2,1,0:T(8,128)(2,1)S(1)} %collective-permute-done.6.refs_3_, ...), custom_call_target="tpu_custom_call" | custom-call | flops 536870912 | bytes 8388608 | tf_op jit(solution)/shard_map/pallas_call | solution.py:139
  106.4 4.6 %collective-permute-start.9 = (bf16[16,64,128]{2,1,0:T(8,128)(2,1)S(1)}, bf16[16,64,128]{2,1,0:T(8,128)(2,1)S(1)}, u32[]{:S(2)}, u32[]{:S(2)}) collective-permute-start(bf16[16,64,128]{2,1,0:T(8,128)(2,1)S(1)} %shard_map.38), channel_id=1, source_target_pairs={{0,6},{1,38},{2,65},{3,97},{4,128},{5,160},{6,195},{7,227},{8,7},{... | collective-permute-start | bytes 786440 | tf_op jit(solution)/shard_map/ppermute | solution.py:206
  111.0 18.1 %collective-permute-done.9 = bf16[16,64,128]{2,1,0:T(8,128)(2,1)S(1)} collective-permute-done((bf16[16,64,128]{2,1,0:T(8,128)(2,1)S(1)}, bf16[16,64,128]{2,1,0:T(8,128)(2,1)S(1)}, u32[]{:S(2)}, u32[]{:S(2)}) %collective-permute-start.9) | collective-permute-done | bytes 262176 | tf_op jit(solution)/shard_map/ppermute | solution.py:206
  129.1 0.8 convert_element_type.8
  (32 shorter events, 1.0 us)
Async XLA Ops:
  0.0 9.8 %copy-start = (s32[1024,16]{0,1:T(8,128)S(1)}, s32[1024,16]{0,1:T(8,128)}, u32[]{:S(2)}) copy-start(s32[1024,16]{0,1:T(8,128)} %param.4) | copy-start | bytes 196612
  0.0 13.3 %collective-permute-start = (bf16[16,64,128]{2,1,0:T(8,128)(2,1)}, bf16[16,64,128]{2,1,0:T(8,128)(2,1)S(1)}, u32[]{:S(2)}, u32[]{:S(2)}) collective-permute-start(bf16[16,64,128]{2,1,0:T(8,128)(2,1)} %param.3), channel_id=1, source_target_pairs={{0,128},{1,65},{2,194},{3,67},{4,132},{5,197},{6,6},{7,7},{8,144},... | collective-permute-start | bytes 786440 | tf_op jit(solution)/shard_map/ppermute | solution.py:168
  15.8 4.4 %collective-permute-start.1 = (bf16[16,64,128]{2,1,0:T(8,128)(2,1)S(1)}, bf16[16,64,128]{2,1,0:T(8,128)(2,1)S(1)}, u32[]{:S(2)}, u32[]{:S(2)}) collective-permute-start(bf16[16,64,128]{2,1,0:T(8,128)(2,1)S(1)} %collective-permute-done), channel_id=1, source_target_pairs={{0,4},{1,2},{2,10},{3,6},{4,12},{5,14},{6,0},{7,8},{8,5},{9,3},{10... | collective-permute-start | bytes 786440 | tf_op jit(solution)/shard_map/ppermute | solution.py:65
  20.3 29.0 %collective-permute-start.2 = (bf16[16,64,128]{2,1,0:T(8,128)(2,1)S(1)}, bf16[16,64,128]{2,1,0:T(8,128)(2,1)S(1)}, u32[]{:S(2)}, u32[]{:S(2)}) collective-permute-start(bf16[16,64,128]{2,1,0:T(8,128)(2,1)S(1)} %collective-permute-done.1.refs_2_), channel_id=1, source_target_pairs={{0,32},{1,33},{2,34},{3,35},{4,36},{5,37},{6,38},{7,39},{8,40},{9,... | collective-permute-start | bytes 786440 | tf_op jit(solution)/shard_map/ppermute | solution.py:65
  25.7 23.6 %collective-permute-start.3 = (bf16[16,64,128]{2,1,0:T(8,128)(2,1)S(1)}, bf16[16,64,128]{2,1,0:T(8,128)(2,1)S(1)}, u32[]{:S(2)}, u32[]{:S(2)}) collective-permute-start(bf16[16,64,128]{2,1,0:T(8,128)(2,1)S(1)} %collective-permute-done.1.refs_2_), channel_id=1, source_target_pairs={{0,48},{1,49},{2,50},{3,51},{4,52},{5,53},{6,54},{7,55},{8,56},{9,... | collective-permute-start | bytes 786440 | tf_op jit(solution)/shard_map/ppermute | solution.py:65
  29.5 45.2 %all-to-all-start = ((bf16[64,64,128]{2,1,0:T(8,128)(2,1)}), bf16[64,64,128]{2,1,0:T(8,128)(2,1)S(1)}, u32[]{:S(2)}, u32[]{:S(2)}) async-start(bf16[64,64,128]{2,1,0:T(8,128)(2,1)} %pad_maximum_fusion), calls=%async_computation | async-start | bytes 2097152 | tf_op jit(solution)/shard_map/all_to_all | solution.py:70
  49.4 25.3 %collective-permute-start.4 = (bf16[32,64,128]{2,1,0:T(8,128)(2,1)S(1)}, bf16[32,64,128]{2,1,0:T(8,128)(2,1)S(1)}, u32[]{:S(2)}, u32[]{:S(2)}) collective-permute-start(bf16[32,64,128]{2,1,0:T(8,128)(2,1)S(1)} %constant_dynamic-update-slice_fusion.refs_4_), channel_id=1, source_target_pairs={{0,1},{1,138},{2,3},{3,196},{4,5},{5,70},{6,7},{7,328},{8,9},{9,20... | collective-permute-start | bytes 1572872 | tf_op jit(solution)/shard_map/ppermute | solution.py:65
  51.3 13.8 %collective-permute-start.6 = (bf16[16,64,128]{2,1,0:T(8,128)(2,1)S(1)}, bf16[16,64,128]{2,1,0:T(8,128)(2,1)S(1)}, u32[]{:S(2)}, u32[]{:S(2)}) collective-permute-start(bf16[16,64,128]{2,1,0:T(8,128)(2,1)S(1)} %collective-permute-done.1.refs_2_), channel_id=1, source_target_pairs={{0,16},{1,17},{2,18},{3,19},{4,20},{5,21},{6,22},{7,23},{8,24},{9,... | collective-permute-start | bytes 786440 | tf_op jit(solution)/shard_map/ppermute | solution.py:65
  53.5 21.2 %collective-permute-start.5 = (bf16[16,64,128]{2,1,0:T(8,128)(2,1)S(1)}, bf16[16,64,128]{2,1,0:T(8,128)(2,1)S(1)}, u32[]{:S(2)}, u32[]{:S(2)}) collective-permute-start(bf16[16,64,128]{2,1,0:T(8,128)(2,1)S(1)} %collective-permute-done.1.refs_2_), channel_id=1, source_target_pairs={{0,479},{1,16},{2,81},{3,18},{4,211},{5,20},{6,221},{7,22},{8,351}... | collective-permute-start | bytes 786440 | tf_op jit(solution)/shard_map/ppermute | solution.py:65
  74.7 4.9 %collective-permute-start.7 = (bf16[64,64,128]{2,1,0:T(8,128)(2,1)S(1)}, bf16[64,64,128]{2,1,0:T(8,128)(2,1)S(1)}, u32[]{:S(2)}, u32[]{:S(2)}) collective-permute-start(bf16[64,64,128]{2,1,0:T(8,128)(2,1)S(1)} %all-to-all-done.refs_7_), channel_id=1, source_target_pairs={{0,8},{1,9},{2,10},{3,11},{4,12},{5,13},{6,14},{7,15},{8,0},{9,1},... | collective-permute-start | bytes 3145736 | tf_op jit(solution)/shard_map/ppermute | solution.py:65
  99.5 4.5 %collective-permute-start.8 = (bf16[64,64,128]{2,1,0:T(8,128)(2,1)S(1)}, bf16[64,64,128]{2,1,0:T(8,128)(2,1)S(1)}, u32[]{:S(2)}, u32[]{:S(2)}) collective-permute-start(bf16[64,64,128]{2,1,0:T(8,128)(2,1)S(1)} %all_to_all.10.refs_7_), channel_id=1, source_target_pairs={{0,8},{1,9},{2,10},{3,11},{4,12},{5,13},{6,14},{7,15},{8,0},{9,1},... | collective-permute-start | bytes 3145736 | tf_op jit(solution)/shard_map/ppermute | solution.py:65
  106.4 22.8 %collective-permute-start.9 = (bf16[16,64,128]{2,1,0:T(8,128)(2,1)S(1)}, bf16[16,64,128]{2,1,0:T(8,128)(2,1)S(1)}, u32[]{:S(2)}, u32[]{:S(2)}) collective-permute-start(bf16[16,64,128]{2,1,0:T(8,128)(2,1)S(1)} %shard_map.38), channel_id=1, source_target_pairs={{0,6},{1,38},{2,65},{3,97},{4,128},{5,160},{6,195},{7,227},{8,7},{... | collective-permute-start | bytes 786440 | tf_op jit(solution)/shard_map/ppermute | solution.py:206

commit v11 on v8

--- a/solution.py
+++ b/solution.py
@@ -56,6 +56,10 @@
     return held_at(panel, spot(panel, group))[1 - lane(panel, group)]
 
 
+def plane_order(panel):
+    return [group for x in range(4) for group in held_at(panel, x)]
+
+
 def arrival(panel, group):
     mine = lane(panel, group)
     return [held_at(panel, x)[core] for core in (mine, 1 - mine) for x in range(4)]
@@ -74,6 +78,18 @@
     [device(half, x, y, core, 0) // GROUPS for x in range(4)]
     for half in range(2) for y in range(4) for core in range(2)
 ]
+CORES = [[2 * chip, 2 * chip + 1] for chip in range(PANELS // 2)]
+
+
+def gather_cores(near, rows):
+    return [
+        lax.all_gather(
+            near[j : j + rows], "row", axis=0, tiled=True, axis_index_groups=CORES
+        )
+        for j in range(0, near.shape[0], rows)
+    ]
+
+
 def gather_row(near):
     return [near, send(near, lambda p, g: place(p, opposite(p, g)))]
 
@@ -85,9 +101,9 @@
     ]
 
 
-def pass_rows(pair, rest):
+def pass_rows(part, pair):
     pair = send(pair, lambda p, g: place((p + (-4 if p % 4 < 2 else 4)) % PANELS, g))
-    rest = send(rest, lambda p, g: place((p + (4 if p % 2 else -4)) % PANELS, g))
+    rest = send(part, lambda p, g: place(((p ^ 1) + (4 if p % 2 else -4)) % PANELS, g))
     return pair, rest
 
 
@@ -99,7 +115,7 @@
     return jnp.where(place_y == inner, flip, jnp.where(flip == 1, 6, flip + 2))
 
 
-def product_kernel(count, group, keep, index_ref, mask_ref, *refs):
+def product_kernel(operands, count, group, keep, index_ref, mask_ref, *refs):
     out_ref, table_ref = refs[-2:]
     rows, width, lanes = out_ref.shape
     filled = 0
@@ -109,7 +125,7 @@
     refs = refs[PIECES:]
     chunks = [
         ref.at[pl.ds(j * rows, rows)]
-        for ref in refs[:2]
+        for ref in refs[:operands]
         for j in range(ref.shape[0] // rows)
     ]
     blocks = count * group
@@ -128,19 +144,21 @@
             total = part if total is None else total + part
         value = total[:, :lanes] + pltpu.roll(total[:, lanes:], width, 1)
         if keep:
-            value = 3.0 * refs[2][i].astype(jnp.float32) - 2.0 * value
+            value = 3.0 * refs[operands][i].astype(jnp.float32) - 2.0 * value
         out_ref[i] = value.astype(out_ref.dtype)
 
 
-def product(index, mask, table, chunks, rows, keep):
+def product(index, mask, table, chunks, rows, kept=()):
     width, lanes = chunks[0].shape[1:]
-    count = sum(chunk.shape[0] for chunk in chunks[:2]) // rows
+    count = sum(chunk.shape[0] for chunk in chunks) // rows
     vmem = pl.BlockSpec(memory_space=pltpu.VMEM)
     return pl.pallas_call(
-        lambda *refs: product_kernel(count, lanes // width, keep, *refs),
+        lambda *refs: product_kernel(
+            len(chunks), count, lanes // width, bool(kept), *refs
+        ),
         out_shape=jax.ShapeDtypeStruct((rows, width, lanes), jnp.bfloat16),
         in_specs=[pl.BlockSpec(memory_space=pltpu.SMEM)]
-        + [vmem] * (1 + len(table) + len(chunks)),
+        + [vmem] * (1 + len(table) + len(chunks) + len(kept)),
         out_specs=vmem,
         scratch_shapes=[
             pltpu.VMEM((sum(piece.shape[0] for piece in table), width, lanes), jnp.bfloat16)
@@ -151,7 +169,7 @@
             bytes_accessed=8 * 1024 * 1024,
             transcendentals=0,
         ),
-    )(index, mask, *table, *chunks)
+    )(index, mask, *table, *chunks, *kept)
 
 
 def shards(density, columns):
@@ -159,9 +177,9 @@
     group = lanes // width
     total, stored = columns.shape
 
-    jobs = np.zeros((PANELS * GROUPS, 2 + GROUPS), np.int32)
+    jobs = np.zeros((PANELS * GROUPS, 2 + 2 * GROUPS), np.int32)
     for job in JOBS:
-        jobs[place(*job)] = [*job, *arrival(*job)]
+        jobs[place(*job)] = [*job, *plane_order(job[0]), *arrival(*job)]
     here = lax.axis_index("row") * GROUPS + lax.axis_index("col")
     job = lax.dynamic_index_in_dim(jnp.array(jobs), here, 0, keepdims=False)
     part = lax.ppermute(density, AXES, route(start, between))
@@ -172,33 +190,32 @@
 
     base = panel * local_rows
     goal = lax.dynamic_slice_in_dim(own, mine * group, group, 1)
-    own = jnp.take(own.reshape(local_rows, GROUPS, group), order, axis=1)
-    own = own.reshape(local_rows, stored)
+    orders = order.reshape(2, GROUPS)
+    own = jnp.take(own.reshape(local_rows, GROUPS, group), orders, axis=1)
+    own = own.swapaxes(0, 1).reshape(2, local_rows, stored)
     distance = jnp.mod(own - base + total // 2, total) - total // 2
     owner = jnp.floor_divide(distance, local_rows)
     index = table_panel(owner, panel) * local_rows + distance - owner * local_rows
-    index = index.reshape(-1)
+    index = index.reshape(2, -1)
     held = lax.dynamic_slice_in_dim(columns, mine * group, group, 1)
-    held = jnp.take(held, own.reshape(-1), axis=0).reshape(local_rows, stored, group)
+    held = jnp.take(held, own.reshape(-1), axis=0).reshape(2, local_rows, stored, group)
     lane_slot = jnp.arange(lanes, dtype=jnp.int32) // width
     found = jnp.where(lane_slot == 0, held[..., :1], held[..., 1:])
     direct = jnp.where(lane_slot == 0, goal[:, None, :1], goal[:, None, 1:])
     swapped = jnp.where(lane_slot == 0, goal[:, None, 1:], goal[:, None, :1])
     mask = jnp.concatenate([found == direct, found == swapped], axis=-1)
-    mask = mask.astype(jnp.float32).reshape(local_rows * stored, 2 * lanes)
-
+    mask = mask.astype(jnp.float32).reshape(2, local_rows * stored, 2 * lanes)
     part, index, mask = lax.optimization_barrier((part, index, mask))
 
     one, two, three = gather_column(part)
     pair = jnp.concatenate([two, three], axis=0)
-    outer, rest = pass_rows(pair, one)
+    outer, rest = pass_rows(part, pair)
     near = gather_ring(part, X_RINGS)
-    near, outer, rest = lax.optimization_barrier((near, outer, rest))
-    left = gather_row(near)
+    left = gather_cores(near, local_rows)
     table = [part, one, pair, outer, rest]
-    square = product(index, mask, table, left, local_rows, False)
+    square = product(index[0], mask[0], table, left, local_rows)
     left = gather_row(gather_ring(square, X_RINGS))
-    result = product(index, mask, table, left + [square], local_rows, True)
+    result = product(index[1], mask[1], table, left, local_rows, [square])
     return lax.ppermute(result, AXES, route(place, start)).astype(jnp.float32)
 
 

time: 129 us -> 134 us (1.039); the launches traced: 127 us -> 134 us
  blocking collectives: 17.5 us -> 29.6 us
  waiting for transfers between devices: 43.9 us -> 35 us
  starting transfers between devices: 50.1 us -> 53.5 us
    ppermute x8 -> x7, waiting for transfers between devices: 24.9 us -> 12.7 us  [send(): return lax.ppermute(value, AXES, route(source, place))]
    all_gather x0 -> x4, blocking collectives: none -> 8.69 us  [gather_cores(): lax.all_gather(near[j:j + rows], 'row', axis=0, tiled=True, axis_index_gr...]
    all_to_all x1, blocking collectives: 17.5 us -> 20.9 us  [gather_ring(): lax.all_to_all(copies, 'row', 0, 0, tiled=True, axis_index_groups=ring)]
    ppermute x1, waiting for transfers between devices: 14.4 us -> 17.6 us  [shards(): return lax.ppermute(result, AXES, route(place, start)).astype(jnp.float32)]
    ppermute x8 -> x7, starting transfers between devices: 18.7 us -> 21.9 us  [send(): return lax.ppermute(value, AXES, route(source, place))]
  transfers between devices with their start and end apart: 11 -> 10, of which waited for: 6 -> 6; matrix products, arithmetic and copies ran while one was open for 3% -> 3% of each run, Pallas kernels for 0% -> 0%
where the time goes in v11:
time: 134 us
  starting transfers between devices  53.5 us (40%)
  waiting for transfers between devices  35 us (26%)
  blocking collectives  29.6 us (22%)
  local copies, waits for them, and re-layouts  4.9 us (4%)
  Pallas kernels  4.61 us (3%)
  between operations  3.52 us (3%)
  other arithmetic  2.51 us (2%)
    ppermute x7, starting transfers between devices, send(): return lax.ppermute(value, AXES, route(source, place))  21.9 us
    all_to_all x1, blocking collectives, gather_ring(): lax.all_to_all(copies, 'row', 0, 0, tiled=True, axis_index_groups=ring)  20.9 us
    all_to_all x1, starting transfers between devices, gather_ring(): lax.all_to_all(copies, 'row', 0, 0, tiled=True, axis_index_groups=ring)  19.1 us
    ppermute x1, waiting for transfers between devices, shards(): return lax.ppermute(result, AXES, route(place, start)).astype(jnp.float32)  17.6 us
    ppermute x7, waiting for transfers between devices, send(): return lax.ppermute(value, AXES, route(source, place))  12.7 us
    all_gather x4, blocking collectives, gather_cores(): lax.all_gather(near[j:j + rows], 'row', axis=0, tiled=True, axis_index_gr...  8.69 us
    ppermute x1, starting transfers between devices, shards(): part = lax.ppermute(density, AXES, route(start, between))  7.91 us
    ppermute x1, starting transfers between devices, shards(): return lax.ppermute(result, AXES, route(place, start)).astype(jnp.float32)  4.62 us
  transfers between devices with their start and end apart: 10, of which 6 were waited for; matrix products, arithmetic and copies ran while one was open for 3% of the time, Pallas kernels for 0%

profile of v11, /device:TPU:4, one launch (start us, length us, event | category | flops | bytes accessed | tf_op | source)
XLA Modules:
  0.0 133.6 jit_solution(11386056881732230770)
XLA Ops:
  0.0 7.9 %collective-permute-start = (bf16[16,64,128]{2,1,0:T(8,128)(2,1)}, bf16[16,64,128]{2,1,0:T(8,128)(2,1)S(1)}, u32[]{:S(2)}, u32[]{:S(2)}) collective-permute-start(bf16[16,64,128]{2,1,0:T(8,128)(2,1)} %param.3), channel_id=1, source_target_pairs={{0,128},{1,65},{2,194},{3,67},{4,132},{5,197},{6,6},{7,7},{8,144},... | collective-permute-start | bytes 786440 | tf_op jit(solution)/shard_map/ppermute | solution.py:185
  7.9 0.7 fusion.8
  8.8 4.6 %collective-permute-done = bf16[16,64,128]{2,1,0:T(8,128)(2,1)S(1)} collective-permute-done((bf16[16,64,128]{2,1,0:T(8,128)(2,1)}, bf16[16,64,128]{2,1,0:T(8,128)(2,1)S(1)}, u32[]{:S(2)}, u32[]{:S(2)}) %collective-permute-start) | collective-permute-done | bytes 262176 | tf_op jit(solution)/shard_map/ppermute | solution.py:185
  13.4 0.6 fusion.13
  15.6 0.6 gather_fusion
  16.7 0.7 collective-permute-start.1
  17.4 0.2 copy.30
  17.6 1.0 gather_fusion.1
  18.7 0.3 copy.29
  19.3 0.2 select_compare_fusion.1
  21.8 1.1 pad_maximum_fusion
  22.9 19.1 %all-to-all-start = ((bf16[64,64,128]{2,1,0:T(8,128)(2,1)}), bf16[64,64,128]{2,1,0:T(8,128)(2,1)S(1)}, u32[]{:S(2)}, u32[]{:S(2)}) async-start(bf16[64,64,128]{2,1,0:T(8,128)(2,1)} %pad_maximum_fusion), calls=%async_computation | async-start | bytes 2097152 | tf_op jit(solution)/shard_map/all_to_all | solution.py:74
  41.9 7.1 %collective-permute-start.6 = (bf16[16,64,128]{2,1,0:T(8,128)(2,1)S(1)}, bf16[16,64,128]{2,1,0:T(8,128)(2,1)S(1)}, u32[]{:S(2)}, u32[]{:S(2)}) collective-permute-start(bf16[16,64,128]{2,1,0:T(8,128)(2,1)S(1)} %collective-permute-done.1.refs_2_), channel_id=1, source_target_pairs={{0,479},{1,16},{2,81},{3,18},{4,211},{5,20},{6,221},{7,22},{8,351}... | collective-permute-start | bytes 786440 | tf_op jit(solution)/shard_map/ppermute | solution.py:69
  49.1 1.9 %collective-permute-start.4 = (bf16[16,64,128]{2,1,0:T(8,128)(2,1)S(1)}, bf16[16,64,128]{2,1,0:T(8,128)(2,1)S(1)}, u32[]{:S(2)}, u32[]{:S(2)}) collective-permute-start(bf16[16,64,128]{2,1,0:T(8,128)(2,1)S(1)} %collective-permute-done.1.refs_2_), channel_id=1, source_target_pairs={{0,48},{1,49},{2,50},{3,51},{4,52},{5,53},{6,54},{7,55},{8,56},{9,... | collective-permute-start | bytes 786440 | tf_op jit(solution)/shard_map/ppermute | solution.py:69
  51.0 6.4 %collective-permute-start.3 = (bf16[16,64,128]{2,1,0:T(8,128)(2,1)S(1)}, bf16[16,64,128]{2,1,0:T(8,128)(2,1)S(1)}, u32[]{:S(2)}, u32[]{:S(2)}) collective-permute-start(bf16[16,64,128]{2,1,0:T(8,128)(2,1)S(1)} %collective-permute-done.1.refs_2_), channel_id=1, source_target_pairs={{0,32},{1,33},{2,34},{3,35},{4,36},{5,37},{6,38},{7,39},{8,40},{9,... | collective-permute-start | bytes 786440 | tf_op jit(solution)/shard_map/ppermute | solution.py:69
  57.4 1.9 %collective-permute-start.2 = (bf16[16,64,128]{2,1,0:T(8,128)(2,1)S(1)}, bf16[16,64,128]{2,1,0:T(8,128)(2,1)S(1)}, u32[]{:S(2)}, u32[]{:S(2)}) collective-permute-start(bf16[16,64,128]{2,1,0:T(8,128)(2,1)S(1)} %collective-permute-done.1.refs_2_), channel_id=1, source_target_pairs={{0,16},{1,17},{2,18},{3,19},{4,20},{5,21},{6,22},{7,23},{8,24},{9,... | collective-permute-start | bytes 786440 | tf_op jit(solution)/shard_map/ppermute | solution.py:69
  59.4 5.2 %collective-permute-done.3 = bf16[16,64,128]{2,1,0:T(8,128)(2,1)S(1)} collective-permute-done((bf16[16,64,128]{2,1,0:T(8,128)(2,1)S(1)}, bf16[16,64,128]{2,1,0:T(8,128)(2,1)S(1)}, u32[]{:S(2)}, u32[]{:S(2)}) %collective-permute-start.3) | collective-permute-done | bytes 262176 | tf_op jit(solution)/shard_map/ppermute | solution.py:69
  64.6 1.8 %collective-permute-done.4 = bf16[16,64,128]{2,1,0:T(8,128)(2,1)S(1)} collective-permute-done((bf16[16,64,128]{2,1,0:T(8,128)(2,1)S(1)}, bf16[16,64,128]{2,1,0:T(8,128)(2,1)S(1)}, u32[]{:S(2)}, u32[]{:S(2)}) %collective-permute-start.4) | collective-permute-done | bytes 262176 | tf_op jit(solution)/shard_map/ppermute | solution.py:69
  66.5 1.9 %collective-permute-start.5 = (bf16[32,64,128]{2,1,0:T(8,128)(2,1)S(1)}, bf16[32,64,128]{2,1,0:T(8,128)(2,1)S(1)}, u32[]{:S(2)}, u32[]{:S(2)}) collective-permute-start(bf16[32,64,128]{2,1,0:T(8,128)(2,1)S(1)} %constant_dynamic-update-slice_fusion.refs_4_), channel_id=1, source_target_pairs={{0,1},{1,138},{2,3},{3,196},{4,5},{5,70},{6,7},{7,328},{8,9},{9,20... | collective-permute-start | bytes 1572872 | tf_op jit(solution)/shard_map/ppermute | solution.py:69
  68.5 2.2 %all_gather.15.refs_10_ = bf16[32,64,128]{2,1,0:T(8,128)(2,1)S(1)} all-gather(bf16[16,64,128]{2,1,0:T(8,128)(2,1)S(1)} %get-tuple-element.19), channel_id=1, replica_groups={{0,8},{16,24},{32,40},{48,56},{64,72},{80,88},{96,104},{112,120},{128,1..., dimensions={0}, use_global_device_ids=true | all-gather | bytes 786432 | tf_op jit(solution)/shard_map/all_gather | solution.py:86
  70.7 2.2 %all_gather.14.refs_9_ = bf16[32,64,128]{2,1,0:T(8,128)(2,1)S(1)} all-gather(bf16[16,64,128]{2,1,0:T(8,128)(2,1)S(1)} %get-tuple-element.20), channel_id=1, replica_groups={{0,8},{16,24},{32,40},{48,56},{64,72},{80,88},{96,104},{112,120},{128,1..., dimensions={0}, use_global_device_ids=true | all-gather | bytes 786432 | tf_op jit(solution)/shard_map/all_gather | solution.py:86
  72.9 2.2 %all_gather.13.refs_8_ = bf16[32,64,128]{2,1,0:T(8,128)(2,1)S(1)} all-gather(bf16[16,64,128]{2,1,0:T(8,128)(2,1)S(1)} %get-tuple-element.21), channel_id=1, replica_groups={{0,8},{16,24},{32,40},{48,56},{64,72},{80,88},{96,104},{112,120},{128,1..., dimensions={0}, use_global_device_ids=true | all-gather | bytes 786432 | tf_op jit(solution)/shard_map/all_gather | solution.py:86
  75.1 2.2 %all_gather.12.refs_7_ = bf16[32,64,128]{2,1,0:T(8,128)(2,1)S(1)} all-gather(bf16[16,64,128]{2,1,0:T(8,128)(2,1)S(1)} %get-tuple-element.22), channel_id=1, replica_groups={{0,8},{16,24},{32,40},{48,56},{64,72},{80,88},{96,104},{112,120},{128,1..., dimensions={0}, use_global_device_ids=true | all-gather | bytes 786432 | tf_op jit(solution)/shard_map/all_gather | solution.py:86
  77.2 3.1 %collective-permute-done.5.refs_5_ = bf16[32,64,128]{2,1,0:T(8,128)(2,1)S(1)} collective-permute-done((bf16[32,64,128]{2,1,0:T(8,128)(2,1)S(1)}, bf16[32,64,128]{2,1,0:T(8,128)(2,1)S(1)}, u32[]{:S(2)}, u32[]{:S(2)}) %collective-permute-start.5) | collective-permute-done | bytes 524320 | tf_op jit(solution)/shard_map/ppermute | solution.py:69
  80.3 2.3 %shard_map.37.refs_9_ = bf16[16,64,128]{2,1,0:T(8,128)(2,1)S(1)} custom-call(s32[256]{0:T(256)S(1)} %bitcast.45, f32[256,256]{1,0:T(8,128)S(1)} %get-tuple-element.23.refs_1_, bf16[16,64,128]{2,1,0:T(8,128)(2,1)S(1)} %collective-permute-done.1.refs_2_, bf16[16,64,128]{2,1,0:T(8,128)(2,1)S(1)} %collective-permute-done.2.refs_3_, ...), custom_call_target="tpu_custom_call" | custom-call | flops 536870912 | bytes 8388608 | tf_op jit(solution)/shard_map/pallas_call | solution.py:155
  82.8 20.9 %all_to_all.10.refs_7_ = bf16[64,64,128]{2,1,0:T(8,128)(2,1)S(1)} all-to-all(bf16[64,64,128]{2,1,0:T(8,128)(2,1)S(1)} %pad_maximum_fusion.1), channel_id=1, replica_groups={{0,64,128,192},{8,72,136,200},{16,80,144,208},{24,88,152,216},{32,96,16..., dimensions={0} | all-to-all | bytes 2097152 | tf_op jit(solution)/shard_map/all_to_all | solution.py:74
  103.6 1.9 %collective-permute-start.7 = (bf16[64,64,128]{2,1,0:T(8,128)(2,1)S(1)}, bf16[64,64,128]{2,1,0:T(8,128)(2,1)S(1)}, u32[]{:S(2)}, u32[]{:S(2)}) collective-permute-start(bf16[64,64,128]{2,1,0:T(8,128)(2,1)S(1)} %all_to_all.10.refs_7_), channel_id=1, source_target_pairs={{0,8},{1,9},{2,10},{3,11},{4,12},{5,13},{6,14},{7,15},{8,0},{9,1},... | collective-permute-start | bytes 3145736 | tf_op jit(solution)/shard_map/ppermute | solution.py:69
  105.5 2.6 %collective-permute-done.7.refs_8_ = bf16[64,64,128]{2,1,0:T(8,128)(2,1)S(1)} collective-permute-done((bf16[64,64,128]{2,1,0:T(8,128)(2,1)S(1)}, bf16[64,64,128]{2,1,0:T(8,128)(2,1)S(1)}, u32[]{:S(2)}, u32[]{:S(2)}) %collective-permute-start.7) | collective-permute-done | bytes 1048608 | tf_op jit(solution)/shard_map/ppermute | solution.py:69
  108.2 2.3 %shard_map.38 = bf16[16,64,128]{2,1,0:T(8,128)(2,1)S(1)} custom-call(s32[256]{0:T(256)S(1)} %bitcast.44, f32[256,256]{1,0:T(8,128)S(1)} %get-tuple-element.24.refs_1_, bf16[16,64,128]{2,1,0:T(8,128)(2,1)S(1)} %collective-permute-done.1.refs_2_, bf16[16,64,128]{2,1,0:T(8,128)(2,1)S(1)} %collective-permute-done.2.refs_3_, ...), custom_call_target="tpu_custom_call" | custom-call | flops 536870912 | bytes 8388608 | tf_op jit(solution)/shard_map/pallas_call | solution.py:155
  110.5 4.6 %collective-permute-start.8 = (bf16[16,64,128]{2,1,0:T(8,128)(2,1)S(1)}, bf16[16,64,128]{2,1,0:T(8,128)(2,1)S(1)}, u32[]{:S(2)}, u32[]{:S(2)}) collective-permute-start(bf16[16,64,128]{2,1,0:T(8,128)(2,1)S(1)} %shard_map.38), channel_id=1, source_target_pairs={{0,6},{1,38},{2,65},{3,97},{4,128},{5,160},{6,195},{7,227},{8,7},{... | collective-permute-start | bytes 786440 | tf_op jit(solution)/shard_map/ppermute | solution.py:219
  115.1 17.6 %collective-permute-done.8 = bf16[16,64,128]{2,1,0:T(8,128)(2,1)S(1)} collective-permute-done((bf16[16,64,128]{2,1,0:T(8,128)(2,1)S(1)}, bf16[16,64,128]{2,1,0:T(8,128)(2,1)S(1)}, u32[]{:S(2)}, u32[]{:S(2)}) %collective-permute-start.8) | collective-permute-done | bytes 262176 | tf_op jit(solution)/shard_map/ppermute | solution.py:219
  132.7 0.8 convert_element_type.8
  (43 shorter events, 1.9 us)
Async XLA Ops:
  0.0 8.7 %copy-start = (s32[1024,16]{0,1:T(8,128)S(1)}, s32[1024,16]{0,1:T(8,128)}, u32[]{:S(2)}) copy-start(s32[1024,16]{0,1:T(8,128)} %param.4) | copy-start | bytes 196612
  0.0 13.3 %collective-permute-start = (bf16[16,64,128]{2,1,0:T(8,128)(2,1)}, bf16[16,64,128]{2,1,0:T(8,128)(2,1)S(1)}, u32[]{:S(2)}, u32[]{:S(2)}) collective-permute-start(bf16[16,64,128]{2,1,0:T(8,128)(2,1)} %param.3), channel_id=1, source_target_pairs={{0,128},{1,65},{2,194},{3,67},{4,132},{5,197},{6,6},{7,7},{8,144},... | collective-permute-start | bytes 786440 | tf_op jit(solution)/shard_map/ppermute | solution.py:185
  16.7 5.0 %collective-permute-start.1 = (bf16[16,64,128]{2,1,0:T(8,128)(2,1)S(1)}, bf16[16,64,128]{2,1,0:T(8,128)(2,1)S(1)}, u32[]{:S(2)}, u32[]{:S(2)}) collective-permute-start(bf16[16,64,128]{2,1,0:T(8,128)(2,1)S(1)} %collective-permute-done), channel_id=1, source_target_pairs={{0,4},{1,2},{2,10},{3,6},{4,12},{5,14},{6,0},{7,8},{8,5},{9,3},{10... | collective-permute-start | bytes 786440 | tf_op jit(solution)/shard_map/ppermute | solution.py:69
  22.9 45.6 %all-to-all-start = ((bf16[64,64,128]{2,1,0:T(8,128)(2,1)}), bf16[64,64,128]{2,1,0:T(8,128)(2,1)S(1)}, u32[]{:S(2)}, u32[]{:S(2)}) async-start(bf16[64,64,128]{2,1,0:T(8,128)(2,1)} %pad_maximum_fusion), calls=%async_computation | async-start | bytes 2097152 | tf_op jit(solution)/shard_map/all_to_all | solution.py:74
  41.9 35.3 %collective-permute-start.6 = (bf16[16,64,128]{2,1,0:T(8,128)(2,1)S(1)}, bf16[16,64,128]{2,1,0:T(8,128)(2,1)S(1)}, u32[]{:S(2)}, u32[]{:S(2)}) collective-permute-start(bf16[16,64,128]{2,1,0:T(8,128)(2,1)S(1)} %collective-permute-done.1.refs_2_), channel_id=1, source_target_pairs={{0,479},{1,16},{2,81},{3,18},{4,211},{5,20},{6,221},{7,22},{8,351}... | collective-permute-start | bytes 786440 | tf_op jit(solution)/shard_map/ppermute | solution.py:69
  49.1 17.4 %collective-permute-start.4 = (bf16[16,64,128]{2,1,0:T(8,128)(2,1)S(1)}, bf16[16,64,128]{2,1,0:T(8,128)(2,1)S(1)}, u32[]{:S(2)}, u32[]{:S(2)}) collective-permute-start(bf16[16,64,128]{2,1,0:T(8,128)(2,1)S(1)} %collective-permute-done.1.refs_2_), channel_id=1, source_target_pairs={{0,48},{1,49},{2,50},{3,51},{4,52},{5,53},{6,54},{7,55},{8,56},{9,... | collective-permute-start | bytes 786440 | tf_op jit(solution)/shard_map/ppermute | solution.py:69
  51.0 13.6 %collective-permute-start.3 = (bf16[16,64,128]{2,1,0:T(8,128)(2,1)S(1)}, bf16[16,64,128]{2,1,0:T(8,128)(2,1)S(1)}, u32[]{:S(2)}, u32[]{:S(2)}) collective-permute-start(bf16[16,64,128]{2,1,0:T(8,128)(2,1)S(1)} %collective-permute-done.1.refs_2_), channel_id=1, source_target_pairs={{0,32},{1,33},{2,34},{3,35},{4,36},{5,37},{6,38},{7,39},{8,40},{9,... | collective-permute-start | bytes 786440 | tf_op jit(solution)/shard_map/ppermute | solution.py:69
  57.4 19.8 %collective-permute-start.2 = (bf16[16,64,128]{2,1,0:T(8,128)(2,1)S(1)}, bf16[16,64,128]{2,1,0:T(8,128)(2,1)S(1)}, u32[]{:S(2)}, u32[]{:S(2)}) collective-permute-start(bf16[16,64,128]{2,1,0:T(8,128)(2,1)S(1)} %collective-permute-done.1.refs_2_), channel_id=1, source_target_pairs={{0,16},{1,17},{2,18},{3,19},{4,20},{5,21},{6,22},{7,23},{8,24},{9,... | collective-permute-start | bytes 786440 | tf_op jit(solution)/shard_map/ppermute | solution.py:69
  66.5 13.8 %collective-permute-start.5 = (bf16[32,64,128]{2,1,0:T(8,128)(2,1)S(1)}, bf16[32,64,128]{2,1,0:T(8,128)(2,1)S(1)}, u32[]{:S(2)}, u32[]{:S(2)}) collective-permute-start(bf16[32,64,128]{2,1,0:T(8,128)(2,1)S(1)} %constant_dynamic-update-slice_fusion.refs_4_), channel_id=1, source_target_pairs={{0,1},{1,138},{2,3},{3,196},{4,5},{5,70},{6,7},{7,328},{8,9},{9,20... | collective-permute-start | bytes 1572872 | tf_op jit(solution)/shard_map/ppermute | solution.py:69
  103.6 4.5 %collective-permute-start.7 = (bf16[64,64,128]{2,1,0:T(8,128)(2,1)S(1)}, bf16[64,64,128]{2,1,0:T(8,128)(2,1)S(1)}, u32[]{:S(2)}, u32[]{:S(2)}) collective-permute-start(bf16[64,64,128]{2,1,0:T(8,128)(2,1)S(1)} %all_to_all.10.refs_7_), channel_id=1, source_target_pairs={{0,8},{1,9},{2,10},{3,11},{4,12},{5,13},{6,14},{7,15},{8,0},{9,1},... | collective-permute-start | bytes 3145736 | tf_op jit(solution)/shard_map/ppermute | solution.py:69
  110.5 22.3 %collective-permute-start.8 = (bf16[16,64,128]{2,1,0:T(8,128)(2,1)S(1)}, bf16[16,64,128]{2,1,0:T(8,128)(2,1)S(1)}, u32[]{:S(2)}, u32[]{:S(2)}) collective-permute-start(bf16[16,64,128]{2,1,0:T(8,128)(2,1)S(1)} %shard_map.38), channel_id=1, source_target_pairs={{0,6},{1,38},{2,65},{3,97},{4,128},{5,160},{6,195},{7,227},{8,7},{... | collective-permute-start | bytes 786440 | tf_op jit(solution)/shard_map/ppermute | solution.py:219

commit v12 on v11

--- a/solution.py
+++ b/solution.py
@@ -56,8 +56,13 @@
     return held_at(panel, spot(panel, group))[1 - lane(panel, group)]
 
 
-def plane_order(panel):
-    return [group for x in range(4) for group in held_at(panel, x)]
+def across(panel, group, flip):
+    return held_at(panel, spot(panel, group) ^ flip)[lane(panel, group)]
+
+
+def near_first(panel, group):
+    near = [across(panel, group, flip) for flip in range(4)]
+    return near + [opposite(panel, other) for other in near]
 
 
 def arrival(panel, group):
@@ -78,16 +83,13 @@
     [device(half, x, y, core, 0) // GROUPS for x in range(4)]
     for half in range(2) for y in range(4) for core in range(2)
 ]
-CORES = [[2 * chip, 2 * chip + 1] for chip in range(PANELS // 2)]
-
-
-def gather_cores(near, rows):
-    return [
-        lax.all_gather(
-            near[j : j + rows], "row", axis=0, tiled=True, axis_index_groups=CORES
-        )
-        for j in range(0, near.shape[0], rows)
+def gather_square(square):
+    near = [
+        send(square, lambda p, g: place(p, across(p, g, flip))) for flip in (1, 2, 3)
     ]
+    near = jnp.concatenate(near, axis=0)
+    far = [send(piece, lambda p, g: place(p, opposite(p, g))) for piece in (square, near)]
+    return [square, near] + far
 
 
 def gather_row(near):
@@ -101,9 +103,9 @@
     ]
 
 
-def pass_rows(part, pair):
+def pass_rows(pair, rest):
     pair = send(pair, lambda p, g: place((p + (-4 if p % 4 < 2 else 4)) % PANELS, g))
-    rest = send(part, lambda p, g: place(((p ^ 1) + (4 if p % 2 else -4)) % PANELS, g))
+    rest = send(rest, lambda p, g: place((p + (4 if p % 2 else -4)) % PANELS, g))
     return pair, rest
 
 
@@ -179,7 +181,7 @@
 
     jobs = np.zeros((PANELS * GROUPS, 2 + 2 * GROUPS), np.int32)
     for job in JOBS:
-        jobs[place(*job)] = [*job, *plane_order(job[0]), *arrival(*job)]
+        jobs[place(*job)] = [*job, *arrival(*job), *near_first(*job)]
     here = lax.axis_index("row") * GROUPS + lax.axis_index("col")
     job = lax.dynamic_index_in_dim(jnp.array(jobs), here, 0, keepdims=False)
     part = lax.ppermute(density, AXES, route(start, between))
@@ -209,12 +211,13 @@
 
     one, two, three = gather_column(part)
     pair = jnp.concatenate([two, three], axis=0)
-    outer, rest = pass_rows(part, pair)
+    outer, rest = pass_rows(pair, one)
     near = gather_ring(part, X_RINGS)
-    left = gather_cores(near, local_rows)
+    near, outer, rest = lax.optimization_barrier((near, outer, rest))
+    left = gather_row(near)
     table = [part, one, pair, outer, rest]
     square = product(index[0], mask[0], table, left, local_rows)
-    left = gather_row(gather_ring(square, X_RINGS))
+    left = gather_square(square)
     result = product(index[1], mask[1], table, left, local_rows, [square])
     return lax.ppermute(result, AXES, route(place, start)).astype(jnp.float32)
 

time: 134 us -> 135 us (level)
  blocking collectives: 29.6 us -> 0 us
  waiting for transfers between devices: 35 us -> 57.3 us
  starting transfers between devices: 53.5 us -> 61.7 us
    ppermute x7 -> x12, waiting for transfers between devices: 12.7 us -> 35.8 us  [send(): return lax.ppermute(value, AXES, route(source, place))]
    all_to_all x1 -> x0, blocking collectives: 20.9 us -> none  [gather_ring(): lax.all_to_all(copies, 'row', 0, 0, tiled=True, axis_index_groups=ring)]
    all_gather x4 -> x0, blocking collectives: 8.69 us -> none  [gather_cores(): lax.all_gather(near[j:j + rows], 'row', axis=0, tiled=True, axis_index_gr...]
    ppermute x7 -> x12, starting transfers between devices: 21.9 us -> 30.4 us  [send(): return lax.ppermute(value, AXES, route(source, place))]
  transfers between devices with their start and end apart: 10 -> 15, of which waited for: 6 -> 9; matrix products, arithmetic and copies ran while one was open for 3% -> 3% of each run, Pallas kernels for 0% -> 0%
where the time goes in v12:
time: 135 us
  starting transfers between devices  61.7 us (46%)
  waiting for transfers between devices  57.3 us (42%)
  local copies, waits for them, and re-layouts  4.93 us (4%)
  Pallas kernels  4.63 us (3%)
  between operations  3.83 us (3%)
  other arithmetic  2.43 us (2%)
    ppermute x12, waiting for transfers between devices, send(): return lax.ppermute(value, AXES, route(source, place))  35.8 us
    ppermute x12, starting transfers between devices, send(): return lax.ppermute(value, AXES, route(source, place))  30.4 us
    all_to_all x1, starting transfers between devices, gather_ring(): lax.all_to_all(copies, 'row', 0, 0, tiled=True, axis_index_groups=ring)  19 us
    ppermute x1, waiting for transfers between devices, shards(): return lax.ppermute(result, AXES, route(place, start)).astype(jnp.float32)  16.9 us
    ppermute x1, starting transfers between devices, shards(): part = lax.ppermute(density, AXES, route(start, between))  7.91 us
    pallas_call x2, Pallas kernels, product(): pl.pallas_call(lambda *refs: product_kernel(len(chunks), count, lanes //...  4.63 us
    ppermute x1, waiting for transfers between devices, shards(): part = lax.ppermute(density, AXES, route(start, between))  4.57 us
    ppermute x1, starting transfers between devices, shards(): return lax.ppermute(result, AXES, route(place, start)).astype(jnp.float32)  4.36 us
  transfers between devices with their start and end apart: 15, of which 9 were waited for; matrix products, arithmetic and copies ran while one was open for 3% of the time, Pallas kernels for 0%

profile of v12, /device:TPU:4, one launch (start us, length us, event | category | flops | bytes accessed | tf_op | source)
XLA Modules:
  0.0 134.8 jit_solution(12930263439801387353)
XLA Ops:
  0.0 7.9 %collective-permute-start = (bf16[16,64,128]{2,1,0:T(8,128)(2,1)}, bf16[16,64,128]{2,1,0:T(8,128)(2,1)S(1)}, u32[]{:S(2)}, u32[]{:S(2)}) collective-permute-start(bf16[16,64,128]{2,1,0:T(8,128)(2,1)} %param.3), channel_id=1, source_target_pairs={{0,128},{1,65},{2,194},{3,67},{4,132},{5,197},{6,6},{7,7},{8,144},... | collective-permute-start | bytes 786440 | tf_op jit(solution)/shard_map/ppermute | solution.py:187
  7.9 0.7 fusion.8
  8.8 4.6 %collective-permute-done = bf16[16,64,128]{2,1,0:T(8,128)(2,1)S(1)} collective-permute-done((bf16[16,64,128]{2,1,0:T(8,128)(2,1)}, bf16[16,64,128]{2,1,0:T(8,128)(2,1)S(1)}, u32[]{:S(2)}, u32[]{:S(2)}) %collective-permute-start) | collective-permute-done | bytes 262176 | tf_op jit(solution)/shard_map/ppermute | solution.py:187
  13.4 0.6 fusion.12
  15.7 0.6 gather_fusion
  16.8 0.7 collective-permute-start.1
  17.7 1.0 gather_fusion.1
  22.1 5.4 %collective-permute-start.3 = (bf16[16,64,128]{2,1,0:T(8,128)(2,1)S(1)}, bf16[16,64,128]{2,1,0:T(8,128)(2,1)S(1)}, u32[]{:S(2)}, u32[]{:S(2)}) collective-permute-start(bf16[16,64,128]{2,1,0:T(8,128)(2,1)S(1)} %collective-permute-done.1.refs_2_), channel_id=1, source_target_pairs={{0,32},{1,33},{2,34},{3,35},{4,36},{5,37},{6,38},{7,39},{8,40},{9,... | collective-permute-start | bytes 786440 | tf_op jit(solution)/shard_map/ppermute | solution.py:74
  27.5 2.7 %collective-permute-start.4 = (bf16[16,64,128]{2,1,0:T(8,128)(2,1)S(1)}, bf16[16,64,128]{2,1,0:T(8,128)(2,1)S(1)}, u32[]{:S(2)}, u32[]{:S(2)}) collective-permute-start(bf16[16,64,128]{2,1,0:T(8,128)(2,1)S(1)} %collective-permute-done.1.refs_2_), channel_id=1, source_target_pairs={{0,48},{1,49},{2,50},{3,51},{4,52},{5,53},{6,54},{7,55},{8,56},{9,... | collective-permute-start | bytes 786440 | tf_op jit(solution)/shard_map/ppermute | solution.py:74
  30.2 1.1 pad_maximum_fusion
  31.3 19.0 %all-to-all-start = ((bf16[64,64,128]{2,1,0:T(8,128)(2,1)}), bf16[64,64,128]{2,1,0:T(8,128)(2,1)S(1)}, u32[]{:S(2)}, u32[]{:S(2)}) async-start(bf16[64,64,128]{2,1,0:T(8,128)(2,1)} %pad_maximum_fusion), calls=%async_computation | async-start | bytes 2097152 | tf_op jit(solution)/shard_map/all_to_all | solution.py:79
  50.3 1.9 %collective-permute-start.2 = (bf16[16,64,128]{2,1,0:T(8,128)(2,1)S(1)}, bf16[16,64,128]{2,1,0:T(8,128)(2,1)S(1)}, u32[]{:S(2)}, u32[]{:S(2)}) collective-permute-start(bf16[16,64,128]{2,1,0:T(8,128)(2,1)S(1)} %collective-permute-done.1.refs_2_), channel_id=1, source_target_pairs={{0,16},{1,17},{2,18},{3,19},{4,20},{5,21},{6,22},{7,23},{8,24},{9,... | collective-permute-start | bytes 786440 | tf_op jit(solution)/shard_map/ppermute | solution.py:74
  52.3 1.9 %collective-permute-start.5 = (bf16[32,64,128]{2,1,0:T(8,128)(2,1)S(1)}, bf16[32,64,128]{2,1,0:T(8,128)(2,1)S(1)}, u32[]{:S(2)}, u32[]{:S(2)}) collective-permute-start(bf16[32,64,128]{2,1,0:T(8,128)(2,1)S(1)} %constant_dynamic-update-slice_fusion.refs_4_), channel_id=1, source_target_pairs={{0,1},{1,138},{2,3},{3,196},{4,5},{5,70},{6,7},{7,328},{8,9},{9,20... | collective-permute-start | bytes 1572872 | tf_op jit(solution)/shard_map/ppermute | solution.py:74
  54.2 6.4 %collective-permute-done.2.refs_3_ = bf16[16,64,128]{2,1,0:T(8,128)(2,1)S(1)} collective-permute-done((bf16[16,64,128]{2,1,0:T(8,128)(2,1)S(1)}, bf16[16,64,128]{2,1,0:T(8,128)(2,1)S(1)}, u32[]{:S(2)}, u32[]{:S(2)}) %collective-permute-start.2) | collective-permute-done | bytes 262176 | tf_op jit(solution)/shard_map/ppermute | solution.py:74
  60.6 1.9 %collective-permute-start.6 = (bf16[16,64,128]{2,1,0:T(8,128)(2,1)S(1)}, bf16[16,64,128]{2,1,0:T(8,128)(2,1)S(1)}, u32[]{:S(2)}, u32[]{:S(2)}) collective-permute-start(bf16[16,64,128]{2,1,0:T(8,128)(2,1)S(1)} %collective-permute-done.2.refs_3_), channel_id=1, source_target_pairs={{0,1},{1,138},{2,3},{3,196},{4,5},{5,70},{6,7},{7,328},{8,9},{9,20... | collective-permute-start | bytes 786440 | tf_op jit(solution)/shard_map/ppermute | solution.py:74
  62.5 13.7 %collective-permute-done.6.refs_6_ = bf16[16,64,128]{2,1,0:T(8,128)(2,1)S(1)} collective-permute-done((bf16[16,64,128]{2,1,0:T(8,128)(2,1)S(1)}, bf16[16,64,128]{2,1,0:T(8,128)(2,1)S(1)}, u32[]{:S(2)}, u32[]{:S(2)}) %collective-permute-start.6) | collective-permute-done | bytes 262176 | tf_op jit(solution)/shard_map/ppermute | solution.py:74
  76.2 2.3 %collective-permute-start.7 = (bf16[64,64,128]{2,1,0:T(8,128)(2,1)S(1)}, bf16[64,64,128]{2,1,0:T(8,128)(2,1)S(1)}, u32[]{:S(2)}, u32[]{:S(2)}) collective-permute-start(bf16[64,64,128]{2,1,0:T(8,128)(2,1)S(1)} %all-to-all-done.refs_7_), channel_id=1, source_target_pairs={{0,8},{1,9},{2,10},{3,11},{4,12},{5,13},{6,14},{7,15},{8,0},{9,1},... | collective-permute-start | bytes 3145736 | tf_op jit(solution)/shard_map/ppermute | solution.py:74
  78.6 2.2 %collective-permute-done.7.refs_8_ = bf16[64,64,128]{2,1,0:T(8,128)(2,1)S(1)} collective-permute-done((bf16[64,64,128]{2,1,0:T(8,128)(2,1)S(1)}, bf16[64,64,128]{2,1,0:T(8,128)(2,1)S(1)}, u32[]{:S(2)}, u32[]{:S(2)}) %collective-permute-start.7) | collective-permute-done | bytes 1048608 | tf_op jit(solution)/shard_map/ppermute | solution.py:74
  80.8 2.3 %shard_map.37.refs_7_.refs_11_ = bf16[16,64,128]{2,1,0:T(8,128)(2,1)S(1)} custom-call(s32[256]{0:T(256)S(1)} %bitcast.45, f32[256,256]{1,0:T(8,128)S(1)} %get-tuple-element.25.refs_1_, bf16[16,64,128]{2,1,0:T(8,128)(2,1)S(1)} %collective-permute-done.1.refs_2_, bf16[16,64,128]{2,1,0:T(8,128)(2,1)S(1)} %collective-permute-done.2.refs_3_, ...), custom_call_target="tpu_custom_call" | custom-call | flops 536870912 | bytes 8388608 | tf_op jit(solution)/shard_map/pallas_call | solution.py:157
  83.1 2.9 %collective-permute-start.8 = (bf16[16,64,128]{2,1,0:T(8,128)(2,1)S(1)}, bf16[16,64,128]{2,1,0:T(8,128)(2,1)S(1)}, u32[]{:S(2)}, u32[]{:S(2)}) collective-permute-start(bf16[16,64,128]{2,1,0:T(8,128)(2,1)S(1)} %shard_map.37.refs_7_.refs_11_), channel_id=1, source_target_pairs={{0,64},{1,65},{2,66},{3,67},{4,68},{5,69},{6,70},{7,71},{8,72},{9,... | collective-permute-start | bytes 786440 | tf_op jit(solution)/shard_map/ppermute | solution.py:74
  86.1 3.8 %collective-permute-start.9 = (bf16[16,64,128]{2,1,0:T(8,128)(2,1)S(1)}, bf16[16,64,128]{2,1,0:T(8,128)(2,1)S(1)}, u32[]{:S(2)}, u32[]{:S(2)}) collective-permute-start(bf16[16,64,128]{2,1,0:T(8,128)(2,1)S(1)} %shard_map.37.refs_7_.refs_11_), channel_id=1, source_target_pairs={{0,128},{1,129},{2,130},{3,131},{4,132},{5,133},{6,134},{7,135},{8... | collective-permute-start | bytes 786440 | tf_op jit(solution)/shard_map/ppermute | solution.py:74
  89.8 2.5 %collective-permute-start.10 = (bf16[16,64,128]{2,1,0:T(8,128)(2,1)S(1)}, bf16[16,64,128]{2,1,0:T(8,128)(2,1)S(1)}, u32[]{:S(2)}, u32[]{:S(2)}) collective-permute-start(bf16[16,64,128]{2,1,0:T(8,128)(2,1)S(1)} %shard_map.37.refs_7_.refs_11_), channel_id=1, source_target_pairs={{0,192},{1,193},{2,194},{3,195},{4,196},{5,197},{6,198},{7,199},{8... | collective-permute-start | bytes 786440 | tf_op jit(solution)/shard_map/ppermute | solution.py:74
  92.4 1.8 %collective-permute-done.8 = bf16[16,64,128]{2,1,0:T(8,128)(2,1)S(1)} collective-permute-done((bf16[16,64,128]{2,1,0:T(8,128)(2,1)S(1)}, bf16[16,64,128]{2,1,0:T(8,128)(2,1)S(1)}, u32[]{:S(2)}, u32[]{:S(2)}) %collective-permute-start.8) | collective-permute-done | bytes 262176 | tf_op jit(solution)/shard_map/ppermute | solution.py:74
  94.2 5.8 %collective-permute-done.9 = bf16[16,64,128]{2,1,0:T(8,128)(2,1)S(1)} collective-permute-done((bf16[16,64,128]{2,1,0:T(8,128)(2,1)S(1)}, bf16[16,64,128]{2,1,0:T(8,128)(2,1)S(1)}, u32[]{:S(2)}, u32[]{:S(2)}) %collective-permute-start.9) | collective-permute-done | bytes 262176 | tf_op jit(solution)/shard_map/ppermute | solution.py:74
  100.0 4.9 %collective-permute-done.10 = bf16[16,64,128]{2,1,0:T(8,128)(2,1)S(1)} collective-permute-done((bf16[16,64,128]{2,1,0:T(8,128)(2,1)S(1)}, bf16[16,64,128]{2,1,0:T(8,128)(2,1)S(1)}, u32[]{:S(2)}, u32[]{:S(2)}) %collective-permute-start.10) | collective-permute-done | bytes 262176 | tf_op jit(solution)/shard_map/ppermute | solution.py:74
  104.9 1.9 %collective-permute-start.12 = (bf16[48,64,128]{2,1,0:T(8,128)(2,1)S(1)}, bf16[48,64,128]{2,1,0:T(8,128)(2,1)S(1)}, u32[]{:S(2)}, u32[]{:S(2)}) collective-permute-start(bf16[48,64,128]{2,1,0:T(8,128)(2,1)S(1)} %constant_dynamic-update-slice_fusion.2.refs_8_), channel_id=1, source_target_pairs={{0,8},{1,9},{2,10},{3,11},{4,12},{5,13},{6,14},{7,15},{8,0},{9,1},... | collective-permute-start | bytes 2359304 | tf_op jit(solution)/shard_map/ppermute | solution.py:74
  106.9 2.4 %collective-permute-start.11 = (bf16[16,64,128]{2,1,0:T(8,128)(2,1)S(1)}, bf16[16,64,128]{2,1,0:T(8,128)(2,1)S(1)}, u32[]{:S(2)}, u32[]{:S(2)}) collective-permute-start(bf16[16,64,128]{2,1,0:T(8,128)(2,1)S(1)} %shard_map.37.refs_7_.refs_11_), channel_id=1, source_target_pairs={{0,8},{1,9},{2,10},{3,11},{4,12},{5,13},{6,14},{7,15},{8,0},{9,1},... | collective-permute-start | bytes 786440 | tf_op jit(solution)/shard_map/ppermute | solution.py:74
  109.3 1.1 collective-permute-done.11.refs_9_
  110.4 2.3 %shard_map.38 = bf16[16,64,128]{2,1,0:T(8,128)(2,1)S(1)} custom-call(s32[256]{0:T(256)S(1)} %bitcast.44, f32[256,256]{1,0:T(8,128)S(1)} %get-tuple-element.26.refs_1_, bf16[16,64,128]{2,1,0:T(8,128)(2,1)S(1)} %collective-permute-done.1.refs_2_, bf16[16,64,128]{2,1,0:T(8,128)(2,1)S(1)} %collective-permute-done.2.refs_3_, ...), custom_call_target="tpu_custom_call" | custom-call | flops 536870912 | bytes 8388608 | tf_op jit(solution)/shard_map/pallas_call | solution.py:157
  112.7 4.4 %collective-permute-start.13 = (bf16[16,64,128]{2,1,0:T(8,128)(2,1)S(1)}, bf16[16,64,128]{2,1,0:T(8,128)(2,1)S(1)}, u32[]{:S(2)}, u32[]{:S(2)}) collective-permute-start(bf16[16,64,128]{2,1,0:T(8,128)(2,1)S(1)} %shard_map.38), channel_id=1, source_target_pairs={{0,6},{1,38},{2,65},{3,97},{4,128},{5,160},{6,195},{7,227},{8,7},{... | collective-permute-start | bytes 786440 | tf_op jit(solution)/shard_map/ppermute | solution.py:222
  117.1 16.9 %collective-permute-done.13 = bf16[16,64,128]{2,1,0:T(8,128)(2,1)S(1)} collective-permute-done((bf16[16,64,128]{2,1,0:T(8,128)(2,1)S(1)}, bf16[16,64,128]{2,1,0:T(8,128)(2,1)S(1)}, u32[]{:S(2)}, u32[]{:S(2)}) %collective-permute-start.13) | collective-permute-done | bytes 262176 | tf_op jit(solution)/shard_map/ppermute | solution.py:222
  133.9 0.8 convert_element_type.8
  (49 shorter events, 2.5 us)
Async XLA Ops:
  0.0 8.7 %copy-start = (s32[1024,16]{0,1:T(8,128)S(1)}, s32[1024,16]{0,1:T(8,128)}, u32[]{:S(2)}) copy-start(s32[1024,16]{0,1:T(8,128)} %param.4) | copy-start | bytes 196612
  0.0 13.3 %collective-permute-start = (bf16[16,64,128]{2,1,0:T(8,128)(2,1)}, bf16[16,64,128]{2,1,0:T(8,128)(2,1)S(1)}, u32[]{:S(2)}, u32[]{:S(2)}) collective-permute-start(bf16[16,64,128]{2,1,0:T(8,128)(2,1)} %param.3), channel_id=1, source_target_pairs={{0,128},{1,65},{2,194},{3,67},{4,132},{5,197},{6,6},{7,7},{8,144},... | collective-permute-start | bytes 786440 | tf_op jit(solution)/shard_map/ppermute | solution.py:187
  16.8 5.2 %collective-permute-start.1 = (bf16[16,64,128]{2,1,0:T(8,128)(2,1)S(1)}, bf16[16,64,128]{2,1,0:T(8,128)(2,1)S(1)}, u32[]{:S(2)}, u32[]{:S(2)}) collective-permute-start(bf16[16,64,128]{2,1,0:T(8,128)(2,1)S(1)} %collective-permute-done), channel_id=1, source_target_pairs={{0,4},{1,2},{2,10},{3,6},{4,12},{5,14},{6,0},{7,8},{8,5},{9,3},{10... | collective-permute-start | bytes 786440 | tf_op jit(solution)/shard_map/ppermute | solution.py:74
  22.1 30.2 %collective-permute-start.3 = (bf16[16,64,128]{2,1,0:T(8,128)(2,1)S(1)}, bf16[16,64,128]{2,1,0:T(8,128)(2,1)S(1)}, u32[]{:S(2)}, u32[]{:S(2)}) collective-permute-start(bf16[16,64,128]{2,1,0:T(8,128)(2,1)S(1)} %collective-permute-done.1.refs_2_), channel_id=1, source_target_pairs={{0,32},{1,33},{2,34},{3,35},{4,36},{5,37},{6,38},{7,39},{8,40},{9,... | collective-permute-start | bytes 786440 | tf_op jit(solution)/shard_map/ppermute | solution.py:74
  27.5 24.8 %collective-permute-start.4 = (bf16[16,64,128]{2,1,0:T(8,128)(2,1)S(1)}, bf16[16,64,128]{2,1,0:T(8,128)(2,1)S(1)}, u32[]{:S(2)}, u32[]{:S(2)}) collective-permute-start(bf16[16,64,128]{2,1,0:T(8,128)(2,1)S(1)} %collective-permute-done.1.refs_2_), channel_id=1, source_target_pairs={{0,48},{1,49},{2,50},{3,51},{4,52},{5,53},{6,54},{7,55},{8,56},{9,... | collective-permute-start | bytes 786440 | tf_op jit(solution)/shard_map/ppermute | solution.py:74
  31.3 44.9 %all-to-all-start = ((bf16[64,64,128]{2,1,0:T(8,128)(2,1)}), bf16[64,64,128]{2,1,0:T(8,128)(2,1)S(1)}, u32[]{:S(2)}, u32[]{:S(2)}) async-start(bf16[64,64,128]{2,1,0:T(8,128)(2,1)} %pad_maximum_fusion), calls=%async_computation | async-start | bytes 2097152 | tf_op jit(solution)/shard_map/all_to_all | solution.py:79
  50.3 10.3 %collective-permute-start.2 = (bf16[16,64,128]{2,1,0:T(8,128)(2,1)S(1)}, bf16[16,64,128]{2,1,0:T(8,128)(2,1)S(1)}, u32[]{:S(2)}, u32[]{:S(2)}) collective-permute-start(bf16[16,64,128]{2,1,0:T(8,128)(2,1)S(1)} %collective-permute-done.1.refs_2_), channel_id=1, source_target_pairs={{0,16},{1,17},{2,18},{3,19},{4,20},{5,21},{6,22},{7,23},{8,24},{9,... | collective-permute-start | bytes 786440 | tf_op jit(solution)/shard_map/ppermute | solution.py:74
  52.3 23.9 %collective-permute-start.5 = (bf16[32,64,128]{2,1,0:T(8,128)(2,1)S(1)}, bf16[32,64,128]{2,1,0:T(8,128)(2,1)S(1)}, u32[]{:S(2)}, u32[]{:S(2)}) collective-permute-start(bf16[32,64,128]{2,1,0:T(8,128)(2,1)S(1)} %constant_dynamic-update-slice_fusion.refs_4_), channel_id=1, source_target_pairs={{0,1},{1,138},{2,3},{3,196},{4,5},{5,70},{6,7},{7,328},{8,9},{9,20... | collective-permute-start | bytes 1572872 | tf_op jit(solution)/shard_map/ppermute | solution.py:74
  60.6 15.6 %collective-permute-start.6 = (bf16[16,64,128]{2,1,0:T(8,128)(2,1)S(1)}, bf16[16,64,128]{2,1,0:T(8,128)(2,1)S(1)}, u32[]{:S(2)}, u32[]{:S(2)}) collective-permute-start(bf16[16,64,128]{2,1,0:T(8,128)(2,1)S(1)} %collective-permute-done.2.refs_3_), channel_id=1, source_target_pairs={{0,1},{1,138},{2,3},{3,196},{4,5},{5,70},{6,7},{7,328},{8,9},{9,20... | collective-permute-start | bytes 786440 | tf_op jit(solution)/shard_map/ppermute | solution.py:74
  76.2 4.6 %collective-permute-start.7 = (bf16[64,64,128]{2,1,0:T(8,128)(2,1)S(1)}, bf16[64,64,128]{2,1,0:T(8,128)(2,1)S(1)}, u32[]{:S(2)}, u32[]{:S(2)}) collective-permute-start(bf16[64,64,128]{2,1,0:T(8,128)(2,1)S(1)} %all-to-all-done.refs_7_), channel_id=1, source_target_pairs={{0,8},{1,9},{2,10},{3,11},{4,12},{5,13},{6,14},{7,15},{8,0},{9,1},... | collective-permute-start | bytes 3145736 | tf_op jit(solution)/shard_map/ppermute | solution.py:74
  83.1 11.0 %collective-permute-start.8 = (bf16[16,64,128]{2,1,0:T(8,128)(2,1)S(1)}, bf16[16,64,128]{2,1,0:T(8,128)(2,1)S(1)}, u32[]{:S(2)}, u32[]{:S(2)}) collective-permute-start(bf16[16,64,128]{2,1,0:T(8,128)(2,1)S(1)} %shard_map.37.refs_7_.refs_11_), channel_id=1, source_target_pairs={{0,64},{1,65},{2,66},{3,67},{4,68},{5,69},{6,70},{7,71},{8,72},{9,... | collective-permute-start | bytes 786440 | tf_op jit(solution)/shard_map/ppermute | solution.py:74
  86.1 13.9 %collective-permute-start.9 = (bf16[16,64,128]{2,1,0:T(8,128)(2,1)S(1)}, bf16[16,64,128]{2,1,0:T(8,128)(2,1)S(1)}, u32[]{:S(2)}, u32[]{:S(2)}) collective-permute-start(bf16[16,64,128]{2,1,0:T(8,128)(2,1)S(1)} %shard_map.37.refs_7_.refs_11_), channel_id=1, source_target_pairs={{0,128},{1,129},{2,130},{3,131},{4,132},{5,133},{6,134},{7,135},{8... | collective-permute-start | bytes 786440 | tf_op jit(solution)/shard_map/ppermute | solution.py:74
  89.8 15.1 %collective-permute-start.10 = (bf16[16,64,128]{2,1,0:T(8,128)(2,1)S(1)}, bf16[16,64,128]{2,1,0:T(8,128)(2,1)S(1)}, u32[]{:S(2)}, u32[]{:S(2)}) collective-permute-start(bf16[16,64,128]{2,1,0:T(8,128)(2,1)S(1)} %shard_map.37.refs_7_.refs_11_), channel_id=1, source_target_pairs={{0,192},{1,193},{2,194},{3,195},{4,196},{5,197},{6,198},{7,199},{8... | collective-permute-start | bytes 786440 | tf_op jit(solution)/shard_map/ppermute | solution.py:74
  104.9 5.5 %collective-permute-start.12 = (bf16[48,64,128]{2,1,0:T(8,128)(2,1)S(1)}, bf16[48,64,128]{2,1,0:T(8,128)(2,1)S(1)}, u32[]{:S(2)}, u32[]{:S(2)}) collective-permute-start(bf16[48,64,128]{2,1,0:T(8,128)(2,1)S(1)} %constant_dynamic-update-slice_fusion.2.refs_8_), channel_id=1, source_target_pairs={{0,8},{1,9},{2,10},{3,11},{4,12},{5,13},{6,14},{7,15},{8,0},{9,1},... | collective-permute-start | bytes 2359304 | tf_op jit(solution)/shard_map/ppermute | solution.py:74
  106.9 3.6 %collective-permute-start.11 = (bf16[16,64,128]{2,1,0:T(8,128)(2,1)S(1)}, bf16[16,64,128]{2,1,0:T(8,128)(2,1)S(1)}, u32[]{:S(2)}, u32[]{:S(2)}) collective-permute-start(bf16[16,64,128]{2,1,0:T(8,128)(2,1)S(1)} %shard_map.37.refs_7_.refs_11_), channel_id=1, source_target_pairs={{0,8},{1,9},{2,10},{3,11},{4,12},{5,13},{6,14},{7,15},{8,0},{9,1},... | collective-permute-start | bytes 786440 | tf_op jit(solution)/shard_map/ppermute | solution.py:74
  112.7 21.2 %collective-permute-start.13 = (bf16[16,64,128]{2,1,0:T(8,128)(2,1)S(1)}, bf16[16,64,128]{2,1,0:T(8,128)(2,1)S(1)}, u32[]{:S(2)}, u32[]{:S(2)}) collective-permute-start(bf16[16,64,128]{2,1,0:T(8,128)(2,1)S(1)} %shard_map.38), channel_id=1, source_target_pairs={{0,6},{1,38},{2,65},{3,97},{4,128},{5,160},{6,195},{7,227},{8,7},{... | collective-permute-start | bytes 786440 | tf_op jit(solution)/shard_map/ppermute | solution.py:222

commit v13 on v9

--- a/solution.py
+++ b/solution.py
@@ -167,7 +167,7 @@
     job = lax.dynamic_index_in_dim(jnp.array(jobs), here, 0, keepdims=False)
     part = lax.ppermute(density, AXES, route(start, between))
     own = lax.dynamic_slice_in_dim(columns, job[0, 0] * local_rows, local_rows, 0)
-    part, own, job = lax.optimization_barrier((part, own, job))
+    part, own = lax.optimization_barrier((part, own))
     part = send(part, between)
     panel, mine, order = job[0, 0], job[0, 1], job[1]
 

time: 129 us -> 128 us (level)
  the two profiles are of different devices: /device:TPU:4 before, /device:TPU:38 now
where the time goes in v13:
time: 128 us; the launch traced here: 127 us
  waiting for transfers between devices  58.1 us (45%)
  starting transfers between devices  36.8 us (29%)
  blocking collectives  18.4 us (14%)
  Pallas kernels  4.61 us (4%)
  between operations  3.46 us (3%)
  local copies, waits for them, and re-layouts  3.33 us (3%)
  other arithmetic  2.51 us (2%)
    ppermute x8, waiting for transfers between devices, send(): return lax.ppermute(value, AXES, route(source, place))  32.4 us
    ppermute x8, starting transfers between devices, send(): return lax.ppermute(value, AXES, route(source, place))  24.1 us
    ppermute x1, waiting for transfers between devices, shards(): return lax.ppermute(result, AXES, route(place, start)).astype(jnp.float32)  22.4 us
    all_to_all x1, blocking collectives, gather_ring(): lax.all_to_all(copies, 'row', 0, 0, tiled=True, axis_index_groups=ring)  18.4 us
    all_to_all x1, starting transfers between devices, gather_ring(): lax.all_to_all(copies, 'row', 0, 0, tiled=True, axis_index_groups=ring)  7.44 us
    pallas_call x2, Pallas kernels, product(): pl.pallas_call(lambda *refs: product_kernel(count, lanes // width, keep,...  4.61 us
    ppermute x1, waiting for transfers between devices, shards(): part = lax.ppermute(density, AXES, route(start, between))  3.27 us
    ppermute x1, starting transfers between devices, shards(): part = lax.ppermute(density, AXES, route(start, between))  2.86 us
  transfers between devices with their start and end apart: 11, of which 7 were waited for; matrix products, arithmetic and copies ran while one was open for 3% of the time, Pallas kernels for 0%

profile of v13, /device:TPU:38, one launch (start us, length us, event | category | flops | bytes accessed | tf_op | source)
XLA Modules:
  0.0 127.3 jit_solution(9914339183011394384)
XLA Ops:
  0.0 2.9 %collective-permute-start = (bf16[16,64,128]{2,1,0:T(8,128)(2,1)}, bf16[16,64,128]{2,1,0:T(8,128)(2,1)S(1)}, u32[]{:S(2)}, u32[]{:S(2)}) collective-permute-start(bf16[16,64,128]{2,1,0:T(8,128)(2,1)} %param.3), channel_id=1, source_target_pairs={{0,128},{1,65},{2,194},{3,67},{4,132},{5,197},{6,6},{7,7},{8,144},... | collective-permute-start | bytes 786440 | tf_op jit(solution)/shard_map/ppermute | solution.py:168
  2.9 0.7 constant_dynamic-slice_fusion.3
  3.6 0.6 fusion.10
  7.5 0.2 copy.24
  7.8 3.3 %collective-permute-done = bf16[16,64,128]{2,1,0:T(8,128)(2,1)S(1)} collective-permute-done((bf16[16,64,128]{2,1,0:T(8,128)(2,1)}, bf16[16,64,128]{2,1,0:T(8,128)(2,1)S(1)}, u32[]{:S(2)}, u32[]{:S(2)}) %collective-permute-start) | collective-permute-done | bytes 262176 | tf_op jit(solution)/shard_map/ppermute | solution.py:168
  11.2 0.1 copy.22
  11.4 0.1 reshape_reshape.3
  11.6 3.3 %collective-permute-start.1 = (bf16[16,64,128]{2,1,0:T(8,128)(2,1)S(1)}, bf16[16,64,128]{2,1,0:T(8,128)(2,1)S(1)}, u32[]{:S(2)}, u32[]{:S(2)}) collective-permute-start(bf16[16,64,128]{2,1,0:T(8,128)(2,1)S(1)} %collective-permute-done), channel_id=1, source_target_pairs={{0,4},{1,2},{2,10},{3,6},{4,12},{5,14},{6,0},{7,8},{8,5},{9,3},{10... | collective-permute-start | bytes 786440 | tf_op jit(solution)/shard_map/ppermute | solution.py:65
  14.9 0.7 gather_fusion
  15.7 0.1 copy.23
  16.1 0.1 select_compare_fusion.1
  16.4 0.1 add.86
  16.6 10.3 %collective-permute-done.1.refs_2_ = bf16[16,64,128]{2,1,0:T(8,128)(2,1)S(1)} collective-permute-done((bf16[16,64,128]{2,1,0:T(8,128)(2,1)S(1)}, bf16[16,64,128]{2,1,0:T(8,128)(2,1)S(1)}, u32[]{:S(2)}, u32[]{:S(2)}) %collective-permute-start.1) | collective-permute-done | bytes 262176 | tf_op jit(solution)/shard_map/ppermute | solution.py:65
  26.9 5.9 %collective-permute-start.3 = (bf16[16,64,128]{2,1,0:T(8,128)(2,1)S(1)}, bf16[16,64,128]{2,1,0:T(8,128)(2,1)S(1)}, u32[]{:S(2)}, u32[]{:S(2)}) collective-permute-start(bf16[16,64,128]{2,1,0:T(8,128)(2,1)S(1)} %collective-permute-done.1.refs_2_), channel_id=1, source_target_pairs={{0,32},{1,33},{2,34},{3,35},{4,36},{5,37},{6,38},{7,39},{8,40},{9,... | collective-permute-start | bytes 786440 | tf_op jit(solution)/shard_map/ppermute | solution.py:65
  32.8 3.7 %collective-permute-start.4 = (bf16[16,64,128]{2,1,0:T(8,128)(2,1)S(1)}, bf16[16,64,128]{2,1,0:T(8,128)(2,1)S(1)}, u32[]{:S(2)}, u32[]{:S(2)}) collective-permute-start(bf16[16,64,128]{2,1,0:T(8,128)(2,1)S(1)} %collective-permute-done.1.refs_2_), channel_id=1, source_target_pairs={{0,48},{1,49},{2,50},{3,51},{4,52},{5,53},{6,54},{7,55},{8,56},{9,... | collective-permute-start | bytes 786440 | tf_op jit(solution)/shard_map/ppermute | solution.py:65
  36.5 1.1 pad_maximum_fusion
  37.6 7.4 %all-to-all-start = ((bf16[64,64,128]{2,1,0:T(8,128)(2,1)}), bf16[64,64,128]{2,1,0:T(8,128)(2,1)S(1)}, u32[]{:S(2)}, u32[]{:S(2)}) async-start(bf16[64,64,128]{2,1,0:T(8,128)(2,1)} %pad_maximum_fusion), calls=%async_computation | async-start | bytes 2097152 | tf_op jit(solution)/shard_map/all_to_all | solution.py:70
  45.0 1.9 %collective-permute-start.2 = (bf16[16,64,128]{2,1,0:T(8,128)(2,1)S(1)}, bf16[16,64,128]{2,1,0:T(8,128)(2,1)S(1)}, u32[]{:S(2)}, u32[]{:S(2)}) collective-permute-start(bf16[16,64,128]{2,1,0:T(8,128)(2,1)S(1)} %collective-permute-done.1.refs_2_), channel_id=1, source_target_pairs={{0,16},{1,17},{2,18},{3,19},{4,20},{5,21},{6,22},{7,23},{8,24},{9,... | collective-permute-start | bytes 786440 | tf_op jit(solution)/shard_map/ppermute | solution.py:65
  47.0 3.3 %collective-permute-start.5 = (bf16[32,64,128]{2,1,0:T(8,128)(2,1)S(1)}, bf16[32,64,128]{2,1,0:T(8,128)(2,1)S(1)}, u32[]{:S(2)}, u32[]{:S(2)}) collective-permute-start(bf16[32,64,128]{2,1,0:T(8,128)(2,1)S(1)} %constant_dynamic-update-slice_fusion.refs_4_), channel_id=1, source_target_pairs={{0,1},{1,138},{2,3},{3,196},{4,5},{5,70},{6,7},{7,328},{8,9},{9,20... | collective-permute-start | bytes 1572872 | tf_op jit(solution)/shard_map/ppermute | solution.py:65
  50.3 4.8 %collective-permute-done.2.refs_3_ = bf16[16,64,128]{2,1,0:T(8,128)(2,1)S(1)} collective-permute-done((bf16[16,64,128]{2,1,0:T(8,128)(2,1)S(1)}, bf16[16,64,128]{2,1,0:T(8,128)(2,1)S(1)}, u32[]{:S(2)}, u32[]{:S(2)}) %collective-permute-start.2) | collective-permute-done | bytes 262176 | tf_op jit(solution)/shard_map/ppermute | solution.py:65
  55.2 2.2 %collective-permute-start.6 = (bf16[16,64,128]{2,1,0:T(8,128)(2,1)S(1)}, bf16[16,64,128]{2,1,0:T(8,128)(2,1)S(1)}, u32[]{:S(2)}, u32[]{:S(2)}) collective-permute-start(bf16[16,64,128]{2,1,0:T(8,128)(2,1)S(1)} %collective-permute-done.2.refs_3_), channel_id=1, source_target_pairs={{0,1},{1,138},{2,3},{3,196},{4,5},{5,70},{6,7},{7,328},{8,9},{9,20... | collective-permute-start | bytes 786440 | tf_op jit(solution)/shard_map/ppermute | solution.py:65
  57.3 12.1 %collective-permute-done.6.refs_6_ = bf16[16,64,128]{2,1,0:T(8,128)(2,1)S(1)} collective-permute-done((bf16[16,64,128]{2,1,0:T(8,128)(2,1)S(1)}, bf16[16,64,128]{2,1,0:T(8,128)(2,1)S(1)}, u32[]{:S(2)}, u32[]{:S(2)}) %collective-permute-start.6) | collective-permute-done | bytes 262176 | tf_op jit(solution)/shard_map/ppermute | solution.py:65
  69.4 1.9 %collective-permute-start.7 = (bf16[64,64,128]{2,1,0:T(8,128)(2,1)S(1)}, bf16[64,64,128]{2,1,0:T(8,128)(2,1)S(1)}, u32[]{:S(2)}, u32[]{:S(2)}) collective-permute-start(bf16[64,64,128]{2,1,0:T(8,128)(2,1)S(1)} %all-to-all-done.refs_7_), channel_id=1, source_target_pairs={{0,8},{1,9},{2,10},{3,11},{4,12},{5,13},{6,14},{7,15},{8,0},{9,1},... | collective-permute-start | bytes 3145736 | tf_op jit(solution)/shard_map/ppermute | solution.py:65
  71.3 2.6 %collective-permute-done.7.refs_8_ = bf16[64,64,128]{2,1,0:T(8,128)(2,1)S(1)} collective-permute-done((bf16[64,64,128]{2,1,0:T(8,128)(2,1)S(1)}, bf16[64,64,128]{2,1,0:T(8,128)(2,1)S(1)}, u32[]{:S(2)}, u32[]{:S(2)}) %collective-permute-start.7) | collective-permute-done | bytes 1048608 | tf_op jit(solution)/shard_map/ppermute | solution.py:65
  73.9 2.3 %shard_map.37.refs_9_ = bf16[16,64,128]{2,1,0:T(8,128)(2,1)S(1)} custom-call(s32[256]{0:T(256)S(1)} %fusion.6.refs_0_, f32[256,256]{1,0:T(8,128)S(1)} %add_convert_fusion.refs_1_, bf16[16,64,128]{2,1,0:T(8,128)(2,1)S(1)} %collective-permute-done.1.refs_2_, bf16[16,64,128]{2,1,0:T(8,128)(2,1)S(1)} %collective-permute-done.2.refs_3_, ...), custom_call_target="tpu_custom_call" | custom-call | flops 536870912 | bytes 8388608 | tf_op jit(solution)/shard_map/pallas_call | solution.py:139
  76.4 18.4 %all_to_all.10.refs_7_ = bf16[64,64,128]{2,1,0:T(8,128)(2,1)S(1)} all-to-all(bf16[64,64,128]{2,1,0:T(8,128)(2,1)S(1)} %pad_maximum_fusion.1), channel_id=1, replica_groups={{0,64,128,192},{8,72,136,200},{16,80,144,208},{24,88,152,216},{32,96,16..., dimensions={0} | all-to-all | bytes 2097152 | tf_op jit(solution)/shard_map/all_to_all | solution.py:70
  94.8 1.9 %collective-permute-start.8 = (bf16[64,64,128]{2,1,0:T(8,128)(2,1)S(1)}, bf16[64,64,128]{2,1,0:T(8,128)(2,1)S(1)}, u32[]{:S(2)}, u32[]{:S(2)}) collective-permute-start(bf16[64,64,128]{2,1,0:T(8,128)(2,1)S(1)} %all_to_all.10.refs_7_), channel_id=1, source_target_pairs={{0,8},{1,9},{2,10},{3,11},{4,12},{5,13},{6,14},{7,15},{8,0},{9,1},... | collective-permute-start | bytes 3145736 | tf_op jit(solution)/shard_map/ppermute | solution.py:65
  96.7 2.6 %collective-permute-done.8.refs_8_ = bf16[64,64,128]{2,1,0:T(8,128)(2,1)S(1)} collective-permute-done((bf16[64,64,128]{2,1,0:T(8,128)(2,1)S(1)}, bf16[64,64,128]{2,1,0:T(8,128)(2,1)S(1)}, u32[]{:S(2)}, u32[]{:S(2)}) %collective-permute-start.8) | collective-permute-done | bytes 1048608 | tf_op jit(solution)/shard_map/ppermute | solution.py:65
  99.4 2.3 %shard_map.38 = bf16[16,64,128]{2,1,0:T(8,128)(2,1)S(1)} custom-call(s32[256]{0:T(256)S(1)} %fusion.6.refs_0_, f32[256,256]{1,0:T(8,128)S(1)} %add_convert_fusion.refs_1_, bf16[16,64,128]{2,1,0:T(8,128)(2,1)S(1)} %collective-permute-done.1.refs_2_, bf16[16,64,128]{2,1,0:T(8,128)(2,1)S(1)} %collective-permute-done.2.refs_3_, ...), custom_call_target="tpu_custom_call" | custom-call | flops 536870912 | bytes 8388608 | tf_op jit(solution)/shard_map/pallas_call | solution.py:139
  101.7 2.4 %collective-permute-start.9 = (bf16[16,64,128]{2,1,0:T(8,128)(2,1)S(1)}, bf16[16,64,128]{2,1,0:T(8,128)(2,1)S(1)}, u32[]{:S(2)}, u32[]{:S(2)}) collective-permute-start(bf16[16,64,128]{2,1,0:T(8,128)(2,1)S(1)} %shard_map.38), channel_id=1, source_target_pairs={{0,6},{1,38},{2,65},{3,97},{4,128},{5,160},{6,195},{7,227},{8,7},{... | collective-permute-start | bytes 786440 | tf_op jit(solution)/shard_map/ppermute | solution.py:206
  104.0 22.4 %collective-permute-done.9 = bf16[16,64,128]{2,1,0:T(8,128)(2,1)S(1)} collective-permute-done((bf16[16,64,128]{2,1,0:T(8,128)(2,1)S(1)}, bf16[16,64,128]{2,1,0:T(8,128)(2,1)S(1)}, u32[]{:S(2)}, u32[]{:S(2)}) %collective-permute-start.9) | collective-permute-done | bytes 262176 | tf_op jit(solution)/shard_map/ppermute | solution.py:206
  126.4 0.8 convert_element_type.8
  (31 shorter events, 1.0 us)
Async XLA Ops:
  0.0 5.4 %copy-start = (s32[1024,16]{0,1:T(8,128)S(1)}, s32[1024,16]{0,1:T(8,128)}, u32[]{:S(2)}) copy-start(s32[1024,16]{0,1:T(8,128)} %param.4) | copy-start | bytes 196612
  0.0 11.0 %collective-permute-start = (bf16[16,64,128]{2,1,0:T(8,128)(2,1)}, bf16[16,64,128]{2,1,0:T(8,128)(2,1)S(1)}, u32[]{:S(2)}, u32[]{:S(2)}) collective-permute-start(bf16[16,64,128]{2,1,0:T(8,128)(2,1)} %param.3), channel_id=1, source_target_pairs={{0,128},{1,65},{2,194},{3,67},{4,132},{5,197},{6,6},{7,7},{8,144},... | collective-permute-start | bytes 786440 | tf_op jit(solution)/shard_map/ppermute | solution.py:168
  11.6 15.3 %collective-permute-start.1 = (bf16[16,64,128]{2,1,0:T(8,128)(2,1)S(1)}, bf16[16,64,128]{2,1,0:T(8,128)(2,1)S(1)}, u32[]{:S(2)}, u32[]{:S(2)}) collective-permute-start(bf16[16,64,128]{2,1,0:T(8,128)(2,1)S(1)} %collective-permute-done), channel_id=1, source_target_pairs={{0,4},{1,2},{2,10},{3,6},{4,12},{5,14},{6,0},{7,8},{8,5},{9,3},{10... | collective-permute-start | bytes 786440 | tf_op jit(solution)/shard_map/ppermute | solution.py:65
  26.9 20.1 %collective-permute-start.3 = (bf16[16,64,128]{2,1,0:T(8,128)(2,1)S(1)}, bf16[16,64,128]{2,1,0:T(8,128)(2,1)S(1)}, u32[]{:S(2)}, u32[]{:S(2)}) collective-permute-start(bf16[16,64,128]{2,1,0:T(8,128)(2,1)S(1)} %collective-permute-done.1.refs_2_), channel_id=1, source_target_pairs={{0,32},{1,33},{2,34},{3,35},{4,36},{5,37},{6,38},{7,39},{8,40},{9,... | collective-permute-start | bytes 786440 | tf_op jit(solution)/shard_map/ppermute | solution.py:65
  32.8 14.2 %collective-permute-start.4 = (bf16[16,64,128]{2,1,0:T(8,128)(2,1)S(1)}, bf16[16,64,128]{2,1,0:T(8,128)(2,1)S(1)}, u32[]{:S(2)}, u32[]{:S(2)}) collective-permute-start(bf16[16,64,128]{2,1,0:T(8,128)(2,1)S(1)} %collective-permute-done.1.refs_2_), channel_id=1, source_target_pairs={{0,48},{1,49},{2,50},{3,51},{4,52},{5,53},{6,54},{7,55},{8,56},{9,... | collective-permute-start | bytes 786440 | tf_op jit(solution)/shard_map/ppermute | solution.py:65
  37.6 31.8 %all-to-all-start = ((bf16[64,64,128]{2,1,0:T(8,128)(2,1)}), bf16[64,64,128]{2,1,0:T(8,128)(2,1)S(1)}, u32[]{:S(2)}, u32[]{:S(2)}) async-start(bf16[64,64,128]{2,1,0:T(8,128)(2,1)} %pad_maximum_fusion), calls=%async_computation | async-start | bytes 2097152 | tf_op jit(solution)/shard_map/all_to_all | solution.py:70
  45.0 10.1 %collective-permute-start.2 = (bf16[16,64,128]{2,1,0:T(8,128)(2,1)S(1)}, bf16[16,64,128]{2,1,0:T(8,128)(2,1)S(1)}, u32[]{:S(2)}, u32[]{:S(2)}) collective-permute-start(bf16[16,64,128]{2,1,0:T(8,128)(2,1)S(1)} %collective-permute-done.1.refs_2_), channel_id=1, source_target_pairs={{0,16},{1,17},{2,18},{3,19},{4,20},{5,21},{6,22},{7,23},{8,24},{9,... | collective-permute-start | bytes 786440 | tf_op jit(solution)/shard_map/ppermute | solution.py:65
  47.0 22.3 %collective-permute-start.5 = (bf16[32,64,128]{2,1,0:T(8,128)(2,1)S(1)}, bf16[32,64,128]{2,1,0:T(8,128)(2,1)S(1)}, u32[]{:S(2)}, u32[]{:S(2)}) collective-permute-start(bf16[32,64,128]{2,1,0:T(8,128)(2,1)S(1)} %constant_dynamic-update-slice_fusion.refs_4_), channel_id=1, source_target_pairs={{0,1},{1,138},{2,3},{3,196},{4,5},{5,70},{6,7},{7,328},{8,9},{9,20... | collective-permute-start | bytes 1572872 | tf_op jit(solution)/shard_map/ppermute | solution.py:65
  55.2 14.2 %collective-permute-start.6 = (bf16[16,64,128]{2,1,0:T(8,128)(2,1)S(1)}, bf16[16,64,128]{2,1,0:T(8,128)(2,1)S(1)}, u32[]{:S(2)}, u32[]{:S(2)}) collective-permute-start(bf16[16,64,128]{2,1,0:T(8,128)(2,1)S(1)} %collective-permute-done.2.refs_3_), channel_id=1, source_target_pairs={{0,1},{1,138},{2,3},{3,196},{4,5},{5,70},{6,7},{7,328},{8,9},{9,20... | collective-permute-start | bytes 786440 | tf_op jit(solution)/shard_map/ppermute | solution.py:65
  69.4 4.5 %collective-permute-start.7 = (bf16[64,64,128]{2,1,0:T(8,128)(2,1)S(1)}, bf16[64,64,128]{2,1,0:T(8,128)(2,1)S(1)}, u32[]{:S(2)}, u32[]{:S(2)}) collective-permute-start(bf16[64,64,128]{2,1,0:T(8,128)(2,1)S(1)} %all-to-all-done.refs_7_), channel_id=1, source_target_pairs={{0,8},{1,9},{2,10},{3,11},{4,12},{5,13},{6,14},{7,15},{8,0},{9,1},... | collective-permute-start | bytes 3145736 | tf_op jit(solution)/shard_map/ppermute | solution.py:65
  94.8 4.5 %collective-permute-start.8 = (bf16[64,64,128]{2,1,0:T(8,128)(2,1)S(1)}, bf16[64,64,128]{2,1,0:T(8,128)(2,1)S(1)}, u32[]{:S(2)}, u32[]{:S(2)}) collective-permute-start(bf16[64,64,128]{2,1,0:T(8,128)(2,1)S(1)} %all_to_all.10.refs_7_), channel_id=1, source_target_pairs={{0,8},{1,9},{2,10},{3,11},{4,12},{5,13},{6,14},{7,15},{8,0},{9,1},... | collective-permute-start | bytes 3145736 | tf_op jit(solution)/shard_map/ppermute | solution.py:65
  101.7 24.8 %collective-permute-start.9 = (bf16[16,64,128]{2,1,0:T(8,128)(2,1)S(1)}, bf16[16,64,128]{2,1,0:T(8,128)(2,1)S(1)}, u32[]{:S(2)}, u32[]{:S(2)}) collective-permute-start(bf16[16,64,128]{2,1,0:T(8,128)(2,1)S(1)} %shard_map.38), channel_id=1, source_target_pairs={{0,6},{1,38},{2,65},{3,97},{4,128},{5,160},{6,195},{7,227},{8,7},{... | collective-permute-start | bytes 786440 | tf_op jit(solution)/shard_map/ppermute | solution.py:206
